TPU v7x, 32 devices: a whole 2x2x4 slice. The times are simulated.
32 devices in a mesh: space: 8 (over z, x), basis: 4 (over y, core).
Axes of the slice: x: 2, y: 2, z: 4, core: 2. Of those that a mesh axis runs over, the one named last changes fastest.
Arguments:
- x_block: float32 [16, 3, 8, 32, 128], P(None, None, 'space', 'basis'), may hold values from -68 to 68
- basis: float32 [64, 3, 8, 32, 128], P('basis', None, 'space'), may hold values from -11 to 11
- material: int32 [8, 32, 128], P('space', 'basis'), may hold values from 0 to 7
- k0_blocks: float32 [8, 7, 3, 3], replicated, may hold values from -4 to 4
- k0_diag: float32 [8, 3], replicated, may hold values from 2 to 8
- ke_blocks: float32 [8, 7, 3, 3], replicated, may hold values from -6 to 6
- mass: float32 [8, 3], replicated, may hold values from 0.5 to 2
- velocities: float32 [1024], replicated, may hold values from 0.5 to 1
- shifts: float32 [1024], replicated, may hold values from 0.5 to 1.5
- sample: int32 [1], replicated, may hold values from 0 to 1023
Outputs:
- orthonormal: float32 [16, 3, 8, 32, 128], P(None, None, 'space', 'basis')
- coefficients: float32 [64, 16], P('basis')
- upper_factor: float32 [16, 16], replicated
All inputs are finite; a program needn't handle non-finite values.
Results may differ from a plain program's by a relative error of at most 0.00015.
Values sent between devices are 32-bit elements; how exact they have to be, the bound alone decides.
No kernel may reach another device: no remote copies, remote signals or barrier semaphores. Data moves between devices by JAX's collectives and lax.ppermute only.
A program may use at most 64 MiB of HBM per device.

v0:
```python
import jax
import jax.numpy as jnp
from jax import lax
from jax.sharding import PartitionSpec as P

exact_precision = lax.Precision.HIGHEST


def with_halo(cells, sides, width):
    for axis, dim in sides:
        count = lax.axis_size(axis)
        ends = count - 1
        head = lax.slice_in_dim(cells, 0, width, axis=dim)
        tail = lax.slice_in_dim(cells, cells.shape[dim] - width, cells.shape[dim], axis=dim)
        cells = jnp.concatenate(
            [
                lax.ppermute(tail, axis, [(i, (i + 1) % count) for i in range(ends)]),
                cells,
                lax.ppermute(head, axis, [((i + 1) % count, i) for i in range(ends)]),
            ],
            axis=dim,
        )
    return cells


def stencil_tables(k0_blocks, k0_diag, ke_blocks, mass, velocities, shifts, sample):
    velocity = jnp.take(velocities, sample, axis=0)[0]
    sigma_value = jnp.take(shifts, sample, axis=0)[0]
    center = (k0_diag - sigma_value * mass)[:, :, None] * jnp.eye(3, dtype=jnp.float32)
    tables = k0_blocks - velocity * velocity * ke_blocks
    return tables.at[:, 0].add(center)


def neighbour_views(rimmed):
    centre = rimmed[:, :, 1:-1, 1:-1, :]
    lower_x = rimmed[:, :, :-2, 1:-1, :]
    upper_x = rimmed[:, :, 2:, 1:-1, :]
    lower_y = rimmed[:, :, 1:-1, :-2, :]
    upper_y = rimmed[:, :, 1:-1, 2:, :]
    zero_col = jnp.zeros(centre.shape[:4] + (1,), centre.dtype)
    lower_z = jnp.concatenate((zero_col, centre[:, :, :, :, :-1]), axis=4)
    upper_z = jnp.concatenate((centre[:, :, :, :, 1:], zero_col), axis=4)
    return [centre, lower_x, upper_x, lower_y, upper_y, lower_z, upper_z]


def cell_fields(tables, material_cells):
    material_count = tables.shape[0]
    fields = jnp.zeros((7, 3, 3) + material_cells.shape, jnp.float32)
    for level in range(material_count):
        chosen = (material_cells == level).astype(jnp.float32)
        fields = fields + tables[level][:, :, :, None, None, None] * chosen[None, None, None]
    return fields


def apply_fields(rimmed, fields):
    stencil_views = neighbour_views(rimmed)
    sums = [None, None, None]
    for offset in range(7):
        view = stencil_views[offset]
        for row in range(3):
            term = fields[offset, row, 0][None] * view[:, 0]
            term = term + fields[offset, row, 1][None] * view[:, 1]
            term = term + fields[offset, row, 2][None] * view[:, 2]
            sums[row] = term if sums[row] is None else sums[row] + term
    return jnp.stack(sums, axis=1)


def fine_image(x_block, material, tables):
    rimmed = with_halo(x_block, (("space", 2), ("basis", 3)), 1)
    return apply_fields(rimmed, cell_fields(tables, material))


def group_sum(partial_value):
    return lax.psum(partial_value, "space")


def scaled_block(fine_block, gram_matrix):
    block_cols = fine_block.shape[0]
    lower_factor = jnp.linalg.cholesky(gram_matrix)
    inverse = jax.scipy.linalg.solve_triangular(
        lower_factor, jnp.eye(block_cols, dtype=jnp.float32), lower=True
    ).T
    orthonormal = jnp.einsum("mcxyz,mn->ncxyz", fine_block, inverse, precision=exact_precision)
    return (orthonormal, lower_factor.T)


def finish(fine_block, row_count):
    gram_partial = jnp.einsum("ncxyz,mcxyz->nm", fine_block, fine_block, precision=exact_precision)
    gram_matrix = lax.psum(gram_partial, ("space", "basis")) / row_count
    return scaled_block(fine_block, gram_matrix)


def shards(
    x_block, basis, material, k0_blocks, k0_diag, ke_blocks, mass, velocities, shifts, sample
):
    tables = stencil_tables(k0_blocks, k0_diag, ke_blocks, mass, velocities, shifts, sample)
    block_cols = x_block.shape[0]
    extent_x = x_block.shape[2]
    extent_z = x_block.shape[4]
    full_y = basis.shape[3]
    group_cols = basis.shape[0]
    row_count = 3.0 * extent_x * lax.axis_size("space") * full_y * extent_z
    running = jnp.zeros((group_cols, block_cols), jnp.float32)
    fine_block = fine_image(x_block, material, tables)
    for repeat in range(2):
        partial_value = jnp.einsum(
            "kcxyz,ncxyz->kn",
            basis,
            lax.all_gather(fine_block, "basis", axis=3, tiled=True),
            precision=exact_precision,
        )
        local_coeffs = group_sum(partial_value) / row_count
        correction = jnp.einsum("kcxyz,kn->ncxyz", basis, local_coeffs, precision=exact_precision)
        fine_block = fine_block - lax.psum_scatter(
            correction, "basis", scatter_dimension=3, tiled=True
        )
        running = running + local_coeffs
    orthonormal, upper_factor = finish(fine_block, row_count)
    return (orthonormal, running, upper_factor)


def solution(mesh):
    in_specs = (
        P(None, None, "space", "basis", None),
        P("basis", None, "space", None, None),
        P("space", "basis", None),
        P(),
        P(),
        P(),
        P(),
        P(),
        P(),
        P(),
    )
    out_specs = (P(None, None, "space", "basis", None), P("basis", None), P())
    return jax.shard_map(shards, mesh=mesh, in_specs=in_specs, out_specs=out_specs, check_vma=False)
```

profile of v0, /device:TPU:0, one launch (start us, length us, event | category | flops | bytes accessed | tf_op | source)
XLA Modules:
  0.0 191.4 jit_solution(11265943552710446355)
XLA Ops:
  7.2 0.0 copy-start
  7.2 0.0 reduce-scatter.9.cloned.1.call-start
  7.3 1.0 copy.71
  8.3 1.3 collective-permute-start.1
  9.6 5.5 %collective-permute-start = (f32[16,3,1,8,128]{4,0,3,1,2:T(8,128)S(1)}, f32[16,3,1,8,128]{4,0,3,1,2:T(8,128)S(1)}, u32[]{:S(2)}, u32[]{:S(2)}) collective-permute-start(f32[16,3,1,8,128]{4,0,3,1,2:T(8,128)S(1)} %copy.71), channel_id=1, source_target_pairs={{0,4},{4,8},{8,12},{12,16},{16,20},{20,24},{24,28},{1,5},{5,9},{9,... | collective-permute-start | bytes 589832 | tf_op jit(solution)/shard_map/ppermute | solution.py:17
  15.1 0.0 copy-start.3
  15.1 0.0 copy-start.2
  15.8 1.3 dynamic-slice.13
  17.1 1.3 dynamic-slice.12
  19.6 0.0 copy-done.4
  19.7 0.1 slice_add_fusion
  19.8 0.1 scatter-add.4
  19.9 0.1 copy.94
  20.0 0.1 copy.101
  20.1 0.1 copy.100
  20.2 0.1 copy.99
  20.4 0.1 copy.98
  20.5 0.1 copy.97
  20.6 0.1 copy.96
  20.7 0.1 copy.95
  20.8 0.6 multiply_add_fusion
  21.5 0.1 fusion.22
  21.6 0.0 copy-start.1
  21.6 0.8 collective-permute-done
  22.4 0.1 copy-done.1
  22.6 0.0 collective-permute-done.1
  22.6 1.3 collective-permute-start.3
  23.9 3.0 %collective-permute-start.2 = (f32[16,3,3,1,128]{4,0,3,1,2:T(8,128)S(1)}, f32[16,3,3,1,128]{4,0,3,1,2:T(8,128)S(1)}, u32[]{:S(2)}, u32[]{:S(2)}) collective-permute-start(f32[16,3,3,1,128]{4,0,3,1,2:T(8,128)S(1)} %get-tuple-element.54), channel_id=1, source_target_pairs={{0,1},{1,2},{2,3},{4,5},{5,6},{6,7},{8,9},{9,10},{10,11},{12,13},{... | collective-permute-start | bytes 221192 | tf_op jit(solution)/shard_map/ppermute | solution.py:17
  27.0 0.0 collective-permute-done.3
  27.0 0.9 collective-permute-done.2
  27.9 0.2 add_add_fusion.2
  28.1 0.2 add_add_fusion.1
  28.3 0.2 add_add_fusion
  28.5 11.5 %all_gather.6 = f32[16,3,1,32,128]{4,0,3,1,2:T(8,128)S(1)} all-gather(f32[16,3,1,8,128]{4,0,3,1,2:T(8,128)S(1)} %pad_maximum_fusion), channel_id=1, replica_groups=mesh['space'=8,'basis'=4] {'basis'}, dimensions={3}, use_global_device_ids=true | all-gather | bytes 983040 | tf_op jit(solution)/shard_map/all_gather | solution.py:109
  40.0 1.4 convolution_bitcast_fusion.4
  41.4 20.0 %psum.21 = f32[16,16]{0,1:T(8,128)S(1)} all-reduce(f32[16,16]{0,1:T(8,128)S(1)} %convolution_bitcast_fusion.4), channel_id=1, replica_groups=mesh['space'=8,'basis'=4] {'space'}, use_global_device_ids=true, to_apply=%region_0.1 | all-reduce | flops 256 | bytes 2048 | tf_op jit(solution)/shard_map/psum | solution.py:74
  61.4 1.2 convolution_bitcast_fusion.1
  62.6 0.1 copy.103
  62.6 1.1 copy.129
  63.8 0.0 reduce-scatter.9.cloned.1.call-update
  63.8 0.0 reduce-scatter.11.cloned.1.call-start
  63.9 19.3 %reduce-scatter.9.cloned.1.call-done = f32[8,6144]{1,0:T(8,128)} async-done(((f32[32,6144]{1,0:T(8,128)}), f32[8,6144]{1,0:T(8,128)}) %reduce-scatter.9.cloned.1.call-update) | async-done | bytes 196624
  83.1 1.0 copy.108
  84.1 8.2 %all_gather.7 = f32[16,3,1,32,128]{4,0,3,1,2:T(8,128)S(1)} all-gather(f32[16,3,1,8,128]{4,0,3,1,2:T(8,128)S(1)} %copy_subtract_fusion.1), channel_id=1, replica_groups=mesh['space'=8,'basis'=4] {'basis'}, dimensions={3}, use_global_device_ids=true | all-gather | bytes 983040 | tf_op jit(solution)/shard_map/all_gather | solution.py:109
  92.4 1.4 convolution_bitcast_fusion.3
  93.8 21.6 %psum.22 = f32[16,16]{0,1:T(8,128)S(1)} all-reduce(f32[16,16]{0,1:T(8,128)S(1)} %convolution_bitcast_fusion.3), channel_id=1, replica_groups=mesh['space'=8,'basis'=4] {'space'}, use_global_device_ids=true, to_apply=%region_2.3 | all-reduce | flops 256 | bytes 2048 | tf_op jit(solution)/shard_map/psum | solution.py:74
  115.4 1.1 convolution_bitcast_fusion
  116.5 0.1 copy.105
  116.6 1.1 copy.128
  117.7 0.0 reduce-scatter.11.cloned.1.call-update
  117.8 0.7 copy.86
  118.4 19.4 %reduce-scatter.11.cloned.1.call-done = f32[8,6144]{1,0:T(8,128)} async-done(((f32[32,6144]{1,0:T(8,128)}), f32[8,6144]{1,0:T(8,128)}) %reduce-scatter.11.cloned.1.call-update) | async-done | bytes 196624
  137.8 1.0 copy.110
  138.8 0.3 convolution_bitcast_fusion.6
  139.2 39.3 %psum.23 = f32[16,16]{0,1:T(8,128)S(1)} all-reduce(f32[16,16]{0,1:T(8,128)S(1)} %convolution_bitcast_fusion.6), channel_id=1, replica_groups=mesh['space'=8,'basis'=4] {'space','basis'}, use_global_device_ids=true, to_apply=%region_4.5 | all-reduce | flops 256 | bytes 2048 | tf_op jit(solution)/shard_map/psum | solution.py:89
  178.5 0.1 copy.84
  178.6 1.5 cholesky.17
  180.1 0.6 compare_reduce_fusion
  180.7 0.6 fusion.15
  181.4 0.7 copy.87
  182.0 1.2 custom-call.7
  183.3 0.2 convolution_bitcast_fusion.5
  183.5 0.3 convolution_bitcast_fusion.2
  183.8 0.7 copy.85
  (27 shorter events, 0.3 us)
Async XLA Ops:
  7.2 32.9 %copy-start = (f32[16,3,1,32,128]{4,3,2,1,0:T(8,128)S(1)}, f32[16,3,1,32,128]{4,3,2,1,0:T(8,128)}, u32[]{:S(2)}) copy-start(f32[16,3,1,32,128]{4,3,2,1,0:T(8,128)} %param.13) | copy-start | bytes 2359300
  7.2 75.9 %reduce-scatter.9.cloned.1.call-start = ((), (), s32[]{:S(2)}) async-start(), calls=%async_computation.2 | async-start | bytes 983040
  7.2 12.4 %copy-start.4 = (s32[1,8,128]{2,1,0:T(8,128)S(1)}, s32[1,8,128]{2,1,0:T(8,128)}, u32[]{:S(2)}) copy-start(s32[1,8,128]{2,1,0:T(8,128)} %param.14) | copy-start | bytes 12292
  7.2 12.4 %copy-start.5 = (f32[8,3]{0,1:T(4,128)S(1)}, f32[8,3]{0,1:T(4,128)}, u32[]{:S(2)}) copy-start(f32[8,3]{0,1:T(4,128)} %param.16) | copy-start | bytes 292
  7.2 12.4 %copy-start.6 = (f32[8,3]{0,1:T(4,128)S(1)}, f32[8,3]{0,1:T(4,128)}, u32[]{:S(2)}) copy-start(f32[8,3]{0,1:T(4,128)} %param.18) | copy-start | bytes 292
  8.3 14.3 %collective-permute-start.1 = (f32[16,3,1,8,128]{4,0,3,1,2:T(8,128)S(1)}, f32[16,3,1,8,128]{4,0,3,1,2:T(8,128)S(1)}, u32[]{:S(2)}, u32[]{:S(2)}) collective-permute-start(f32[16,3,1,8,128]{4,0,3,1,2:T(8,128)S(1)} %copy.71), channel_id=1, source_target_pairs={{4,0},{8,4},{12,8},{16,12},{20,16},{24,20},{28,24},{5,1},{9,5},{13... | collective-permute-start | bytes 589832 | tf_op jit(solution)/shard_map/ppermute | solution.py:19
  9.6 12.8 %collective-permute-start = (f32[16,3,1,8,128]{4,0,3,1,2:T(8,128)S(1)}, f32[16,3,1,8,128]{4,0,3,1,2:T(8,128)S(1)}, u32[]{:S(2)}, u32[]{:S(2)}) collective-permute-start(f32[16,3,1,8,128]{4,0,3,1,2:T(8,128)S(1)} %copy.71), channel_id=1, source_target_pairs={{0,4},{4,8},{8,12},{12,16},{16,20},{20,24},{24,28},{1,5},{5,9},{9,... | collective-permute-start | bytes 589832 | tf_op jit(solution)/shard_map/ppermute | solution.py:17
  15.1 4.6 %copy-start.3 = (f32[8,7,3,3]{1,0,3,2:T(8,128)S(1)}, f32[8,7,3,3]{1,0,3,2:T(8,128)}, u32[]{:S(2)}) copy-start(f32[8,7,3,3]{1,0,3,2:T(8,128)} %param.17) | copy-start | bytes 6052
  15.1 4.6 %copy-start.2 = (f32[8,7,3,3]{1,0,3,2:T(8,128)S(1)}, f32[8,7,3,3]{1,0,3,2:T(8,128)}, u32[]{:S(2)}) copy-start(f32[8,7,3,3]{1,0,3,2:T(8,128)} %param.15) | copy-start | bytes 6052
  21.6 0.9 copy-start.1
  22.6 4.4 %collective-permute-start.3 = (f32[16,3,3,1,128]{4,0,3,1,2:T(8,128)S(1)}, f32[16,3,3,1,128]{4,0,3,1,2:T(8,128)S(1)}, u32[]{:S(2)}, u32[]{:S(2)}) collective-permute-start(f32[16,3,3,1,128]{4,0,3,1,2:T(8,128)S(1)} %get-tuple-element.53), channel_id=1, source_target_pairs={{1,0},{2,1},{3,2},{5,4},{6,5},{7,6},{9,8},{10,9},{11,10},{13,12},{... | collective-permute-start | bytes 221192 | tf_op jit(solution)/shard_map/ppermute | solution.py:19
  23.9 3.9 %collective-permute-start.2 = (f32[16,3,3,1,128]{4,0,3,1,2:T(8,128)S(1)}, f32[16,3,3,1,128]{4,0,3,1,2:T(8,128)S(1)}, u32[]{:S(2)}, u32[]{:S(2)}) collective-permute-start(f32[16,3,3,1,128]{4,0,3,1,2:T(8,128)S(1)} %get-tuple-element.54), channel_id=1, source_target_pairs={{0,1},{1,2},{2,3},{4,5},{5,6},{6,7},{8,9},{9,10},{10,11},{12,13},{... | collective-permute-start | bytes 221192 | tf_op jit(solution)/shard_map/ppermute | solution.py:17
  63.8 74.0 %reduce-scatter.11.cloned.1.call-start = ((), (), s32[]{:S(2)}) async-start(), calls=%async_computation.3 | async-start | bytes 983040
Sparse Core Ops, SparseCore 0:
  63.9 19.1 reduce-scatter.8
  117.9 19.9 reduce-scatter.10
where the time goes:
time: 192 us; the launch traced here: 191 us
  blocking collectives  101 us (53%)
  waiting for transfers between devices  40.3 us (21%)
  between operations  16.4 us (9%)
  local copies, waits for them, and re-layouts  11.4 us (6%)
  starting transfers between devices  11.2 us (6%)
  matrix products  5.96 us (3%)
  other arithmetic  5.42 us (3%)
    psum x2, blocking collectives, group_sum(): return lax.psum(partial_value, 'space')  41.6 us
    psum x1, blocking collectives, finish(): gram_matrix = lax.psum(gram_partial, ('space', 'basis')) / row_count  39.3 us
    unnamed x4, waiting for transfers between devices  38.7 us
    all_gather x2, blocking collectives, shards(): lax.all_gather(fine_block, 'basis', axis=3, tiled=True)  19.7 us
    ppermute x2, starting transfers between devices, with_halo(): lax.ppermute(tail, axis, [(i, (i + 1) % count) for i in range(ends)])  8.52 us
    unnamed x26, local copies, waits for them, and re-layouts  7.63 us
  transfers between devices with their start and end apart: 6, of which 4 were waited for; matrix products, arithmetic and copies ran while one was open for 3% of the time, Pallas kernels for 0%

commit v1 on v0

v1 whole, which is shorter than its diff:
```python
import jax
import jax.numpy as jnp
from jax import lax
from jax.sharding import PartitionSpec as P

exact_precision = lax.Precision.HIGHEST


def from_lower(values, axis):
    count = lax.axis_size(axis)
    return lax.ppermute(values, axis, [(i, i + 1) for i in range(count - 1)])


def from_upper(values, axis):
    count = lax.axis_size(axis)
    return lax.ppermute(values, axis, [(i + 1, i) for i in range(count - 1)])


def stencil_tables(k0_blocks, k0_diag, ke_blocks, mass, velocities, shifts, sample):
    velocity = jnp.take(velocities, sample, axis=0)[0]
    sigma_value = jnp.take(shifts, sample, axis=0)[0]
    center = (k0_diag - sigma_value * mass)[:, :, None] * jnp.eye(3, dtype=jnp.float32)
    tables = k0_blocks - velocity * velocity * ke_blocks
    return tables.at[:, 0].add(center)


def cell_fields(tables, material_cells):
    fields = jnp.zeros((7, 3, 3) + material_cells.shape, jnp.float32)
    for level in range(tables.shape[0]):
        chosen = (material_cells == level).astype(jnp.float32)
        fields = fields + tables[level][:, :, :, None, None, None] * chosen[None, None, None]
    return fields


def apply_fields(views, fields):
    sums = [None, None, None]
    for offset in range(7):
        view = views[offset]
        for row in range(3):
            term = fields[offset, row, 0][None] * view[:, 0]
            term = term + fields[offset, row, 1][None] * view[:, 1]
            term = term + fields[offset, row, 2][None] * view[:, 2]
            sums[row] = term if sums[row] is None else sums[row] + term
    return jnp.stack(sums, axis=1)


def neighbour_views(x_block):
    extent_x = x_block.shape[2]
    extent_y = x_block.shape[3]
    extent_z = x_block.shape[4]
    before_x = from_lower(x_block[:, :, extent_x - 1 :], "space")
    after_x = from_upper(x_block[:, :, :1], "space")
    before_y = from_lower(x_block[:, :, :, extent_y - 1 :], "basis")
    after_y = from_upper(x_block[:, :, :, :1], "basis")
    zero_col = jnp.zeros(x_block.shape[:4] + (1,), x_block.dtype)
    return [
        x_block,
        jnp.concatenate((before_x, x_block[:, :, : extent_x - 1]), axis=2),
        jnp.concatenate((x_block[:, :, 1:], after_x), axis=2),
        jnp.concatenate((before_y, x_block[:, :, :, : extent_y - 1]), axis=3),
        jnp.concatenate((x_block[:, :, :, 1:], after_y), axis=3),
        jnp.concatenate((zero_col, x_block[:, :, :, :, : extent_z - 1]), axis=4),
        jnp.concatenate((x_block[:, :, :, :, 1:], zero_col), axis=4),
    ]


def own_rows(basis):
    group_cols, comps, extent_x, full_y, extent_z = basis.shape
    count = lax.axis_size("basis")
    pieces = basis.reshape(group_cols, comps, extent_x, count, full_y // count, extent_z)
    pieces = jnp.moveaxis(pieces, 3, 0)
    pieces = lax.all_to_all(pieces, "basis", 0, 0)
    return pieces.reshape((count * group_cols,) + pieces.shape[2:])


def total_sum(part):
    for axis in ("basis", "space"):
        part = jnp.sum(lax.all_gather(part, axis, axis=0), axis=0)
    return part


def shards(
    x_block, basis, material, k0_blocks, k0_diag, ke_blocks, mass, velocities, shifts, sample
):
    tables = stencil_tables(k0_blocks, k0_diag, ke_blocks, mass, velocities, shifts, sample)
    block_cols, comps, extent_x, _, extent_z = x_block.shape
    group_cols = basis.shape[0]
    row_count = float(comps * extent_x * lax.axis_size("space") * basis.shape[3] * extent_z)

    views = neighbour_views(x_block)
    rows = own_rows(basis)
    basis_cols = rows.shape[0]
    applied = apply_fields(views, cell_fields(tables, material))
    joined = jnp.concatenate((rows, applied), axis=0)
    part = jnp.einsum("kcxyz,ncxyz->kn", joined, joined, precision=exact_precision)
    sums = total_sum(part) / row_count
    basis_gram = sums[:basis_cols, :basis_cols]
    first = sums[:basis_cols, basis_cols:]
    block_gram = sums[basis_cols:, basis_cols:]

    def times(left, right):
        return jnp.matmul(left, right, precision=exact_precision)

    gram_first = times(basis_gram, first)
    coeffs = first + (first - gram_first)
    cross = times(coeffs.T, first)
    gram_matrix = block_gram - cross - cross.T + times(coeffs.T, times(basis_gram, coeffs))
    lower_factor = jnp.linalg.cholesky(gram_matrix)
    inverse = lax.linalg.triangular_solve(
        lower_factor, jnp.eye(block_cols, dtype=jnp.float32), left_side=True, lower=True
    ).T
    weights = jnp.concatenate((-times(coeffs, inverse), inverse), axis=0)
    orthonormal = jnp.einsum("kcxyz,kn->ncxyz", joined, weights, precision=exact_precision)
    own_coeffs = lax.dynamic_slice_in_dim(
        coeffs, lax.axis_index("basis") * group_cols, group_cols, axis=0
    )
    return (orthonormal, own_coeffs, lower_factor.T)


def solution(mesh):
    in_specs = (
        P(None, None, "space", "basis", None),
        P("basis", None, "space", None, None),
        P("space", "basis", None),
        P(),
        P(),
        P(),
        P(),
        P(),
        P(),
        P(),
    )
    out_specs = (P(None, None, "space", "basis", None), P("basis", None), P())
    return jax.shard_map(shards, mesh=mesh, in_specs=in_specs, out_specs=out_specs, check_vma=False)
```

time: 192 us -> 77.4 us (0.40)
  blocking collectives: 101 us -> 37.4 us
  waiting for transfers between devices: 40.3 us -> 4.33 us
  between operations: 16.4 us -> 2.92 us
  matrix products: 5.96 us -> 2.42 us
  starting transfers between devices: 11.2 us -> 14.7 us
    psum x3 -> x0, blocking collectives: 80.9 us -> none  [the longest x2 41.6 us: group_sum(): return lax.psum(partial_value, 'space')]
    unnamed x4 -> x0, waiting for transfers between devices: 38.7 us -> none
    all_gather x2, blocking collectives: 19.7 us -> 37.4 us  [total_sum(): part = jnp.sum(lax.all_gather(part, axis, axis=0), axis=0)]
    unnamed x26 -> x14, local copies, waits for them, and re-layouts: 7.63 us -> 3.08 us
    all_to_all x0 -> x1, waiting for transfers between devices: none -> 4.32 us  [own_rows(): pieces = lax.all_to_all(pieces, 'basis', 0, 0)]
    all_to_all x0 -> x1, starting transfers between devices: none -> 3.62 us  [own_rows(): pieces = lax.all_to_all(pieces, 'basis', 0, 0)]
    dot_general x6 -> x7, matrix products: 5.76 us -> 2.22 us  [the longest x1 0.93 us: shards(): jnp.einsum('kcxyz,ncxyz->kn', joined, joined, precision=exact_precision)]
    transpose x0 -> x1, local copies, waits for them, and re-layouts: none -> 2.47 us  [own_rows(): pieces = jnp.moveaxis(pieces, 3, 0)]
  transfers between devices with their start and end apart: 6 -> 5, of which waited for: 4 -> 1; matrix products, arithmetic and copies ran while one was open for 3% -> 10% of each run, Pallas kernels for 0% -> 0%
where the time goes in v1:
time: 77.4 us; the launch traced here: 76.9 us
  blocking collectives  37.4 us (48%)
  starting transfers between devices  14.7 us (19%)
  local copies, waits for them, and re-layouts  9.64 us (12%)
  other arithmetic  5.48 us (7%)
  waiting for transfers between devices  4.33 us (6%)
  between operations  2.92 us (4%)
  matrix products  2.42 us (3%)
    all_gather x2, blocking collectives, total_sum(): part = jnp.sum(lax.all_gather(part, axis, axis=0), axis=0)  37.4 us
    ppermute x2, starting transfers between devices, from_lower(): return lax.ppermute(values, axis, [(i, i + 1) for i in range(count - 1)])  8.51 us
    all_to_all x1, waiting for transfers between devices, own_rows(): pieces = lax.all_to_all(pieces, 'basis', 0, 0)  4.32 us
    all_to_all x1, starting transfers between devices, own_rows(): pieces = lax.all_to_all(pieces, 'basis', 0, 0)  3.62 us
    unnamed x14, local copies, waits for them, and re-layouts  3.08 us
    ppermute x2, starting transfers between devices, from_upper(): return lax.ppermute(values, axis, [(i + 1, i) for i in range(count - 1)])  2.58 us
    transpose x1, local copies, waits for them, and re-layouts, own_rows(): pieces = jnp.moveaxis(pieces, 3, 0)  2.47 us
    another operation x3, other arithmetic, shards(): lower_factor = jnp.linalg.cholesky(gram_matrix)  2.14 us
  transfers between devices with their start and end apart: 5, of which 1 were waited for; matrix products, arithmetic and copies ran while one was open for 10% of the time, Pallas kernels for 0%

profile of v1, /device:TPU:0, one launch (start us, length us, event | category | flops | bytes accessed | tf_op | source)
XLA Modules:
  0.0 76.9 jit_solution(6014518297585862536)
XLA Ops:
  0.6 1.0 %copy.128 = f32[16,3,1,8,128]{4,0,3,1,2:T(8,128)S(1)} copy(f32[16,3,1,8,128]{4,3,2,1,0:T(8,128)} %param.12) | data formatting | bytes 393216 | tf_op args[0]
  1.6 1.3 %collective-permute-start.1 = (f32[16,3,1,8,128]{4,0,3,1,2:T(8,128)S(1)}, f32[16,3,1,8,128]{4,0,3,1,2:T(8,128)S(1)}, u32[]{:S(2)}, u32[]{:S(2)}) collective-permute-start(f32[16,3,1,8,128]{4,0,3,1,2:T(8,128)S(1)} %copy.128), channel_id=1, source_target_pairs={{4,0},{8,4},{12,8},{16,12},{20,16},{24,20},{28,24},{5,1},{9,5},{13... | collective-permute-start | bytes 589832 | tf_op jit(solution)/shard_map/ppermute | solution.py:16
  2.9 5.5 %collective-permute-start = (f32[16,3,1,8,128]{4,0,3,1,2:T(8,128)S(1)}, f32[16,3,1,8,128]{4,0,3,1,2:T(8,128)S(1)}, u32[]{:S(2)}, u32[]{:S(2)}) collective-permute-start(f32[16,3,1,8,128]{4,0,3,1,2:T(8,128)S(1)} %copy.128), channel_id=1, source_target_pairs={{0,4},{4,8},{8,12},{12,16},{16,20},{20,24},{24,28},{1,5},{5,9},{9,... | collective-permute-start | bytes 589832 | tf_op jit(solution)/shard_map/ppermute | solution.py:11
  8.4 1.3 %collective-permute-start.3 = (f32[16,3,1,1,128]{4,0,3,1,2:T(8,128)S(1)}, f32[16,3,1,1,128]{4,0,3,1,2:T(8,128)S(1)}, u32[]{:S(2)}, u32[]{:S(2)}) collective-permute-start(f32[16,3,1,1,128]{4,0,3,1,2:T(8,128)S(1)} %get-tuple-element.120), channel_id=1, source_target_pairs={{1,0},{2,1},{3,2},{5,4},{6,5},{7,6},{9,8},{10,9},{11,10},{13,12},{... | collective-permute-start | bytes 73736 | tf_op jit(solution)/shard_map/ppermute | solution.py:16
  9.7 3.0 %collective-permute-start.2 = (f32[16,3,1,1,128]{4,0,3,1,2:T(8,128)S(1)}, f32[16,3,1,1,128]{4,0,3,1,2:T(8,128)S(1)}, u32[]{:S(2)}, u32[]{:S(2)}) collective-permute-start(f32[16,3,1,1,128]{4,0,3,1,2:T(8,128)S(1)} %get-tuple-element.121), channel_id=1, source_target_pairs={{0,1},{1,2},{2,3},{4,5},{5,6},{6,7},{8,9},{9,10},{10,11},{12,13},{... | collective-permute-start | bytes 73736 | tf_op jit(solution)/shard_map/ppermute | solution.py:11
  12.7 2.5 %copy.118 = f32[4,16,3,1,8,128]{5,1,4,2,3,0:T(8,128)} copy(f32[4,16,3,1,8,128]{5,4,0,2,1,3:T(8,128)} %bitcast.195) | data formatting | bytes 1572864 | tf_op jit(solution)/shard_map/transpose | solution.py:71
  15.2 0.0 copy-start.2
  15.2 0.0 copy-start.3
  15.2 0.0 copy-start.4
  15.2 3.6 %all-to-all-start = ((f32[4,16,3,1,8,128]{5,1,4,2,3,0:T(8,128)}), f32[4,16,3,1,8,128]{5,1,4,2,3,0:T(8,128)S(1)}, u32[]{:S(2)}, u32[]{:S(2)}) async-start(f32[4,16,3,1,8,128]{5,1,4,2,3,0:T(8,128)} %copy.118), calls=%async_computation | async-start | bytes 1572864 | tf_op jit(solution)/shard_map/all_to_all | solution.py:72
  18.8 0.0 copy-start.1
  18.9 0.0 copy-start
  19.6 1.3 %dynamic-slice.13 = f32[1]{0:T(128)} dynamic-slice(f32[1024]{0:T(1024)} %param.20, s32[]{:T(128)} %bitcast.3), dynamic_slice_sizes={1} | dynamic-slice | bytes 12 | tf_op jit(solution)/shard_map/jit(_take)/gather | solution.py:21
  20.8 1.3 %dynamic-slice.12 = f32[1]{0:T(128)} dynamic-slice(f32[1024]{0:T(1024)} %param.19, s32[]{:T(128)} %bitcast.3), dynamic_slice_sizes={1} | dynamic-slice | bytes 12 | tf_op jit(solution)/shard_map/jit(_take)/gather | solution.py:20
  23.4 0.0 copy-done.2
  23.4 0.0 copy-done.3
  23.4 0.0 copy-done.4
  23.5 0.0 copy-done.1
  23.5 0.0 copy-done
  23.5 0.1 slice_add_fusion
  23.6 0.1 scatter-add.4
  23.7 0.1 copy.149
  23.8 0.1 copy.156
  23.9 0.1 copy.155
  24.0 0.1 copy.154
  24.1 0.1 copy.153
  24.2 0.1 copy.152
  24.4 0.1 copy.151
  24.5 0.1 copy.150
  24.6 0.6 multiply_add_fusion
  25.3 0.1 fusion.23
  25.4 0.0 collective-permute-done.3
  25.4 0.0 collective-permute-done.2
  25.5 0.0 collective-permute-done.1
  25.5 0.0 collective-permute-done
  25.5 0.2 add_add_fusion.2
  25.7 0.2 add_add_fusion.1
  25.9 0.2 add_add_fusion
  26.2 4.3 %all-to-all-done = f32[4,16,3,1,8,128]{5,1,4,2,3,0:T(8,128)S(1)} async-done(((f32[4,16,3,1,8,128]{5,1,4,2,3,0:T(8,128)}), f32[4,16,3,1,8,128]{5,1,4,2,3,0:T(8,128)S(1)}, u32[]{:S(2)}, u32[]{:S(2)}) %all-to-all-start) | async-done | bytes 786464 | tf_op jit(solution)/shard_map/all_to_all | solution.py:72
  30.5 0.1 copy.119
  30.6 0.9 %convolution_bitcast_fusion.1 = f32[80,80]{1,0:T(8,128)S(1)} fusion(f32[16,1,1,8,128]{4,0,3,1,2:T(8,128)S(1)} %add_add_fusion, f32[16,1,1,8,128]{4,0,3,1,2:T(8,128)S(1)} %add_add_fusion.1, f32[16,1,1,8,128]{4,0,3,1,2:T(8,128)S(1)} %get-tuple-element.52, f32[64,3,1,8,128]{4,0,3,1,2:T(8,128)S(1)} %bitcast.196), kind=kOutput, calls=%fused_computation.1 | convolution fusion | flops 236666880 | bytes 1008640 | tf_op jit(solution)/shard_map/kcxyz,ncxyz->kn/dot_general | solution.py:95
  31.5 5.5 %all-gather = f32[320,80]{1,0:T(8,128)S(1)} all-gather(f32[80,80]{1,0:T(8,128)S(1)} %convolution_bitcast_fusion.1), channel_id=2, replica_groups=mesh['space'=8,'basis'=4] {'basis'}, dimensions={0}, use_global_device_ids=true | all-gather | bytes 128000 | tf_op jit(solution)/shard_map/all_gather | solution.py:78
  37.0 31.9 %all-gather.1 = f32[640,80]{1,0:T(8,128)S(1)} all-gather(f32[80,80]{1,0:T(8,128)S(1)} %reduce_sum.18), channel_id=3, replica_groups=mesh['space'=8,'basis'=4] {'space'}, dimensions={0}, use_global_device_ids=true | all-gather | bytes 230400 | tf_op jit(solution)/shard_map/all_gather | solution.py:78
  68.9 0.1 copy.139
  69.0 0.1 fusion
  69.2 0.1 fusion.15
  69.3 0.2 fusion.5
  69.4 0.1 constant_dynamic-slice_fusion
  69.5 0.7 copy.144
  70.2 0.1 copy.140
  70.3 0.1 convolution_add_fusion
  70.4 0.1 copy.142
  70.5 1.5 %cholesky.17 = f32[16,16]{1,0:T(8,128)S(1)} custom-call(f32[16,16]{1,0:T(8,128)S(1)} %fusion.13), custom_call_target="Cholesky" | custom-call | tf_op jit(solution)/shard_map/jit(cholesky)/cholesky | solution.py:108
  72.0 0.6 compare_reduce_fusion
  72.6 0.6 fusion.17
  73.3 0.7 copy.145
  74.0 1.2 %custom-call.6 = f32[1,16,16]{1,2,0:T(8,128)S(1)} custom-call(f32[1,16,16]{2,1,0:T(8,128)S(1)} %get-tuple-element.133), custom_call_target="InvertDiagBlocksLowerTriangular" | custom-call | tf_op jit(solution)/shard_map/triangular_solve | solution.py:109
  75.2 0.2 fusion.11
  75.4 0.1 convolution_negate_fusion
  75.5 0.6 convolution_bitcast_fusion
  76.1 0.7 copy.143
  (16 shorter events, 0.2 us)
Async XLA Ops:
  1.6 23.9 %collective-permute-start.1 = (f32[16,3,1,8,128]{4,0,3,1,2:T(8,128)S(1)}, f32[16,3,1,8,128]{4,0,3,1,2:T(8,128)S(1)}, u32[]{:S(2)}, u32[]{:S(2)}) collective-permute-start(f32[16,3,1,8,128]{4,0,3,1,2:T(8,128)S(1)} %copy.128), channel_id=1, source_target_pairs={{4,0},{8,4},{12,8},{16,12},{20,16},{24,20},{28,24},{5,1},{9,5},{13... | collective-permute-start | bytes 589832 | tf_op jit(solution)/shard_map/ppermute | solution.py:16
  2.9 22.6 %collective-permute-start = (f32[16,3,1,8,128]{4,0,3,1,2:T(8,128)S(1)}, f32[16,3,1,8,128]{4,0,3,1,2:T(8,128)S(1)}, u32[]{:S(2)}, u32[]{:S(2)}) collective-permute-start(f32[16,3,1,8,128]{4,0,3,1,2:T(8,128)S(1)} %copy.128), channel_id=1, source_target_pairs={{0,4},{4,8},{8,12},{12,16},{16,20},{20,24},{24,28},{1,5},{5,9},{9,... | collective-permute-start | bytes 589832 | tf_op jit(solution)/shard_map/ppermute | solution.py:11
  8.4 17.0 %collective-permute-start.3 = (f32[16,3,1,1,128]{4,0,3,1,2:T(8,128)S(1)}, f32[16,3,1,1,128]{4,0,3,1,2:T(8,128)S(1)}, u32[]{:S(2)}, u32[]{:S(2)}) collective-permute-start(f32[16,3,1,1,128]{4,0,3,1,2:T(8,128)S(1)} %get-tuple-element.120), channel_id=1, source_target_pairs={{1,0},{2,1},{3,2},{5,4},{6,5},{7,6},{9,8},{10,9},{11,10},{13,12},{... | collective-permute-start | bytes 73736 | tf_op jit(solution)/shard_map/ppermute | solution.py:16
  9.7 15.7 %collective-permute-start.2 = (f32[16,3,1,1,128]{4,0,3,1,2:T(8,128)S(1)}, f32[16,3,1,1,128]{4,0,3,1,2:T(8,128)S(1)}, u32[]{:S(2)}, u32[]{:S(2)}) collective-permute-start(f32[16,3,1,1,128]{4,0,3,1,2:T(8,128)S(1)} %get-tuple-element.121), channel_id=1, source_target_pairs={{0,1},{1,2},{2,3},{4,5},{5,6},{6,7},{8,9},{9,10},{10,11},{12,13},{... | collective-permute-start | bytes 73736 | tf_op jit(solution)/shard_map/ppermute | solution.py:11
  15.2 8.2 %copy-start.2 = (s32[1,8,128]{2,1,0:T(8,128)S(1)}, s32[1,8,128]{2,1,0:T(8,128)}, u32[]{:S(2)}) copy-start(s32[1,8,128]{2,1,0:T(8,128)} %param.14) | copy-start | bytes 12292
  15.2 8.2 %copy-start.3 = (f32[8,3]{0,1:T(4,128)S(1)}, f32[8,3]{0,1:T(4,128)}, u32[]{:S(2)}) copy-start(f32[8,3]{0,1:T(4,128)} %param.16) | copy-start | bytes 292
  15.2 8.2 %copy-start.4 = (f32[8,3]{0,1:T(4,128)S(1)}, f32[8,3]{0,1:T(4,128)}, u32[]{:S(2)}) copy-start(f32[8,3]{0,1:T(4,128)} %param.18) | copy-start | bytes 292
  15.2 15.3 %all-to-all-start = ((f32[4,16,3,1,8,128]{5,1,4,2,3,0:T(8,128)}), f32[4,16,3,1,8,128]{5,1,4,2,3,0:T(8,128)S(1)}, u32[]{:S(2)}, u32[]{:S(2)}) async-start(f32[4,16,3,1,8,128]{5,1,4,2,3,0:T(8,128)} %copy.118), calls=%async_computation | async-start | bytes 1572864 | tf_op jit(solution)/shard_map/all_to_all | solution.py:72
  18.8 4.6 %copy-start.1 = (f32[8,7,3,3]{1,0,3,2:T(8,128)S(1)}, f32[8,7,3,3]{1,0,3,2:T(8,128)}, u32[]{:S(2)}) copy-start(f32[8,7,3,3]{1,0,3,2:T(8,128)} %param.17) | copy-start | bytes 6052
  18.9 4.6 %copy-start = (f32[8,7,3,3]{1,0,3,2:T(8,128)S(1)}, f32[8,7,3,3]{1,0,3,2:T(8,128)}, u32[]{:S(2)}) copy-start(f32[8,7,3,3]{1,0,3,2:T(8,128)} %param.15) | copy-start | bytes 6052

commit v2 on v1

--- a/solution.py
+++ b/solution.py
@@ -75,7 +75,9 @@
 
 def total_sum(part):
     for axis in ("basis", "space"):
-        part = jnp.sum(lax.all_gather(part, axis, axis=0), axis=0)
+        count = lax.axis_size(axis)
+        copies = jnp.broadcast_to(part[None], (count,) + part.shape)
+        part = jnp.sum(lax.all_to_all(copies, axis, 0, 0), axis=0)
     return part
 
 

time: 77.4 us -> 64.8 us (0.84)
  blocking collectives: 37.4 us -> 7.34 us
  waiting for transfers between devices: 4.33 us -> 14.7 us
  starting transfers between devices: 14.7 us -> 20.9 us
    all_gather x2 -> x0, blocking collectives: 37.4 us -> none  [total_sum(): part = jnp.sum(lax.all_gather(part, axis, axis=0), axis=0)]
    all_to_all x0 -> x1, waiting for transfers between devices: none -> 10.4 us  [total_sum(): part = jnp.sum(lax.all_to_all(copies, axis, 0, 0), axis=0)]
    all_to_all x0 -> x1, blocking collectives: none -> 7.34 us  [total_sum(): part = jnp.sum(lax.all_to_all(copies, axis, 0, 0), axis=0)]
    all_to_all x0 -> x1, starting transfers between devices: none -> 6.2 us  [total_sum(): part = jnp.sum(lax.all_to_all(copies, axis, 0, 0), axis=0)]
  transfers between devices with their start and end apart: 5 -> 6, of which waited for: 1 -> 2; matrix products, arithmetic and copies ran while one was open for 10% -> 12% of each run, Pallas kernels for 0% -> 0%
where the time goes in v2:
time: 64.8 us; the launch traced here: 64.2 us
  starting transfers between devices  20.9 us (32%)
  waiting for transfers between devices  14.7 us (23%)
  local copies, waits for them, and re-layouts  10.4 us (16%)
  blocking collectives  7.34 us (11%)
  other arithmetic  5.48 us (8%)
  between operations  2.92 us (5%)
  matrix products  2.42 us (4%)
    all_to_all x1, waiting for transfers between devices, total_sum(): part = jnp.sum(lax.all_to_all(copies, axis, 0, 0), axis=0)  10.4 us
    ppermute x2, starting transfers between devices, from_lower(): return lax.ppermute(values, axis, [(i, i + 1) for i in range(count - 1)])  8.51 us
    all_to_all x1, blocking collectives, total_sum(): part = jnp.sum(lax.all_to_all(copies, axis, 0, 0), axis=0)  7.34 us
    all_to_all x1, starting transfers between devices, total_sum(): part = jnp.sum(lax.all_to_all(copies, axis, 0, 0), axis=0)  6.2 us
    all_to_all x1, waiting for transfers between devices, own_rows(): pieces = lax.all_to_all(pieces, 'basis', 0, 0)  4.31 us
    all_to_all x1, starting transfers between devices, own_rows(): pieces = lax.all_to_all(pieces, 'basis', 0, 0)  3.62 us
    unnamed x14, local copies, waits for them, and re-layouts  3.08 us
    ppermute x2, starting transfers between devices, from_upper(): return lax.ppermute(values, axis, [(i + 1, i) for i in range(count - 1)])  2.58 us
  transfers between devices with their start and end apart: 6, of which 2 were waited for; matrix products, arithmetic and copies ran while one was open for 12% of the time, Pallas kernels for 0%

profile of v2, /device:TPU:0, one launch (start us, length us, event | category | flops | bytes accessed | tf_op | source)
XLA Modules:
  0.0 64.2 jit_solution(3936080809821720808)
XLA Ops:
  0.6 1.0 %copy.128 = f32[16,3,1,8,128]{4,0,3,1,2:T(8,128)S(1)} copy(f32[16,3,1,8,128]{4,3,2,1,0:T(8,128)} %param.12) | data formatting | bytes 393216 | tf_op args[0]
  1.6 1.3 %collective-permute-start.1 = (f32[16,3,1,8,128]{4,0,3,1,2:T(8,128)S(1)}, f32[16,3,1,8,128]{4,0,3,1,2:T(8,128)S(1)}, u32[]{:S(2)}, u32[]{:S(2)}) collective-permute-start(f32[16,3,1,8,128]{4,0,3,1,2:T(8,128)S(1)} %copy.128), channel_id=1, source_target_pairs={{4,0},{8,4},{12,8},{16,12},{20,16},{24,20},{28,24},{5,1},{9,5},{13... | collective-permute-start | bytes 589832 | tf_op jit(solution)/shard_map/ppermute | solution.py:16
  2.9 5.5 %collective-permute-start = (f32[16,3,1,8,128]{4,0,3,1,2:T(8,128)S(1)}, f32[16,3,1,8,128]{4,0,3,1,2:T(8,128)S(1)}, u32[]{:S(2)}, u32[]{:S(2)}) collective-permute-start(f32[16,3,1,8,128]{4,0,3,1,2:T(8,128)S(1)} %copy.128), channel_id=1, source_target_pairs={{0,4},{4,8},{8,12},{12,16},{16,20},{20,24},{24,28},{1,5},{5,9},{9,... | collective-permute-start | bytes 589832 | tf_op jit(solution)/shard_map/ppermute | solution.py:11
  8.4 1.3 %collective-permute-start.3 = (f32[16,3,1,1,128]{4,0,3,1,2:T(8,128)S(1)}, f32[16,3,1,1,128]{4,0,3,1,2:T(8,128)S(1)}, u32[]{:S(2)}, u32[]{:S(2)}) collective-permute-start(f32[16,3,1,1,128]{4,0,3,1,2:T(8,128)S(1)} %get-tuple-element.120), channel_id=1, source_target_pairs={{1,0},{2,1},{3,2},{5,4},{6,5},{7,6},{9,8},{10,9},{11,10},{13,12},{... | collective-permute-start | bytes 73736 | tf_op jit(solution)/shard_map/ppermute | solution.py:16
  9.7 3.0 %collective-permute-start.2 = (f32[16,3,1,1,128]{4,0,3,1,2:T(8,128)S(1)}, f32[16,3,1,1,128]{4,0,3,1,2:T(8,128)S(1)}, u32[]{:S(2)}, u32[]{:S(2)}) collective-permute-start(f32[16,3,1,1,128]{4,0,3,1,2:T(8,128)S(1)} %get-tuple-element.121), channel_id=1, source_target_pairs={{0,1},{1,2},{2,3},{4,5},{5,6},{6,7},{8,9},{9,10},{10,11},{12,13},{... | collective-permute-start | bytes 73736 | tf_op jit(solution)/shard_map/ppermute | solution.py:11
  12.7 2.5 %copy.118 = f32[4,16,3,1,8,128]{5,1,4,2,3,0:T(8,128)} copy(f32[4,16,3,1,8,128]{5,4,0,2,1,3:T(8,128)} %bitcast.192) | data formatting | bytes 1572864 | tf_op jit(solution)/shard_map/transpose | solution.py:71
  15.2 0.0 copy-start.2
  15.2 0.0 copy-start.3
  15.2 0.0 copy-start.4
  15.2 3.6 %all-to-all-start = ((f32[4,16,3,1,8,128]{5,1,4,2,3,0:T(8,128)}), f32[4,16,3,1,8,128]{5,1,4,2,3,0:T(8,128)S(1)}, u32[]{:S(2)}, u32[]{:S(2)}) async-start(f32[4,16,3,1,8,128]{5,1,4,2,3,0:T(8,128)} %copy.118), calls=%async_computation | async-start | bytes 1572864 | tf_op jit(solution)/shard_map/all_to_all | solution.py:72
  18.9 0.0 copy-start.1
  18.9 0.0 copy-start
  19.6 1.3 %dynamic-slice.13 = f32[1]{0:T(128)} dynamic-slice(f32[1024]{0:T(1024)} %param.20, s32[]{:T(128)} %bitcast.3), dynamic_slice_sizes={1} | dynamic-slice | bytes 12 | tf_op jit(solution)/shard_map/jit(_take)/gather | solution.py:21
  20.8 1.3 %dynamic-slice.12 = f32[1]{0:T(128)} dynamic-slice(f32[1024]{0:T(1024)} %param.19, s32[]{:T(128)} %bitcast.3), dynamic_slice_sizes={1} | dynamic-slice | bytes 12 | tf_op jit(solution)/shard_map/jit(_take)/gather | solution.py:20
  23.4 0.0 copy-done.2
  23.4 0.0 copy-done.3
  23.4 0.0 copy-done.4
  23.5 0.0 copy-done.1
  23.5 0.0 copy-done
  23.5 0.1 slice_add_fusion
  23.6 0.1 scatter-add.4
  23.7 0.1 copy.149
  23.8 0.1 copy.156
  23.9 0.1 copy.155
  24.0 0.1 copy.154
  24.1 0.1 copy.153
  24.3 0.1 copy.152
  24.4 0.1 copy.151
  24.5 0.1 copy.150
  24.6 0.6 multiply_add_fusion
  25.3 0.1 fusion.23
  25.4 0.0 collective-permute-done.3
  25.4 0.0 collective-permute-done.2
  25.5 0.0 collective-permute-done.1
  25.5 0.0 collective-permute-done
  25.5 0.2 add_add_fusion.2
  25.7 0.2 add_add_fusion.1
  25.9 0.2 add_add_fusion
  26.2 4.3 %all-to-all-done = f32[4,16,3,1,8,128]{5,1,4,2,3,0:T(8,128)S(1)} async-done(((f32[4,16,3,1,8,128]{5,1,4,2,3,0:T(8,128)}), f32[4,16,3,1,8,128]{5,1,4,2,3,0:T(8,128)S(1)}, u32[]{:S(2)}, u32[]{:S(2)}) %all-to-all-start) | async-done | bytes 786464 | tf_op jit(solution)/shard_map/all_to_all | solution.py:72
  30.5 0.1 copy.119
  30.6 0.9 %convolution_bitcast_fusion.1 = f32[80,80]{1,0:T(8,128)S(1)} fusion(f32[16,1,1,8,128]{4,0,3,1,2:T(8,128)S(1)} %add_add_fusion, f32[16,1,1,8,128]{4,0,3,1,2:T(8,128)S(1)} %add_add_fusion.1, f32[16,1,1,8,128]{4,0,3,1,2:T(8,128)S(1)} %get-tuple-element.52, f32[64,3,1,8,128]{4,0,3,1,2:T(8,128)S(1)} %bitcast.193), kind=kOutput, calls=%fused_computation.1 | convolution fusion | flops 236666880 | bytes 1008640 | tf_op jit(solution)/shard_map/kcxyz,ncxyz->kn/dot_general | solution.py:97
  31.5 7.3 %all_to_all.15 = f32[4,80,80]{2,1,0:T(8,128)S(1)} all-to-all(f32[4,80,80]{2,1,0:T(8,128)S(1)} %broadcast_in_dim.11), channel_id=1, replica_groups=mesh['space'=8,'basis'=4] {'basis'}, dimensions={0} | all-to-all | bytes 204800 | tf_op jit(solution)/shard_map/all_to_all | solution.py:80
  38.9 0.7 %broadcast_in_dim.12 = f32[8,80,80]{2,1,0:T(8,128)} broadcast(f32[80,80]{1,0:T(8,128)S(1)} %reduce_sum.18), dimensions={1,2} | broadcast | bytes 230400 | tf_op jit(solution)/shard_map/broadcast_in_dim | solution.py:79
  39.6 6.2 %all-to-all-start.2 = ((f32[8,80,80]{2,1,0:T(8,128)}), f32[8,80,80]{2,1,0:T(8,128)S(1)}, u32[]{:S(2)}, u32[]{:S(2)}) async-start(f32[8,80,80]{2,1,0:T(8,128)} %broadcast_in_dim.12), calls=%async_computation.2 | async-start | bytes 655360 | tf_op jit(solution)/shard_map/all_to_all | solution.py:80
  45.8 10.4 %all-to-all-done.2 = f32[8,80,80]{2,1,0:T(8,128)S(1)} async-done(((f32[8,80,80]{2,1,0:T(8,128)}), f32[8,80,80]{2,1,0:T(8,128)S(1)}, u32[]{:S(2)}, u32[]{:S(2)}) %all-to-all-start.2) | async-done | bytes 204832 | tf_op jit(solution)/shard_map/all_to_all | solution.py:80
  56.3 0.1 copy.139
  56.3 0.1 fusion
  56.5 0.1 fusion.15
  56.6 0.2 fusion.5
  56.8 0.1 constant_dynamic-slice_fusion
  56.9 0.7 %copy.144 = f32[16,16]{1,0:T(8,128)} copy(f32[16,16]{0,1:T(8,128)S(1)} %constant_dynamic-slice_fusion) | data formatting | bytes 2048
  57.5 0.1 copy.140
  57.6 0.1 convolution_add_fusion
  57.7 0.1 copy.142
  57.8 1.5 %cholesky.17 = f32[16,16]{1,0:T(8,128)S(1)} custom-call(f32[16,16]{1,0:T(8,128)S(1)} %fusion.13), custom_call_target="Cholesky" | custom-call | tf_op jit(solution)/shard_map/jit(cholesky)/cholesky | solution.py:110
  59.3 0.6 %compare_reduce_fusion = pred[]{:T(512)} fusion(f32[16]{0:T(128)S(1)} %select_reduce_fusion), kind=kLoop, calls=%fused_computation.129 | loop fusion | flops 31 | bytes 65 | tf_op jit(solution)/shard_map/jit(cholesky)/cholesky | solution.py:110
  60.0 0.6 %fusion.17 = (f32[16,16]{0,1:T(8,128)S(1)}, f32[1,16,16]{2,1,0:T(8,128)S(1)}) fusion(f32[16,16]{1,0:T(8,128)S(1)} %cholesky.17, pred[]{:T(512)} %compare_reduce_fusion), kind=kLoop, calls=%fused_computation.54 | loop fusion | flops 1024 | bytes 3073 | tf_op jit(solution)/shard_map/transpose | solution.py:119
  60.6 0.7 %copy.145 = f32[16,16]{1,0:T(8,128)} copy(f32[16,16]{0,1:T(8,128)S(1)} %get-tuple-element.132) | data formatting | bytes 2048
  61.3 1.2 %custom-call.6 = f32[1,16,16]{1,2,0:T(8,128)S(1)} custom-call(f32[1,16,16]{2,1,0:T(8,128)S(1)} %get-tuple-element.133), custom_call_target="InvertDiagBlocksLowerTriangular" | custom-call | tf_op jit(solution)/shard_map/triangular_solve | solution.py:111
  62.5 0.2 fusion.11
  62.7 0.1 convolution_negate_fusion
  62.9 0.6 convolution_bitcast_fusion
  63.5 0.7 %copy.143 = f32[16,3,1,8,128]{4,3,2,1,0:T(8,128)} copy(f32[16,3,1,8,128]{4,0,3,1,2:T(8,128)S(1)} %convolution_bitcast_fusion) | data formatting | bytes 393216
  (17 shorter events, 0.2 us)
Async XLA Ops:
  1.6 23.9 %collective-permute-start.1 = (f32[16,3,1,8,128]{4,0,3,1,2:T(8,128)S(1)}, f32[16,3,1,8,128]{4,0,3,1,2:T(8,128)S(1)}, u32[]{:S(2)}, u32[]{:S(2)}) collective-permute-start(f32[16,3,1,8,128]{4,0,3,1,2:T(8,128)S(1)} %copy.128), channel_id=1, source_target_pairs={{4,0},{8,4},{12,8},{16,12},{20,16},{24,20},{28,24},{5,1},{9,5},{13... | collective-permute-start | bytes 589832 | tf_op jit(solution)/shard_map/ppermute | solution.py:16
  2.9 22.6 %collective-permute-start = (f32[16,3,1,8,128]{4,0,3,1,2:T(8,128)S(1)}, f32[16,3,1,8,128]{4,0,3,1,2:T(8,128)S(1)}, u32[]{:S(2)}, u32[]{:S(2)}) collective-permute-start(f32[16,3,1,8,128]{4,0,3,1,2:T(8,128)S(1)} %copy.128), channel_id=1, source_target_pairs={{0,4},{4,8},{8,12},{12,16},{16,20},{20,24},{24,28},{1,5},{5,9},{9,... | collective-permute-start | bytes 589832 | tf_op jit(solution)/shard_map/ppermute | solution.py:11
  8.4 17.0 %collective-permute-start.3 = (f32[16,3,1,1,128]{4,0,3,1,2:T(8,128)S(1)}, f32[16,3,1,1,128]{4,0,3,1,2:T(8,128)S(1)}, u32[]{:S(2)}, u32[]{:S(2)}) collective-permute-start(f32[16,3,1,1,128]{4,0,3,1,2:T(8,128)S(1)} %get-tuple-element.120), channel_id=1, source_target_pairs={{1,0},{2,1},{3,2},{5,4},{6,5},{7,6},{9,8},{10,9},{11,10},{13,12},{... | collective-permute-start | bytes 73736 | tf_op jit(solution)/shard_map/ppermute | solution.py:16
  9.7 15.8 %collective-permute-start.2 = (f32[16,3,1,1,128]{4,0,3,1,2:T(8,128)S(1)}, f32[16,3,1,1,128]{4,0,3,1,2:T(8,128)S(1)}, u32[]{:S(2)}, u32[]{:S(2)}) collective-permute-start(f32[16,3,1,1,128]{4,0,3,1,2:T(8,128)S(1)} %get-tuple-element.121), channel_id=1, source_target_pairs={{0,1},{1,2},{2,3},{4,5},{5,6},{6,7},{8,9},{9,10},{10,11},{12,13},{... | collective-permute-start | bytes 73736 | tf_op jit(solution)/shard_map/ppermute | solution.py:11
  15.2 8.2 %copy-start.2 = (s32[1,8,128]{2,1,0:T(8,128)S(1)}, s32[1,8,128]{2,1,0:T(8,128)}, u32[]{:S(2)}) copy-start(s32[1,8,128]{2,1,0:T(8,128)} %param.14) | copy-start | bytes 12292
  15.2 8.2 %copy-start.3 = (f32[8,3]{0,1:T(4,128)S(1)}, f32[8,3]{0,1:T(4,128)}, u32[]{:S(2)}) copy-start(f32[8,3]{0,1:T(4,128)} %param.16) | copy-start | bytes 292
  15.2 8.2 %copy-start.4 = (f32[8,3]{0,1:T(4,128)S(1)}, f32[8,3]{0,1:T(4,128)}, u32[]{:S(2)}) copy-start(f32[8,3]{0,1:T(4,128)} %param.18) | copy-start | bytes 292
  15.2 15.3 %all-to-all-start = ((f32[4,16,3,1,8,128]{5,1,4,2,3,0:T(8,128)}), f32[4,16,3,1,8,128]{5,1,4,2,3,0:T(8,128)S(1)}, u32[]{:S(2)}, u32[]{:S(2)}) async-start(f32[4,16,3,1,8,128]{5,1,4,2,3,0:T(8,128)} %copy.118), calls=%async_computation | async-start | bytes 1572864 | tf_op jit(solution)/shard_map/all_to_all | solution.py:72
  18.9 4.6 %copy-start.1 = (f32[8,7,3,3]{1,0,3,2:T(8,128)S(1)}, f32[8,7,3,3]{1,0,3,2:T(8,128)}, u32[]{:S(2)}) copy-start(f32[8,7,3,3]{1,0,3,2:T(8,128)} %param.17) | copy-start | bytes 6052
  18.9 4.6 %copy-start = (f32[8,7,3,3]{1,0,3,2:T(8,128)S(1)}, f32[8,7,3,3]{1,0,3,2:T(8,128)}, u32[]{:S(2)}) copy-start(f32[8,7,3,3]{1,0,3,2:T(8,128)} %param.15) | copy-start | bytes 6052
  39.6 16.6 %all-to-all-start.2 = ((f32[8,80,80]{2,1,0:T(8,128)}), f32[8,80,80]{2,1,0:T(8,128)S(1)}, u32[]{:S(2)}, u32[]{:S(2)}) async-start(f32[8,80,80]{2,1,0:T(8,128)} %broadcast_in_dim.12), calls=%async_computation.2 | async-start | bytes 655360 | tf_op jit(solution)/shard_map/all_to_all | solution.py:80

commit v3 on v2

v3 whole, which is shorter than its diff:
```python
import functools

import jax
import jax.numpy as jnp
from jax import lax
from jax.experimental import pallas as pl
from jax.experimental.pallas import tpu as pltpu
from jax.sharding import PartitionSpec as P

exact_precision = lax.Precision.HIGHEST
VMEM = pl.BlockSpec(memory_space=pltpu.VMEM)
SMEM = pl.BlockSpec(memory_space=pltpu.SMEM)
ANY = pl.BlockSpec(memory_space=pl.ANY)


def f32(*shape):
    return jax.ShapeDtypeStruct(shape, jnp.float32)


def from_lower(values, axis):
    count = lax.axis_size(axis)
    return lax.ppermute(values, axis, [(i, i + 1) for i in range(count - 1)])


def from_upper(values, axis):
    count = lax.axis_size(axis)
    return lax.ppermute(values, axis, [(i + 1, i) for i in range(count - 1)])


def stencil_tables(k0_blocks, k0_diag, ke_blocks, mass, velocities, shifts, sample):
    velocity = jnp.take(velocities, sample, axis=0)[0]
    sigma_value = jnp.take(shifts, sample, axis=0)[0]
    center = (k0_diag - sigma_value * mass)[:, :, None] * jnp.eye(3, dtype=jnp.float32)
    tables = k0_blocks - velocity * velocity * ke_blocks
    return tables.at[:, 0].add(center)


def pack_kernel(basis_ref, x_ref, sent_ref, first_ref, last_ref, sems):
    count, cols, comps, rows, lanes = sent_ref.shape
    copies = [
        pltpu.make_async_copy(
            basis_ref.at[:, :, 0, pl.ds(rows * piece, rows), :], sent_ref.at[piece], sems.at[piece]
        )
        for piece in range(count)
    ]
    for copy in copies:
        copy.start()
    block_cols = x_ref.shape[0] // (comps * rows)
    for comp in range(comps):
        there = pl.ds(comp * block_cols, block_cols)
        for edge_ref, row in ((first_ref, 0), (last_ref, rows - 1)):
            edge_ref[there, :] = x_ref[pl.ds(comp * rows + row, block_cols, stride=comps * rows), :]
    for copy in copies:
        copy.wait()


def pack(basis, x_rows, block_cols):
    group_cols, comps, _, full_y, lanes = basis.shape
    count = lax.axis_size("basis")
    edge = f32(comps * block_cols, lanes)
    return pl.pallas_call(
        pack_kernel,
        out_shape=(f32(count, group_cols, comps, full_y // count, lanes), edge, edge),
        in_specs=[ANY, VMEM],
        out_specs=(ANY, VMEM, VMEM),
        scratch_shapes=[pltpu.SemaphoreType.DMA((count,))],
        name="pack",
    )(basis, x_rows)


def stencil_kernel(
    comps, x_ref, before_x_ref, after_x_ref, before_y_ref, after_y_ref, table_ref, material_ref,
    applied_ref,
):
    rows, lanes = material_ref.shape
    levels = table_ref.shape[1]
    block_cols = x_ref.shape[0] // (comps * rows)
    lane = lax.broadcasted_iota(jnp.int32, (block_cols, lanes), 1)
    level = lax.broadcasted_iota(jnp.int32, (levels, lanes), 0)

    def line(ref, comp, row):
        return ref[pl.ds(comp * rows + row, block_cols, stride=comps * rows), :]

    def edge(ref, comp):
        return ref[pl.ds(comp * block_cols, block_cols), :]

    for row in range(rows):
        chosen = (jnp.broadcast_to(material_ref[row : row + 1, :], (levels, lanes)) == level)
        fields = jnp.dot(
            table_ref[...], chosen.astype(jnp.float32),
            precision=exact_precision, preferred_element_type=jnp.float32,
        )
        sums = [None] * comps
        for comp in range(comps):
            centre = line(x_ref, comp, row)
            views = [
                centre,
                line(before_x_ref, comp, row),
                line(after_x_ref, comp, row),
                line(x_ref, comp, row - 1) if row > 0 else edge(before_y_ref, comp),
                line(x_ref, comp, row + 1) if row < rows - 1 else edge(after_y_ref, comp),
                jnp.where(lane == 0, 0.0, pltpu.roll(centre, 1, 1)),
                jnp.where(lane == lanes - 1, 0.0, pltpu.roll(centre, lanes - 1, 1)),
            ]
            for offset, view in enumerate(views):
                for out in range(comps):
                    entry = (offset * comps + out) * comps + comp
                    term = fields[entry : entry + 1, :] * view
                    sums[out] = term if sums[out] is None else sums[out] + term
        for out in range(comps):
            applied_ref[out * rows + row] = sums[out]


def stencil(x_rows, halos, table, material, comps):
    rows, lanes = material.shape
    block_cols = x_rows.shape[0] // (comps * rows)
    return pl.pallas_call(
        functools.partial(stencil_kernel, comps),
        out_shape=f32(comps * rows, block_cols, lanes),
        in_specs=[VMEM] * 7,
        out_specs=VMEM,
        name="stencil",
    )(x_rows, *halos, table, material)


def three_parts(values):
    high = values.astype(jnp.bfloat16)
    rest = values - high.astype(jnp.float32)
    middle = rest.astype(jnp.bfloat16)
    low = (rest - middle.astype(jnp.float32)).astype(jnp.bfloat16)
    return high, middle, low


def sums_kernel(basis_ref, applied_ref, stack_ref, sums_ref):
    lines, block_cols, lanes = applied_ref.shape
    basis_cols = basis_ref.shape[0] // lines
    joined = basis_cols + block_cols
    for line in range(lines):
        there = pl.ds(line * lanes, lanes)
        for place, values in (
            (0, basis_ref[pl.ds(line, basis_cols, stride=lines), :]),
            (basis_cols, applied_ref[line]),
        ):
            for index, part in enumerate(three_parts(values)):
                stack_ref[pl.ds(index * joined + place, values.shape[0]), there] = part
    stack = stack_ref[...]
    products = lax.dot_general(
        stack, stack, (((1,), (1,)), ((), ())), preferred_element_type=jnp.float32
    )
    wide = products[:joined] + products[joined : 2 * joined] + products[2 * joined :]
    total = wide[:, :joined] + wide[:, joined : 2 * joined] + wide[:, 2 * joined :]
    half = basis_cols // 2
    sums_ref[pl.ds(0, half), :] = jnp.concatenate(
        (total[:half, :basis_cols], total[half:basis_cols, :basis_cols]), axis=1
    )
    sums_ref[pl.ds(half, block_cols), :] = jnp.concatenate(
        (total[basis_cols:], jnp.zeros((block_cols, sums_ref.shape[1] - joined), jnp.float32)), axis=1
    )


def sums(basis_rows, applied):
    lines, block_cols, lanes = applied.shape
    basis_cols = basis_rows.shape[0] // lines
    joined = basis_cols + block_cols
    return pl.pallas_call(
        sums_kernel,
        out_shape=(
            jax.ShapeDtypeStruct((3 * joined, lines * lanes), jnp.bfloat16),
            f32(basis_cols // 2 + block_cols, 2 * basis_cols),
        ),
        in_specs=[VMEM] * 2,
        out_specs=(VMEM, VMEM),
        name="sums",
    )(basis_rows, applied)


def exchange_total(part):
    other = jnp.zeros_like(part)
    for axis in ("basis", "space"):
        count = lax.axis_size(axis)
        step = 1
        while step < count:
            part = part + other
            other = lax.ppermute(part, axis, [(i, i ^ step) for i in range(count)])
            step *= 2
    return part, other


def finish_kernel(
    row_count, place_ref, part_ref, other_ref, stack_ref, block_ref, coeffs_ref, upper_ref,
    coeffs_scratch,
):
    block_cols = upper_ref.shape[0]
    basis_cols = part_ref.shape[1] // 2
    half = basis_cols // 2
    joined = basis_cols + block_cols
    lines = block_ref.shape[0] // block_cols
    lanes = block_ref.shape[1]
    total = (part_ref[...] + other_ref[...]) / row_count
    gram = jnp.concatenate((total[:half, :basis_cols], total[:half, basis_cols:]), axis=0)
    first = total[half:, :basis_cols]
    block_gram = total[half:, basis_cols:joined]

    def times(left, right, right_dim=0):
        return lax.dot_general(
            left, right, (((1,), (right_dim,)), ((), ())),
            precision=exact_precision, preferred_element_type=jnp.float32,
        )

    coeffs = first + (first - times(first, gram))
    image = times(coeffs, gram)
    matrix = block_gram - times(coeffs, first, 1) - times(first - image, coeffs, 1)
    coeffs_scratch[...] = coeffs.T
    group_cols = coeffs_ref.shape[0]
    start = pl.multiple_of(place_ref[0] * group_cols, group_cols)
    coeffs_ref[...] = coeffs_scratch[pl.ds(start, group_cols), :]

    row = lax.broadcasted_iota(jnp.int32, (block_cols, block_cols), 0)
    column = lax.broadcasted_iota(jnp.int32, (block_cols, block_cols), 1)
    unit = jnp.where(row == column, 1.0, 0.0)
    pad = jnp.zeros((block_cols, 2 * basis_cols - joined - block_cols), jnp.float32)
    work = jnp.concatenate((-coeffs, unit, matrix, pad), axis=1)
    height = lax.broadcasted_iota(jnp.int32, work.shape, 0)
    for step in range(block_cols):
        pivots = jnp.broadcast_to(work[:, joined + step : joined + step + 1], work.shape)
        pivot = pivots[step : step + 1, :]
        pivot_row = work[step : step + 1, :]
        scaled = pivot_row / pivot
        new_row = pivot_row * lax.rsqrt(pivot)
        work = jnp.where(
            height > step, work - pivots * scaled, jnp.where(height == step, new_row, work)
        )
    upper_ref[...] = work[:, joined : joined + block_cols]
    weights = three_parts(work[:, :joined])
    wide = jnp.concatenate(
        [jnp.concatenate((part, part, part), axis=1) for part in weights], axis=0
    )
    result = jnp.dot(wide, stack_ref[...], preferred_element_type=jnp.float32)
    result = result[:block_cols] + result[block_cols : 2 * block_cols] + result[2 * block_cols :]
    for line in range(lines):
        block_ref[pl.ds(line, block_cols, stride=lines), :] = result[
            :, line * lanes : (line + 1) * lanes
        ]


def finish(place, part, other, stack, row_count, block_cols, group_cols, lines):
    lanes = stack.shape[1] // lines
    basis_cols = part.shape[1] // 2
    return pl.pallas_call(
        functools.partial(finish_kernel, row_count),
        out_shape=(
            f32(block_cols * lines, lanes), f32(group_cols, block_cols), f32(block_cols, block_cols),
        ),
        in_specs=[SMEM] + [VMEM] * 3,
        out_specs=(VMEM, VMEM, VMEM),
        scratch_shapes=[pltpu.VMEM((basis_cols, block_cols), jnp.float32)],
        name="finish",
    )(place, part, other, stack)


def shards(
    x_block, basis, material, k0_blocks, k0_diag, ke_blocks, mass, velocities, shifts, sample
):
    block_cols, comps, extent_x, rows, lanes = x_block.shape
    group_cols = basis.shape[0]
    lines = comps * rows
    row_count = float(comps * extent_x * lax.axis_size("space") * basis.shape[3] * lanes)

    x_rows = x_block.reshape(block_cols * lines, lanes)
    sent, first_row, last_row = pack(basis, x_rows, block_cols)
    basis_rows = lax.all_to_all(sent, "basis", 0, 0).reshape(-1, lanes)
    halos = (
        from_lower(x_rows, "space"),
        from_upper(x_rows, "space"),
        from_lower(last_row, "basis"),
        from_upper(first_row, "basis"),
    )
    tables = stencil_tables(k0_blocks, k0_diag, ke_blocks, mass, velocities, shifts, sample)
    table = tables.reshape(tables.shape[0], -1).T
    applied = stencil(x_rows, halos, table, material.reshape(rows, lanes), comps)
    stack, part = sums(basis_rows, applied)
    part, other = exchange_total(part)
    place = lax.axis_index("basis").astype(jnp.int32).reshape(1)
    block, coeffs, upper = finish(
        place, part, other, stack, row_count, block_cols, group_cols, lines
    )
    return (block.reshape(x_block.shape), coeffs, upper)


def solution(mesh):
    in_specs = (
        P(None, None, "space", "basis", None),
        P("basis", None, "space", None, None),
        P("space", "basis", None),
        P(),
        P(),
        P(),
        P(),
        P(),
        P(),
        P(),
    )
    out_specs = (P(None, None, "space", "basis", None), P("basis", None), P())
    return jax.shard_map(shards, mesh=mesh, in_specs=in_specs, out_specs=out_specs, check_vma=False)
```

time: 64.8 us -> 82.9 us (1.28)
  Pallas kernels: 0 us -> 36.1 us
  blocking collectives: 7.34 us -> 0 us
  local copies, waits for them, and re-layouts: 10.4 us -> 5.66 us
  other arithmetic: 5.48 us -> 0.85 us
  starting transfers between devices: 20.9 us -> 23.8 us
  matrix products: 2.42 us -> 0 us
  waiting for transfers between devices: 14.7 us -> 13.1 us
    pallas_call x0 -> x4, Pallas kernels: none -> 36.1 us  [the longest x1 26.5 us: pack(): pl.pallas_call(pack_kernel, out_shape=(f32(count, group_cols, comps, full...]
    all_to_all x2 -> x1, waiting for transfers between devices: 14.7 us -> 2.86 us  [shards(): basis_rows = lax.all_to_all(sent, 'basis', 0, 0).reshape(-1, lanes)]
    ppermute x0 -> x5, waiting for transfers between devices: none -> 10.2 us  [exchange_total(): other = lax.ppermute(part, axis, [(i, i ^ step) for i in range(count)])]
    ppermute x0 -> x5, starting transfers between devices: none -> 9.18 us  [exchange_total(): other = lax.ppermute(part, axis, [(i, i ^ step) for i in range(count)])]
    all_to_all x1 -> x0, blocking collectives: 7.34 us -> none  [total_sum(): part = jnp.sum(lax.all_to_all(copies, axis, 0, 0), axis=0)]
    all_to_all x2 -> x1, starting transfers between devices: 9.83 us -> 5.61 us  [shards(): basis_rows = lax.all_to_all(sent, 'basis', 0, 0).reshape(-1, lanes)]
    another operation x4 -> x0, other arithmetic: 3.37 us -> none  [the longest x3 2.14 us: shards(): lower_factor = jnp.linalg.cholesky(gram_matrix)]
    transpose x1 -> x0, local copies, waits for them, and re-layouts: 2.48 us -> none  [own_rows(): pieces = jnp.moveaxis(pieces, 3, 0)]
  transfers between devices with their start and end apart: 6 -> 10, of which waited for: 2 -> 6; matrix products, arithmetic and copies ran while one was open for 12% -> 4% of each run, Pallas kernels for 0% -> 35%
where the time goes in v3:
time: 82.9 us; the launch traced here: 82.3 us
  Pallas kernels  36.1 us (44%)
  starting transfers between devices  23.8 us (29%)
  waiting for transfers between devices  13.1 us (16%)
  local copies, waits for them, and re-layouts  5.66 us (7%)
  between operations  2.79 us (3%)
  other arithmetic  0.85 us (1%)
    pallas_call x1, Pallas kernels, pack(): pl.pallas_call(pack_kernel, out_shape=(f32(count, group_cols, comps, full...  26.5 us
    ppermute x5, waiting for transfers between devices, exchange_total(): other = lax.ppermute(part, axis, [(i, i ^ step) for i in range(count)])  10.2 us
    ppermute x5, starting transfers between devices, exchange_total(): other = lax.ppermute(part, axis, [(i, i ^ step) for i in range(count)])  9.18 us
    ppermute x2, starting transfers between devices, from_lower(): return lax.ppermute(values, axis, [(i, i + 1) for i in range(count - 1)])  6.45 us
    all_to_all x1, starting transfers between devices, shards(): basis_rows = lax.all_to_all(sent, 'basis', 0, 0).reshape(-1, lanes)  5.61 us
    pallas_call x1, Pallas kernels, finish(): pl.pallas_call(functools.partial(finish_kernel, row_count), out_shape=(f3...  4.4 us
    all_to_all x1, waiting for transfers between devices, shards(): basis_rows = lax.all_to_all(sent, 'basis', 0, 0).reshape(-1, lanes)  2.86 us
    pallas_call x1, Pallas kernels, sums(): pl.pallas_call(sums_kernel, out_shape=(jax.ShapeDtypeStruct((3 * joined,...  2.78 us
  transfers between devices with their start and end apart: 10, of which 6 were waited for; matrix products, arithmetic and copies ran while one was open for 4% of the time, Pallas kernels for 35%

profile of v3, /device:TPU:0, one launch (start us, length us, event | category | flops | bytes accessed | tf_op | source)
XLA Modules:
  0.0 82.3 jit_solution(9720191107464065645)
XLA Ops:
  0.6 0.0 copy-start.9
  0.6 0.0 copy-start.10
  0.7 0.0 copy-start.4
  0.7 0.0 copy-start.5
  0.7 5.0 %collective-permute-start = (f32[384,128]{1,0:T(8,128)}, f32[384,128]{1,0:T(8,128)S(1)}, u32[]{:S(2)}, u32[]{:S(2)}) collective-permute-start(f32[384,128]{1,0:T(8,128)} %bitcast.14), channel_id=1, source_target_pairs={{0,4},{4,8},{8,12},{12,16},{16,20},{20,24},{24,28},{1,5},{5,9},{9,... | collective-permute-start | bytes 589832 | tf_op jit(solution)/shard_map/ppermute | solution.py:22
  5.7 1.3 %collective-permute-start.1 = (f32[384,128]{1,0:T(8,128)}, f32[384,128]{1,0:T(8,128)S(1)}, u32[]{:S(2)}, u32[]{:S(2)}) collective-permute-start(f32[384,128]{1,0:T(8,128)} %bitcast.15), channel_id=1, source_target_pairs={{4,0},{8,4},{12,8},{16,12},{20,16},{24,20},{28,24},{5,1},{9,5},{13... | collective-permute-start | bytes 589832 | tf_op jit(solution)/shard_map/ppermute | solution.py:27
  7.0 26.5 %pack.1 = (f32[4,16,3,8,128]{4,3,2,1,0:T(8,128)}, f32[48,128]{1,0:T(8,128)}, f32[48,128]{1,0:T(8,128)}) custom-call(f32[16,3,1,32,128]{4,3,2,1,0:T(8,128)} %basis_ref.1, f32[384,128]{1,0:T(8,128)} %bitcast.16), custom_call_target="tpu_custom_call" | custom-call | tf_op jit(solution)/shard_map/pack/pallas_call | solution.py:61
  33.5 1.5 %collective-permute-start.2 = (f32[48,128]{1,0:T(8,128)}, f32[48,128]{1,0:T(8,128)S(1)}, u32[]{:S(2)}, u32[]{:S(2)}) collective-permute-start(f32[48,128]{1,0:T(8,128)} %get-tuple-element.24), channel_id=1, source_target_pairs={{0,1},{1,2},{2,3},{4,5},{5,6},{6,7},{8,9},{9,10},{10,11},{12,13},{... | collective-permute-start | bytes 73736 | tf_op jit(solution)/shard_map/ppermute | solution.py:22
  34.9 1.3 %collective-permute-start.3 = (f32[48,128]{1,0:T(8,128)}, f32[48,128]{1,0:T(8,128)S(1)}, u32[]{:S(2)}, u32[]{:S(2)}) collective-permute-start(f32[48,128]{1,0:T(8,128)} %get-tuple-element.25), channel_id=1, source_target_pairs={{1,0},{2,1},{3,2},{5,4},{6,5},{7,6},{9,8},{10,9},{11,10},{13,12},{... | collective-permute-start | bytes 73736 | tf_op jit(solution)/shard_map/ppermute | solution.py:27
  36.2 5.6 %all-to-all-start = ((f32[4,16,3,8,128]{4,3,2,1,0:T(8,128)}), f32[4,16,3,8,128]{4,3,2,1,0:T(8,128)S(1)}, u32[]{:S(2)}, u32[]{:S(2)}) async-start(f32[4,16,3,8,128]{4,3,2,1,0:T(8,128)} %get-tuple-element.23), calls=%async_computation | async-start | bytes 1572864 | tf_op jit(solution)/shard_map/all_to_all | solution.py:271
  42.5 1.3 %dynamic-slice.13 = f32[1]{0:T(128)} dynamic-slice(f32[1024]{0:T(1024)} %param.20, s32[]{:T(128)} %bitcast.3), dynamic_slice_sizes={1} | dynamic-slice | bytes 12 | tf_op jit(solution)/shard_map/jit(_take)/gather | solution.py:32
  44.4 0.0 copy-done.9
  44.4 0.0 copy-done.10
  44.5 1.3 %dynamic-slice.12 = f32[1]{0:T(128)} dynamic-slice(f32[1024]{0:T(1024)} %param.19, s32[]{:T(128)} %bitcast.3), dynamic_slice_sizes={1} | dynamic-slice | bytes 12 | tf_op jit(solution)/shard_map/jit(_take)/gather | solution.py:31
  46.4 0.0 copy-done.4
  46.4 0.0 copy-done.5
  46.4 0.1 slice_add_fusion
  46.5 0.1 scatter-add.4
  46.6 0.1 copy.15
  46.8 0.6 reshape.76
  47.4 0.0 collective-permute-done.2.before_y_ref
  47.4 0.0 copy-start.6
  47.4 0.0 collective-permute-done.3.after_y_ref
  47.4 0.0 copy-start.7
  47.4 0.0 collective-permute-done.before_x_ref
  47.4 0.0 copy-start.1
  47.5 0.0 collective-permute-done.1.after_x_ref
  47.5 0.0 copy-start.2
  47.5 0.5 copy-done.6
  48.0 0.0 copy-done.7
  48.0 0.1 copy-done.1
  48.1 0.1 copy-done.2
  48.2 2.5 %stencil.1.applied_ref = f32[24,16,128]{2,1,0:T(8,128)} custom-call(f32[384,128]{1,0:T(8,128)} %bitcast.17, f32[384,128]{1,0:T(8,128)} %copy-done.1, f32[384,128]{1,0:T(8,128)} %copy-done.2, f32[48,128]{1,0:T(8,128)} %copy-done.6, f32[48,128]{1,0:T(8,128)} %copy-done.7, f32[63,8]{1,0:T(8,128)} %bitcast.18, s32[8,128]{1,0:T(8,128)} %bitcast.19), custom_call_target="tpu_custom_call" | custom-call | tf_op jit(solution)/shard_map/stencil/pallas_call | solution.py:117
  50.6 2.9 %all-to-all-done = f32[4,16,3,8,128]{4,3,2,1,0:T(8,128)S(1)} async-done(((f32[4,16,3,8,128]{4,3,2,1,0:T(8,128)}), f32[4,16,3,8,128]{4,3,2,1,0:T(8,128)S(1)}, u32[]{:S(2)}, u32[]{:S(2)}) %all-to-all-start) | async-done | bytes 786464 | tf_op jit(solution)/shard_map/all_to_all | solution.py:271
  53.5 0.0 copy-start
  53.5 0.9 %copy-done = f32[4,16,3,8,128]{4,3,2,1,0:T(8,128)} copy-done((f32[4,16,3,8,128]{4,3,2,1,0:T(8,128)}, f32[4,16,3,8,128]{4,3,2,1,0:T(8,128)S(1)}, u32[]{:S(2)}) %copy-start) | copy-done | bytes 786456
  54.4 2.8 %sums.1 = (bf16[240,3072]{1,0:T(8,128)(2,1)}, f32[48,128]{1,0:T(8,128)}) custom-call(f32[1536,128]{1,0:T(8,128)} %bitcast.13, f32[24,16,128]{2,1,0:T(8,128)} %stencil.1.applied_ref), custom_call_target="tpu_custom_call" | custom-call | tf_op jit(solution)/shard_map/sums/pallas_call | solution.py:165
  57.2 0.0 collective-permute-start.4
  57.2 1.4 %collective-permute-done.4 = f32[48,128]{1,0:T(8,128)S(1)} collective-permute-done((f32[48,128]{1,0:T(8,128)}, f32[48,128]{1,0:T(8,128)S(1)}, u32[]{:S(2)}, u32[]{:S(2)}) %collective-permute-start.4) | collective-permute-done | bytes 24608 | tf_op jit(solution)/shard_map/ppermute | solution.py:184
  58.6 0.7 add.26
  59.3 0.4 collective-permute-start.5
  59.8 3.4 %collective-permute-done.5 = f32[48,128]{1,0:T(8,128)S(1)} collective-permute-done((f32[48,128]{1,0:T(8,128)S(1)}, f32[48,128]{1,0:T(8,128)S(1)}, u32[]{:S(2)}, u32[]{:S(2)}) %collective-permute-start.5) | collective-permute-done | bytes 24608 | tf_op jit(solution)/shard_map/ppermute | solution.py:184
  63.2 2.7 %collective-permute-start.6 = (f32[48,128]{1,0:T(8,128)S(1)}, f32[48,128]{1,0:T(8,128)S(1)}, u32[]{:S(2)}, u32[]{:S(2)}) collective-permute-start(f32[48,128]{1,0:T(8,128)S(1)} %add.27), channel_id=1, source_target_pairs={{0,4},{4,0},{8,12},{12,8},{16,20},{20,16},{24,28},{28,24},{1,5},{5... | collective-permute-start | bytes 73736 | tf_op jit(solution)/shard_map/ppermute | solution.py:184
  65.8 1.8 %collective-permute-done.6 = f32[48,128]{1,0:T(8,128)S(1)} collective-permute-done((f32[48,128]{1,0:T(8,128)S(1)}, f32[48,128]{1,0:T(8,128)S(1)}, u32[]{:S(2)}, u32[]{:S(2)}) %collective-permute-start.6) | collective-permute-done | bytes 24608 | tf_op jit(solution)/shard_map/ppermute | solution.py:184
  67.6 3.0 %collective-permute-start.7 = (f32[48,128]{1,0:T(8,128)S(1)}, f32[48,128]{1,0:T(8,128)S(1)}, u32[]{:S(2)}, u32[]{:S(2)}) collective-permute-start(f32[48,128]{1,0:T(8,128)S(1)} %add.28), channel_id=1, source_target_pairs={{0,8},{4,12},{8,0},{12,4},{16,24},{20,28},{24,16},{28,20},{1,9},{5... | collective-permute-start | bytes 73736 | tf_op jit(solution)/shard_map/ppermute | solution.py:184
  70.6 1.8 %collective-permute-done.7 = f32[48,128]{1,0:T(8,128)S(1)} collective-permute-done((f32[48,128]{1,0:T(8,128)S(1)}, f32[48,128]{1,0:T(8,128)S(1)}, u32[]{:S(2)}, u32[]{:S(2)}) %collective-permute-start.7) | collective-permute-done | bytes 24608 | tf_op jit(solution)/shard_map/ppermute | solution.py:184
  72.4 0.0 copy-start.3
  72.4 3.1 %collective-permute-start.8 = (f32[48,128]{1,0:T(8,128)S(1)}, f32[48,128]{1,0:T(8,128)S(1)}, u32[]{:S(2)}, u32[]{:S(2)}) collective-permute-start(f32[48,128]{1,0:T(8,128)S(1)} %add.29.part_ref), channel_id=1, source_target_pairs={{0,16},{4,20},{8,24},{12,28},{16,0},{20,4},{24,8},{28,12},{1,17},{... | collective-permute-start | bytes 73736 | tf_op jit(solution)/shard_map/ppermute | solution.py:184
  75.5 1.8 %collective-permute-done.8.other_ref = f32[48,128]{1,0:T(8,128)S(1)} collective-permute-done((f32[48,128]{1,0:T(8,128)S(1)}, f32[48,128]{1,0:T(8,128)S(1)}, u32[]{:S(2)}, u32[]{:S(2)}) %collective-permute-start.8) | collective-permute-done | bytes 24608 | tf_op jit(solution)/shard_map/ppermute | solution.py:184
  77.3 0.0 copy-start.8
  77.3 0.0 copy-done.3
  77.3 0.6 copy-done.8
  77.9 4.4 %finish.1 = (f32[384,128]{1,0:T(8,128)}, f32[16,16]{1,0:T(8,128)}, f32[16,16]{1,0:T(8,128)}) custom-call(s32[1]{0:T(128)} %bitcast.place_ref, f32[48,128]{1,0:T(8,128)} %copy-done.3, f32[48,128]{1,0:T(8,128)} %copy-done.8, bf16[240,3072]{1,0:T(8,128)(2,1)} %get-tuple-element.27.stack_ref), custom_call_target="tpu_custom_call" | custom-call | tf_op jit(solution)/shard_map/finish/pallas_call | solution.py:249
  (6 shorter events, 0.0 us)
Async XLA Ops:
  0.6 43.8 %copy-start.9 = (f32[8,3]{0,1:T(4,128)S(1)}, f32[8,3]{0,1:T(4,128)}, u32[]{:S(2)}) copy-start(f32[8,3]{0,1:T(4,128)} %param.16) | copy-start | bytes 292
  0.6 43.8 %copy-start.10 = (f32[8,3]{0,1:T(4,128)S(1)}, f32[8,3]{0,1:T(4,128)}, u32[]{:S(2)}) copy-start(f32[8,3]{0,1:T(4,128)} %param.18) | copy-start | bytes 292
  0.7 45.8 %copy-start.4 = (f32[8,7,3,3]{1,0,3,2:T(8,128)S(1)}, f32[8,7,3,3]{1,0,3,2:T(8,128)}, u32[]{:S(2)}) copy-start(f32[8,7,3,3]{1,0,3,2:T(8,128)} %param.15) | copy-start | bytes 6052
  0.7 45.8 %copy-start.5 = (f32[8,7,3,3]{1,0,3,2:T(8,128)S(1)}, f32[8,7,3,3]{1,0,3,2:T(8,128)}, u32[]{:S(2)}) copy-start(f32[8,7,3,3]{1,0,3,2:T(8,128)} %param.17) | copy-start | bytes 6052
  0.7 46.8 %collective-permute-start = (f32[384,128]{1,0:T(8,128)}, f32[384,128]{1,0:T(8,128)S(1)}, u32[]{:S(2)}, u32[]{:S(2)}) collective-permute-start(f32[384,128]{1,0:T(8,128)} %bitcast.14), channel_id=1, source_target_pairs={{0,4},{4,8},{8,12},{12,16},{16,20},{20,24},{24,28},{1,5},{5,9},{9,... | collective-permute-start | bytes 589832 | tf_op jit(solution)/shard_map/ppermute | solution.py:22
  5.7 41.8 %collective-permute-start.1 = (f32[384,128]{1,0:T(8,128)}, f32[384,128]{1,0:T(8,128)S(1)}, u32[]{:S(2)}, u32[]{:S(2)}) collective-permute-start(f32[384,128]{1,0:T(8,128)} %bitcast.15), channel_id=1, source_target_pairs={{4,0},{8,4},{12,8},{16,12},{20,16},{24,20},{28,24},{5,1},{9,5},{13... | collective-permute-start | bytes 589832 | tf_op jit(solution)/shard_map/ppermute | solution.py:27
  33.5 13.9 %collective-permute-start.2 = (f32[48,128]{1,0:T(8,128)}, f32[48,128]{1,0:T(8,128)S(1)}, u32[]{:S(2)}, u32[]{:S(2)}) collective-permute-start(f32[48,128]{1,0:T(8,128)} %get-tuple-element.24), channel_id=1, source_target_pairs={{0,1},{1,2},{2,3},{4,5},{5,6},{6,7},{8,9},{9,10},{10,11},{12,13},{... | collective-permute-start | bytes 73736 | tf_op jit(solution)/shard_map/ppermute | solution.py:22
  34.9 12.5 %collective-permute-start.3 = (f32[48,128]{1,0:T(8,128)}, f32[48,128]{1,0:T(8,128)S(1)}, u32[]{:S(2)}, u32[]{:S(2)}) collective-permute-start(f32[48,128]{1,0:T(8,128)} %get-tuple-element.25), channel_id=1, source_target_pairs={{1,0},{2,1},{3,2},{5,4},{6,5},{7,6},{9,8},{10,9},{11,10},{13,12},{... | collective-permute-start | bytes 73736 | tf_op jit(solution)/shard_map/ppermute | solution.py:27
  36.2 17.3 %all-to-all-start = ((f32[4,16,3,8,128]{4,3,2,1,0:T(8,128)}), f32[4,16,3,8,128]{4,3,2,1,0:T(8,128)S(1)}, u32[]{:S(2)}, u32[]{:S(2)}) async-start(f32[4,16,3,8,128]{4,3,2,1,0:T(8,128)} %get-tuple-element.23), calls=%async_computation | async-start | bytes 1572864 | tf_op jit(solution)/shard_map/all_to_all | solution.py:271
  47.4 0.6 copy-start.6
  47.4 0.6 copy-start.7
  47.4 0.7 copy-start.1
  47.5 0.7 copy-start.2
  53.5 0.9 %copy-start = (f32[4,16,3,8,128]{4,3,2,1,0:T(8,128)}, f32[4,16,3,8,128]{4,3,2,1,0:T(8,128)S(1)}, u32[]{:S(2)}) copy-start(f32[4,16,3,8,128]{4,3,2,1,0:T(8,128)S(1)} %all-to-all-done) | copy-start | bytes 2359300
  57.2 1.4 %collective-permute-start.4 = (f32[48,128]{1,0:T(8,128)}, f32[48,128]{1,0:T(8,128)S(1)}, u32[]{:S(2)}, u32[]{:S(2)}) collective-permute-start(f32[48,128]{1,0:T(8,128)} %get-tuple-element.26), channel_id=1, source_target_pairs={{0,1},{1,0},{2,3},{3,2},{4,5},{5,4},{6,7},{7,6},{8,9},{9,8},{10,11... | collective-permute-start | bytes 73736 | tf_op jit(solution)/shard_map/ppermute | solution.py:184
  59.3 3.8 %collective-permute-start.5 = (f32[48,128]{1,0:T(8,128)S(1)}, f32[48,128]{1,0:T(8,128)S(1)}, u32[]{:S(2)}, u32[]{:S(2)}) collective-permute-start(f32[48,128]{1,0:T(8,128)S(1)} %add.26), channel_id=1, source_target_pairs={{0,2},{1,3},{2,0},{3,1},{4,6},{5,7},{6,4},{7,5},{8,10},{9,11},{10,... | collective-permute-start | bytes 73736 | tf_op jit(solution)/shard_map/ppermute | solution.py:184
  63.2 4.5 %collective-permute-start.6 = (f32[48,128]{1,0:T(8,128)S(1)}, f32[48,128]{1,0:T(8,128)S(1)}, u32[]{:S(2)}, u32[]{:S(2)}) collective-permute-start(f32[48,128]{1,0:T(8,128)S(1)} %add.27), channel_id=1, source_target_pairs={{0,4},{4,0},{8,12},{12,8},{16,20},{20,16},{24,28},{28,24},{1,5},{5... | collective-permute-start | bytes 73736 | tf_op jit(solution)/shard_map/ppermute | solution.py:184
  67.6 4.8 %collective-permute-start.7 = (f32[48,128]{1,0:T(8,128)S(1)}, f32[48,128]{1,0:T(8,128)S(1)}, u32[]{:S(2)}, u32[]{:S(2)}) collective-permute-start(f32[48,128]{1,0:T(8,128)S(1)} %add.28), channel_id=1, source_target_pairs={{0,8},{4,12},{8,0},{12,4},{16,24},{20,28},{24,16},{28,20},{1,9},{5... | collective-permute-start | bytes 73736 | tf_op jit(solution)/shard_map/ppermute | solution.py:184
  72.4 4.9 %copy-start.3 = (f32[48,128]{1,0:T(8,128)}, f32[48,128]{1,0:T(8,128)S(1)}, u32[]{:S(2)}) copy-start(f32[48,128]{1,0:T(8,128)S(1)} %add.29.part_ref) | copy-start | bytes 73732
  72.4 4.9 %collective-permute-start.8 = (f32[48,128]{1,0:T(8,128)S(1)}, f32[48,128]{1,0:T(8,128)S(1)}, u32[]{:S(2)}, u32[]{:S(2)}) collective-permute-start(f32[48,128]{1,0:T(8,128)S(1)} %add.29.part_ref), channel_id=1, source_target_pairs={{0,16},{4,20},{8,24},{12,28},{16,0},{20,4},{24,8},{28,12},{1,17},{... | collective-permute-start | bytes 73736 | tf_op jit(solution)/shard_map/ppermute | solution.py:184
  77.3 0.6 copy-start.8

commit v4 on v3

--- a/solution.py
+++ b/solution.py
@@ -10,7 +10,7 @@
 exact_precision = lax.Precision.HIGHEST
 VMEM = pl.BlockSpec(memory_space=pltpu.VMEM)
 SMEM = pl.BlockSpec(memory_space=pltpu.SMEM)
-ANY = pl.BlockSpec(memory_space=pl.ANY)
+HBM = pl.BlockSpec(memory_space=pltpu.HBM)
 
 
 def f32(*shape):
@@ -35,43 +35,71 @@
     return tables.at[:, 0].add(center)
 
 
-def pack_kernel(basis_ref, x_ref, sent_ref, first_ref, last_ref, sems):
-    count, cols, comps, rows, lanes = sent_ref.shape
-    copies = [
-        pltpu.make_async_copy(
-            basis_ref.at[:, :, 0, pl.ds(rows * piece, rows), :], sent_ref.at[piece], sems.at[piece]
-        )
-        for piece in range(count)
-    ]
-    for copy in copies:
-        copy.start()
+def partners(count):
+    return range(1, count), [k for k in range(1, count) if k & (k + 1) == 0]
+
+
+def pack_kernel(comps, place_ref, basis_ref, x_ref, *refs):
+    *piece_refs, x_out_ref, sems = refs
+    group_cols = basis_ref.shape[0]
+    rows, lanes = piece_refs[0].shape[2:]
     block_cols = x_ref.shape[0] // (comps * rows)
+    place = place_ref[0]
+    x_copy = pltpu.make_async_copy(x_ref, x_out_ref, sems.at[len(piece_refs)])
+    x_copy.start()
+    copies = []
+    for k, piece_ref in enumerate(piece_refs):
+        start = pl.multiple_of((place ^ k) * rows, rows)
+        copies.append(
+            pltpu.make_async_copy(
+                basis_ref.at[:, :, 0, pl.ds(start, rows), :],
+                piece_ref.at[pl.ds(0, group_cols)],
+                sems.at[k],
+            )
+        )
+        copies[-1].start()
+    x_copy.wait()
+    with_edge = [k for k in partners(len(piece_refs))[1]]
     for comp in range(comps):
-        there = pl.ds(comp * block_cols, block_cols)
-        for edge_ref, row in ((first_ref, 0), (last_ref, rows - 1)):
-            edge_ref[there, :] = x_ref[pl.ds(comp * rows + row, block_cols, stride=comps * rows), :]
+        first, last = (
+            x_out_ref[pl.ds(comp * rows + row, block_cols, stride=comps * rows), :]
+            for row in (0, rows - 1)
+        )
+        for k in with_edge:
+            edge = jnp.where((place ^ k) > place, last, first)
+            for part in range(block_cols // rows):
+                tile = comp * (block_cols // rows) + part
+                piece_refs[k][group_cols + tile // comps, tile % comps] = edge[
+                    part * rows : (part + 1) * rows
+                ]
     for copy in copies:
         copy.wait()
 
 
-def pack(basis, x_rows, block_cols):
+def pack(place, basis, x_rows, block_cols):
     group_cols, comps, _, full_y, lanes = basis.shape
     count = lax.axis_size("basis")
-    edge = f32(comps * block_cols, lanes)
+    rows = full_y // count
+    with_edge = partners(count)[1]
+    more = block_cols // rows
+    pieces = [
+        f32(group_cols + (more if k in with_edge else 0), comps, rows, lanes) for k in range(count)
+    ]
     return pl.pallas_call(
-        pack_kernel,
-        out_shape=(f32(count, group_cols, comps, full_y // count, lanes), edge, edge),
-        in_specs=[ANY, VMEM],
-        out_specs=(ANY, VMEM, VMEM),
-        scratch_shapes=[pltpu.SemaphoreType.DMA((count,))],
+        functools.partial(pack_kernel, comps),
+        out_shape=(*pieces, f32(*x_rows.shape)),
+        in_specs=[SMEM, HBM, HBM],
+        out_specs=(VMEM,) * (count + 1),
+        scratch_shapes=[pltpu.SemaphoreType.DMA((count + 1,))],
         name="pack",
-    )(basis, x_rows)
+    )(place, basis, x_rows)
 
 
 def stencil_kernel(
-    comps, x_ref, before_x_ref, after_x_ref, before_y_ref, after_y_ref, table_ref, material_ref,
-    applied_ref,
+    comps, edge_ks, place_ref, x_ref, before_x_ref, after_x_ref, table_ref, material_ref, *refs
 ):
+    *edge_refs, applied_ref = refs
+    place = place_ref[0]
     rows, lanes = material_ref.shape
     levels = table_ref.shape[1]
     block_cols = x_ref.shape[0] // (comps * rows)
@@ -81,8 +109,13 @@
     def line(ref, comp, row):
         return ref[pl.ds(comp * rows + row, block_cols, stride=comps * rows), :]
 
-    def edge(ref, comp):
-        return ref[pl.ds(comp * block_cols, block_cols), :]
+    def edge(comp, step):
+        result = jnp.zeros((block_cols, lanes), jnp.float32)
+        for k, ref in zip(edge_ks, edge_refs):
+            begin = ref.shape[0] - comps * block_cols + comp * block_cols
+            here = (place ^ k) == place + step
+            result = jnp.where(here, ref[pl.ds(begin, block_cols), :], result)
+        return result
 
     for row in range(rows):
         chosen = (jnp.broadcast_to(material_ref[row : row + 1, :], (levels, lanes)) == level)
@@ -97,8 +130,8 @@
                 centre,
                 line(before_x_ref, comp, row),
                 line(after_x_ref, comp, row),
-                line(x_ref, comp, row - 1) if row > 0 else edge(before_y_ref, comp),
-                line(x_ref, comp, row + 1) if row < rows - 1 else edge(after_y_ref, comp),
+                line(x_ref, comp, row - 1) if row > 0 else edge(comp, -1),
+                line(x_ref, comp, row + 1) if row < rows - 1 else edge(comp, 1),
                 jnp.where(lane == 0, 0.0, pltpu.roll(centre, 1, 1)),
                 jnp.where(lane == lanes - 1, 0.0, pltpu.roll(centre, lanes - 1, 1)),
             ]
@@ -111,16 +144,16 @@
             applied_ref[out * rows + row] = sums[out]
 
 
-def stencil(x_rows, halos, table, material, comps):
+def stencil(place, x_rows, halos, edges, table, material, comps):
     rows, lanes = material.shape
     block_cols = x_rows.shape[0] // (comps * rows)
     return pl.pallas_call(
-        functools.partial(stencil_kernel, comps),
+        functools.partial(stencil_kernel, comps, tuple(edges)),
         out_shape=f32(comps * rows, block_cols, lanes),
-        in_specs=[VMEM] * 7,
+        in_specs=[SMEM] + [VMEM] * (5 + len(edges)),
         out_specs=VMEM,
         name="stencil",
-    )(x_rows, *halos, table, material)
+    )(place, x_rows, *halos, table, material, *edges.values())
 
 
 def three_parts(values):
@@ -131,18 +164,23 @@
     return high, middle, low
 
 
-def sums_kernel(basis_ref, applied_ref, stack_ref, sums_ref):
+def sums_kernel(group_cols, place_ref, applied_ref, *refs):
+    *piece_refs, stack_ref, sums_ref = refs
     lines, block_cols, lanes = applied_ref.shape
-    basis_cols = basis_ref.shape[0] // lines
+    basis_cols = len(piece_refs) * group_cols
     joined = basis_cols + block_cols
+
+    def store(begin, line, values):
+        for index, part in enumerate(three_parts(values)):
+            there = pl.ds(index * joined + begin, values.shape[0])
+            stack_ref[there, pl.ds(line * lanes, lanes)] = part
+
+    for k, piece_ref in enumerate(piece_refs):
+        begin = pl.multiple_of((place_ref[0] ^ k) * group_cols, group_cols)
+        for line in range(lines):
+            store(begin, line, piece_ref[pl.ds(line, group_cols, stride=lines), :])
     for line in range(lines):
-        there = pl.ds(line * lanes, lanes)
-        for place, values in (
-            (0, basis_ref[pl.ds(line, basis_cols, stride=lines), :]),
-            (basis_cols, applied_ref[line]),
-        ):
-            for index, part in enumerate(three_parts(values)):
-                stack_ref[pl.ds(index * joined + place, values.shape[0]), there] = part
+        store(basis_cols, line, applied_ref[line])
     stack = stack_ref[...]
     products = lax.dot_general(
         stack, stack, (((1,), (1,)), ((), ())), preferred_element_type=jnp.float32
@@ -158,45 +196,48 @@
     )
 
 
-def sums(basis_rows, applied):
+def sums(place, applied, pieces, group_cols):
     lines, block_cols, lanes = applied.shape
-    basis_cols = basis_rows.shape[0] // lines
+    basis_cols = len(pieces) * group_cols
     joined = basis_cols + block_cols
     return pl.pallas_call(
-        sums_kernel,
+        functools.partial(sums_kernel, group_cols),
         out_shape=(
             jax.ShapeDtypeStruct((3 * joined, lines * lanes), jnp.bfloat16),
             f32(basis_cols // 2 + block_cols, 2 * basis_cols),
         ),
-        in_specs=[VMEM] * 2,
+        in_specs=[SMEM] + [VMEM] * (1 + len(pieces)),
         out_specs=(VMEM, VMEM),
         name="sums",
-    )(basis_rows, applied)
-
-
-def exchange_total(part):
-    other = jnp.zeros_like(part)
-    for axis in ("basis", "space"):
-        count = lax.axis_size(axis)
-        step = 1
-        while step < count:
-            part = part + other
-            other = lax.ppermute(part, axis, [(i, i ^ step) for i in range(count)])
-            step *= 2
-    return part, other
+    )(place, applied, *pieces)
+
+
+def exchange_sum(part, axis):
+    count = lax.axis_size(axis)
+    terms = [part] + [
+        lax.ppermute(part, axis, [(i, i ^ k) for i in range(count)]) for k in range(1, count)
+    ]
+    while len(terms) > 1:
+        terms = [a + b for a, b in zip(terms[::2], terms[1::2])]
+    return terms[0]
+
+
+def exchange(part, axis):
+    count = lax.axis_size(axis)
+    return lax.all_to_all(jnp.broadcast_to(part[None], (count,) + part.shape), axis, 0, 0)
 
 
 def finish_kernel(
-    row_count, place_ref, part_ref, other_ref, stack_ref, block_ref, coeffs_ref, upper_ref,
+    row_count, place_ref, parts_ref, stack_ref, block_ref, coeffs_ref, upper_ref,
     coeffs_scratch,
 ):
     block_cols = upper_ref.shape[0]
-    basis_cols = part_ref.shape[1] // 2
+    basis_cols = parts_ref.shape[2] // 2
     half = basis_cols // 2
     joined = basis_cols + block_cols
     lines = block_ref.shape[0] // block_cols
     lanes = block_ref.shape[1]
-    total = (part_ref[...] + other_ref[...]) / row_count
+    total = jnp.sum(parts_ref[...], axis=0) / row_count
     gram = jnp.concatenate((total[:half, :basis_cols], total[:half, basis_cols:]), axis=0)
     first = total[half:, :basis_cols]
     block_gram = total[half:, basis_cols:joined]
@@ -243,19 +284,19 @@
         ]
 
 
-def finish(place, part, other, stack, row_count, block_cols, group_cols, lines):
+def finish(place, parts, stack, row_count, block_cols, group_cols, lines):
     lanes = stack.shape[1] // lines
-    basis_cols = part.shape[1] // 2
+    basis_cols = parts.shape[2] // 2
     return pl.pallas_call(
         functools.partial(finish_kernel, row_count),
         out_shape=(
             f32(block_cols * lines, lanes), f32(group_cols, block_cols), f32(block_cols, block_cols),
         ),
-        in_specs=[SMEM] + [VMEM] * 3,
+        in_specs=[SMEM] + [VMEM] * 2,
         out_specs=(VMEM, VMEM, VMEM),
         scratch_shapes=[pltpu.VMEM((basis_cols, block_cols), jnp.float32)],
         name="finish",
-    )(place, part, other, stack)
+    )(place, parts, stack)
 
 
 def shards(
@@ -266,24 +307,20 @@
     lines = comps * rows
     row_count = float(comps * extent_x * lax.axis_size("space") * basis.shape[3] * lanes)
 
-    x_rows = x_block.reshape(block_cols * lines, lanes)
-    sent, first_row, last_row = pack(basis, x_rows, block_cols)
-    basis_rows = lax.all_to_all(sent, "basis", 0, 0).reshape(-1, lanes)
-    halos = (
-        from_lower(x_rows, "space"),
-        from_upper(x_rows, "space"),
-        from_lower(last_row, "basis"),
-        from_upper(first_row, "basis"),
-    )
+    place = lax.axis_index("basis").astype(jnp.int32).reshape(1)
+    count = lax.axis_size("basis")
+    *pieces, x_rows = pack(place, basis, x_block.reshape(block_cols * lines, lanes), block_cols)
+    for k in reversed(partners(count)[0]):
+        pieces[k] = lax.ppermute(pieces[k], "basis", [(i, i ^ k) for i in range(count)])
+    pieces = [piece.reshape(-1, lanes) for piece in pieces]
+    halos = (from_lower(x_rows, "space"), from_upper(x_rows, "space"))
     tables = stencil_tables(k0_blocks, k0_diag, ke_blocks, mass, velocities, shifts, sample)
     table = tables.reshape(tables.shape[0], -1).T
-    applied = stencil(x_rows, halos, table, material.reshape(rows, lanes), comps)
-    stack, part = sums(basis_rows, applied)
-    part, other = exchange_total(part)
-    place = lax.axis_index("basis").astype(jnp.int32).reshape(1)
-    block, coeffs, upper = finish(
-        place, part, other, stack, row_count, block_cols, group_cols, lines
-    )
+    edges = {k: pieces[k] for k in partners(count)[1]}
+    applied = stencil(place, x_rows, halos, edges, table, material.reshape(rows, lanes), comps)
+    stack, part = sums(place, applied, pieces, group_cols)
+    parts = exchange(exchange_sum(part, "basis"), "space")
+    block, coeffs, upper = finish(place, parts, stack, row_count, block_cols, group_cols, lines)
     return (block.reshape(x_block.shape), coeffs, upper)
 
 

time: 82.9 us -> 52.5 us (0.63)
  Pallas kernels: 36.1 us -> 12.4 us
  blocking collectives: 0 us -> 13.4 us
  starting transfers between devices: 23.8 us -> 11.2 us
  waiting for transfers between devices: 13.1 us -> 5.33 us
  other arithmetic: 0.85 us -> 2.32 us
  local copies, waits for them, and re-layouts: 5.66 us -> 4.75 us
    pallas_call x3, Pallas kernels: 31.7 us -> 7.94 us  [the longest x1 3.01 us: sums(): pl.pallas_call(functools.partial(sums_kernel, group_cols), out_shape=(jax...]
    all_to_all x0 -> x1, blocking collectives: none -> 13.4 us  [exchange(): lax.all_to_all(jnp.broadcast_to(part[None], (count,) + part.shape), axis,...]
    all_to_all x1 -> x0, starting transfers between devices: 5.61 us -> none  [shards(): basis_rows = lax.all_to_all(sent, 'basis', 0, 0).reshape(-1, lanes)]
    ppermute x5 -> x6, waiting for transfers between devices: 10.2 us -> 5.33 us  [the longest x3 3.76 us: exchange_sum(): lax.ppermute(part, axis, [(i, i ^ k) for i in range(count)])]
    ppermute x5 -> x6, starting transfers between devices: 9.18 us -> 4.4 us  [the longest x3 2.31 us: shards(): lax.ppermute(pieces[k], 'basis', [(i, i ^ k) for i in range(count)])]
    all_to_all x1 -> x0, waiting for transfers between devices: 2.86 us -> none  [shards(): basis_rows = lax.all_to_all(sent, 'basis', 0, 0).reshape(-1, lanes)]
    ppermute x2 -> x1, starting transfers between devices: 2.58 us -> 1.29 us  [from_upper(): return lax.ppermute(values, axis, [(i + 1, i) for i in range(count - 1)])]
    ppermute x2 -> x1, starting transfers between devices: 6.45 us -> 5.48 us  [from_lower(): return lax.ppermute(values, axis, [(i, i + 1) for i in range(count - 1)])]
  transfers between devices with their start and end apart: 10 -> 8, of which waited for: 6 -> 3; matrix products, arithmetic and copies ran while one was open for 4% -> 10% of each run, Pallas kernels for 35% -> 5%
where the time goes in v4:
time: 52.5 us; the launch traced here: 52 us
  blocking collectives  13.4 us (26%)
  Pallas kernels  12.4 us (24%)
  starting transfers between devices  11.2 us (21%)
  waiting for transfers between devices  5.33 us (10%)
  local copies, waits for them, and re-layouts  4.75 us (9%)
  between operations  2.6 us (5%)
  other arithmetic  2.32 us (4%)
    all_to_all x1, blocking collectives, exchange(): lax.all_to_all(jnp.broadcast_to(part[None], (count,) + part.shape), axis,...  13.4 us
    ppermute x1, starting transfers between devices, from_lower(): return lax.ppermute(values, axis, [(i, i + 1) for i in range(count - 1)])  5.48 us
    pallas_call x1, Pallas kernels, finish(): pl.pallas_call(functools.partial(finish_kernel, row_count), out_shape=(f3...  4.5 us
    ppermute x3, waiting for transfers between devices, exchange_sum(): lax.ppermute(part, axis, [(i, i ^ k) for i in range(count)])  3.76 us
    pallas_call x1, Pallas kernels, sums(): pl.pallas_call(functools.partial(sums_kernel, group_cols), out_shape=(jax...  3.01 us
    pallas_call x1, Pallas kernels, stencil(): pl.pallas_call(functools.partial(stencil_kernel, comps, tuple(edges)), ou...  2.65 us
    ppermute x3, starting transfers between devices, shards(): lax.ppermute(pieces[k], 'basis', [(i, i ^ k) for i in range(count)])  2.31 us
    pallas_call x1, Pallas kernels, pack(): pl.pallas_call(functools.partial(pack_kernel, comps), out_shape=(*pieces,...  2.28 us
  transfers between devices with their start and end apart: 8, of which 3 were waited for; matrix products, arithmetic and copies ran while one was open for 10% of the time, Pallas kernels for 5%

profile of v4, /device:TPU:0, one launch (start us, length us, event | category | flops | bytes accessed | tf_op | source)
XLA Modules:
  0.0 52.0 jit_solution(6230299821637303483)
XLA Ops:
  0.6 2.3 %pack.1 = (f32[16,3,8,128]{3,2,1,0:T(8,128)}, f32[18,3,8,128]{3,2,1,0:T(8,128)}, f32[16,3,8,128]{3,2,1,0:T(8,128)}, f32[18,3,8,128]{3,2,1,0:T(8,128)}, f32[384,128]{1,0:T(8,128)}) custom-call(s32[1]{0:T(128)} %bitcast.place_ref, f32[16,3,1,32,128]{4,3,2,1,0:T(8,128)} %basis_ref.1, f32[384,128]{1,0:T(8,128)} %bitcast.20), custom_call_target="tpu_custom_call" | custom-call | tf_op jit(solution)/shard_map/pack/pallas_call | solution.py:88
  2.9 1.3 %collective-permute-start.1 = (f32[384,128]{1,0:T(8,128)}, f32[384,128]{1,0:T(8,128)S(1)}, u32[]{:S(2)}, u32[]{:S(2)}) collective-permute-start(f32[384,128]{1,0:T(8,128)} %get-tuple-element.25.x_ref), channel_id=1, source_target_pairs={{4,0},{8,4},{12,8},{16,12},{20,16},{24,20},{28,24},{5,1},{9,5},{13... | collective-permute-start | bytes 589832 | tf_op jit(solution)/shard_map/ppermute | solution.py:27
  4.2 5.5 %collective-permute-start = (f32[384,128]{1,0:T(8,128)}, f32[384,128]{1,0:T(8,128)S(1)}, u32[]{:S(2)}, u32[]{:S(2)}) collective-permute-start(f32[384,128]{1,0:T(8,128)} %get-tuple-element.25.x_ref), channel_id=1, source_target_pairs={{0,4},{4,8},{8,12},{12,16},{16,20},{20,24},{24,28},{1,5},{5,9},{9,... | collective-permute-start | bytes 589832 | tf_op jit(solution)/shard_map/ppermute | solution.py:22
  9.7 2.1 %collective-permute-start.4 = (f32[16,3,8,128]{3,2,1,0:T(8,128)}, f32[16,3,8,128]{3,2,1,0:T(8,128)S(1)}, u32[]{:S(2)}, u32[]{:S(2)}) collective-permute-start(f32[16,3,8,128]{3,2,1,0:T(8,128)} %get-tuple-element.29), channel_id=1, source_target_pairs={{0,2},{1,3},{2,0},{3,1},{4,6},{5,7},{6,4},{7,5},{8,10},{9,11},{10,... | collective-permute-start | bytes 589832 | tf_op jit(solution)/shard_map/ppermute | solution.py:314
  11.8 0.0 collective-permute-start.2
  11.8 0.2 collective-permute-start.3
  12.7 1.2 %dynamic-slice.13 = f32[1]{0:T(128)} dynamic-slice(f32[1024]{0:T(1024)} %param.20, s32[]{:T(128)} %bitcast.2), dynamic_slice_sizes={1} | dynamic-slice | bytes 12 | tf_op jit(solution)/shard_map/jit(_take)/gather | solution.py:32
  13.9 1.3 %dynamic-slice.12 = f32[1]{0:T(128)} dynamic-slice(f32[1024]{0:T(1024)} %param.19, s32[]{:T(128)} %bitcast.2), dynamic_slice_sizes={1} | dynamic-slice | bytes 12 | tf_op jit(solution)/shard_map/jit(_take)/gather | solution.py:31
  16.4 0.7 %multiply_subtract_fusion.1 = f32[8,3]{0,1:T(4,128)S(1)} fusion(f32[8,3]{0,1:T(4,128)} %param.16, f32[8,3]{0,1:T(4,128)} %param.18, f32[]{:T(128)} %bitcast.4), kind=kLoop, calls=%fused_computation.4 | loop fusion | flops 48 | bytes 292 | tf_op jit(solution)/shard_map/sub | solution.py:33
  17.1 0.8 %multiply_subtract_fusion = f32[8,7,3,3]{1,0,3,2:T(8,128)S(1)} fusion(f32[8,7,3,3]{1,0,3,2:T(8,128)} %param.15, f32[8,7,3,3]{1,0,3,2:T(8,128)} %param.17, f32[]{:T(128)} %bitcast.3), kind=kLoop, calls=%fused_computation.1 | loop fusion | flops 1008 | bytes 6052 | tf_op jit(solution)/shard_map/sub | solution.py:34
  17.9 0.1 slice_add_fusion
  18.0 0.1 scatter-add.4
  18.1 0.1 copy.15
  18.2 0.6 %reshape.85 = f32[8,63]{0,1:T(8,128)} reshape(f32[8,7,3,3]{0,3,2,1:T(4,128)S(1)} %copy.15) | data formatting | bytes 4032 | tf_op jit(solution)/shard_map/reshape | solution.py:318
  18.9 0.0 collective-permute-done.1.after_x_ref
  18.9 0.0 copy-start.3
  18.9 0.0 collective-permute-done.before_x_ref
  18.9 0.0 copy-start.4
  18.9 0.0 collective-permute-done.2
  18.9 0.0 copy-start
  18.9 1.6 %collective-permute-done.3 = f32[18,3,8,128]{3,2,1,0:T(8,128)S(1)} collective-permute-done((f32[18,3,8,128]{3,2,1,0:T(8,128)}, f32[18,3,8,128]{3,2,1,0:T(8,128)S(1)}, u32[]{:S(2)}, u32[]{:S(2)}) %collective-permute-start.3) | collective-permute-done | bytes 221216 | tf_op jit(solution)/shard_map/ppermute | solution.py:314
  20.5 0.0 copy-start.1
  20.5 0.0 copy-done.3
  20.5 0.0 copy-done.4
  20.5 0.0 copy-done
  20.5 0.7 %copy-done.1 = f32[18,3,8,128]{3,2,1,0:T(8,128)} copy-done((f32[18,3,8,128]{3,2,1,0:T(8,128)}, f32[18,3,8,128]{3,2,1,0:T(8,128)S(1)}, u32[]{:S(2)}) %copy-start.1) | copy-done | bytes 221208
  21.2 2.6 %stencil.1.applied_ref = f32[24,16,128]{2,1,0:T(8,128)} custom-call(s32[1]{0:T(128)} %bitcast.place_ref, f32[384,128]{1,0:T(8,128)} %get-tuple-element.25.x_ref, f32[384,128]{1,0:T(8,128)} %copy-done.4, f32[384,128]{1,0:T(8,128)} %copy-done.3, f32[63,8]{1,0:T(8,128)} %bitcast.23, s32[8,128]{1,0:T(8,128)} %bitcast.24, f32[432,128]{1,0:T(8,128)} %bitcast.16, ...), custom_call_target="tpu_custom_call" | custom-call | tf_op jit(solution)/shard_map/stencil/pallas_call | solution.py:150
  23.8 0.0 collective-permute-done.4
  23.8 0.0 copy-start.2
  23.8 0.7 %copy-done.2 = f32[16,3,8,128]{3,2,1,0:T(8,128)} copy-done((f32[16,3,8,128]{3,2,1,0:T(8,128)}, f32[16,3,8,128]{3,2,1,0:T(8,128)S(1)}, u32[]{:S(2)}) %copy-start.2) | copy-done | bytes 196632
  24.5 3.0 %sums.1 = (bf16[240,3072]{1,0:T(8,128)(2,1)}, f32[48,128]{1,0:T(8,128)}) custom-call(s32[1]{0:T(128)} %bitcast.place_ref, f32[24,16,128]{2,1,0:T(8,128)} %stencil.1.applied_ref, f32[384,128]{1,0:T(8,128)} %bitcast.21, f32[432,128]{1,0:T(8,128)} %bitcast.17, f32[384,128]{1,0:T(8,128)} %bitcast.22, f32[432,128]{1,0:T(8,128)} %bitcast.19), custom_call_target="tpu_custom_call" | custom-call | tf_op jit(solution)/shard_map/sums/pallas_call | solution.py:203
  27.5 1.8 %collective-permute-start.7 = (f32[48,128]{1,0:T(8,128)}, f32[48,128]{1,0:T(8,128)S(1)}, u32[]{:S(2)}, u32[]{:S(2)}) collective-permute-start(f32[48,128]{1,0:T(8,128)} %get-tuple-element.30), channel_id=1, source_target_pairs={{0,3},{1,2},{2,1},{3,0},{4,7},{5,6},{6,5},{7,4},{8,11},{9,10},{10,... | collective-permute-start | bytes 73736 | tf_op jit(solution)/shard_map/ppermute | solution.py:218
  29.3 0.3 collective-permute-start.6
  29.6 0.0 collective-permute-start.5
  29.6 1.4 %collective-permute-done.7 = f32[48,128]{1,0:T(8,128)S(1)} collective-permute-done((f32[48,128]{1,0:T(8,128)}, f32[48,128]{1,0:T(8,128)S(1)}, u32[]{:S(2)}, u32[]{:S(2)}) %collective-permute-start.7) | collective-permute-done | bytes 24608 | tf_op jit(solution)/shard_map/ppermute | solution.py:218
  31.0 2.3 %collective-permute-done.6 = f32[48,128]{1,0:T(8,128)S(1)} collective-permute-done((f32[48,128]{1,0:T(8,128)}, f32[48,128]{1,0:T(8,128)S(1)}, u32[]{:S(2)}, u32[]{:S(2)}) %collective-permute-start.6) | collective-permute-done | bytes 24608 | tf_op jit(solution)/shard_map/ppermute | solution.py:218
  33.3 0.0 collective-permute-done.5
  33.3 0.7 %add_add_fusion = f32[48,128]{1,0:T(8,128)S(1)} fusion(f32[48,128]{1,0:T(8,128)S(1)} %collective-permute-done.6, f32[48,128]{1,0:T(8,128)S(1)} %collective-permute-done.7, f32[48,128]{1,0:T(8,128)} %get-tuple-element.30, f32[48,128]{1,0:T(8,128)S(1)} %collective-permute-done.5), kind=kLoop, calls=%fused_computation.2 | loop fusion | flops 18432 | bytes 122880 | tf_op jit(solution)/shard_map/add | solution.py:221
  34.1 13.4 %all_to_all.5.parts_ref = f32[8,48,128]{2,1,0:T(8,128)} all-to-all(f32[8,48,128]{2,1,0:T(8,128)S(1)} %broadcast_in_dim.14), channel_id=1, replica_groups=mesh['space'=8,'basis'=4] {'space'}, dimensions={0} | all-to-all | bytes 393216 | tf_op jit(solution)/shard_map/all_to_all | solution.py:227
  47.5 4.5 %finish.1 = (f32[384,128]{1,0:T(8,128)}, f32[16,16]{1,0:T(8,128)}, f32[16,16]{1,0:T(8,128)}) custom-call(s32[1]{0:T(128)} %bitcast.place_ref, f32[8,48,128]{2,1,0:T(8,128)} %all_to_all.5.parts_ref, bf16[240,3072]{1,0:T(8,128)(2,1)} %get-tuple-element.31.stack_ref), custom_call_target="tpu_custom_call" | custom-call | tf_op jit(solution)/shard_map/finish/pallas_call | solution.py:290
  (2 shorter events, 0.0 us)
Async XLA Ops:
  2.9 16.0 %collective-permute-start.1 = (f32[384,128]{1,0:T(8,128)}, f32[384,128]{1,0:T(8,128)S(1)}, u32[]{:S(2)}, u32[]{:S(2)}) collective-permute-start(f32[384,128]{1,0:T(8,128)} %get-tuple-element.25.x_ref), channel_id=1, source_target_pairs={{4,0},{8,4},{12,8},{16,12},{20,16},{24,20},{28,24},{5,1},{9,5},{13... | collective-permute-start | bytes 589832 | tf_op jit(solution)/shard_map/ppermute | solution.py:27
  4.2 14.7 %collective-permute-start = (f32[384,128]{1,0:T(8,128)}, f32[384,128]{1,0:T(8,128)S(1)}, u32[]{:S(2)}, u32[]{:S(2)}) collective-permute-start(f32[384,128]{1,0:T(8,128)} %get-tuple-element.25.x_ref), channel_id=1, source_target_pairs={{0,4},{4,8},{8,12},{12,16},{16,20},{20,24},{24,28},{1,5},{5,9},{9,... | collective-permute-start | bytes 589832 | tf_op jit(solution)/shard_map/ppermute | solution.py:22
  9.7 14.1 %collective-permute-start.4 = (f32[16,3,8,128]{3,2,1,0:T(8,128)}, f32[16,3,8,128]{3,2,1,0:T(8,128)S(1)}, u32[]{:S(2)}, u32[]{:S(2)}) collective-permute-start(f32[16,3,8,128]{3,2,1,0:T(8,128)} %get-tuple-element.29), channel_id=1, source_target_pairs={{0,2},{1,3},{2,0},{3,1},{4,6},{5,7},{6,4},{7,5},{8,10},{9,11},{10,... | collective-permute-start | bytes 589832 | tf_op jit(solution)/shard_map/ppermute | solution.py:314
  11.8 7.1 %collective-permute-start.2 = (f32[18,3,8,128]{3,2,1,0:T(8,128)}, f32[18,3,8,128]{3,2,1,0:T(8,128)S(1)}, u32[]{:S(2)}, u32[]{:S(2)}) collective-permute-start(f32[18,3,8,128]{3,2,1,0:T(8,128)} %get-tuple-element.26), channel_id=1, source_target_pairs={{0,1},{1,0},{2,3},{3,2},{4,5},{5,4},{6,7},{7,6},{8,9},{9,8},{10,11... | collective-permute-start | bytes 663560 | tf_op jit(solution)/shard_map/ppermute | solution.py:314
  11.8 8.7 %collective-permute-start.3 = (f32[18,3,8,128]{3,2,1,0:T(8,128)}, f32[18,3,8,128]{3,2,1,0:T(8,128)S(1)}, u32[]{:S(2)}, u32[]{:S(2)}) collective-permute-start(f32[18,3,8,128]{3,2,1,0:T(8,128)} %get-tuple-element.27), channel_id=1, source_target_pairs={{0,3},{1,2},{2,1},{3,0},{4,7},{5,6},{6,5},{7,4},{8,11},{9,10},{10,... | collective-permute-start | bytes 663560 | tf_op jit(solution)/shard_map/ppermute | solution.py:314
  18.9 1.6 %copy-start.3 = (f32[384,128]{1,0:T(8,128)}, f32[384,128]{1,0:T(8,128)S(1)}, u32[]{:S(2)}) copy-start(f32[384,128]{1,0:T(8,128)S(1)} %collective-permute-done.1.after_x_ref) | copy-start | bytes 589828
  18.9 1.6 %copy-start.4 = (f32[384,128]{1,0:T(8,128)}, f32[384,128]{1,0:T(8,128)S(1)}, u32[]{:S(2)}) copy-start(f32[384,128]{1,0:T(8,128)S(1)} %collective-permute-done.before_x_ref) | copy-start | bytes 589828
  18.9 1.6 %copy-start = (f32[18,3,8,128]{3,2,1,0:T(8,128)}, f32[18,3,8,128]{3,2,1,0:T(8,128)S(1)}, u32[]{:S(2)}) copy-start(f32[18,3,8,128]{3,2,1,0:T(8,128)S(1)} %collective-permute-done.2) | copy-start | bytes 663556
  20.5 0.7 %copy-start.1 = (f32[18,3,8,128]{3,2,1,0:T(8,128)}, f32[18,3,8,128]{3,2,1,0:T(8,128)S(1)}, u32[]{:S(2)}) copy-start(f32[18,3,8,128]{3,2,1,0:T(8,128)S(1)} %collective-permute-done.3) | copy-start | bytes 663556
  23.8 0.7 %copy-start.2 = (f32[16,3,8,128]{3,2,1,0:T(8,128)}, f32[16,3,8,128]{3,2,1,0:T(8,128)S(1)}, u32[]{:S(2)}) copy-start(f32[16,3,8,128]{3,2,1,0:T(8,128)S(1)} %collective-permute-done.4) | copy-start | bytes 589828
  27.5 3.5 %collective-permute-start.7 = (f32[48,128]{1,0:T(8,128)}, f32[48,128]{1,0:T(8,128)S(1)}, u32[]{:S(2)}, u32[]{:S(2)}) collective-permute-start(f32[48,128]{1,0:T(8,128)} %get-tuple-element.30), channel_id=1, source_target_pairs={{0,3},{1,2},{2,1},{3,0},{4,7},{5,6},{6,5},{7,4},{8,11},{9,10},{10,... | collective-permute-start | bytes 73736 | tf_op jit(solution)/shard_map/ppermute | solution.py:218
  29.3 4.0 %collective-permute-start.6 = (f32[48,128]{1,0:T(8,128)}, f32[48,128]{1,0:T(8,128)S(1)}, u32[]{:S(2)}, u32[]{:S(2)}) collective-permute-start(f32[48,128]{1,0:T(8,128)} %get-tuple-element.30), channel_id=1, source_target_pairs={{0,2},{1,3},{2,0},{3,1},{4,6},{5,7},{6,4},{7,5},{8,10},{9,11},{10,... | collective-permute-start | bytes 73736 | tf_op jit(solution)/shard_map/ppermute | solution.py:218
  29.6 3.8 %collective-permute-start.5 = (f32[48,128]{1,0:T(8,128)}, f32[48,128]{1,0:T(8,128)S(1)}, u32[]{:S(2)}, u32[]{:S(2)}) collective-permute-start(f32[48,128]{1,0:T(8,128)} %get-tuple-element.30), channel_id=1, source_target_pairs={{0,1},{1,0},{2,3},{3,2},{4,5},{5,4},{6,7},{7,6},{8,9},{9,8},{10,11... | collective-permute-start | bytes 73736 | tf_op jit(solution)/shard_map/ppermute | solution.py:218

commit v5 on v4

v5 whole, which is shorter than its diff:
```python
import functools

import jax
import jax.numpy as jnp
from jax import lax
from jax.experimental import pallas as pl
from jax.experimental.pallas import tpu as pltpu
from jax.sharding import PartitionSpec as P

exact_precision = lax.Precision.HIGHEST
VMEM = pl.BlockSpec(memory_space=pltpu.VMEM)
SMEM = pl.BlockSpec(memory_space=pltpu.SMEM)
HBM = pl.BlockSpec(memory_space=pltpu.HBM)


def f32(*shape):
    return jax.ShapeDtypeStruct(shape, jnp.float32)


def from_lower(values, axis):
    count = lax.axis_size(axis)
    return lax.ppermute(values, axis, [(i, i + 1) for i in range(count - 1)])


def from_upper(values, axis):
    count = lax.axis_size(axis)
    return lax.ppermute(values, axis, [(i + 1, i) for i in range(count - 1)])


def partners(count):
    return range(1, count), [k for k in range(1, count) if k & (k + 1) == 0]


def pack_kernel(comps, place_ref, basis_ref, x_ref, material_ref, *refs):
    *piece_refs, x_out_ref, material_out_ref, sems = refs
    count = len(piece_refs)
    tiles, _, rows, lanes = basis_ref.shape
    block_cols = x_ref.shape[0] // (comps * rows)
    place = place_ref[0]
    x_copy = pltpu.make_async_copy(x_ref, x_out_ref, sems.at[count])
    x_copy.start()
    copies = [pltpu.make_async_copy(material_ref, material_out_ref, sems.at[count + 1])]
    for k in reversed(range(count)):
        copies.append(
            pltpu.make_async_copy(
                basis_ref.at[:, place ^ k], piece_refs[k].at[pl.ds(0, tiles)], sems.at[k]
            )
        )
    for copy in copies:
        copy.start()
    x_copy.wait()
    for comp in range(comps):
        first, last = (
            x_out_ref[pl.ds(comp * rows + row, block_cols, stride=comps * rows), :]
            for row in (0, rows - 1)
        )
        for k in partners(count)[1]:
            edge = jnp.where((place ^ k) > place, last, first)
            for part in range(block_cols // rows):
                piece_refs[k][tiles + comp * (block_cols // rows) + part] = edge[
                    part * rows : (part + 1) * rows
                ]
    for copy in copies:
        copy.wait()


def pack(place, basis, x_rows, material, block_cols):
    group_cols, comps, _, full_y, lanes = basis.shape
    count = lax.axis_size("basis")
    rows = full_y // count
    tiles = group_cols * comps
    edge_tiles = block_cols * comps // rows
    pieces = [
        f32(tiles + (edge_tiles if k in partners(count)[1] else 0), rows, lanes)
        for k in range(count)
    ]
    return pl.pallas_call(
        functools.partial(pack_kernel, comps),
        out_shape=(*pieces, f32(*x_rows.shape), jax.ShapeDtypeStruct(material.shape, jnp.int32)),
        in_specs=[SMEM, HBM, HBM, HBM],
        out_specs=(VMEM,) * (count + 2),
        scratch_shapes=[pltpu.SemaphoreType.DMA((count + 2,))],
        name="pack",
    )(place, basis.reshape(tiles, count, rows, lanes), x_rows, material)


def three_parts(values):
    high = values.astype(jnp.bfloat16)
    rest = values - high.astype(jnp.float32)
    middle = rest.astype(jnp.bfloat16)
    low = (rest - middle.astype(jnp.float32)).astype(jnp.bfloat16)
    return high, middle, low


def line_of(ref, comp, row, comps, rows, block_cols):
    return ref[pl.ds(comp * rows + row, block_cols, stride=comps * rows), :]


def ahead_kernel(
    sample_ref, velocities_ref, shifts_ref, k0_ref, ke_ref, diag_ref, mass_ref, material_ref,
    x_ref, own_ref, fields_ref, applied_ref, stack_ref,
):
    comps, _, levels, offsets = k0_ref.shape
    rows, lanes = material_ref.shape
    lines = comps * rows
    block_cols = x_ref.shape[0] // lines
    velocity = velocities_ref[sample_ref[0]]
    sigma = shifts_ref[sample_ref[0]]
    entry_rows = fields_ref.shape[1]
    stride = entry_rows // (comps * comps)
    gap = jnp.zeros((levels, stride - offsets), jnp.float32)
    wide = []
    for out in range(comps):
        for comp in range(comps):
            wide += [k0_ref[out, comp] - velocity * velocity * ke_ref[out, comp], gap]
    wide.append(jnp.zeros((levels, lanes - entry_rows), jnp.float32))
    table = jnp.concatenate(wide, axis=1).T[:entry_rows]
    entry = lax.broadcasted_iota(jnp.int32, table.shape, 0)
    for comp in range(comps):
        centre = diag_ref[comp : comp + 1, :] - sigma * mass_ref[comp : comp + 1, :]
        table = table + jnp.where(entry == comp * (comps + 1) * stride, centre, 0.0)

    lane = lax.broadcasted_iota(jnp.int32, (block_cols, lanes), 1)
    level = lax.broadcasted_iota(jnp.int32, (levels, lanes), 0)
    for row in range(rows):
        chosen = jnp.broadcast_to(material_ref[row : row + 1, :], (levels, lanes)) == level
        fields = jnp.dot(
            table, chosen.astype(jnp.float32),
            precision=exact_precision, preferred_element_type=jnp.float32,
        )
        fields_ref[row] = fields
        sums = [None] * comps
        for comp in range(comps):
            centre = line_of(x_ref, comp, row, comps, rows, block_cols)
            views = {
                0: centre,
                5: jnp.where(lane == 0, 0.0, pltpu.roll(centre, 1, 1)),
                6: jnp.where(lane == lanes - 1, 0.0, pltpu.roll(centre, lanes - 1, 1)),
            }
            if row > 0:
                views[3] = line_of(x_ref, comp, row - 1, comps, rows, block_cols)
            if row < rows - 1:
                views[4] = line_of(x_ref, comp, row + 1, comps, rows, block_cols)
            for offset, view in views.items():
                for out in range(comps):
                    place = (out * comps + comp) * stride + offset
                    term = fields[place : place + 1, :] * view
                    sums[out] = term if sums[out] is None else sums[out] + term
        for out in range(comps):
            applied_ref[out * rows + row] = sums[out]

    group_cols = own_ref.shape[0] // lines
    for line in range(lines):
        values = own_ref[pl.ds(line, group_cols, stride=lines), :]
        for index, part in enumerate(three_parts(values)):
            stack_ref[pl.ds(index * group_cols, group_cols), pl.ds(line * lanes, lanes)] = part


def ahead(sample, velocities, shifts, k0, ke, diag, mass, material, x_rows, own, comps):
    rows, lanes = material.shape
    lines = comps * rows
    offsets = k0.shape[1]
    stride = -(-offsets // 8) * 8
    return pl.pallas_call(
        ahead_kernel,
        out_shape=(
            f32(rows, comps * comps * stride, lanes),
            f32(lines, x_rows.shape[0] // lines, lanes),
            jax.ShapeDtypeStruct((3 * own.shape[0] // lines, lines * lanes), jnp.bfloat16),
        ),
        in_specs=[SMEM] * 3 + [VMEM] * 7,
        out_specs=(VMEM,) * 3,
        name="ahead",
    )(
        sample, velocities, shifts,
        jnp.transpose(k0, (2, 3, 0, 1)), jnp.transpose(ke, (2, 3, 0, 1)), diag.T, mass.T,
        material, x_rows, own,
    )


def sums_kernel(
    comps, edge_ks, place_ref, fields_ref, applied_ref, own_ref, before_x_ref, after_x_ref, *refs
):
    *piece_refs, stack_ref, sums_ref = refs
    lines, block_cols, lanes = applied_ref.shape
    rows = lines // comps
    stride = fields_ref.shape[1] // (comps * comps)
    group_cols = own_ref.shape[0] // 3
    basis_cols = (1 + len(piece_refs)) * group_cols
    joined = basis_cols + block_cols
    place = place_ref[0]

    def store(begin, line, values):
        for index, part in enumerate(three_parts(values)):
            there = pl.ds(index * joined + begin, values.shape[0])
            stack_ref[there, pl.ds(line * lanes, lanes)] = part

    begin = pl.multiple_of(place * group_cols, group_cols)
    for index in range(3):
        stack_ref[pl.ds(index * joined + begin, group_cols), :] = own_ref[
            pl.ds(index * group_cols, group_cols), :
        ]
    for k, piece_ref in enumerate(piece_refs, 1):
        begin = pl.multiple_of((place ^ k) * group_cols, group_cols)
        for line in range(lines):
            store(begin, line, piece_ref[pl.ds(line, group_cols, stride=lines), :])

    def edge(comp, step):
        result = jnp.zeros((block_cols, lanes), jnp.float32)
        for k in edge_ks:
            ref = piece_refs[k - 1]
            begin = ref.shape[0] - (comps - comp) * block_cols
            here = (place ^ k) == place + step
            result = jnp.where(here, ref[pl.ds(begin, block_cols), :], result)
        return result

    for row in range(rows):
        totals = [applied_ref[out * rows + row] for out in range(comps)]
        for comp in range(comps):
            views = {
                1: line_of(before_x_ref, comp, row, comps, rows, block_cols),
                2: line_of(after_x_ref, comp, row, comps, rows, block_cols),
            }
            if row == 0:
                views[3] = edge(comp, -1)
            if row == rows - 1:
                views[4] = edge(comp, 1)
            for offset, view in views.items():
                for out in range(comps):
                    entry = (out * comps + comp) * stride + offset
                    totals[out] = totals[out] + fields_ref[row, entry : entry + 1, :] * view
        for out in range(comps):
            store(basis_cols, out * rows + row, totals[out])

    stack = stack_ref[...]
    products = lax.dot_general(
        stack, stack, (((1,), (1,)), ((), ())), preferred_element_type=jnp.float32
    )
    wide = products[:joined] + products[joined : 2 * joined] + products[2 * joined :]
    total = wide[:, :joined] + wide[:, joined : 2 * joined] + wide[:, 2 * joined :]
    half = basis_cols // 2
    sums_ref[pl.ds(0, half), :] = jnp.concatenate(
        (total[:half, :basis_cols], total[half:basis_cols, :basis_cols]), axis=1
    )
    sums_ref[pl.ds(half, block_cols), :] = jnp.concatenate(
        (total[basis_cols:], jnp.zeros((block_cols, sums_ref.shape[1] - joined), jnp.float32)), axis=1
    )


def sums(place, fields, applied, own, halos, pieces, comps):
    lines, block_cols, lanes = applied.shape
    basis_cols = (1 + len(pieces)) * (own.shape[0] // 3)
    joined = basis_cols + block_cols
    return pl.pallas_call(
        functools.partial(sums_kernel, comps, partners(1 + len(pieces))[1]),
        out_shape=(
            jax.ShapeDtypeStruct((3 * joined, lines * lanes), jnp.bfloat16),
            f32(basis_cols // 2 + block_cols, 2 * basis_cols),
        ),
        in_specs=[SMEM] + [VMEM] * (3 + len(halos) + len(pieces)),
        out_specs=(VMEM, VMEM),
        name="sums",
    )(place, fields, applied, own, *halos, *pieces)


def exchange_sum(part, axis):
    count = lax.axis_size(axis)
    terms = [part] + [
        lax.ppermute(part, axis, [(i, i ^ k) for i in range(count)]) for k in range(1, count)
    ]
    while len(terms) > 1:
        terms = [a + b for a, b in zip(terms[::2], terms[1::2])]
    return terms[0]


def exchange(part, axis):
    count = lax.axis_size(axis)
    return lax.all_to_all(jnp.broadcast_to(part[None], (count,) + part.shape), axis, 0, 0)


def finish_kernel(
    row_count, place_ref, parts_ref, stack_ref, block_ref, coeffs_ref, upper_ref,
    coeffs_scratch,
):
    block_cols = upper_ref.shape[0]
    basis_cols = parts_ref.shape[2] // 2
    half = basis_cols // 2
    joined = basis_cols + block_cols
    lines = block_ref.shape[0] // block_cols
    lanes = block_ref.shape[1]
    total = jnp.sum(parts_ref[...], axis=0) / row_count
    gram = jnp.concatenate((total[:half, :basis_cols], total[:half, basis_cols:]), axis=0)
    first = total[half:, :basis_cols]
    block_gram = total[half:, basis_cols:joined]

    def times(left, right, right_dim=0):
        return lax.dot_general(
            left, right, (((1,), (right_dim,)), ((), ())),
            precision=exact_precision, preferred_element_type=jnp.float32,
        )

    coeffs = first + (first - times(first, gram))
    image = times(coeffs, gram)
    matrix = block_gram - times(coeffs, first, 1) - times(first - image, coeffs, 1)
    coeffs_scratch[...] = coeffs.T
    group_cols = coeffs_ref.shape[0]
    start = pl.multiple_of(place_ref[0] * group_cols, group_cols)
    coeffs_ref[...] = coeffs_scratch[pl.ds(start, group_cols), :]

    row = lax.broadcasted_iota(jnp.int32, (block_cols, block_cols), 0)
    column = lax.broadcasted_iota(jnp.int32, (block_cols, block_cols), 1)
    unit = jnp.where(row == column, 1.0, 0.0)
    pad = jnp.zeros((block_cols, 2 * basis_cols - joined - block_cols), jnp.float32)
    work = jnp.concatenate((-coeffs, unit, matrix, pad), axis=1)
    height = lax.broadcasted_iota(jnp.int32, work.shape, 0)
    for step in range(block_cols):
        pivots = jnp.broadcast_to(work[:, joined + step : joined + step + 1], work.shape)
        pivot = pivots[step : step + 1, :]
        pivot_row = work[step : step + 1, :]
        scaled = pivot_row / pivot
        new_row = pivot_row * lax.rsqrt(pivot)
        work = jnp.where(
            height > step, work - pivots * scaled, jnp.where(height == step, new_row, work)
        )
    upper_ref[...] = work[:, joined : joined + block_cols]
    weights = three_parts(work[:, :joined])
    wide = jnp.concatenate(
        [jnp.concatenate((part, part, part), axis=1) for part in weights], axis=0
    )
    result = jnp.dot(wide, stack_ref[...], preferred_element_type=jnp.float32)
    result = result[:block_cols] + result[block_cols : 2 * block_cols] + result[2 * block_cols :]
    for line in range(lines):
        block_ref[pl.ds(line, block_cols, stride=lines), :] = result[
            :, line * lanes : (line + 1) * lanes
        ]


def finish(place, parts, stack, row_count, block_cols, group_cols, lines):
    lanes = stack.shape[1] // lines
    basis_cols = parts.shape[2] // 2
    return pl.pallas_call(
        functools.partial(finish_kernel, row_count),
        out_shape=(
            f32(block_cols * lines, lanes), f32(group_cols, block_cols), f32(block_cols, block_cols),
        ),
        in_specs=[SMEM] + [VMEM] * 2,
        out_specs=(VMEM, VMEM, VMEM),
        scratch_shapes=[pltpu.VMEM((basis_cols, block_cols), jnp.float32)],
        name="finish",
    )(place, parts, stack)


def shards(
    x_block, basis, material, k0_blocks, k0_diag, ke_blocks, mass, velocities, shifts, sample
):
    block_cols, comps, extent_x, rows, lanes = x_block.shape
    group_cols = basis.shape[0]
    lines = comps * rows
    row_count = float(comps * extent_x * lax.axis_size("space") * basis.shape[3] * lanes)

    place = lax.axis_index("basis").astype(jnp.int32).reshape(1)
    count = lax.axis_size("basis")
    own, *pieces, x_rows, material = pack(
        place, basis, x_block.reshape(block_cols * lines, lanes), material.reshape(rows, lanes), block_cols
    )
    halos = [None, None]
    order = (3, "upper", 2, "lower", 1)
    pieces = dict(enumerate(pieces, 1))
    for name in order:
        if name == "lower":
            halos[0] = from_lower(x_rows, "space")
        elif name == "upper":
            halos[1] = from_upper(x_rows, "space")
        else:
            pieces[name] = lax.ppermute(pieces[name], "basis", [(i, i ^ name) for i in range(count)])
    pieces = [pieces[k].reshape(-1, lanes) for k in partners(count)[0]]
    fields, applied, own = ahead(
        sample, velocities, shifts, k0_blocks, ke_blocks, k0_diag, mass, material, x_rows,
        own.reshape(-1, lanes), comps,
    )
    stack, part = sums(place, fields, applied, own, halos, pieces, comps)
    parts = exchange(exchange_sum(part, "basis"), "space")
    block, coeffs, upper = finish(place, parts, stack, row_count, block_cols, group_cols, lines)
    return (block.reshape(x_block.shape), coeffs, upper)


def solution(mesh):
    in_specs = (
        P(None, None, "space", "basis", None),
        P("basis", None, "space", None, None),
        P("space", "basis", None),
        P(),
        P(),
        P(),
        P(),
        P(),
        P(),
        P(),
    )
    out_specs = (P(None, None, "space", "basis", None), P("basis", None), P())
    return jax.shard_map(shards, mesh=mesh, in_specs=in_specs, out_specs=out_specs, check_vma=False)
```

time: 52.5 us -> 47.8 us (0.910)
  local copies, waits for them, and re-layouts: 4.75 us -> 0.79 us
  waiting for transfers between devices: 5.33 us -> 7.42 us
  other arithmetic: 2.32 us -> 0.75 us
  between operations: 2.6 us -> 1.35 us
    ppermute x1, waiting for transfers between devices: 0.01 us -> 3.01 us  [from_lower(): return lax.ppermute(values, axis, [(i, i + 1) for i in range(count - 1)])]
    gather x2 -> x0, local copies, waits for them, and re-layouts: 2.51 us -> none  [the longest x1 1.27 us: stencil_tables(): velocity = jnp.take(velocities, sample, axis=0)[0]]
    sub x2 -> x0, other arithmetic: 1.5 us -> none  [the longest x1 0.79 us: stencil_tables(): tables = k0_blocks - velocity * velocity * ke_blocks]
    ppermute x1, starting transfers between devices: 5.48 us -> 4.56 us  [from_lower(): return lax.ppermute(values, axis, [(i, i + 1) for i in range(count - 1)])]
    ppermute x3, starting transfers between devices: 2.31 us -> 3.2 us  [shards(): lax.ppermute(pieces[name], 'basis', [(i, i ^ name) for i in range(count)])]
    reshape x1 -> x0, local copies, waits for them, and re-layouts: 0.63 us -> none  [shards(): table = tables.reshape(tables.shape[0], -1).T]
    unnamed x10, local copies, waits for them, and re-layouts: 1.36 us -> 0.78 us
  transfers between devices with their start and end apart: 8 -> 8, of which waited for: 3 -> 4; matrix products, arithmetic and copies ran while one was open for 10% -> 0% of each run, Pallas kernels for 5% -> 6%
where the time goes in v5:
time: 47.8 us; the launch traced here: 47.5 us
  blocking collectives  13.4 us (28%)
  Pallas kernels  12.9 us (27%)
  starting transfers between devices  10.9 us (23%)
  waiting for transfers between devices  7.42 us (16%)
  between operations  1.35 us (3%)
  local copies, waits for them, and re-layouts  0.79 us (2%)
  other arithmetic  0.75 us (2%)
    all_to_all x1, blocking collectives, exchange(): lax.all_to_all(jnp.broadcast_to(part[None], (count,) + part.shape), axis,...  13.4 us
    ppermute x1, starting transfers between devices, from_lower(): return lax.ppermute(values, axis, [(i, i + 1) for i in range(count - 1)])  4.56 us
    pallas_call x1, Pallas kernels, finish(): pl.pallas_call(functools.partial(finish_kernel, row_count), out_shape=(f3...  4.49 us
    ppermute x3, waiting for transfers between devices, exchange_sum(): lax.ppermute(part, axis, [(i, i ^ k) for i in range(count)])  3.32 us
    pallas_call x1, Pallas kernels, sums(): pl.pallas_call(functools.partial(sums_kernel, comps, partners(1 + len(pie...  3.31 us
    ppermute x3, starting transfers between devices, shards(): lax.ppermute(pieces[name], 'basis', [(i, i ^ name) for i in range(count)])  3.2 us
    ppermute x1, waiting for transfers between devices, from_lower(): return lax.ppermute(values, axis, [(i, i + 1) for i in range(count - 1)])  3.01 us
    pallas_call x1, Pallas kernels, ahead(): pl.pallas_call(ahead_kernel, out_shape=(f32(rows, comps * comps * stride,...  2.78 us
  transfers between devices with their start and end apart: 8, of which 4 were waited for; matrix products, arithmetic and copies ran while one was open for 0% of the time, Pallas kernels for 6%

profile of v5, /device:TPU:0, one launch (start us, length us, event | category | flops | bytes accessed | tf_op | source)
XLA Modules:
  0.0 47.5 jit_solution(14859569525369525827)
XLA Ops:
  0.6 2.3 %pack.1 = (f32[48,8,128]{2,1,0:T(8,128)}, f32[54,8,128]{2,1,0:T(8,128)}, f32[48,8,128]{2,1,0:T(8,128)}, f32[54,8,128]{2,1,0:T(8,128)}, f32[384,128]{1,0:T(8,128)}, /*index=5*/s32[8,128]{1,0:T(8,128)}) custom-call(s32[1]{0:T(128)} %bitcast.place_ref, f32[48,4,8,128]{3,2,1,0:T(8,128)} %bitcast.15, f32[384,128]{1,0:T(8,128)} %bitcast.18, s32[8,128]{1,0:T(8,128)} %bitcast.23), custom_call_target="tpu_custom_call" | custom-call | tf_op jit(solution)/shard_map/pack/pallas_call | solution.py:77
  3.0 0.5 %collective-permute-start.2 = (f32[54,8,128]{2,1,0:T(8,128)}, f32[54,8,128]{2,1,0:T(8,128)S(1)}, u32[]{:S(2)}, u32[]{:S(2)}) collective-permute-start(f32[54,8,128]{2,1,0:T(8,128)} %get-tuple-element.23), channel_id=1, source_target_pairs={{0,1},{1,0},{2,3},{3,2},{4,5},{5,4},{6,7},{7,6},{8,9},{9,8},{10,11... | collective-permute-start | bytes 663560 | tf_op jit(solution)/shard_map/ppermute | solution.py:375
  3.5 2.6 %collective-permute-start.4 = (f32[54,8,128]{2,1,0:T(8,128)}, f32[54,8,128]{2,1,0:T(8,128)S(1)}, u32[]{:S(2)}, u32[]{:S(2)}) collective-permute-start(f32[54,8,128]{2,1,0:T(8,128)} %get-tuple-element.25), channel_id=1, source_target_pairs={{0,3},{1,2},{2,1},{3,0},{4,7},{5,6},{6,5},{7,4},{8,11},{9,10},{10,... | collective-permute-start | bytes 663560 | tf_op jit(solution)/shard_map/ppermute | solution.py:375
  6.1 0.0 collective-permute-start.3
  6.2 1.3 %collective-permute-start.1 = (f32[384,128]{1,0:T(8,128)}, f32[384,128]{1,0:T(8,128)S(1)}, u32[]{:S(2)}, u32[]{:S(2)}) collective-permute-start(f32[384,128]{1,0:T(8,128)} %get-tuple-element.18.x_ref), channel_id=1, source_target_pairs={{4,0},{8,4},{12,8},{16,12},{20,16},{24,20},{28,24},{5,1},{9,5},{13... | collective-permute-start | bytes 589832 | tf_op jit(solution)/shard_map/ppermute | solution.py:27
  7.4 4.6 %collective-permute-start = (f32[384,128]{1,0:T(8,128)}, f32[384,128]{1,0:T(8,128)S(1)}, u32[]{:S(2)}, u32[]{:S(2)}) collective-permute-start(f32[384,128]{1,0:T(8,128)} %get-tuple-element.18.x_ref), channel_id=1, source_target_pairs={{0,4},{4,8},{8,12},{12,16},{16,20},{20,24},{24,28},{1,5},{5,9},{9,... | collective-permute-start | bytes 589832 | tf_op jit(solution)/shard_map/ppermute | solution.py:22
  12.7 2.8 %ahead.1 = (f32[8,72,128]{2,1,0:T(8,128)}, f32[24,16,128]{2,1,0:T(8,128)}, bf16[48,3072]{1,0:T(8,128)(2,1)}) custom-call(s32[1]{0:T(128)S(6)} %copy.14.sample_ref, f32[1024]{0:T(1024)} %velocities_ref.1, f32[1024]{0:T(1024)} %shifts_ref.1, f32[3,3,8,7]{3,2,1,0:T(8,128)} %bitcast.21, f32[3,3,8,7]{3,2,1,0:T(8,128)} %bitcast.22, f32[3,8]{1,0:T(4,128)} %bitcast.24, ...), custom_call_target="tpu_custom_call" | custom-call | tf_op jit(solution)/shard_map/ahead/pallas_call | solution.py:164
  15.4 1.1 %collective-permute-done.3 = f32[48,8,128]{2,1,0:T(8,128)S(1)} collective-permute-done((f32[48,8,128]{2,1,0:T(8,128)}, f32[48,8,128]{2,1,0:T(8,128)S(1)}, u32[]{:S(2)}, u32[]{:S(2)}) %collective-permute-start.3) | collective-permute-done | bytes 196640 | tf_op jit(solution)/shard_map/ppermute | solution.py:375
  16.5 0.0 copy-start.2
  16.5 0.0 collective-permute-done.1.after_x_ref
  16.5 0.0 copy-start.3
  16.5 3.0 %collective-permute-done.before_x_ref = f32[384,128]{1,0:T(8,128)S(1)} collective-permute-done((f32[384,128]{1,0:T(8,128)}, f32[384,128]{1,0:T(8,128)S(1)}, u32[]{:S(2)}, u32[]{:S(2)}) %collective-permute-start) | collective-permute-done | bytes 196640 | tf_op jit(solution)/shard_map/ppermute | solution.py:22
  19.5 0.0 copy-start.4
  19.5 0.0 collective-permute-done.2
  19.5 0.0 copy-start
  19.5 0.0 collective-permute-done.4
  19.5 0.0 copy-start.1
  19.6 0.0 copy-done.2
  19.6 0.0 copy-done.3
  19.6 0.6 %copy-done.4 = f32[384,128]{1,0:T(8,128)} copy-done((f32[384,128]{1,0:T(8,128)}, f32[384,128]{1,0:T(8,128)S(1)}, u32[]{:S(2)}) %copy-start.4) | copy-done | bytes 196632
  20.2 0.1 copy-done
  20.3 0.1 copy-done.1
  20.3 3.3 %sums.1 = (bf16[240,3072]{1,0:T(8,128)(2,1)}, f32[48,128]{1,0:T(8,128)}) custom-call(s32[1]{0:T(128)} %bitcast.place_ref, f32[8,72,128]{2,1,0:T(8,128)} %get-tuple-element.20.fields_ref, f32[24,16,128]{2,1,0:T(8,128)} %get-tuple-element.21.applied_ref, bf16[48,3072]{1,0:T(8,128)(2,1)} %get-tuple-element.22.own_ref, f32[384,128]{1,0:T(8,128)} %copy-done.4, ...), custom_call_target="tpu_custom_call" | custom-call | tf_op jit(solution)/shard_map/sums/pallas_call | solution.py:254
  23.7 1.1 %collective-permute-start.7 = (f32[48,128]{1,0:T(8,128)}, f32[48,128]{1,0:T(8,128)S(1)}, u32[]{:S(2)}, u32[]{:S(2)}) collective-permute-start(f32[48,128]{1,0:T(8,128)} %get-tuple-element.26), channel_id=1, source_target_pairs={{0,3},{1,2},{2,1},{3,0},{4,7},{5,6},{6,5},{7,4},{8,11},{9,10},{10,... | collective-permute-start | bytes 73736 | tf_op jit(solution)/shard_map/ppermute | solution.py:269
  24.8 0.5 %collective-permute-start.6 = (f32[48,128]{1,0:T(8,128)}, f32[48,128]{1,0:T(8,128)S(1)}, u32[]{:S(2)}, u32[]{:S(2)}) collective-permute-start(f32[48,128]{1,0:T(8,128)} %get-tuple-element.26), channel_id=1, source_target_pairs={{0,2},{1,3},{2,0},{3,1},{4,6},{5,7},{6,4},{7,5},{8,10},{9,11},{10,... | collective-permute-start | bytes 73736 | tf_op jit(solution)/shard_map/ppermute | solution.py:269
  25.3 0.2 collective-permute-start.5
  25.5 1.7 %collective-permute-done.7 = f32[48,128]{1,0:T(8,128)S(1)} collective-permute-done((f32[48,128]{1,0:T(8,128)}, f32[48,128]{1,0:T(8,128)S(1)}, u32[]{:S(2)}, u32[]{:S(2)}) %collective-permute-start.7) | collective-permute-done | bytes 24608 | tf_op jit(solution)/shard_map/ppermute | solution.py:269
  27.2 1.6 %collective-permute-done.6 = f32[48,128]{1,0:T(8,128)S(1)} collective-permute-done((f32[48,128]{1,0:T(8,128)}, f32[48,128]{1,0:T(8,128)S(1)}, u32[]{:S(2)}, u32[]{:S(2)}) %collective-permute-start.6) | collective-permute-done | bytes 24608 | tf_op jit(solution)/shard_map/ppermute | solution.py:269
  28.8 0.0 collective-permute-done.5
  28.8 0.7 %add_add_fusion = f32[48,128]{1,0:T(8,128)S(1)} fusion(f32[48,128]{1,0:T(8,128)S(1)} %collective-permute-done.6, f32[48,128]{1,0:T(8,128)S(1)} %collective-permute-done.7, f32[48,128]{1,0:T(8,128)} %get-tuple-element.26, f32[48,128]{1,0:T(8,128)S(1)} %collective-permute-done.5), kind=kLoop, calls=%fused_computation | loop fusion | flops 18432 | bytes 122880 | tf_op jit(solution)/shard_map/add | solution.py:272
  29.6 13.4 %all_to_all.5.parts_ref = f32[8,48,128]{2,1,0:T(8,128)} all-to-all(f32[8,48,128]{2,1,0:T(8,128)S(1)} %broadcast_in_dim.2), channel_id=1, replica_groups=mesh['space'=8,'basis'=4] {'space'}, dimensions={0} | all-to-all | bytes 393216 | tf_op jit(solution)/shard_map/all_to_all | solution.py:278
  43.0 4.5 %finish.1 = (f32[384,128]{1,0:T(8,128)}, f32[16,16]{1,0:T(8,128)}, f32[16,16]{1,0:T(8,128)}) custom-call(s32[1]{0:T(128)} %bitcast.place_ref, f32[8,48,128]{2,1,0:T(8,128)} %all_to_all.5.parts_ref, bf16[240,3072]{1,0:T(8,128)(2,1)} %get-tuple-element.27.stack_ref), custom_call_target="tpu_custom_call" | custom-call | tf_op jit(solution)/shard_map/finish/pallas_call | solution.py:341
  (1 shorter events, 0.0 us)
Async XLA Ops:
  3.0 16.6 %collective-permute-start.2 = (f32[54,8,128]{2,1,0:T(8,128)}, f32[54,8,128]{2,1,0:T(8,128)S(1)}, u32[]{:S(2)}, u32[]{:S(2)}) collective-permute-start(f32[54,8,128]{2,1,0:T(8,128)} %get-tuple-element.23), channel_id=1, source_target_pairs={{0,1},{1,0},{2,3},{3,2},{4,5},{5,4},{6,7},{7,6},{8,9},{9,8},{10,11... | collective-permute-start | bytes 663560 | tf_op jit(solution)/shard_map/ppermute | solution.py:375
  3.5 16.1 %collective-permute-start.4 = (f32[54,8,128]{2,1,0:T(8,128)}, f32[54,8,128]{2,1,0:T(8,128)S(1)}, u32[]{:S(2)}, u32[]{:S(2)}) collective-permute-start(f32[54,8,128]{2,1,0:T(8,128)} %get-tuple-element.25), channel_id=1, source_target_pairs={{0,3},{1,2},{2,1},{3,0},{4,7},{5,6},{6,5},{7,4},{8,11},{9,10},{10,... | collective-permute-start | bytes 663560 | tf_op jit(solution)/shard_map/ppermute | solution.py:375
  6.1 10.4 %collective-permute-start.3 = (f32[48,8,128]{2,1,0:T(8,128)}, f32[48,8,128]{2,1,0:T(8,128)S(1)}, u32[]{:S(2)}, u32[]{:S(2)}) collective-permute-start(f32[48,8,128]{2,1,0:T(8,128)} %get-tuple-element.24), channel_id=1, source_target_pairs={{0,2},{1,3},{2,0},{3,1},{4,6},{5,7},{6,4},{7,5},{8,10},{9,11},{10,... | collective-permute-start | bytes 589832 | tf_op jit(solution)/shard_map/ppermute | solution.py:375
  6.2 10.4 %collective-permute-start.1 = (f32[384,128]{1,0:T(8,128)}, f32[384,128]{1,0:T(8,128)S(1)}, u32[]{:S(2)}, u32[]{:S(2)}) collective-permute-start(f32[384,128]{1,0:T(8,128)} %get-tuple-element.18.x_ref), channel_id=1, source_target_pairs={{4,0},{8,4},{12,8},{16,12},{20,16},{24,20},{28,24},{5,1},{9,5},{13... | collective-permute-start | bytes 589832 | tf_op jit(solution)/shard_map/ppermute | solution.py:27
  7.4 12.1 %collective-permute-start = (f32[384,128]{1,0:T(8,128)}, f32[384,128]{1,0:T(8,128)S(1)}, u32[]{:S(2)}, u32[]{:S(2)}) collective-permute-start(f32[384,128]{1,0:T(8,128)} %get-tuple-element.18.x_ref), channel_id=1, source_target_pairs={{0,4},{4,8},{8,12},{12,16},{16,20},{20,24},{24,28},{1,5},{5,9},{9,... | collective-permute-start | bytes 589832 | tf_op jit(solution)/shard_map/ppermute | solution.py:22
  16.5 3.0 %copy-start.2 = (f32[48,8,128]{2,1,0:T(8,128)}, f32[48,8,128]{2,1,0:T(8,128)S(1)}, u32[]{:S(2)}) copy-start(f32[48,8,128]{2,1,0:T(8,128)S(1)} %collective-permute-done.3) | copy-start | bytes 589828
  16.5 3.1 %copy-start.3 = (f32[384,128]{1,0:T(8,128)}, f32[384,128]{1,0:T(8,128)S(1)}, u32[]{:S(2)}) copy-start(f32[384,128]{1,0:T(8,128)S(1)} %collective-permute-done.1.after_x_ref) | copy-start | bytes 589828
  19.5 0.7 %copy-start.4 = (f32[384,128]{1,0:T(8,128)}, f32[384,128]{1,0:T(8,128)S(1)}, u32[]{:S(2)}) copy-start(f32[384,128]{1,0:T(8,128)S(1)} %collective-permute-done.before_x_ref) | copy-start | bytes 589828
  19.5 0.7 %copy-start = (f32[54,8,128]{2,1,0:T(8,128)}, f32[54,8,128]{2,1,0:T(8,128)S(1)}, u32[]{:S(2)}) copy-start(f32[54,8,128]{2,1,0:T(8,128)S(1)} %collective-permute-done.2) | copy-start | bytes 663556
  19.5 0.8 %copy-start.1 = (f32[54,8,128]{2,1,0:T(8,128)}, f32[54,8,128]{2,1,0:T(8,128)S(1)}, u32[]{:S(2)}) copy-start(f32[54,8,128]{2,1,0:T(8,128)S(1)} %collective-permute-done.4) | copy-start | bytes 663556
  23.7 3.5 %collective-permute-start.7 = (f32[48,128]{1,0:T(8,128)}, f32[48,128]{1,0:T(8,128)S(1)}, u32[]{:S(2)}, u32[]{:S(2)}) collective-permute-start(f32[48,128]{1,0:T(8,128)} %get-tuple-element.26), channel_id=1, source_target_pairs={{0,3},{1,2},{2,1},{3,0},{4,7},{5,6},{6,5},{7,4},{8,11},{9,10},{10,... | collective-permute-start | bytes 73736 | tf_op jit(solution)/shard_map/ppermute | solution.py:269
  24.8 4.0 %collective-permute-start.6 = (f32[48,128]{1,0:T(8,128)}, f32[48,128]{1,0:T(8,128)S(1)}, u32[]{:S(2)}, u32[]{:S(2)}) collective-permute-start(f32[48,128]{1,0:T(8,128)} %get-tuple-element.26), channel_id=1, source_target_pairs={{0,2},{1,3},{2,0},{3,1},{4,6},{5,7},{6,4},{7,5},{8,10},{9,11},{10,... | collective-permute-start | bytes 73736 | tf_op jit(solution)/shard_map/ppermute | solution.py:269
  25.3 3.5 %collective-permute-start.5 = (f32[48,128]{1,0:T(8,128)}, f32[48,128]{1,0:T(8,128)S(1)}, u32[]{:S(2)}, u32[]{:S(2)}) collective-permute-start(f32[48,128]{1,0:T(8,128)} %get-tuple-element.26), channel_id=1, source_target_pairs={{0,1},{1,0},{2,3},{3,2},{4,5},{5,4},{6,7},{7,6},{8,9},{9,8},{10,11... | collective-permute-start | bytes 73736 | tf_op jit(solution)/shard_map/ppermute | solution.py:269

commit v6 on v5

--- a/solution.py
+++ b/solution.py
@@ -11,10 +11,23 @@
 VMEM = pl.BlockSpec(memory_space=pltpu.VMEM)
 SMEM = pl.BlockSpec(memory_space=pltpu.SMEM)
 HBM = pl.BlockSpec(memory_space=pltpu.HBM)
+SCRATCH = pltpu.CompilerParams(vmem_limit_bytes=8 * 2**20)
 
 
 def f32(*shape):
     return jax.ShapeDtypeStruct(shape, jnp.float32)
+
+
+def near(*shape, dtype=jnp.float32):
+    return pltpu.VMEM(shape, dtype)
+
+
+def kept(*arrays):
+    return [pltpu.with_memory_space_constraint(array, pltpu.VMEM) for array in arrays]
+
+
+def far(*arrays):
+    return [pltpu.with_memory_space_constraint(array, pltpu.HBM) for array in arrays]
 
 
 def from_lower(values, axis):
@@ -71,17 +84,18 @@
     tiles = group_cols * comps
     edge_tiles = block_cols * comps // rows
     pieces = [
-        f32(tiles + (edge_tiles if k in partners(count)[1] else 0), rows, lanes)
+        near(tiles + (edge_tiles if k in partners(count)[1] else 0), rows, lanes)
         for k in range(count)
     ]
     return pl.pallas_call(
         functools.partial(pack_kernel, comps),
-        out_shape=(*pieces, f32(*x_rows.shape), jax.ShapeDtypeStruct(material.shape, jnp.int32)),
+        out_shape=(*pieces, near(*x_rows.shape), near(*material.shape, dtype=jnp.int32)),
         in_specs=[SMEM, HBM, HBM, HBM],
         out_specs=(VMEM,) * (count + 2),
         scratch_shapes=[pltpu.SemaphoreType.DMA((count + 2,))],
+        compiler_params=SCRATCH,
         name="pack",
-    )(place, basis.reshape(tiles, count, rows, lanes), x_rows, material)
+    )(place, *far(basis.reshape(tiles, count, rows, lanes), x_rows, material))
 
 
 def three_parts(values):
@@ -97,9 +111,25 @@
 
 
 def ahead_kernel(
-    sample_ref, velocities_ref, shifts_ref, k0_ref, ke_ref, diag_ref, mass_ref, material_ref,
-    x_ref, own_ref, fields_ref, applied_ref, stack_ref,
+    sample_ref, *refs
 ):
+    far_refs, refs = refs[:6], refs[6:]
+    material_ref, x_ref, own_ref, fields_ref, applied_ref, stack_ref, *near_refs, sems = refs
+    velocities_ref, shifts_ref, k0_ref, ke_ref, diag_ref, mass_ref = near_refs
+    copies = [
+        pltpu.make_async_copy(source, target, sems.at[index])
+        for index, (source, target) in enumerate(zip(far_refs, near_refs))
+    ]
+    for copy in copies:
+        copy.start()
+    group_cols = stack_ref.shape[0] // 3
+    for line in range(applied_ref.shape[0]):
+        values = own_ref[pl.ds(line, group_cols, stride=applied_ref.shape[0]), :]
+        for index, part in enumerate(three_parts(values)):
+            there = pl.ds(line * values.shape[1], values.shape[1])
+            stack_ref[pl.ds(index * group_cols, group_cols), there] = part
+    for copy in copies:
+        copy.wait()
     comps, _, levels, offsets = k0_ref.shape
     rows, lanes = material_ref.shape
     lines = comps * rows
@@ -149,33 +179,29 @@
         for out in range(comps):
             applied_ref[out * rows + row] = sums[out]
 
-    group_cols = own_ref.shape[0] // lines
-    for line in range(lines):
-        values = own_ref[pl.ds(line, group_cols, stride=lines), :]
-        for index, part in enumerate(three_parts(values)):
-            stack_ref[pl.ds(index * group_cols, group_cols), pl.ds(line * lanes, lanes)] = part
-
 
 def ahead(sample, velocities, shifts, k0, ke, diag, mass, material, x_rows, own, comps):
     rows, lanes = material.shape
     lines = comps * rows
-    offsets = k0.shape[1]
-    stride = -(-offsets // 8) * 8
+    stride = -(-k0.shape[1] // 8) * 8
+    k0, ke = (jnp.transpose(blocks, (2, 3, 0, 1)) for blocks in (k0, ke))
+    tables = far(velocities, shifts, k0, ke, diag.T, mass.T)
     return pl.pallas_call(
         ahead_kernel,
         out_shape=(
-            f32(rows, comps * comps * stride, lanes),
-            f32(lines, x_rows.shape[0] // lines, lanes),
-            jax.ShapeDtypeStruct((3 * own.shape[0] // lines, lines * lanes), jnp.bfloat16),
+            near(rows, comps * comps * stride, lanes),
+            near(lines, x_rows.shape[0] // lines, lanes),
+            near(3 * own.shape[0] // lines, lines * lanes, dtype=jnp.bfloat16),
         ),
-        in_specs=[SMEM] * 3 + [VMEM] * 7,
+        in_specs=[SMEM] + [HBM] * 6 + [VMEM] * 3,
         out_specs=(VMEM,) * 3,
+        scratch_shapes=[
+            (pltpu.SMEM if array.ndim == 1 else pltpu.VMEM)(array.shape, jnp.float32)
+            for array in tables
+        ] + [pltpu.SemaphoreType.DMA((len(tables),))],
+        compiler_params=SCRATCH,
         name="ahead",
-    )(
-        sample, velocities, shifts,
-        jnp.transpose(k0, (2, 3, 0, 1)), jnp.transpose(ke, (2, 3, 0, 1)), diag.T, mass.T,
-        material, x_rows, own,
-    )
+    )(sample, *tables, *kept(material, x_rows, own))
 
 
 def sums_kernel(
@@ -254,13 +280,14 @@
     return pl.pallas_call(
         functools.partial(sums_kernel, comps, partners(1 + len(pieces))[1]),
         out_shape=(
-            jax.ShapeDtypeStruct((3 * joined, lines * lanes), jnp.bfloat16),
-            f32(basis_cols // 2 + block_cols, 2 * basis_cols),
+            near(3 * joined, lines * lanes, dtype=jnp.bfloat16),
+            near(basis_cols // 2 + block_cols, 2 * basis_cols),
         ),
         in_specs=[SMEM] + [VMEM] * (3 + len(halos) + len(pieces)),
         out_specs=(VMEM, VMEM),
+        compiler_params=SCRATCH,
         name="sums",
-    )(place, fields, applied, own, *halos, *pieces)
+    )(place, *kept(fields, applied, own, *halos, *pieces))
 
 
 def exchange_sum(part, axis):
@@ -346,8 +373,9 @@
         in_specs=[SMEM] + [VMEM] * 2,
         out_specs=(VMEM, VMEM, VMEM),
         scratch_shapes=[pltpu.VMEM((basis_cols, block_cols), jnp.float32)],
+        compiler_params=SCRATCH,
         name="finish",
-    )(place, parts, stack)
+    )(place, *kept(parts, stack))
 
 
 def shards(

time: 47.8 us -> 41 us (0.86)
  Pallas kernels: 12.9 us -> 7.07 us
  local copies, waits for them, and re-layouts: 0.79 us -> 0.01 us
  other arithmetic: 0.75 us -> 0.01 us
  waiting for transfers between devices: 7.42 us -> 8 us
    pallas_call x1, Pallas kernels: 3.31 us -> 1.05 us  [sums(): pl.pallas_call(functools.partial(sums_kernel, comps, partners(1 + len(pie...]
    pallas_call x1, Pallas kernels: 4.49 us -> 3.01 us  [finish(): pl.pallas_call(functools.partial(finish_kernel, row_count), out_shape=(f3...]
    pallas_call x1, Pallas kernels: 2.78 us -> 1.66 us  [ahead(): pl.pallas_call(ahead_kernel, out_shape=(near(rows, comps * comps * stride...]
    pallas_call x1, Pallas kernels: 2.31 us -> 1.36 us  [pack(): pl.pallas_call(functools.partial(pack_kernel, comps), out_shape=(*pieces,...]
    ppermute x3, waiting for transfers between devices: 1.08 us -> 1.98 us  [shards(): lax.ppermute(pieces[name], 'basis', [(i, i ^ name) for i in range(count)])]
    unnamed x10 -> x0, local copies, waits for them, and re-layouts: 0.78 us -> none
    add x1, other arithmetic: 0.75 us -> 0.01 us  [exchange_sum(): terms = [a + b for a, b in zip(terms[::2], terms[1::2])]]
  transfers between devices with their start and end apart: 8 -> 8, of which waited for: 4 -> 4; matrix products, arithmetic and copies ran while one was open for 0% -> 0% of each run, Pallas kernels for 6% -> 4%
where the time goes in v6:
time: 41 us; the launch traced here: 40.7 us
  blocking collectives  13.4 us (33%)
  starting transfers between devices  10.9 us (27%)
  waiting for transfers between devices  8 us (20%)
  Pallas kernels  7.07 us (17%)
  between operations  1.33 us (3%)
    all_to_all x1, blocking collectives, exchange(): lax.all_to_all(jnp.broadcast_to(part[None], (count,) + part.shape), axis,...  13.4 us
    ppermute x1, starting transfers between devices, from_lower(): return lax.ppermute(values, axis, [(i, i + 1) for i in range(count - 1)])  4.56 us
    ppermute x3, starting transfers between devices, shards(): lax.ppermute(pieces[name], 'basis', [(i, i ^ name) for i in range(count)])  3.2 us
    ppermute x3, waiting for transfers between devices, exchange_sum(): lax.ppermute(part, axis, [(i, i ^ k) for i in range(count)])  3.11 us
    pallas_call x1, Pallas kernels, finish(): pl.pallas_call(functools.partial(finish_kernel, row_count), out_shape=(f3...  3.01 us
    ppermute x1, waiting for transfers between devices, from_lower(): return lax.ppermute(values, axis, [(i, i + 1) for i in range(count - 1)])  2.91 us
    ppermute x3, waiting for transfers between devices, shards(): lax.ppermute(pieces[name], 'basis', [(i, i ^ name) for i in range(count)])  1.98 us
    ppermute x3, starting transfers between devices, exchange_sum(): lax.ppermute(part, axis, [(i, i ^ k) for i in range(count)])  1.89 us
  transfers between devices with their start and end apart: 8, of which 4 were waited for; matrix products, arithmetic and copies ran while one was open for 0% of the time, Pallas kernels for 4%

profile of v6, /device:TPU:0, one launch (start us, length us, event | category | flops | bytes accessed | tf_op | source)
XLA Modules:
  0.0 40.7 jit_solution(7587974675554808561)
XLA Ops:
  0.6 1.4 %pack.1 = (f32[48,8,128]{2,1,0:T(8,128)S(1)}, f32[54,8,128]{2,1,0:T(8,128)S(1)}, f32[48,8,128]{2,1,0:T(8,128)S(1)}, f32[54,8,128]{2,1,0:T(8,128)S(1)}, f32[384,128]{1,0:T(8,128)S(1)}, /*index=5*/s32[8,128]{1,0:T(8,128)S(1)}) custom-call(s32[1]{0:T(128)} %bitcast.place_ref, f32[48,4,8,128]{3,2,1,0:T(8,128)} %bitcast.19, f32[384,128]{1,0:T(8,128)} %bitcast.20, ...), custom_call_target="tpu_custom_call" | custom-call | tf_op jit(solution)/shard_map/pack/pallas_call | solution.py:90
  2.0 0.5 %collective-permute-start.2 = (f32[54,8,128]{2,1,0:T(8,128)S(1)}, f32[54,8,128]{2,1,0:T(8,128)S(1)}, u32[]{:S(2)}, u32[]{:S(2)}) collective-permute-start(f32[54,8,128]{2,1,0:T(8,128)S(1)} %get-tuple-element.23), channel_id=1, source_target_pairs={{0,1},{1,0},{2,3},{3,2},{4,5},{5,4},{6,7},{7,6},{8,9},{9,8},{10,11... | collective-permute-start | bytes 663560 | tf_op jit(solution)/shard_map/ppermute | solution.py:403
  2.5 2.6 %collective-permute-start.4 = (f32[54,8,128]{2,1,0:T(8,128)S(1)}, f32[54,8,128]{2,1,0:T(8,128)S(1)}, u32[]{:S(2)}, u32[]{:S(2)}) collective-permute-start(f32[54,8,128]{2,1,0:T(8,128)S(1)} %get-tuple-element.25), channel_id=1, source_target_pairs={{0,3},{1,2},{2,1},{3,0},{4,7},{5,6},{6,5},{7,4},{8,11},{9,10},{10,... | collective-permute-start | bytes 663560 | tf_op jit(solution)/shard_map/ppermute | solution.py:403
  5.2 0.0 collective-permute-start.3
  5.2 1.3 %collective-permute-start.1 = (f32[384,128]{1,0:T(8,128)S(1)}, f32[384,128]{1,0:T(8,128)S(1)}, u32[]{:S(2)}, u32[]{:S(2)}) collective-permute-start(f32[384,128]{1,0:T(8,128)S(1)} %get-tuple-element.18.refs_7_), channel_id=1, source_target_pairs={{4,0},{8,4},{12,8},{16,12},{20,16},{24,20},{28,24},{5,1},{9,5},{13... | collective-permute-start | bytes 589832 | tf_op jit(solution)/shard_map/ppermute | solution.py:40
  6.5 4.6 %collective-permute-start = (f32[384,128]{1,0:T(8,128)S(1)}, f32[384,128]{1,0:T(8,128)S(1)}, u32[]{:S(2)}, u32[]{:S(2)}) collective-permute-start(f32[384,128]{1,0:T(8,128)S(1)} %get-tuple-element.18.refs_7_), channel_id=1, source_target_pairs={{0,4},{4,8},{8,12},{12,16},{16,20},{20,24},{24,28},{1,5},{5,9},{9,... | collective-permute-start | bytes 589832 | tf_op jit(solution)/shard_map/ppermute | solution.py:35
  11.7 1.7 %ahead.1 = (f32[8,72,128]{2,1,0:T(8,128)S(1)}, f32[24,16,128]{2,1,0:T(8,128)S(1)}, bf16[48,3072]{1,0:T(8,128)(2,1)S(1)}) custom-call(s32[1]{0:T(128)S(6)} %copy.14.sample_ref, f32[1024]{0:T(1024)} %refs_0_.1, f32[1024]{0:T(1024)} %refs_1_.1, f32[3,3,8,7]{3,2,1,0:T(8,128)} %bitcast.21, f32[3,3,8,7]{3,2,1,0:T(8,128)} %bitcast.22, f32[3,8]{1,0:T(4,128)} %bitcast.24, ...), custom_call_target="tpu_custom_call" | custom-call | tf_op jit(solution)/shard_map/ahead/pallas_call | solution.py:189
  13.4 2.0 %collective-permute-done.3 = f32[48,8,128]{2,1,0:T(8,128)S(1)} collective-permute-done((f32[48,8,128]{2,1,0:T(8,128)S(1)}, f32[48,8,128]{2,1,0:T(8,128)S(1)}, u32[]{:S(2)}, u32[]{:S(2)}) %collective-permute-start.3) | collective-permute-done | bytes 196640 | tf_op jit(solution)/shard_map/ppermute | solution.py:403
  15.3 0.0 collective-permute-done.1.after_x_ref
  15.3 2.9 %collective-permute-done.before_x_ref = f32[384,128]{1,0:T(8,128)S(1)} collective-permute-done((f32[384,128]{1,0:T(8,128)S(1)}, f32[384,128]{1,0:T(8,128)S(1)}, u32[]{:S(2)}, u32[]{:S(2)}) %collective-permute-start) | collective-permute-done | bytes 196640 | tf_op jit(solution)/shard_map/ppermute | solution.py:35
  18.3 0.0 collective-permute-done.2
  18.3 0.0 collective-permute-done.4
  18.3 1.1 %sums.1 = (bf16[240,3072]{1,0:T(8,128)(2,1)S(1)}, f32[48,128]{1,0:T(8,128)S(1)}) custom-call(s32[1]{0:T(128)} %bitcast.place_ref, f32[8,72,128]{2,1,0:T(8,128)S(1)} %get-tuple-element.20.fields_ref, f32[24,16,128]{2,1,0:T(8,128)S(1)} %get-tuple-element.21.applied_ref, bf16[48,3072]{1,0:T(8,128)(2,1)S(1)} %get-tuple-element.22.own_ref, ...), custom_call_target="tpu_custom_call" | custom-call | tf_op jit(solution)/shard_map/sums/pallas_call | solution.py:280
  19.3 1.2 %collective-permute-start.7 = (f32[48,128]{1,0:T(8,128)S(1)}, f32[48,128]{1,0:T(8,128)S(1)}, u32[]{:S(2)}, u32[]{:S(2)}) collective-permute-start(f32[48,128]{1,0:T(8,128)S(1)} %get-tuple-element.26), channel_id=1, source_target_pairs={{0,3},{1,2},{2,1},{3,0},{4,7},{5,6},{6,5},{7,4},{8,11},{9,10},{10,... | collective-permute-start | bytes 73736 | tf_op jit(solution)/shard_map/ppermute | solution.py:296
  20.5 0.5 %collective-permute-start.6 = (f32[48,128]{1,0:T(8,128)S(1)}, f32[48,128]{1,0:T(8,128)S(1)}, u32[]{:S(2)}, u32[]{:S(2)}) collective-permute-start(f32[48,128]{1,0:T(8,128)S(1)} %get-tuple-element.26), channel_id=1, source_target_pairs={{0,2},{1,3},{2,0},{3,1},{4,6},{5,7},{6,4},{7,5},{8,10},{9,11},{10,... | collective-permute-start | bytes 73736 | tf_op jit(solution)/shard_map/ppermute | solution.py:296
  21.0 0.2 collective-permute-start.5
  21.2 1.5 %collective-permute-done.7 = f32[48,128]{1,0:T(8,128)S(1)} collective-permute-done((f32[48,128]{1,0:T(8,128)S(1)}, f32[48,128]{1,0:T(8,128)S(1)}, u32[]{:S(2)}, u32[]{:S(2)}) %collective-permute-start.7) | collective-permute-done | bytes 24608 | tf_op jit(solution)/shard_map/ppermute | solution.py:296
  22.7 1.6 %collective-permute-done.6 = f32[48,128]{1,0:T(8,128)S(1)} collective-permute-done((f32[48,128]{1,0:T(8,128)S(1)}, f32[48,128]{1,0:T(8,128)S(1)}, u32[]{:S(2)}, u32[]{:S(2)}) %collective-permute-start.6) | collective-permute-done | bytes 24608 | tf_op jit(solution)/shard_map/ppermute | solution.py:296
  24.3 0.0 collective-permute-done.5
  24.4 13.4 %all_to_all.5.parts_ref = f32[8,48,128]{2,1,0:T(8,128)S(1)} all-to-all(f32[8,48,128]{2,1,0:T(8,128)S(1)} %broadcast_in_dim.2), channel_id=1, replica_groups=mesh['space'=8,'basis'=4] {'space'}, dimensions={0} | all-to-all | bytes 393216 | tf_op jit(solution)/shard_map/all_to_all | solution.py:305
  37.7 3.0 %finish.1 = (f32[384,128]{1,0:T(8,128)}, f32[16,16]{1,0:T(8,128)}, f32[16,16]{1,0:T(8,128)}) custom-call(s32[1]{0:T(128)} %bitcast.place_ref, f32[8,48,128]{2,1,0:T(8,128)S(1)} %all_to_all.5.parts_ref, bf16[240,3072]{1,0:T(8,128)(2,1)S(1)} %get-tuple-element.27.stack_ref), custom_call_target="tpu_custom_call" | custom-call | tf_op jit(solution)/shard_map/finish/pallas_call | solution.py:368
  (2 shorter events, 0.0 us)
Async XLA Ops:
  2.0 16.3 %collective-permute-start.2 = (f32[54,8,128]{2,1,0:T(8,128)S(1)}, f32[54,8,128]{2,1,0:T(8,128)S(1)}, u32[]{:S(2)}, u32[]{:S(2)}) collective-permute-start(f32[54,8,128]{2,1,0:T(8,128)S(1)} %get-tuple-element.23), channel_id=1, source_target_pairs={{0,1},{1,0},{2,3},{3,2},{4,5},{5,4},{6,7},{7,6},{8,9},{9,8},{10,11... | collective-permute-start | bytes 663560 | tf_op jit(solution)/shard_map/ppermute | solution.py:403
  2.5 15.8 %collective-permute-start.4 = (f32[54,8,128]{2,1,0:T(8,128)S(1)}, f32[54,8,128]{2,1,0:T(8,128)S(1)}, u32[]{:S(2)}, u32[]{:S(2)}) collective-permute-start(f32[54,8,128]{2,1,0:T(8,128)S(1)} %get-tuple-element.25), channel_id=1, source_target_pairs={{0,3},{1,2},{2,1},{3,0},{4,7},{5,6},{6,5},{7,4},{8,11},{9,10},{10,... | collective-permute-start | bytes 663560 | tf_op jit(solution)/shard_map/ppermute | solution.py:403
  5.2 10.2 %collective-permute-start.3 = (f32[48,8,128]{2,1,0:T(8,128)S(1)}, f32[48,8,128]{2,1,0:T(8,128)S(1)}, u32[]{:S(2)}, u32[]{:S(2)}) collective-permute-start(f32[48,8,128]{2,1,0:T(8,128)S(1)} %get-tuple-element.24), channel_id=1, source_target_pairs={{0,2},{1,3},{2,0},{3,1},{4,6},{5,7},{6,4},{7,5},{8,10},{9,11},{10,... | collective-permute-start | bytes 589832 | tf_op jit(solution)/shard_map/ppermute | solution.py:403
  5.2 10.1 %collective-permute-start.1 = (f32[384,128]{1,0:T(8,128)S(1)}, f32[384,128]{1,0:T(8,128)S(1)}, u32[]{:S(2)}, u32[]{:S(2)}) collective-permute-start(f32[384,128]{1,0:T(8,128)S(1)} %get-tuple-element.18.refs_7_), channel_id=1, source_target_pairs={{4,0},{8,4},{12,8},{16,12},{20,16},{24,20},{28,24},{5,1},{9,5},{13... | collective-permute-start | bytes 589832 | tf_op jit(solution)/shard_map/ppermute | solution.py:40
  6.5 11.8 %collective-permute-start = (f32[384,128]{1,0:T(8,128)S(1)}, f32[384,128]{1,0:T(8,128)S(1)}, u32[]{:S(2)}, u32[]{:S(2)}) collective-permute-start(f32[384,128]{1,0:T(8,128)S(1)} %get-tuple-element.18.refs_7_), channel_id=1, source_target_pairs={{0,4},{4,8},{8,12},{12,16},{16,20},{20,24},{24,28},{1,5},{5,9},{9,... | collective-permute-start | bytes 589832 | tf_op jit(solution)/shard_map/ppermute | solution.py:35
  19.3 3.3 %collective-permute-start.7 = (f32[48,128]{1,0:T(8,128)S(1)}, f32[48,128]{1,0:T(8,128)S(1)}, u32[]{:S(2)}, u32[]{:S(2)}) collective-permute-start(f32[48,128]{1,0:T(8,128)S(1)} %get-tuple-element.26), channel_id=1, source_target_pairs={{0,3},{1,2},{2,1},{3,0},{4,7},{5,6},{6,5},{7,4},{8,11},{9,10},{10,... | collective-permute-start | bytes 73736 | tf_op jit(solution)/shard_map/ppermute | solution.py:296
  20.5 3.8 %collective-permute-start.6 = (f32[48,128]{1,0:T(8,128)S(1)}, f32[48,128]{1,0:T(8,128)S(1)}, u32[]{:S(2)}, u32[]{:S(2)}) collective-permute-start(f32[48,128]{1,0:T(8,128)S(1)} %get-tuple-element.26), channel_id=1, source_target_pairs={{0,2},{1,3},{2,0},{3,1},{4,6},{5,7},{6,4},{7,5},{8,10},{9,11},{10,... | collective-permute-start | bytes 73736 | tf_op jit(solution)/shard_map/ppermute | solution.py:296
  21.0 3.3 %collective-permute-start.5 = (f32[48,128]{1,0:T(8,128)S(1)}, f32[48,128]{1,0:T(8,128)S(1)}, u32[]{:S(2)}, u32[]{:S(2)}) collective-permute-start(f32[48,128]{1,0:T(8,128)S(1)} %get-tuple-element.26), channel_id=1, source_target_pairs={{0,1},{1,0},{2,3},{3,2},{4,5},{5,4},{6,7},{7,6},{8,9},{9,8},{10,11... | collective-permute-start | bytes 73736 | tf_op jit(solution)/shard_map/ppermute | solution.py:296

commit v7 on v6

--- a/solution.py
+++ b/solution.py
@@ -30,14 +30,9 @@
     return [pltpu.with_memory_space_constraint(array, pltpu.HBM) for array in arrays]
 
 
-def from_lower(values, axis):
-    count = lax.axis_size(axis)
-    return lax.ppermute(values, axis, [(i, i + 1) for i in range(count - 1)])
-
-
-def from_upper(values, axis):
-    count = lax.axis_size(axis)
-    return lax.ppermute(values, axis, [(i + 1, i) for i in range(count - 1)])
+def swap(values, axis, first):
+    pairs = [(i, i + 1) for i in range(first, lax.axis_size(axis) - 1, 2)]
+    return lax.ppermute(values, axis, pairs + [(j, i) for i, j in pairs])
 
 
 def partners(count):
@@ -204,10 +199,10 @@
     )(sample, *tables, *kept(material, x_rows, own))
 
 
-def sums_kernel(
-    comps, edge_ks, place_ref, fields_ref, applied_ref, own_ref, before_x_ref, after_x_ref, *refs
-):
-    *piece_refs, stack_ref, sums_ref = refs
+def sums_kernel(comps, names, edge_ks, place_ref, slab_ref, fields_ref, applied_ref, own_ref, *refs):
+    *refs, stack_ref, sums_ref = refs
+    got = dict(zip(names, refs))
+    piece_refs = [got[k] for k in range(1, len(got) - 1)]
     lines, block_cols, lanes = applied_ref.shape
     rows = lines // comps
     stride = fields_ref.shape[1] // (comps * comps)
@@ -215,6 +210,7 @@
     basis_cols = (1 + len(piece_refs)) * group_cols
     joined = basis_cols + block_cols
     place = place_ref[0]
+    swapped = slab_ref[0] % 2 == 1
 
     def store(begin, line, values):
         for index, part in enumerate(three_parts(values)):
@@ -244,17 +240,24 @@
         totals = [applied_ref[out * rows + row] for out in range(comps)]
         for comp in range(comps):
             views = {
-                1: line_of(before_x_ref, comp, row, comps, rows, block_cols),
-                2: line_of(after_x_ref, comp, row, comps, rows, block_cols),
+                name: line_of(got[name], comp, row, comps, rows, block_cols)
+                for name in ("even", "odd")
             }
             if row == 0:
                 views[3] = edge(comp, -1)
             if row == rows - 1:
                 views[4] = edge(comp, 1)
-            for offset, view in views.items():
-                for out in range(comps):
-                    entry = (out * comps + comp) * stride + offset
-                    totals[out] = totals[out] + fields_ref[row, entry : entry + 1, :] * view
+            for out in range(comps):
+                entries = fields_ref[row, pl.ds((out * comps + comp) * stride, stride), :]
+                below, above = entries[1:2], entries[2:3]
+                chosen = {
+                    "even": jnp.where(swapped, below, above),
+                    "odd": jnp.where(swapped, above, below),
+                    3: entries[3:4],
+                    4: entries[4:5],
+                }
+                for name, view in views.items():
+                    totals[out] = totals[out] + chosen[name] * view
         for out in range(comps):
             store(basis_cols, out * rows + row, totals[out])
 
@@ -273,21 +276,22 @@
     )
 
 
-def sums(place, fields, applied, own, halos, pieces, comps):
+def sums(place, slab, fields, applied, own, got, comps):
+    count = len(got) - 1
     lines, block_cols, lanes = applied.shape
-    basis_cols = (1 + len(pieces)) * (own.shape[0] // 3)
+    basis_cols = count * (own.shape[0] // 3)
     joined = basis_cols + block_cols
     return pl.pallas_call(
-        functools.partial(sums_kernel, comps, partners(1 + len(pieces))[1]),
+        functools.partial(sums_kernel, comps, tuple(got), partners(count)[1]),
         out_shape=(
             near(3 * joined, lines * lanes, dtype=jnp.bfloat16),
             near(basis_cols // 2 + block_cols, 2 * basis_cols),
         ),
-        in_specs=[SMEM] + [VMEM] * (3 + len(halos) + len(pieces)),
+        in_specs=[SMEM] * 2 + [VMEM] * (3 + len(got)),
         out_specs=(VMEM, VMEM),
         compiler_params=SCRATCH,
         name="sums",
-    )(place, *kept(fields, applied, own, *halos, *pieces))
+    )(place, slab, *kept(fields, applied, own, *got.values()))
 
 
 def exchange_sum(part, axis):
@@ -387,26 +391,24 @@
     row_count = float(comps * extent_x * lax.axis_size("space") * basis.shape[3] * lanes)
 
     place = lax.axis_index("basis").astype(jnp.int32).reshape(1)
+    slab = lax.axis_index("space").astype(jnp.int32).reshape(1)
     count = lax.axis_size("basis")
-    own, *pieces, x_rows, material = pack(
-        place, basis, x_block.reshape(block_cols * lines, lanes), material.reshape(rows, lanes), block_cols
-    )
-    halos = [None, None]
-    order = (3, "upper", 2, "lower", 1)
-    pieces = dict(enumerate(pieces, 1))
-    for name in order:
-        if name == "lower":
-            halos[0] = from_lower(x_rows, "space")
-        elif name == "upper":
-            halos[1] = from_upper(x_rows, "space")
+    x_far = x_block.reshape(block_cols * lines, lanes)
+    own, *pieces, x_rows, material = pack(place, basis, x_far, material.reshape(rows, lanes), block_cols)
+    got = {}
+    for name in (3, "even", 2, "odd", 1):
+        if name == "even":
+            got[name] = swap(x_far, "space", 0)
+        elif name == "odd":
+            got[name] = swap(x_far, "space", 1)
         else:
-            pieces[name] = lax.ppermute(pieces[name], "basis", [(i, i ^ name) for i in range(count)])
-    pieces = [pieces[k].reshape(-1, lanes) for k in partners(count)[0]]
+            piece = lax.ppermute(pieces[name - 1], "basis", [(i, i ^ name) for i in range(count)])
+            got[name] = piece.reshape(-1, lanes)
     fields, applied, own = ahead(
         sample, velocities, shifts, k0_blocks, ke_blocks, k0_diag, mass, material, x_rows,
         own.reshape(-1, lanes), comps,
     )
-    stack, part = sums(place, fields, applied, own, halos, pieces, comps)
+    stack, part = sums(place, slab, fields, applied, own, got, comps)
     parts = exchange(exchange_sum(part, "basis"), "space")
     block, coeffs, upper = finish(place, parts, stack, row_count, block_cols, group_cols, lines)
     return (block.reshape(x_block.shape), coeffs, upper)

time: 41 us -> 40.3 us (0.983)
  waiting for transfers between devices: 8 us -> 7.48 us
    ppermute x3, waiting for transfers between devices: 3.11 us -> 2.18 us  [exchange_sum(): lax.ppermute(part, axis, [(i, i ^ k) for i in range(count)])]
  transfers between devices with their start and end apart: 8 -> 8, of which waited for: 4 -> 3; matrix products, arithmetic and copies ran while one was open for 0% -> 0% of each run, Pallas kernels for 4% -> 4%
where the time goes in v7:
time: 40.3 us; the launch traced here: 40 us
  blocking collectives  13.6 us (34%)
  starting transfers between devices  10.5 us (26%)
  waiting for transfers between devices  7.48 us (19%)
  Pallas kernels  7.05 us (17%)
  between operations  1.34 us (3%)
    all_to_all x1, blocking collectives, exchange(): lax.all_to_all(jnp.broadcast_to(part[None], (count,) + part.shape), axis,...  13.6 us
    ppermute x2, waiting for transfers between devices, swap(): return lax.ppermute(values, axis, pairs + [(j, i) for i, j in pairs])  5.29 us
    ppermute x2, starting transfers between devices, swap(): return lax.ppermute(values, axis, pairs + [(j, i) for i, j in pairs])  5 us
    ppermute x3, starting transfers between devices, shards(): lax.ppermute(pieces[name - 1], 'basis', [(i, i ^ name) for i in range(cou...  3.65 us
    pallas_call x1, Pallas kernels, finish(): pl.pallas_call(functools.partial(finish_kernel, row_count), out_shape=(f3...  3 us
    ppermute x3, waiting for transfers between devices, exchange_sum(): lax.ppermute(part, axis, [(i, i ^ k) for i in range(count)])  2.18 us
    ppermute x3, starting transfers between devices, exchange_sum(): lax.ppermute(part, axis, [(i, i ^ k) for i in range(count)])  1.89 us
    pallas_call x1, Pallas kernels, ahead(): pl.pallas_call(ahead_kernel, out_shape=(near(rows, comps * comps * stride...  1.65 us
  transfers between devices with their start and end apart: 8, of which 3 were waited for; matrix products, arithmetic and copies ran while one was open for 0% of the time, Pallas kernels for 4%

profile of v7, /device:TPU:0, one launch (start us, length us, event | category | flops | bytes accessed | tf_op | source)
XLA Modules:
  0.0 40.0 jit_solution(338225392594674096)
XLA Ops:
  0.6 1.4 %pack.1 = (f32[48,8,128]{2,1,0:T(8,128)S(1)}, f32[54,8,128]{2,1,0:T(8,128)S(1)}, f32[48,8,128]{2,1,0:T(8,128)S(1)}, f32[54,8,128]{2,1,0:T(8,128)S(1)}, f32[384,128]{1,0:T(8,128)S(1)}, /*index=5*/s32[8,128]{1,0:T(8,128)S(1)}) custom-call(s32[1]{0:T(128)} %bitcast.place_ref, f32[48,4,8,128]{3,2,1,0:T(8,128)} %bitcast.20, f32[384,128]{1,0:T(8,128)} %bitcast.21, ...), custom_call_target="tpu_custom_call" | custom-call | tf_op jit(solution)/shard_map/pack/pallas_call | solution.py:85
  2.0 2.5 %collective-permute-start = (f32[54,8,128]{2,1,0:T(8,128)S(1)}, f32[54,8,128]{2,1,0:T(8,128)S(1)}, u32[]{:S(2)}, u32[]{:S(2)}) collective-permute-start(f32[54,8,128]{2,1,0:T(8,128)S(1)} %get-tuple-element.23), channel_id=1, source_target_pairs={{0,3},{1,2},{2,1},{3,0},{4,7},{5,6},{6,5},{7,4},{8,11},{9,10},{10,... | collective-permute-start | bytes 663560 | tf_op jit(solution)/shard_map/ppermute | solution.py:405
  4.5 0.7 %collective-permute-start.4 = (f32[54,8,128]{2,1,0:T(8,128)S(1)}, f32[54,8,128]{2,1,0:T(8,128)S(1)}, u32[]{:S(2)}, u32[]{:S(2)}) collective-permute-start(f32[54,8,128]{2,1,0:T(8,128)S(1)} %get-tuple-element.25), channel_id=1, source_target_pairs={{0,1},{1,0},{2,3},{3,2},{4,5},{5,4},{6,7},{7,6},{8,9},{9,8},{10,11... | collective-permute-start | bytes 663560 | tf_op jit(solution)/shard_map/ppermute | solution.py:405
  5.2 0.7 %collective-permute-start.3 = (f32[384,128]{1,0:T(8,128)}, f32[384,128]{1,0:T(8,128)S(1)}, u32[]{:S(2)}, u32[]{:S(2)}) collective-permute-start(f32[384,128]{1,0:T(8,128)} %bitcast.22), channel_id=1, source_target_pairs={{4,8},{12,16},{20,24},{8,4},{16,12},{24,20},{5,9},{13,17},{21,25},... | collective-permute-start | bytes 589832 | tf_op jit(solution)/shard_map/ppermute | solution.py:35
  5.8 4.3 %collective-permute-start.1 = (f32[384,128]{1,0:T(8,128)}, f32[384,128]{1,0:T(8,128)S(1)}, u32[]{:S(2)}, u32[]{:S(2)}) collective-permute-start(f32[384,128]{1,0:T(8,128)} %bitcast.23), channel_id=1, source_target_pairs={{0,4},{8,12},{16,20},{24,28},{4,0},{12,8},{20,16},{28,24},{1,5},{9... | collective-permute-start | bytes 589832 | tf_op jit(solution)/shard_map/ppermute | solution.py:35
  10.2 0.5 %collective-permute-start.2 = (f32[48,8,128]{2,1,0:T(8,128)S(1)}, f32[48,8,128]{2,1,0:T(8,128)S(1)}, u32[]{:S(2)}, u32[]{:S(2)}) collective-permute-start(f32[48,8,128]{2,1,0:T(8,128)S(1)} %get-tuple-element.24), channel_id=1, source_target_pairs={{0,2},{1,3},{2,0},{3,1},{4,6},{5,7},{6,4},{7,5},{8,10},{9,11},{10,... | collective-permute-start | bytes 589832 | tf_op jit(solution)/shard_map/ppermute | solution.py:405
  11.3 1.7 %ahead.1 = (f32[8,72,128]{2,1,0:T(8,128)S(1)}, f32[24,16,128]{2,1,0:T(8,128)S(1)}, bf16[48,3072]{1,0:T(8,128)(2,1)S(1)}) custom-call(s32[1]{0:T(128)S(6)} %copy.14.sample_ref, f32[1024]{0:T(1024)} %refs_0_.1, f32[1024]{0:T(1024)} %refs_1_.1, f32[3,3,8,7]{3,2,1,0:T(8,128)} %bitcast.24, f32[3,3,8,7]{3,2,1,0:T(8,128)} %bitcast.25, f32[3,8]{1,0:T(4,128)} %bitcast.27, ...), custom_call_target="tpu_custom_call" | custom-call | tf_op jit(solution)/shard_map/ahead/pallas_call | solution.py:184
  13.0 0.0 collective-permute-done.3.refs_3_
  13.0 5.3 %collective-permute-done.1.refs_1_ = f32[384,128]{1,0:T(8,128)S(1)} collective-permute-done((f32[384,128]{1,0:T(8,128)}, f32[384,128]{1,0:T(8,128)S(1)}, u32[]{:S(2)}, u32[]{:S(2)}) %collective-permute-start.1) | collective-permute-done | bytes 196640 | tf_op jit(solution)/shard_map/ppermute | solution.py:35
  18.3 0.0 collective-permute-done.2
  18.3 0.0 collective-permute-done
  18.3 0.0 collective-permute-done.4
  18.3 1.0 %sums.1 = (bf16[240,3072]{1,0:T(8,128)(2,1)S(1)}, f32[48,128]{1,0:T(8,128)S(1)}) custom-call(s32[1]{0:T(128)} %bitcast.place_ref, s32[1]{0:T(128)} %bitcast.1.slab_ref, f32[8,72,128]{2,1,0:T(8,128)S(1)} %get-tuple-element.20.fields_ref, f32[24,16,128]{2,1,0:T(8,128)S(1)} %get-tuple-element.21.applied_ref, bf16[48,3072]{1,0:T(8,128)(2,1)S(1)} %get-tuple-element.22.own_ref, ...), custom_call_target="tpu_custom_call" | custom-call | tf_op jit(solution)/shard_map/sums/pallas_call | solution.py:284
  19.3 0.2 collective-permute-start.7
  19.5 1.5 %collective-permute-start.6 = (f32[48,128]{1,0:T(8,128)S(1)}, f32[48,128]{1,0:T(8,128)S(1)}, u32[]{:S(2)}, u32[]{:S(2)}) collective-permute-start(f32[48,128]{1,0:T(8,128)S(1)} %get-tuple-element.26), channel_id=1, source_target_pairs={{0,2},{1,3},{2,0},{3,1},{4,6},{5,7},{6,4},{7,5},{8,10},{9,11},{10,... | collective-permute-start | bytes 73736 | tf_op jit(solution)/shard_map/ppermute | solution.py:300
  21.0 0.2 collective-permute-start.5
  21.2 1.5 %collective-permute-done.7 = f32[48,128]{1,0:T(8,128)S(1)} collective-permute-done((f32[48,128]{1,0:T(8,128)S(1)}, f32[48,128]{1,0:T(8,128)S(1)}, u32[]{:S(2)}, u32[]{:S(2)}) %collective-permute-start.7) | collective-permute-done | bytes 24608 | tf_op jit(solution)/shard_map/ppermute | solution.py:300
  22.7 0.7 %collective-permute-done.6 = f32[48,128]{1,0:T(8,128)S(1)} collective-permute-done((f32[48,128]{1,0:T(8,128)S(1)}, f32[48,128]{1,0:T(8,128)S(1)}, u32[]{:S(2)}, u32[]{:S(2)}) %collective-permute-start.6) | collective-permute-done | bytes 24608 | tf_op jit(solution)/shard_map/ppermute | solution.py:300
  23.4 0.0 collective-permute-done.5
  23.4 13.6 %all_to_all.5.parts_ref = f32[8,48,128]{2,1,0:T(8,128)S(1)} all-to-all(f32[8,48,128]{2,1,0:T(8,128)S(1)} %broadcast_in_dim.2), channel_id=1, replica_groups=mesh['space'=8,'basis'=4] {'space'}, dimensions={0} | all-to-all | bytes 393216 | tf_op jit(solution)/shard_map/all_to_all | solution.py:309
  37.0 3.0 %finish.1 = (f32[384,128]{1,0:T(8,128)}, f32[16,16]{1,0:T(8,128)}, f32[16,16]{1,0:T(8,128)}) custom-call(s32[1]{0:T(128)} %bitcast.place_ref, f32[8,48,128]{2,1,0:T(8,128)S(1)} %all_to_all.5.parts_ref, bf16[240,3072]{1,0:T(8,128)(2,1)S(1)} %get-tuple-element.27.stack_ref), custom_call_target="tpu_custom_call" | custom-call | tf_op jit(solution)/shard_map/finish/pallas_call | solution.py:372
  (2 shorter events, 0.0 us)
Async XLA Ops:
  2.0 16.3 %collective-permute-start = (f32[54,8,128]{2,1,0:T(8,128)S(1)}, f32[54,8,128]{2,1,0:T(8,128)S(1)}, u32[]{:S(2)}, u32[]{:S(2)}) collective-permute-start(f32[54,8,128]{2,1,0:T(8,128)S(1)} %get-tuple-element.23), channel_id=1, source_target_pairs={{0,3},{1,2},{2,1},{3,0},{4,7},{5,6},{6,5},{7,4},{8,11},{9,10},{10,... | collective-permute-start | bytes 663560 | tf_op jit(solution)/shard_map/ppermute | solution.py:405
  4.5 13.8 %collective-permute-start.4 = (f32[54,8,128]{2,1,0:T(8,128)S(1)}, f32[54,8,128]{2,1,0:T(8,128)S(1)}, u32[]{:S(2)}, u32[]{:S(2)}) collective-permute-start(f32[54,8,128]{2,1,0:T(8,128)S(1)} %get-tuple-element.25), channel_id=1, source_target_pairs={{0,1},{1,0},{2,3},{3,2},{4,5},{5,4},{6,7},{7,6},{8,9},{9,8},{10,11... | collective-permute-start | bytes 663560 | tf_op jit(solution)/shard_map/ppermute | solution.py:405
  5.2 7.8 %collective-permute-start.3 = (f32[384,128]{1,0:T(8,128)}, f32[384,128]{1,0:T(8,128)S(1)}, u32[]{:S(2)}, u32[]{:S(2)}) collective-permute-start(f32[384,128]{1,0:T(8,128)} %bitcast.22), channel_id=1, source_target_pairs={{4,8},{12,16},{20,24},{8,4},{16,12},{24,20},{5,9},{13,17},{21,25},... | collective-permute-start | bytes 589832 | tf_op jit(solution)/shard_map/ppermute | solution.py:35
  5.8 12.5 %collective-permute-start.1 = (f32[384,128]{1,0:T(8,128)}, f32[384,128]{1,0:T(8,128)S(1)}, u32[]{:S(2)}, u32[]{:S(2)}) collective-permute-start(f32[384,128]{1,0:T(8,128)} %bitcast.23), channel_id=1, source_target_pairs={{0,4},{8,12},{16,20},{24,28},{4,0},{12,8},{20,16},{28,24},{1,5},{9... | collective-permute-start | bytes 589832 | tf_op jit(solution)/shard_map/ppermute | solution.py:35
  10.2 8.1 %collective-permute-start.2 = (f32[48,8,128]{2,1,0:T(8,128)S(1)}, f32[48,8,128]{2,1,0:T(8,128)S(1)}, u32[]{:S(2)}, u32[]{:S(2)}) collective-permute-start(f32[48,8,128]{2,1,0:T(8,128)S(1)} %get-tuple-element.24), channel_id=1, source_target_pairs={{0,2},{1,3},{2,0},{3,1},{4,6},{5,7},{6,4},{7,5},{8,10},{9,11},{10,... | collective-permute-start | bytes 589832 | tf_op jit(solution)/shard_map/ppermute | solution.py:405
  19.3 3.3 %collective-permute-start.7 = (f32[48,128]{1,0:T(8,128)S(1)}, f32[48,128]{1,0:T(8,128)S(1)}, u32[]{:S(2)}, u32[]{:S(2)}) collective-permute-start(f32[48,128]{1,0:T(8,128)S(1)} %get-tuple-element.26), channel_id=1, source_target_pairs={{0,3},{1,2},{2,1},{3,0},{4,7},{5,6},{6,5},{7,4},{8,11},{9,10},{10,... | collective-permute-start | bytes 73736 | tf_op jit(solution)/shard_map/ppermute | solution.py:300
  19.5 3.9 %collective-permute-start.6 = (f32[48,128]{1,0:T(8,128)S(1)}, f32[48,128]{1,0:T(8,128)S(1)}, u32[]{:S(2)}, u32[]{:S(2)}) collective-permute-start(f32[48,128]{1,0:T(8,128)S(1)} %get-tuple-element.26), channel_id=1, source_target_pairs={{0,2},{1,3},{2,0},{3,1},{4,6},{5,7},{6,4},{7,5},{8,10},{9,11},{10,... | collective-permute-start | bytes 73736 | tf_op jit(solution)/shard_map/ppermute | solution.py:300
  21.0 2.4 %collective-permute-start.5 = (f32[48,128]{1,0:T(8,128)S(1)}, f32[48,128]{1,0:T(8,128)S(1)}, u32[]{:S(2)}, u32[]{:S(2)}) collective-permute-start(f32[48,128]{1,0:T(8,128)S(1)} %get-tuple-element.26), channel_id=1, source_target_pairs={{0,1},{1,0},{2,3},{3,2},{4,5},{5,4},{6,7},{7,6},{8,9},{9,8},{10,11... | collective-permute-start | bytes 73736 | tf_op jit(solution)/shard_map/ppermute | solution.py:300

commit v8 on v7

--- a/solution.py
+++ b/solution.py
@@ -294,32 +294,39 @@
     )(place, slab, *kept(fields, applied, own, *got.values()))
 
 
-def exchange_sum(part, axis):
-    count = lax.axis_size(axis)
-    terms = [part] + [
-        lax.ppermute(part, axis, [(i, i ^ k) for i in range(count)]) for k in range(1, count)
-    ]
+def exchange(part, axes, stride, radix):
+    count = lax.axis_size(axes)
+    masks = [stride * k for k in range(1, radix)]
+    return [part] + [lax.ppermute(part, axes, [(i, i ^ m) for i in range(count)]) for m in masks]
+
+
+def pair_sum(terms):
     while len(terms) > 1:
         terms = [a + b for a, b in zip(terms[::2], terms[1::2])]
     return terms[0]
 
 
-def exchange(part, axis):
-    count = lax.axis_size(axis)
-    return lax.all_to_all(jnp.broadcast_to(part[None], (count,) + part.shape), axis, 0, 0)
+def exchange_all(part, axes, widest=8):
+    count = lax.axis_size(axes)
+    stride, terms = 1, [part]
+    while stride < count:
+        radix = min(widest, count // stride)
+        terms = exchange(pair_sum(terms), axes, stride, radix)
+        stride *= radix
+    return terms
 
 
 def finish_kernel(
-    row_count, place_ref, parts_ref, stack_ref, block_ref, coeffs_ref, upper_ref,
-    coeffs_scratch,
+    row_count, place_ref, stack_ref, *refs
 ):
+    *part_refs, block_ref, coeffs_ref, upper_ref, coeffs_scratch = refs
     block_cols = upper_ref.shape[0]
-    basis_cols = parts_ref.shape[2] // 2
+    basis_cols = part_refs[0].shape[1] // 2
     half = basis_cols // 2
     joined = basis_cols + block_cols
     lines = block_ref.shape[0] // block_cols
     lanes = block_ref.shape[1]
-    total = jnp.sum(parts_ref[...], axis=0) / row_count
+    total = pair_sum([ref[...] for ref in part_refs]) / row_count
     gram = jnp.concatenate((total[:half, :basis_cols], total[:half, basis_cols:]), axis=0)
     first = total[half:, :basis_cols]
     block_gram = total[half:, basis_cols:joined]
@@ -368,18 +375,18 @@
 
 def finish(place, parts, stack, row_count, block_cols, group_cols, lines):
     lanes = stack.shape[1] // lines
-    basis_cols = parts.shape[2] // 2
+    basis_cols = parts[0].shape[1] // 2
     return pl.pallas_call(
         functools.partial(finish_kernel, row_count),
         out_shape=(
             f32(block_cols * lines, lanes), f32(group_cols, block_cols), f32(block_cols, block_cols),
         ),
-        in_specs=[SMEM] + [VMEM] * 2,
+        in_specs=[SMEM] + [VMEM] * (1 + len(parts)),
         out_specs=(VMEM, VMEM, VMEM),
         scratch_shapes=[pltpu.VMEM((basis_cols, block_cols), jnp.float32)],
         compiler_params=SCRATCH,
         name="finish",
-    )(place, *kept(parts, stack))
+    )(place, *kept(stack, *parts))
 
 
 def shards(
@@ -409,7 +416,7 @@
         own.reshape(-1, lanes), comps,
     )
     stack, part = sums(place, slab, fields, applied, own, got, comps)
-    parts = exchange(exchange_sum(part, "basis"), "space")
+    parts = exchange_all(part, ("space", "basis"))
     block, coeffs, upper = finish(place, parts, stack, row_count, block_cols, group_cols, lines)
     return (block.reshape(x_block.shape), coeffs, upper)
 

time: 40.3 us -> 40.3 us (level)
  blocking collectives: 13.6 us -> 0 us
  starting transfers between devices: 10.5 us -> 19.8 us
  waiting for transfers between devices: 7.48 us -> 11.9 us
    all_to_all x1 -> x0, blocking collectives: 13.6 us -> none  [exchange(): lax.all_to_all(jnp.broadcast_to(part[None], (count,) + part.shape), axis,...]
    ppermute x3 -> x10, starting transfers between devices: 1.89 us -> 11.2 us  [exchange(): lax.ppermute(part, axes, [(i, i ^ m) for i in range(count)])]
    ppermute x3 -> x10, waiting for transfers between devices: 2.18 us -> 6.59 us  [exchange(): lax.ppermute(part, axes, [(i, i ^ m) for i in range(count)])]
  transfers between devices with their start and end apart: 8 -> 15, of which waited for: 3 -> 6; matrix products, arithmetic and copies ran while one was open for 0% -> 0% of each run, Pallas kernels for 4% -> 4%
where the time goes in v8:
time: 40.3 us; the launch traced here: 40.1 us
  starting transfers between devices  19.8 us (49%)
  waiting for transfers between devices  11.9 us (30%)
  Pallas kernels  7.06 us (18%)
  between operations  1.34 us (3%)
    ppermute x10, starting transfers between devices, exchange(): lax.ppermute(part, axes, [(i, i ^ m) for i in range(count)])  11.2 us
    ppermute x10, waiting for transfers between devices, exchange(): lax.ppermute(part, axes, [(i, i ^ m) for i in range(count)])  6.59 us
    ppermute x2, waiting for transfers between devices, swap(): return lax.ppermute(values, axis, pairs + [(j, i) for i, j in pairs])  5.29 us
    ppermute x2, starting transfers between devices, swap(): return lax.ppermute(values, axis, pairs + [(j, i) for i, j in pairs])  5 us
    ppermute x3, starting transfers between devices, shards(): lax.ppermute(pieces[name - 1], 'basis', [(i, i ^ name) for i in range(cou...  3.65 us
    pallas_call x1, Pallas kernels, finish(): pl.pallas_call(functools.partial(finish_kernel, row_count), out_shape=(f3...  3.01 us
    pallas_call x1, Pallas kernels, ahead(): pl.pallas_call(ahead_kernel, out_shape=(near(rows, comps * comps * stride...  1.65 us
    pallas_call x1, Pallas kernels, pack(): pl.pallas_call(functools.partial(pack_kernel, comps), out_shape=(*pieces,...  1.36 us
  transfers between devices with their start and end apart: 15, of which 6 were waited for; matrix products, arithmetic and copies ran while one was open for 0% of the time, Pallas kernels for 4%

profile of v8, /device:TPU:0, one launch (start us, length us, event | category | flops | bytes accessed | tf_op | source)
XLA Modules:
  0.0 40.1 jit_solution(15145737357719331695)
XLA Ops:
  0.6 1.4 %pack.1 = (f32[48,8,128]{2,1,0:T(8,128)S(1)}, f32[54,8,128]{2,1,0:T(8,128)S(1)}, f32[48,8,128]{2,1,0:T(8,128)S(1)}, f32[54,8,128]{2,1,0:T(8,128)S(1)}, f32[384,128]{1,0:T(8,128)S(1)}, /*index=5*/s32[8,128]{1,0:T(8,128)S(1)}) custom-call(s32[1]{0:T(128)} %bitcast.place_ref, f32[48,4,8,128]{3,2,1,0:T(8,128)} %bitcast.20, f32[384,128]{1,0:T(8,128)} %bitcast.21, ...), custom_call_target="tpu_custom_call" | custom-call | tf_op jit(solution)/shard_map/pack/pallas_call | solution.py:85
  2.0 2.5 %collective-permute-start = (f32[54,8,128]{2,1,0:T(8,128)S(1)}, f32[54,8,128]{2,1,0:T(8,128)S(1)}, u32[]{:S(2)}, u32[]{:S(2)}) collective-permute-start(f32[54,8,128]{2,1,0:T(8,128)S(1)} %get-tuple-element.23), channel_id=1, source_target_pairs={{0,3},{1,2},{2,1},{3,0},{4,7},{5,6},{6,5},{7,4},{8,11},{9,10},{10,... | collective-permute-start | bytes 663560 | tf_op jit(solution)/shard_map/ppermute | solution.py:412
  4.5 0.7 %collective-permute-start.4 = (f32[54,8,128]{2,1,0:T(8,128)S(1)}, f32[54,8,128]{2,1,0:T(8,128)S(1)}, u32[]{:S(2)}, u32[]{:S(2)}) collective-permute-start(f32[54,8,128]{2,1,0:T(8,128)S(1)} %get-tuple-element.25), channel_id=1, source_target_pairs={{0,1},{1,0},{2,3},{3,2},{4,5},{5,4},{6,7},{7,6},{8,9},{9,8},{10,11... | collective-permute-start | bytes 663560 | tf_op jit(solution)/shard_map/ppermute | solution.py:412
  5.2 0.7 %collective-permute-start.3 = (f32[384,128]{1,0:T(8,128)}, f32[384,128]{1,0:T(8,128)S(1)}, u32[]{:S(2)}, u32[]{:S(2)}) collective-permute-start(f32[384,128]{1,0:T(8,128)} %bitcast.22), channel_id=1, source_target_pairs={{4,8},{12,16},{20,24},{8,4},{16,12},{24,20},{5,9},{13,17},{21,25},... | collective-permute-start | bytes 589832 | tf_op jit(solution)/shard_map/ppermute | solution.py:35
  5.8 4.3 %collective-permute-start.1 = (f32[384,128]{1,0:T(8,128)}, f32[384,128]{1,0:T(8,128)S(1)}, u32[]{:S(2)}, u32[]{:S(2)}) collective-permute-start(f32[384,128]{1,0:T(8,128)} %bitcast.23), channel_id=1, source_target_pairs={{0,4},{8,12},{16,20},{24,28},{4,0},{12,8},{20,16},{28,24},{1,5},{9... | collective-permute-start | bytes 589832 | tf_op jit(solution)/shard_map/ppermute | solution.py:35
  10.2 0.5 %collective-permute-start.2 = (f32[48,8,128]{2,1,0:T(8,128)S(1)}, f32[48,8,128]{2,1,0:T(8,128)S(1)}, u32[]{:S(2)}, u32[]{:S(2)}) collective-permute-start(f32[48,8,128]{2,1,0:T(8,128)S(1)} %get-tuple-element.24), channel_id=1, source_target_pairs={{0,2},{1,3},{2,0},{3,1},{4,6},{5,7},{6,4},{7,5},{8,10},{9,11},{10,... | collective-permute-start | bytes 589832 | tf_op jit(solution)/shard_map/ppermute | solution.py:412
  11.3 1.7 %ahead.1 = (f32[8,72,128]{2,1,0:T(8,128)S(1)}, f32[24,16,128]{2,1,0:T(8,128)S(1)}, bf16[48,3072]{1,0:T(8,128)(2,1)S(1)}) custom-call(s32[1]{0:T(128)S(6)} %copy.14.sample_ref, f32[1024]{0:T(1024)} %refs_0_.1, f32[1024]{0:T(1024)} %refs_1_.1, f32[3,3,8,7]{3,2,1,0:T(8,128)} %bitcast.24, f32[3,3,8,7]{3,2,1,0:T(8,128)} %bitcast.25, f32[3,8]{1,0:T(4,128)} %bitcast.27, ...), custom_call_target="tpu_custom_call" | custom-call | tf_op jit(solution)/shard_map/ahead/pallas_call | solution.py:184
  13.0 0.0 collective-permute-done.3.refs_3_
  13.0 5.3 %collective-permute-done.1.refs_1_ = f32[384,128]{1,0:T(8,128)S(1)} collective-permute-done((f32[384,128]{1,0:T(8,128)}, f32[384,128]{1,0:T(8,128)S(1)}, u32[]{:S(2)}, u32[]{:S(2)}) %collective-permute-start.1) | collective-permute-done | bytes 196640 | tf_op jit(solution)/shard_map/ppermute | solution.py:35
  18.3 0.0 collective-permute-done.2
  18.3 0.0 collective-permute-done
  18.3 0.0 collective-permute-done.4
  18.3 1.0 %sums.1 = (bf16[240,3072]{1,0:T(8,128)(2,1)S(1)}, f32[48,128]{1,0:T(8,128)S(1)}) custom-call(s32[1]{0:T(128)} %bitcast.place_ref, s32[1]{0:T(128)} %bitcast.1.slab_ref, f32[8,72,128]{2,1,0:T(8,128)S(1)} %get-tuple-element.20.fields_ref, f32[24,16,128]{2,1,0:T(8,128)S(1)} %get-tuple-element.21.applied_ref, bf16[48,3072]{1,0:T(8,128)(2,1)S(1)} %get-tuple-element.22.own_ref, ...), custom_call_target="tpu_custom_call" | custom-call | tf_op jit(solution)/shard_map/sums/pallas_call | solution.py:284
  19.3 2.0 %collective-permute-start.11 = (f32[48,128]{1,0:T(8,128)S(1)}, f32[48,128]{1,0:T(8,128)S(1)}, u32[]{:S(2)}, u32[]{:S(2)}) collective-permute-start(f32[48,128]{1,0:T(8,128)S(1)} %get-tuple-element.27), channel_id=1, source_target_pairs={{0,7},{1,6},{2,5},{3,4},{4,3},{5,2},{6,1},{7,0},{8,15},{9,14},{10,... | collective-permute-start | bytes 73736 | tf_op jit(solution)/shard_map/ppermute | solution.py:300
  21.3 0.6 %collective-permute-start.10 = (f32[48,128]{1,0:T(8,128)S(1)}, f32[48,128]{1,0:T(8,128)S(1)}, u32[]{:S(2)}, u32[]{:S(2)}) collective-permute-start(f32[48,128]{1,0:T(8,128)S(1)} %get-tuple-element.27), channel_id=1, source_target_pairs={{0,6},{1,7},{2,4},{3,5},{4,2},{5,3},{6,0},{7,1},{8,14},{9,15},{10,... | collective-permute-start | bytes 73736 | tf_op jit(solution)/shard_map/ppermute | solution.py:300
  21.9 2.2 %collective-permute-start.9 = (f32[48,128]{1,0:T(8,128)S(1)}, f32[48,128]{1,0:T(8,128)S(1)}, u32[]{:S(2)}, u32[]{:S(2)}) collective-permute-start(f32[48,128]{1,0:T(8,128)S(1)} %get-tuple-element.27), channel_id=1, source_target_pairs={{0,5},{1,4},{2,7},{3,6},{4,1},{5,0},{6,3},{7,2},{8,13},{9,12},{10,... | collective-permute-start | bytes 73736 | tf_op jit(solution)/shard_map/ppermute | solution.py:300
  24.1 0.2 collective-permute-start.8
  24.3 0.4 %collective-permute-start.7 = (f32[48,128]{1,0:T(8,128)S(1)}, f32[48,128]{1,0:T(8,128)S(1)}, u32[]{:S(2)}, u32[]{:S(2)}) collective-permute-start(f32[48,128]{1,0:T(8,128)S(1)} %get-tuple-element.27), channel_id=1, source_target_pairs={{0,3},{1,2},{2,1},{3,0},{4,7},{5,6},{6,5},{7,4},{8,11},{9,10},{10,... | collective-permute-start | bytes 73736 | tf_op jit(solution)/shard_map/ppermute | solution.py:300
  24.7 0.0 collective-permute-done.11
  24.8 1.3 %collective-permute-start.6 = (f32[48,128]{1,0:T(8,128)S(1)}, f32[48,128]{1,0:T(8,128)S(1)}, u32[]{:S(2)}, u32[]{:S(2)}) collective-permute-start(f32[48,128]{1,0:T(8,128)S(1)} %get-tuple-element.27), channel_id=1, source_target_pairs={{0,2},{1,3},{2,0},{3,1},{4,6},{5,7},{6,4},{7,5},{8,10},{9,11},{10,... | collective-permute-start | bytes 73736 | tf_op jit(solution)/shard_map/ppermute | solution.py:300
  26.0 0.2 collective-permute-done.10
  26.2 0.0 collective-permute-start.5
  26.2 0.0 collective-permute-done.9
  26.2 1.7 %collective-permute-done.8 = f32[48,128]{1,0:T(8,128)S(1)} collective-permute-done((f32[48,128]{1,0:T(8,128)S(1)}, f32[48,128]{1,0:T(8,128)S(1)}, u32[]{:S(2)}, u32[]{:S(2)}) %collective-permute-start.8) | collective-permute-done | bytes 24608 | tf_op jit(solution)/shard_map/ppermute | solution.py:300
  27.9 0.0 collective-permute-done.7
  27.9 0.6 %collective-permute-done.6 = f32[48,128]{1,0:T(8,128)S(1)} collective-permute-done((f32[48,128]{1,0:T(8,128)S(1)}, f32[48,128]{1,0:T(8,128)S(1)}, u32[]{:S(2)}, u32[]{:S(2)}) %collective-permute-start.6) | collective-permute-done | bytes 24608 | tf_op jit(solution)/shard_map/ppermute | solution.py:300
  28.6 0.0 collective-permute-done.5
  28.6 3.8 %collective-permute-start.14 = (f32[48,128]{1,0:T(8,128)S(1)}, f32[48,128]{1,0:T(8,128)S(1)}, u32[]{:S(2)}, u32[]{:S(2)}) collective-permute-start(f32[48,128]{1,0:T(8,128)S(1)} %add_add_fusion.refs_0_), channel_id=1, source_target_pairs={{0,24},{1,25},{2,26},{3,27},{4,28},{5,29},{6,30},{7,31},{8,16},{9,... | collective-permute-start | bytes 73736 | tf_op jit(solution)/shard_map/ppermute | solution.py:300
  32.4 0.0 collective-permute-start.13
  32.4 0.7 %collective-permute-start.12 = (f32[48,128]{1,0:T(8,128)S(1)}, f32[48,128]{1,0:T(8,128)S(1)}, u32[]{:S(2)}, u32[]{:S(2)}) collective-permute-start(f32[48,128]{1,0:T(8,128)S(1)} %add_add_fusion.refs_0_), channel_id=1, source_target_pairs={{0,8},{1,9},{2,10},{3,11},{4,12},{5,13},{6,14},{7,15},{8,0},{9,1},... | collective-permute-start | bytes 73736 | tf_op jit(solution)/shard_map/ppermute | solution.py:300
  33.1 1.2 %collective-permute-done.14.refs_3_ = f32[48,128]{1,0:T(8,128)S(1)} collective-permute-done((f32[48,128]{1,0:T(8,128)S(1)}, f32[48,128]{1,0:T(8,128)S(1)}, u32[]{:S(2)}, u32[]{:S(2)}) %collective-permute-start.14) | collective-permute-done | bytes 24608 | tf_op jit(solution)/shard_map/ppermute | solution.py:300
  34.3 2.8 %collective-permute-done.13.refs_2_ = f32[48,128]{1,0:T(8,128)S(1)} collective-permute-done((f32[48,128]{1,0:T(8,128)S(1)}, f32[48,128]{1,0:T(8,128)S(1)}, u32[]{:S(2)}, u32[]{:S(2)}) %collective-permute-start.13) | collective-permute-done | bytes 24608 | tf_op jit(solution)/shard_map/ppermute | solution.py:300
  37.1 0.0 collective-permute-done.12.refs_1_
  37.1 3.0 %finish.1 = (f32[384,128]{1,0:T(8,128)}, f32[16,16]{1,0:T(8,128)}, f32[16,16]{1,0:T(8,128)}) custom-call(s32[1]{0:T(128)} %bitcast.place_ref, bf16[240,3072]{1,0:T(8,128)(2,1)S(1)} %get-tuple-element.26.stack_ref, f32[48,128]{1,0:T(8,128)S(1)} %add_add_fusion.refs_0_, f32[48,128]{1,0:T(8,128)S(1)} %collective-permute-done.12.refs_1_, ...), custom_call_target="tpu_custom_call" | custom-call | tf_op jit(solution)/shard_map/finish/pallas_call | solution.py:379
  (1 shorter events, 0.0 us)
Async XLA Ops:
  2.0 16.3 %collective-permute-start = (f32[54,8,128]{2,1,0:T(8,128)S(1)}, f32[54,8,128]{2,1,0:T(8,128)S(1)}, u32[]{:S(2)}, u32[]{:S(2)}) collective-permute-start(f32[54,8,128]{2,1,0:T(8,128)S(1)} %get-tuple-element.23), channel_id=1, source_target_pairs={{0,3},{1,2},{2,1},{3,0},{4,7},{5,6},{6,5},{7,4},{8,11},{9,10},{10,... | collective-permute-start | bytes 663560 | tf_op jit(solution)/shard_map/ppermute | solution.py:412
  4.5 13.8 %collective-permute-start.4 = (f32[54,8,128]{2,1,0:T(8,128)S(1)}, f32[54,8,128]{2,1,0:T(8,128)S(1)}, u32[]{:S(2)}, u32[]{:S(2)}) collective-permute-start(f32[54,8,128]{2,1,0:T(8,128)S(1)} %get-tuple-element.25), channel_id=1, source_target_pairs={{0,1},{1,0},{2,3},{3,2},{4,5},{5,4},{6,7},{7,6},{8,9},{9,8},{10,11... | collective-permute-start | bytes 663560 | tf_op jit(solution)/shard_map/ppermute | solution.py:412
  5.2 7.8 %collective-permute-start.3 = (f32[384,128]{1,0:T(8,128)}, f32[384,128]{1,0:T(8,128)S(1)}, u32[]{:S(2)}, u32[]{:S(2)}) collective-permute-start(f32[384,128]{1,0:T(8,128)} %bitcast.22), channel_id=1, source_target_pairs={{4,8},{12,16},{20,24},{8,4},{16,12},{24,20},{5,9},{13,17},{21,25},... | collective-permute-start | bytes 589832 | tf_op jit(solution)/shard_map/ppermute | solution.py:35
  5.8 12.5 %collective-permute-start.1 = (f32[384,128]{1,0:T(8,128)}, f32[384,128]{1,0:T(8,128)S(1)}, u32[]{:S(2)}, u32[]{:S(2)}) collective-permute-start(f32[384,128]{1,0:T(8,128)} %bitcast.23), channel_id=1, source_target_pairs={{0,4},{8,12},{16,20},{24,28},{4,0},{12,8},{20,16},{28,24},{1,5},{9... | collective-permute-start | bytes 589832 | tf_op jit(solution)/shard_map/ppermute | solution.py:35
  10.2 8.1 %collective-permute-start.2 = (f32[48,8,128]{2,1,0:T(8,128)S(1)}, f32[48,8,128]{2,1,0:T(8,128)S(1)}, u32[]{:S(2)}, u32[]{:S(2)}) collective-permute-start(f32[48,8,128]{2,1,0:T(8,128)S(1)} %get-tuple-element.24), channel_id=1, source_target_pairs={{0,2},{1,3},{2,0},{3,1},{4,6},{5,7},{6,4},{7,5},{8,10},{9,11},{10,... | collective-permute-start | bytes 589832 | tf_op jit(solution)/shard_map/ppermute | solution.py:412
  19.3 5.4 %collective-permute-start.11 = (f32[48,128]{1,0:T(8,128)S(1)}, f32[48,128]{1,0:T(8,128)S(1)}, u32[]{:S(2)}, u32[]{:S(2)}) collective-permute-start(f32[48,128]{1,0:T(8,128)S(1)} %get-tuple-element.27), channel_id=1, source_target_pairs={{0,7},{1,6},{2,5},{3,4},{4,3},{5,2},{6,1},{7,0},{8,15},{9,14},{10,... | collective-permute-start | bytes 73736 | tf_op jit(solution)/shard_map/ppermute | solution.py:300
  21.3 4.9 %collective-permute-start.10 = (f32[48,128]{1,0:T(8,128)S(1)}, f32[48,128]{1,0:T(8,128)S(1)}, u32[]{:S(2)}, u32[]{:S(2)}) collective-permute-start(f32[48,128]{1,0:T(8,128)S(1)} %get-tuple-element.27), channel_id=1, source_target_pairs={{0,6},{1,7},{2,4},{3,5},{4,2},{5,3},{6,0},{7,1},{8,14},{9,15},{10,... | collective-permute-start | bytes 73736 | tf_op jit(solution)/shard_map/ppermute | solution.py:300
  21.9 4.3 %collective-permute-start.9 = (f32[48,128]{1,0:T(8,128)S(1)}, f32[48,128]{1,0:T(8,128)S(1)}, u32[]{:S(2)}, u32[]{:S(2)}) collective-permute-start(f32[48,128]{1,0:T(8,128)S(1)} %get-tuple-element.27), channel_id=1, source_target_pairs={{0,5},{1,4},{2,7},{3,6},{4,1},{5,0},{6,3},{7,2},{8,13},{9,12},{10,... | collective-permute-start | bytes 73736 | tf_op jit(solution)/shard_map/ppermute | solution.py:300
  24.1 3.8 %collective-permute-start.8 = (f32[48,128]{1,0:T(8,128)S(1)}, f32[48,128]{1,0:T(8,128)S(1)}, u32[]{:S(2)}, u32[]{:S(2)}) collective-permute-start(f32[48,128]{1,0:T(8,128)S(1)} %get-tuple-element.27), channel_id=1, source_target_pairs={{0,4},{1,5},{2,6},{3,7},{4,0},{5,1},{6,2},{7,3},{8,12},{9,13},{10,... | collective-permute-start | bytes 73736 | tf_op jit(solution)/shard_map/ppermute | solution.py:300
  24.3 3.6 %collective-permute-start.7 = (f32[48,128]{1,0:T(8,128)S(1)}, f32[48,128]{1,0:T(8,128)S(1)}, u32[]{:S(2)}, u32[]{:S(2)}) collective-permute-start(f32[48,128]{1,0:T(8,128)S(1)} %get-tuple-element.27), channel_id=1, source_target_pairs={{0,3},{1,2},{2,1},{3,0},{4,7},{5,6},{6,5},{7,4},{8,11},{9,10},{10,... | collective-permute-start | bytes 73736 | tf_op jit(solution)/shard_map/ppermute | solution.py:300
  24.8 3.8 %collective-permute-start.6 = (f32[48,128]{1,0:T(8,128)S(1)}, f32[48,128]{1,0:T(8,128)S(1)}, u32[]{:S(2)}, u32[]{:S(2)}) collective-permute-start(f32[48,128]{1,0:T(8,128)S(1)} %get-tuple-element.27), channel_id=1, source_target_pairs={{0,2},{1,3},{2,0},{3,1},{4,6},{5,7},{6,4},{7,5},{8,10},{9,11},{10,... | collective-permute-start | bytes 73736 | tf_op jit(solution)/shard_map/ppermute | solution.py:300
  26.2 2.3 %collective-permute-start.5 = (f32[48,128]{1,0:T(8,128)S(1)}, f32[48,128]{1,0:T(8,128)S(1)}, u32[]{:S(2)}, u32[]{:S(2)}) collective-permute-start(f32[48,128]{1,0:T(8,128)S(1)} %get-tuple-element.27), channel_id=1, source_target_pairs={{0,1},{1,0},{2,3},{3,2},{4,5},{5,4},{6,7},{7,6},{8,9},{9,8},{10,11... | collective-permute-start | bytes 73736 | tf_op jit(solution)/shard_map/ppermute | solution.py:300
  28.6 5.7 %collective-permute-start.14 = (f32[48,128]{1,0:T(8,128)S(1)}, f32[48,128]{1,0:T(8,128)S(1)}, u32[]{:S(2)}, u32[]{:S(2)}) collective-permute-start(f32[48,128]{1,0:T(8,128)S(1)} %add_add_fusion.refs_0_), channel_id=1, source_target_pairs={{0,24},{1,25},{2,26},{3,27},{4,28},{5,29},{6,30},{7,31},{8,16},{9,... | collective-permute-start | bytes 73736 | tf_op jit(solution)/shard_map/ppermute | solution.py:300
  32.4 4.7 %collective-permute-start.13 = (f32[48,128]{1,0:T(8,128)S(1)}, f32[48,128]{1,0:T(8,128)S(1)}, u32[]{:S(2)}, u32[]{:S(2)}) collective-permute-start(f32[48,128]{1,0:T(8,128)S(1)} %add_add_fusion.refs_0_), channel_id=1, source_target_pairs={{0,16},{1,17},{2,18},{3,19},{4,20},{5,21},{6,22},{7,23},{8,24},{9,... | collective-permute-start | bytes 73736 | tf_op jit(solution)/shard_map/ppermute | solution.py:300
  32.4 4.7 %collective-permute-start.12 = (f32[48,128]{1,0:T(8,128)S(1)}, f32[48,128]{1,0:T(8,128)S(1)}, u32[]{:S(2)}, u32[]{:S(2)}) collective-permute-start(f32[48,128]{1,0:T(8,128)S(1)} %add_add_fusion.refs_0_), channel_id=1, source_target_pairs={{0,8},{1,9},{2,10},{3,11},{4,12},{5,13},{6,14},{7,15},{8,0},{9,1},... | collective-permute-start | bytes 73736 | tf_op jit(solution)/shard_map/ppermute | solution.py:300

commit v9 on v7

--- a/solution.py
+++ b/solution.py
@@ -11,6 +11,7 @@
 VMEM = pl.BlockSpec(memory_space=pltpu.VMEM)
 SMEM = pl.BlockSpec(memory_space=pltpu.SMEM)
 HBM = pl.BlockSpec(memory_space=pltpu.HBM)
+EARLY = pl.CostEstimate(flops=10**9, bytes_accessed=10**6, transcendentals=0)
 SCRATCH = pltpu.CompilerParams(vmem_limit_bytes=8 * 2**20)
 
 
@@ -199,10 +200,79 @@
     )(sample, *tables, *kept(material, x_rows, own))
 
 
+def side_terms(field_row, swapped, side, out, comp, comps):
+    stride = field_row.shape[0] // (comps * comps)
+    begin = (out * comps + comp) * stride
+    below, above = field_row[begin + 1 : begin + 2], field_row[begin + 2 : begin + 3]
+    other = (below, above) if side == "even" else (above, below)
+    return jnp.where(swapped, *other)
+
+
+def side_kernel(comps, side, slab_ref, fields_ref, applied_ref, halo_ref, out_ref):
+    lines, block_cols, _ = applied_ref.shape
+    rows = lines // comps
+    swapped = slab_ref[0] % 2 == 1
+    for row in range(rows):
+        field_row = fields_ref[row]
+        views = [line_of(halo_ref, comp, row, comps, rows, block_cols) for comp in range(comps)]
+        for out in range(comps):
+            total = applied_ref[out * rows + row]
+            for comp, view in enumerate(views):
+                total = total + side_terms(field_row, swapped, side, out, comp, comps) * view
+            out_ref[out * rows + row] = total
+
+
+def add_side(slab, fields, applied, halo, comps, side):
+    return pl.pallas_call(
+        functools.partial(side_kernel, comps, side),
+        out_shape=near(*applied.shape),
+        in_specs=[SMEM] + [VMEM] * 3,
+        out_specs=VMEM,
+        compiler_params=SCRATCH,
+        cost_estimate=EARLY,
+        name="side",
+    )(slab, *kept(fields, applied, halo))
+
+
+def fold(total, basis_cols, block_cols, lanes):
+    half = basis_cols // 2
+    row = lax.broadcasted_iota(jnp.int32, (half, half), 0)
+    column = lax.broadcasted_iota(jnp.int32, (half, half), 1)
+    last = total[half:basis_cols, half:basis_cols]
+    shared = jnp.where(row >= column, total[:half, :half], last)
+    diagonal = jnp.sum(jnp.where(row == column, last, 0.0), axis=1, keepdims=True)
+    below = total[basis_cols:]
+    first = jnp.concatenate((below[:, :half], below[:, half:basis_cols]), axis=0)
+    rest = jnp.zeros((half - block_cols, block_cols), jnp.float32)
+    block = jnp.concatenate((below[:, basis_cols:], rest), axis=0)
+    pad = jnp.zeros((half, lanes - 3 * half - block_cols - 1), jnp.float32)
+    return jnp.concatenate(
+        (shared, total[:half, half:basis_cols], first, block, diagonal, pad), axis=1
+    )
+
+
+def unfold(folded, block_cols):
+    half = folded.shape[0]
+    row = lax.broadcasted_iota(jnp.int32, (half, half), 0)
+    column = lax.broadcasted_iota(jnp.int32, (half, half), 1)
+    shared, across = folded[:, :half], folded[:, half : 2 * half]
+    turned = shared.T
+    start = jnp.where(row >= column, shared, turned)
+    end = jnp.where(row < column, shared, turned)
+    diagonal = folded[:, 3 * half + block_cols : 3 * half + block_cols + 1]
+    end = jnp.where(row == column, diagonal, end)
+    gram = jnp.concatenate(
+        (jnp.concatenate((start, across), axis=1), jnp.concatenate((across.T, end), axis=1)), axis=0
+    )
+    first = folded[:, 2 * half : 3 * half]
+    first = jnp.concatenate((first[:block_cols], first[block_cols : 2 * block_cols]), axis=1)
+    return gram, first, folded[:block_cols, 3 * half : 3 * half + block_cols]
+
+
 def sums_kernel(comps, names, edge_ks, place_ref, slab_ref, fields_ref, applied_ref, own_ref, *refs):
     *refs, stack_ref, sums_ref = refs
     got = dict(zip(names, refs))
-    piece_refs = [got[k] for k in range(1, len(got) - 1)]
+    piece_refs = [got[k] for k in range(1, len(got))]
     lines, block_cols, lanes = applied_ref.shape
     rows = lines // comps
     stride = fields_ref.shape[1] // (comps * comps)
@@ -237,27 +307,20 @@
         return result
 
     for row in range(rows):
+        field_row = fields_ref[row]
         totals = [applied_ref[out * rows + row] for out in range(comps)]
         for comp in range(comps):
-            views = {
-                name: line_of(got[name], comp, row, comps, rows, block_cols)
-                for name in ("even", "odd")
-            }
+            views = {}
             if row == 0:
                 views[3] = edge(comp, -1)
             if row == rows - 1:
                 views[4] = edge(comp, 1)
+            side = line_of(got["even"], comp, row, comps, rows, block_cols)
             for out in range(comps):
-                entries = fields_ref[row, pl.ds((out * comps + comp) * stride, stride), :]
-                below, above = entries[1:2], entries[2:3]
-                chosen = {
-                    "even": jnp.where(swapped, below, above),
-                    "odd": jnp.where(swapped, above, below),
-                    3: entries[3:4],
-                    4: entries[4:5],
-                }
-                for name, view in views.items():
-                    totals[out] = totals[out] + chosen[name] * view
+                entry = (out * comps + comp) * stride
+                totals[out] += side_terms(field_row, swapped, "even", out, comp, comps) * side
+                for offset, view in views.items():
+                    totals[out] += field_row[entry + offset : entry + offset + 1] * view
         for out in range(comps):
             store(basis_cols, out * rows + row, totals[out])
 
@@ -267,17 +330,11 @@
     )
     wide = products[:joined] + products[joined : 2 * joined] + products[2 * joined :]
     total = wide[:, :joined] + wide[:, joined : 2 * joined] + wide[:, 2 * joined :]
-    half = basis_cols // 2
-    sums_ref[pl.ds(0, half), :] = jnp.concatenate(
-        (total[:half, :basis_cols], total[half:basis_cols, :basis_cols]), axis=1
-    )
-    sums_ref[pl.ds(half, block_cols), :] = jnp.concatenate(
-        (total[basis_cols:], jnp.zeros((block_cols, sums_ref.shape[1] - joined), jnp.float32)), axis=1
-    )
+    sums_ref[...] = fold(total, basis_cols, block_cols, sums_ref.shape[1])
 
 
 def sums(place, slab, fields, applied, own, got, comps):
-    count = len(got) - 1
+    count = len(got)
     lines, block_cols, lanes = applied.shape
     basis_cols = count * (own.shape[0] // 3)
     joined = basis_cols + block_cols
@@ -285,7 +342,7 @@
         functools.partial(sums_kernel, comps, tuple(got), partners(count)[1]),
         out_shape=(
             near(3 * joined, lines * lanes, dtype=jnp.bfloat16),
-            near(basis_cols // 2 + block_cols, 2 * basis_cols),
+            near(basis_cols // 2, 2 * basis_cols),
         ),
         in_specs=[SMEM] * 2 + [VMEM] * (3 + len(got)),
         out_specs=(VMEM, VMEM),
@@ -315,14 +372,11 @@
 ):
     block_cols = upper_ref.shape[0]
     basis_cols = parts_ref.shape[2] // 2
-    half = basis_cols // 2
     joined = basis_cols + block_cols
     lines = block_ref.shape[0] // block_cols
     lanes = block_ref.shape[1]
     total = jnp.sum(parts_ref[...], axis=0) / row_count
-    gram = jnp.concatenate((total[:half, :basis_cols], total[:half, basis_cols:]), axis=0)
-    first = total[half:, :basis_cols]
-    block_gram = total[half:, basis_cols:joined]
+    gram, first, block_gram = unfold(total, block_cols)
 
     def times(left, right, right_dim=0):
         return lax.dot_general(
@@ -396,7 +450,7 @@
     x_far = x_block.reshape(block_cols * lines, lanes)
     own, *pieces, x_rows, material = pack(place, basis, x_far, material.reshape(rows, lanes), block_cols)
     got = {}
-    for name in (3, "even", 2, "odd", 1):
+    for name in ("odd", 3, "even", 2, 1):
         if name == "even":
             got[name] = swap(x_far, "space", 0)
         elif name == "odd":
@@ -408,6 +462,7 @@
         sample, velocities, shifts, k0_blocks, ke_blocks, k0_diag, mass, material, x_rows,
         own.reshape(-1, lanes), comps,
     )
+    applied = add_side(slab, fields, applied, got.pop("odd"), comps, "odd")
     stack, part = sums(place, slab, fields, applied, own, got, comps)
     parts = exchange(exchange_sum(part, "basis"), "space")
     block, coeffs, upper = finish(place, parts, stack, row_count, block_cols, group_cols, lines)

time: 40.3 us -> 39.9 us (0.990)
  waiting for transfers between devices: 7.48 us -> 5.66 us
  blocking collectives: 13.6 us -> 14.8 us
    ppermute x2, waiting for transfers between devices: 5.29 us -> 2.35 us  [swap(): return lax.ppermute(values, axis, pairs + [(j, i) for i, j in pairs])]
    ppermute x3, waiting for transfers between devices: 0.01 us -> 1.26 us  [shards(): lax.ppermute(pieces[name - 1], 'basis', [(i, i ^ name) for i in range(cou...]
    all_to_all x1, blocking collectives: 13.6 us -> 14.8 us  [exchange(): lax.all_to_all(jnp.broadcast_to(part[None], (count,) + part.shape), axis,...]
  transfers between devices with their start and end apart: 8 -> 8, of which waited for: 3 -> 4; matrix products, arithmetic and copies ran while one was open for 0% -> 0% of each run, Pallas kernels for 4% -> 8%
where the time goes in v9:
time: 39.9 us; the launch traced here: 39.6 us
  blocking collectives  14.8 us (37%)
  starting transfers between devices  10.5 us (26%)
  Pallas kernels  7.33 us (18%)
  waiting for transfers between devices  5.66 us (14%)
  between operations  1.36 us (3%)
    all_to_all x1, blocking collectives, exchange(): lax.all_to_all(jnp.broadcast_to(part[None], (count,) + part.shape), axis,...  14.8 us
    ppermute x2, starting transfers between devices, swap(): return lax.ppermute(values, axis, pairs + [(j, i) for i, j in pairs])  4.95 us
    ppermute x3, starting transfers between devices, shards(): lax.ppermute(pieces[name - 1], 'basis', [(i, i ^ name) for i in range(cou...  3.65 us
    pallas_call x1, Pallas kernels, finish(): pl.pallas_call(functools.partial(finish_kernel, row_count), out_shape=(f3...  3.12 us
    ppermute x2, waiting for transfers between devices, swap(): return lax.ppermute(values, axis, pairs + [(j, i) for i, j in pairs])  2.35 us
    ppermute x3, waiting for transfers between devices, exchange_sum(): lax.ppermute(part, axis, [(i, i ^ k) for i in range(count)])  2.05 us
    ppermute x3, starting transfers between devices, exchange_sum(): lax.ppermute(part, axis, [(i, i ^ k) for i in range(count)])  1.92 us
    pallas_call x1, Pallas kernels, ahead(): pl.pallas_call(ahead_kernel, out_shape=(near(rows, comps * comps * stride...  1.66 us
  transfers between devices with their start and end apart: 8, of which 4 were waited for; matrix products, arithmetic and copies ran while one was open for 0% of the time, Pallas kernels for 8%

profile of v9, /device:TPU:0, one launch (start us, length us, event | category | flops | bytes accessed | tf_op | source)
XLA Modules:
  0.0 39.6 jit_solution(11326004027308098193)
XLA Ops:
  0.6 0.7 %collective-permute-start = (f32[384,128]{1,0:T(8,128)}, f32[384,128]{1,0:T(8,128)S(1)}, u32[]{:S(2)}, u32[]{:S(2)}) collective-permute-start(f32[384,128]{1,0:T(8,128)} %bitcast.21), channel_id=1, source_target_pairs={{4,8},{12,16},{20,24},{8,4},{16,12},{24,20},{5,9},{13,17},{21,25},... | collective-permute-start | bytes 589832 | tf_op jit(solution)/shard_map/ppermute | solution.py:36
  1.3 1.4 %pack.1 = (f32[48,8,128]{2,1,0:T(8,128)S(1)}, f32[54,8,128]{2,1,0:T(8,128)S(1)}, f32[48,8,128]{2,1,0:T(8,128)S(1)}, f32[54,8,128]{2,1,0:T(8,128)S(1)}, f32[384,128]{1,0:T(8,128)S(1)}, /*index=5*/s32[8,128]{1,0:T(8,128)S(1)}) custom-call(s32[1]{0:T(128)} %bitcast.place_ref, f32[48,4,8,128]{3,2,1,0:T(8,128)} %bitcast.20, f32[384,128]{1,0:T(8,128)} %bitcast.22, ...), custom_call_target="tpu_custom_call" | custom-call | tf_op jit(solution)/shard_map/pack/pallas_call | solution.py:86
  2.7 2.5 %collective-permute-start.1 = (f32[54,8,128]{2,1,0:T(8,128)S(1)}, f32[54,8,128]{2,1,0:T(8,128)S(1)}, u32[]{:S(2)}, u32[]{:S(2)}) collective-permute-start(f32[54,8,128]{2,1,0:T(8,128)S(1)} %get-tuple-element.23), channel_id=1, source_target_pairs={{0,3},{1,2},{2,1},{3,0},{4,7},{5,6},{6,5},{7,4},{8,11},{9,10},{10,... | collective-permute-start | bytes 663560 | tf_op jit(solution)/shard_map/ppermute | solution.py:459
  5.2 0.7 %collective-permute-start.4 = (f32[54,8,128]{2,1,0:T(8,128)S(1)}, f32[54,8,128]{2,1,0:T(8,128)S(1)}, u32[]{:S(2)}, u32[]{:S(2)}) collective-permute-start(f32[54,8,128]{2,1,0:T(8,128)S(1)} %get-tuple-element.25), channel_id=1, source_target_pairs={{0,1},{1,0},{2,3},{3,2},{4,5},{5,4},{6,7},{7,6},{8,9},{9,8},{10,11... | collective-permute-start | bytes 663560 | tf_op jit(solution)/shard_map/ppermute | solution.py:459
  5.8 4.3 %collective-permute-start.2 = (f32[384,128]{1,0:T(8,128)}, f32[384,128]{1,0:T(8,128)S(1)}, u32[]{:S(2)}, u32[]{:S(2)}) collective-permute-start(f32[384,128]{1,0:T(8,128)} %bitcast.23), channel_id=1, source_target_pairs={{0,4},{8,12},{16,20},{24,28},{4,0},{12,8},{20,16},{28,24},{1,5},{9... | collective-permute-start | bytes 589832 | tf_op jit(solution)/shard_map/ppermute | solution.py:36
  10.1 0.5 %collective-permute-start.3 = (f32[48,8,128]{2,1,0:T(8,128)S(1)}, f32[48,8,128]{2,1,0:T(8,128)S(1)}, u32[]{:S(2)}, u32[]{:S(2)}) collective-permute-start(f32[48,8,128]{2,1,0:T(8,128)S(1)} %get-tuple-element.24), channel_id=1, source_target_pairs={{0,2},{1,3},{2,0},{3,1},{4,6},{5,7},{6,4},{7,5},{8,10},{9,11},{10,... | collective-permute-start | bytes 589832 | tf_op jit(solution)/shard_map/ppermute | solution.py:459
  11.3 1.7 %ahead.1 = (f32[8,72,128]{2,1,0:T(8,128)S(1)}, f32[24,16,128]{2,1,0:T(8,128)S(1)}, bf16[48,3072]{1,0:T(8,128)(2,1)S(1)}) custom-call(s32[1]{0:T(128)S(6)} %copy.14.sample_ref, f32[1024]{0:T(1024)} %refs_0_.1, f32[1024]{0:T(1024)} %refs_1_.1, f32[3,3,8,7]{3,2,1,0:T(8,128)} %bitcast.24, f32[3,3,8,7]{3,2,1,0:T(8,128)} %bitcast.25, f32[3,8]{1,0:T(4,128)} %bitcast.27, ...), custom_call_target="tpu_custom_call" | custom-call | tf_op jit(solution)/shard_map/ahead/pallas_call | solution.py:185
  12.9 0.0 collective-permute-done.halo_ref
  12.9 0.1 side.1.applied_ref
  13.0 2.3 %collective-permute-done.2.refs_1_ = f32[384,128]{1,0:T(8,128)S(1)} collective-permute-done((f32[384,128]{1,0:T(8,128)}, f32[384,128]{1,0:T(8,128)S(1)}, u32[]{:S(2)}, u32[]{:S(2)}) %collective-permute-start.2) | collective-permute-done | bytes 196640 | tf_op jit(solution)/shard_map/ppermute | solution.py:36
  15.4 1.3 %collective-permute-done.3 = f32[48,8,128]{2,1,0:T(8,128)S(1)} collective-permute-done((f32[48,8,128]{2,1,0:T(8,128)S(1)}, f32[48,8,128]{2,1,0:T(8,128)S(1)}, u32[]{:S(2)}, u32[]{:S(2)}) %collective-permute-start.3) | collective-permute-done | bytes 196640 | tf_op jit(solution)/shard_map/ppermute | solution.py:459
  16.6 0.0 collective-permute-done.1
  16.6 0.0 collective-permute-done.4
  16.6 1.1 %sums.1 = (bf16[240,3072]{1,0:T(8,128)(2,1)S(1)}, f32[32,128]{1,0:T(8,128)S(1)}) custom-call(s32[1]{0:T(128)} %bitcast.place_ref, s32[1]{0:T(128)} %bitcast.1.slab_ref, f32[8,72,128]{2,1,0:T(8,128)S(1)} %get-tuple-element.20.fields_ref, f32[24,16,128]{2,1,0:T(8,128)S(1)} %side.1.applied_ref, bf16[48,3072]{1,0:T(8,128)(2,1)S(1)} %get-tuple-element.22.own_ref, ...), custom_call_target="tpu_custom_call" | custom-call | tf_op jit(solution)/shard_map/sums/pallas_call | solution.py:341
  17.7 0.1 collective-permute-start.7
  17.8 1.1 %collective-permute-start.6 = (f32[32,128]{1,0:T(8,128)S(1)}, f32[32,128]{1,0:T(8,128)S(1)}, u32[]{:S(2)}, u32[]{:S(2)}) collective-permute-start(f32[32,128]{1,0:T(8,128)S(1)} %get-tuple-element.26), channel_id=1, source_target_pairs={{0,2},{1,3},{2,0},{3,1},{4,6},{5,7},{6,4},{7,5},{8,10},{9,11},{10,... | collective-permute-start | bytes 49160 | tf_op jit(solution)/shard_map/ppermute | solution.py:357
  18.9 0.8 %collective-permute-start.5 = (f32[32,128]{1,0:T(8,128)S(1)}, f32[32,128]{1,0:T(8,128)S(1)}, u32[]{:S(2)}, u32[]{:S(2)}) collective-permute-start(f32[32,128]{1,0:T(8,128)S(1)} %get-tuple-element.26), channel_id=1, source_target_pairs={{0,1},{1,0},{2,3},{3,2},{4,5},{5,4},{6,7},{7,6},{8,9},{9,8},{10,11... | collective-permute-start | bytes 49160 | tf_op jit(solution)/shard_map/ppermute | solution.py:357
  19.7 1.3 %collective-permute-done.7 = f32[32,128]{1,0:T(8,128)S(1)} collective-permute-done((f32[32,128]{1,0:T(8,128)S(1)}, f32[32,128]{1,0:T(8,128)S(1)}, u32[]{:S(2)}, u32[]{:S(2)}) %collective-permute-start.7) | collective-permute-done | bytes 16416 | tf_op jit(solution)/shard_map/ppermute | solution.py:357
  21.0 0.7 %collective-permute-done.6 = f32[32,128]{1,0:T(8,128)S(1)} collective-permute-done((f32[32,128]{1,0:T(8,128)S(1)}, f32[32,128]{1,0:T(8,128)S(1)}, u32[]{:S(2)}, u32[]{:S(2)}) %collective-permute-start.6) | collective-permute-done | bytes 16416 | tf_op jit(solution)/shard_map/ppermute | solution.py:357
  21.7 0.0 collective-permute-done.5
  21.8 14.8 %all_to_all.5.parts_ref = f32[8,32,128]{2,1,0:T(8,128)S(1)} all-to-all(f32[8,32,128]{2,1,0:T(8,128)S(1)} %broadcast_in_dim.2), channel_id=1, replica_groups=mesh['space'=8,'basis'=4] {'space'}, dimensions={0} | all-to-all | bytes 262144 | tf_op jit(solution)/shard_map/all_to_all | solution.py:366
  36.5 3.1 %finish.1 = (f32[384,128]{1,0:T(8,128)}, f32[16,16]{1,0:T(8,128)}, f32[16,16]{1,0:T(8,128)}) custom-call(s32[1]{0:T(128)} %bitcast.place_ref, f32[8,32,128]{2,1,0:T(8,128)S(1)} %all_to_all.5.parts_ref, bf16[240,3072]{1,0:T(8,128)(2,1)S(1)} %get-tuple-element.27.stack_ref), custom_call_target="tpu_custom_call" | custom-call | tf_op jit(solution)/shard_map/finish/pallas_call | solution.py:426
  (2 shorter events, 0.0 us)
Async XLA Ops:
  0.6 12.3 %collective-permute-start = (f32[384,128]{1,0:T(8,128)}, f32[384,128]{1,0:T(8,128)S(1)}, u32[]{:S(2)}, u32[]{:S(2)}) collective-permute-start(f32[384,128]{1,0:T(8,128)} %bitcast.21), channel_id=1, source_target_pairs={{4,8},{12,16},{20,24},{8,4},{16,12},{24,20},{5,9},{13,17},{21,25},... | collective-permute-start | bytes 589832 | tf_op jit(solution)/shard_map/ppermute | solution.py:36
  2.7 14.0 %collective-permute-start.1 = (f32[54,8,128]{2,1,0:T(8,128)S(1)}, f32[54,8,128]{2,1,0:T(8,128)S(1)}, u32[]{:S(2)}, u32[]{:S(2)}) collective-permute-start(f32[54,8,128]{2,1,0:T(8,128)S(1)} %get-tuple-element.23), channel_id=1, source_target_pairs={{0,3},{1,2},{2,1},{3,0},{4,7},{5,6},{6,5},{7,4},{8,11},{9,10},{10,... | collective-permute-start | bytes 663560 | tf_op jit(solution)/shard_map/ppermute | solution.py:459
  5.2 11.5 %collective-permute-start.4 = (f32[54,8,128]{2,1,0:T(8,128)S(1)}, f32[54,8,128]{2,1,0:T(8,128)S(1)}, u32[]{:S(2)}, u32[]{:S(2)}) collective-permute-start(f32[54,8,128]{2,1,0:T(8,128)S(1)} %get-tuple-element.25), channel_id=1, source_target_pairs={{0,1},{1,0},{2,3},{3,2},{4,5},{5,4},{6,7},{7,6},{8,9},{9,8},{10,11... | collective-permute-start | bytes 663560 | tf_op jit(solution)/shard_map/ppermute | solution.py:459
  5.8 9.6 %collective-permute-start.2 = (f32[384,128]{1,0:T(8,128)}, f32[384,128]{1,0:T(8,128)S(1)}, u32[]{:S(2)}, u32[]{:S(2)}) collective-permute-start(f32[384,128]{1,0:T(8,128)} %bitcast.23), channel_id=1, source_target_pairs={{0,4},{8,12},{16,20},{24,28},{4,0},{12,8},{20,16},{28,24},{1,5},{9... | collective-permute-start | bytes 589832 | tf_op jit(solution)/shard_map/ppermute | solution.py:36
  10.1 6.5 %collective-permute-start.3 = (f32[48,8,128]{2,1,0:T(8,128)S(1)}, f32[48,8,128]{2,1,0:T(8,128)S(1)}, u32[]{:S(2)}, u32[]{:S(2)}) collective-permute-start(f32[48,8,128]{2,1,0:T(8,128)S(1)} %get-tuple-element.24), channel_id=1, source_target_pairs={{0,2},{1,3},{2,0},{3,1},{4,6},{5,7},{6,4},{7,5},{8,10},{9,11},{10,... | collective-permute-start | bytes 589832 | tf_op jit(solution)/shard_map/ppermute | solution.py:459
  17.7 3.2 %collective-permute-start.7 = (f32[32,128]{1,0:T(8,128)S(1)}, f32[32,128]{1,0:T(8,128)S(1)}, u32[]{:S(2)}, u32[]{:S(2)}) collective-permute-start(f32[32,128]{1,0:T(8,128)S(1)} %get-tuple-element.26), channel_id=1, source_target_pairs={{0,3},{1,2},{2,1},{3,0},{4,7},{5,6},{6,5},{7,4},{8,11},{9,10},{10,... | collective-permute-start | bytes 49160 | tf_op jit(solution)/shard_map/ppermute | solution.py:357
  17.8 3.9 %collective-permute-start.6 = (f32[32,128]{1,0:T(8,128)S(1)}, f32[32,128]{1,0:T(8,128)S(1)}, u32[]{:S(2)}, u32[]{:S(2)}) collective-permute-start(f32[32,128]{1,0:T(8,128)S(1)} %get-tuple-element.26), channel_id=1, source_target_pairs={{0,2},{1,3},{2,0},{3,1},{4,6},{5,7},{6,4},{7,5},{8,10},{9,11},{10,... | collective-permute-start | bytes 49160 | tf_op jit(solution)/shard_map/ppermute | solution.py:357
  18.9 2.8 %collective-permute-start.5 = (f32[32,128]{1,0:T(8,128)S(1)}, f32[32,128]{1,0:T(8,128)S(1)}, u32[]{:S(2)}, u32[]{:S(2)}) collective-permute-start(f32[32,128]{1,0:T(8,128)S(1)} %get-tuple-element.26), channel_id=1, source_target_pairs={{0,1},{1,0},{2,3},{3,2},{4,5},{5,4},{6,7},{7,6},{8,9},{9,8},{10,11... | collective-permute-start | bytes 49160 | tf_op jit(solution)/shard_map/ppermute | solution.py:357

commit v10 on v9

--- a/solution.py
+++ b/solution.py
@@ -12,6 +12,7 @@
 SMEM = pl.BlockSpec(memory_space=pltpu.SMEM)
 HBM = pl.BlockSpec(memory_space=pltpu.HBM)
 EARLY = pl.CostEstimate(flops=10**9, bytes_accessed=10**6, transcendentals=0)
+NEXT = pl.CostEstimate(flops=10**6, bytes_accessed=10**6, transcendentals=0)
 SCRATCH = pltpu.CompilerParams(vmem_limit_bytes=8 * 2**20)
 
 
@@ -119,11 +120,9 @@
     for copy in copies:
         copy.start()
     group_cols = stack_ref.shape[0] // 3
-    for line in range(applied_ref.shape[0]):
-        values = own_ref[pl.ds(line, group_cols, stride=applied_ref.shape[0]), :]
-        for index, part in enumerate(three_parts(values)):
-            there = pl.ds(line * values.shape[1], values.shape[1])
-            stack_ref[pl.ds(index * group_cols, group_cols), there] = part
+    split_lines(
+        own_ref, stack_ref, applied_ref.shape[0], group_cols, [i * group_cols for i in range(3)]
+    )
     for copy in copies:
         copy.wait()
     comps, _, levels, offsets = k0_ref.shape
@@ -234,6 +233,57 @@
     )(slab, *kept(fields, applied, halo))
 
 
+def split_lines(piece_ref, stack_ref, lines, group_cols, begins):
+    lanes = piece_ref.shape[1]
+    for line in range(lines):
+        values = piece_ref[pl.ds(line, group_cols, stride=lines), :]
+        for begin, part in zip(begins, three_parts(values)):
+            stack_ref[pl.ds(begin, group_cols), pl.ds(line * lanes, lanes)] = part
+
+
+def edges_kernel(comps, ks, group_cols, place_ref, fields_ref, applied_ref, *refs):
+    piece_refs, out_ref, parts_refs = refs[: len(ks)], refs[len(ks)], refs[len(ks) + 1 :]
+    lines, block_cols, lanes = applied_ref.shape
+    rows = lines // comps
+    stride = fields_ref.shape[1] // (comps * comps)
+    place = place_ref[0]
+
+    def edge(comp, step):
+        result = jnp.zeros((block_cols, lanes), jnp.float32)
+        for k, ref in zip(ks, piece_refs):
+            begin = ref.shape[0] - (comps - comp) * block_cols
+            here = (place ^ k) == place + step
+            result = jnp.where(here, ref[pl.ds(begin, block_cols), :], result)
+        return result
+
+    out_ref[...] = applied_ref[...]
+    for row, offset, step in ((0, 3, -1), (rows - 1, 4, 1)):
+        field_row = fields_ref[row]
+        views = [edge(comp, step) for comp in range(comps)]
+        for out in range(comps):
+            total = out_ref[out * rows + row]
+            for comp, view in enumerate(views):
+                entry = (out * comps + comp) * stride + offset
+                total = total + field_row[entry : entry + 1] * view
+            out_ref[out * rows + row] = total
+    for piece_ref, parts_ref in zip(piece_refs, parts_refs):
+        split_lines(piece_ref, parts_ref, lines, group_cols, [i * group_cols for i in range(3)])
+
+
+def add_edges(place, fields, applied, pieces, comps, group_cols):
+    lines, _, lanes = applied.shape
+    parts = near(3 * group_cols, lines * lanes, dtype=jnp.bfloat16)
+    return pl.pallas_call(
+        functools.partial(edges_kernel, comps, tuple(pieces), group_cols),
+        out_shape=(near(*applied.shape),) + (parts,) * len(pieces),
+        in_specs=[SMEM] + [VMEM] * (2 + len(pieces)),
+        out_specs=(VMEM,) * (1 + len(pieces)),
+        compiler_params=SCRATCH,
+        cost_estimate=NEXT,
+        name="edges",
+    )(place, *kept(fields, applied, *pieces.values()))
+
+
 def fold(total, basis_cols, block_cols, lanes):
     half = basis_cols // 2
     row = lax.broadcasted_iota(jnp.int32, (half, half), 0)
@@ -269,60 +319,38 @@
     return gram, first, folded[:block_cols, 3 * half : 3 * half + block_cols]
 
 
-def sums_kernel(comps, names, edge_ks, place_ref, slab_ref, fields_ref, applied_ref, own_ref, *refs):
+def sums_kernel(
+    comps, split, raw, place_ref, slab_ref, fields_ref, applied_ref, halo_ref, *refs
+):
     *refs, stack_ref, sums_ref = refs
-    got = dict(zip(names, refs))
-    piece_refs = [got[k] for k in range(1, len(got))]
     lines, block_cols, lanes = applied_ref.shape
     rows = lines // comps
-    stride = fields_ref.shape[1] // (comps * comps)
-    group_cols = own_ref.shape[0] // 3
-    basis_cols = (1 + len(piece_refs)) * group_cols
+    group_cols = refs[0].shape[0] // 3
+    basis_cols = (len(split) + len(raw)) * group_cols
     joined = basis_cols + block_cols
     place = place_ref[0]
     swapped = slab_ref[0] % 2 == 1
-
-    def store(begin, line, values):
-        for index, part in enumerate(three_parts(values)):
-            there = pl.ds(index * joined + begin, values.shape[0])
-            stack_ref[there, pl.ds(line * lanes, lanes)] = part
-
-    begin = pl.multiple_of(place * group_cols, group_cols)
-    for index in range(3):
-        stack_ref[pl.ds(index * joined + begin, group_cols), :] = own_ref[
-            pl.ds(index * group_cols, group_cols), :
-        ]
-    for k, piece_ref in enumerate(piece_refs, 1):
+    for k, ref in zip(split + raw, refs):
         begin = pl.multiple_of((place ^ k) * group_cols, group_cols)
-        for line in range(lines):
-            store(begin, line, piece_ref[pl.ds(line, group_cols, stride=lines), :])
-
-    def edge(comp, step):
-        result = jnp.zeros((block_cols, lanes), jnp.float32)
-        for k in edge_ks:
-            ref = piece_refs[k - 1]
-            begin = ref.shape[0] - (comps - comp) * block_cols
-            here = (place ^ k) == place + step
-            result = jnp.where(here, ref[pl.ds(begin, block_cols), :], result)
-        return result
-
+        begins = [index * joined + begin for index in range(3)]
+        if k in split:
+            for index in range(3):
+                stack_ref[pl.ds(begins[index], group_cols), :] = ref[
+                    pl.ds(index * group_cols, group_cols), :
+                ]
+        else:
+            split_lines(ref, stack_ref, lines, group_cols, begins)
     for row in range(rows):
         field_row = fields_ref[row]
-        totals = [applied_ref[out * rows + row] for out in range(comps)]
-        for comp in range(comps):
-            views = {}
-            if row == 0:
-                views[3] = edge(comp, -1)
-            if row == rows - 1:
-                views[4] = edge(comp, 1)
-            side = line_of(got["even"], comp, row, comps, rows, block_cols)
-            for out in range(comps):
-                entry = (out * comps + comp) * stride
-                totals[out] += side_terms(field_row, swapped, "even", out, comp, comps) * side
-                for offset, view in views.items():
-                    totals[out] += field_row[entry + offset : entry + offset + 1] * view
+        views = [line_of(halo_ref, comp, row, comps, rows, block_cols) for comp in range(comps)]
         for out in range(comps):
-            store(basis_cols, out * rows + row, totals[out])
+            line = out * rows + row
+            total = applied_ref[line]
+            for comp, view in enumerate(views):
+                total = total + side_terms(field_row, swapped, "odd", out, comp, comps) * view
+            for index, part in enumerate(three_parts(total)):
+                there = pl.ds(index * joined + basis_cols, block_cols)
+                stack_ref[there, pl.ds(line * lanes, lanes)] = part
 
     stack = stack_ref[...]
     products = lax.dot_general(
@@ -333,22 +361,21 @@
     sums_ref[...] = fold(total, basis_cols, block_cols, sums_ref.shape[1])
 
 
-def sums(place, slab, fields, applied, own, got, comps):
-    count = len(got)
+def sums(place, slab, fields, applied, halo, split, raw, comps):
     lines, block_cols, lanes = applied.shape
-    basis_cols = count * (own.shape[0] // 3)
+    basis_cols = (len(split) + len(raw)) * (split[0].shape[0] // 3)
     joined = basis_cols + block_cols
     return pl.pallas_call(
-        functools.partial(sums_kernel, comps, tuple(got), partners(count)[1]),
+        functools.partial(sums_kernel, comps, tuple(split), tuple(raw)),
         out_shape=(
             near(3 * joined, lines * lanes, dtype=jnp.bfloat16),
             near(basis_cols // 2, 2 * basis_cols),
         ),
-        in_specs=[SMEM] * 2 + [VMEM] * (3 + len(got)),
+        in_specs=[SMEM] * 2 + [VMEM] * (3 + len(split) + len(raw)),
         out_specs=(VMEM, VMEM),
         compiler_params=SCRATCH,
         name="sums",
-    )(place, slab, *kept(fields, applied, own, *got.values()))
+    )(place, slab, *kept(fields, applied, halo, *split.values(), *raw.values()))
 
 
 def exchange_sum(part, axis):
@@ -450,7 +477,7 @@
     x_far = x_block.reshape(block_cols * lines, lanes)
     own, *pieces, x_rows, material = pack(place, basis, x_far, material.reshape(rows, lanes), block_cols)
     got = {}
-    for name in ("odd", 3, "even", 2, 1):
+    for name in ("even", 3, "odd", 2, 1):
         if name == "even":
             got[name] = swap(x_far, "space", 0)
         elif name == "odd":
@@ -462,8 +489,11 @@
         sample, velocities, shifts, k0_blocks, ke_blocks, k0_diag, mass, material, x_rows,
         own.reshape(-1, lanes), comps,
     )
-    applied = add_side(slab, fields, applied, got.pop("odd"), comps, "odd")
-    stack, part = sums(place, slab, fields, applied, own, got, comps)
+    applied = add_side(slab, fields, applied, got.pop("even"), comps, "even")
+    pieces = {k: got.pop(k) for k in reversed(partners(count)[1])}
+    applied, *parts = add_edges(place, fields, applied, pieces, comps, group_cols)
+    split = {0: own, **dict(zip(pieces, parts))}
+    stack, part = sums(place, slab, fields, applied, got.pop("odd"), split, got, comps)
     parts = exchange(exchange_sum(part, "basis"), "space")
     block, coeffs, upper = finish(place, parts, stack, row_count, block_cols, group_cols, lines)
     return (block.reshape(x_block.shape), coeffs, upper)

time: 39.9 us -> 37.9 us (0.950)
  waiting for transfers between devices: 5.66 us -> 9.11 us
  blocking collectives: 14.8 us -> 12 us
  starting transfers between devices: 10.5 us -> 7.86 us
    ppermute x3, waiting for transfers between devices: 1.26 us -> 6.49 us  [shards(): lax.ppermute(pieces[name - 1], 'basis', [(i, i ^ name) for i in range(cou...]
    all_to_all x1, blocking collectives: 14.8 us -> 12 us  [exchange(): lax.all_to_all(jnp.broadcast_to(part[None], (count,) + part.shape), axis,...]
    ppermute x2, waiting for transfers between devices: 2.35 us -> 0.01 us  [swap(): return lax.ppermute(values, axis, pairs + [(j, i) for i, j in pairs])]
    ppermute x3, starting transfers between devices: 3.65 us -> 2.27 us  [shards(): lax.ppermute(pieces[name - 1], 'basis', [(i, i ^ name) for i in range(cou...]
    ppermute x2, starting transfers between devices: 4.95 us -> 3.66 us  [swap(): return lax.ppermute(values, axis, pairs + [(j, i) for i, j in pairs])]
    ppermute x3, waiting for transfers between devices: 2.05 us -> 2.62 us  [exchange_sum(): lax.ppermute(part, axis, [(i, i ^ k) for i in range(count)])]
    pallas_call x1 -> x2, Pallas kernels: 1.09 us -> 1.11 us  [the longest x1 0.95 us: sums(): pl.pallas_call(functools.partial(sums_kernel, comps, tuple(split), tuple(...]
  transfers between devices with their start and end apart: 8 -> 8, of which waited for: 4 -> 4; matrix products, arithmetic and copies ran while one was open for 0% -> 0% of each run, Pallas kernels for 8% -> 9%
where the time goes in v10:
time: 37.9 us; the launch traced here: 37.7 us
  blocking collectives  12 us (32%)
  waiting for transfers between devices  9.11 us (24%)
  starting transfers between devices  7.86 us (21%)
  Pallas kernels  7.32 us (19%)
  between operations  1.35 us (4%)
    all_to_all x1, blocking collectives, exchange(): lax.all_to_all(jnp.broadcast_to(part[None], (count,) + part.shape), axis,...  12 us
    ppermute x3, waiting for transfers between devices, shards(): lax.ppermute(pieces[name - 1], 'basis', [(i, i ^ name) for i in range(cou...  6.49 us
    ppermute x2, starting transfers between devices, swap(): return lax.ppermute(values, axis, pairs + [(j, i) for i, j in pairs])  3.66 us
    pallas_call x1, Pallas kernels, finish(): pl.pallas_call(functools.partial(finish_kernel, row_count), out_shape=(f3...  3.13 us
    ppermute x3, waiting for transfers between devices, exchange_sum(): lax.ppermute(part, axis, [(i, i ^ k) for i in range(count)])  2.62 us
    ppermute x3, starting transfers between devices, shards(): lax.ppermute(pieces[name - 1], 'basis', [(i, i ^ name) for i in range(cou...  2.27 us
    ppermute x3, starting transfers between devices, exchange_sum(): lax.ppermute(part, axis, [(i, i ^ k) for i in range(count)])  1.93 us
    pallas_call x1, Pallas kernels, ahead(): pl.pallas_call(ahead_kernel, out_shape=(near(rows, comps * comps * stride...  1.64 us
  transfers between devices with their start and end apart: 8, of which 4 were waited for; matrix products, arithmetic and copies ran while one was open for 0% of the time, Pallas kernels for 9%

profile of v10, /device:TPU:0, one launch (start us, length us, event | category | flops | bytes accessed | tf_op | source)
XLA Modules:
  0.0 37.7 jit_solution(11035180676643096320)
XLA Ops:
  0.6 3.0 %collective-permute-start = (f32[384,128]{1,0:T(8,128)}, f32[384,128]{1,0:T(8,128)S(1)}, u32[]{:S(2)}, u32[]{:S(2)}) collective-permute-start(f32[384,128]{1,0:T(8,128)} %bitcast.21), channel_id=1, source_target_pairs={{0,4},{8,12},{16,20},{24,28},{4,0},{12,8},{20,16},{28,24},{1,5},{9... | collective-permute-start | bytes 589832 | tf_op jit(solution)/shard_map/ppermute | solution.py:37
  3.6 1.3 %pack.1 = (f32[48,8,128]{2,1,0:T(8,128)S(1)}, f32[54,8,128]{2,1,0:T(8,128)S(1)}, f32[48,8,128]{2,1,0:T(8,128)S(1)}, f32[54,8,128]{2,1,0:T(8,128)S(1)}, f32[384,128]{1,0:T(8,128)S(1)}, /*index=5*/s32[8,128]{1,0:T(8,128)S(1)}) custom-call(s32[1]{0:T(128)} %bitcast.place_ref, f32[48,4,8,128]{3,2,1,0:T(8,128)} %bitcast.20, f32[384,128]{1,0:T(8,128)} %bitcast.22, ...), custom_call_target="tpu_custom_call" | custom-call | tf_op jit(solution)/shard_map/pack/pallas_call | solution.py:87
  5.0 0.7 %collective-permute-start.1 = (f32[54,8,128]{2,1,0:T(8,128)S(1)}, f32[54,8,128]{2,1,0:T(8,128)S(1)}, u32[]{:S(2)}, u32[]{:S(2)}) collective-permute-start(f32[54,8,128]{2,1,0:T(8,128)S(1)} %get-tuple-element.25), channel_id=1, source_target_pairs={{0,3},{1,2},{2,1},{3,0},{4,7},{5,6},{6,5},{7,4},{8,11},{9,10},{10,... | collective-permute-start | bytes 663560 | tf_op jit(solution)/shard_map/ppermute | solution.py:486
  5.7 1.0 %collective-permute-start.2 = (f32[54,8,128]{2,1,0:T(8,128)S(1)}, f32[54,8,128]{2,1,0:T(8,128)S(1)}, u32[]{:S(2)}, u32[]{:S(2)}) collective-permute-start(f32[54,8,128]{2,1,0:T(8,128)S(1)} %get-tuple-element.26), channel_id=1, source_target_pairs={{0,1},{1,0},{2,3},{3,2},{4,5},{5,4},{6,7},{7,6},{8,9},{9,8},{10,11... | collective-permute-start | bytes 663560 | tf_op jit(solution)/shard_map/ppermute | solution.py:486
  6.7 0.7 %collective-permute-start.3 = (f32[384,128]{1,0:T(8,128)}, f32[384,128]{1,0:T(8,128)S(1)}, u32[]{:S(2)}, u32[]{:S(2)}) collective-permute-start(f32[384,128]{1,0:T(8,128)} %bitcast.23), channel_id=1, source_target_pairs={{4,8},{12,16},{20,24},{8,4},{16,12},{24,20},{5,9},{13,17},{21,25},... | collective-permute-start | bytes 589832 | tf_op jit(solution)/shard_map/ppermute | solution.py:37
  7.4 0.6 %collective-permute-start.4 = (f32[48,8,128]{2,1,0:T(8,128)S(1)}, f32[48,8,128]{2,1,0:T(8,128)S(1)}, u32[]{:S(2)}, u32[]{:S(2)}) collective-permute-start(f32[48,8,128]{2,1,0:T(8,128)S(1)} %get-tuple-element.31), channel_id=1, source_target_pairs={{0,2},{1,3},{2,0},{3,1},{4,6},{5,7},{6,4},{7,5},{8,10},{9,11},{10,... | collective-permute-start | bytes 589832 | tf_op jit(solution)/shard_map/ppermute | solution.py:486
  8.6 1.6 %ahead.1 = (f32[8,72,128]{2,1,0:T(8,128)S(1)}, f32[24,16,128]{2,1,0:T(8,128)S(1)}, bf16[48,3072]{1,0:T(8,128)(2,1)S(1)}) custom-call(s32[1]{0:T(128)S(6)} %copy.14.sample_ref, f32[1024]{0:T(1024)} %refs_0_.1, f32[1024]{0:T(1024)} %refs_1_.1, f32[3,3,8,7]{3,2,1,0:T(8,128)} %bitcast.24, f32[3,3,8,7]{3,2,1,0:T(8,128)} %bitcast.25, f32[3,8]{1,0:T(4,128)} %bitcast.27, ...), custom_call_target="tpu_custom_call" | custom-call | tf_op jit(solution)/shard_map/ahead/pallas_call | solution.py:184
  10.2 0.0 collective-permute-done.halo_ref
  10.2 0.1 side.1.applied_ref
  10.3 2.4 %collective-permute-done.1 = f32[54,8,128]{2,1,0:T(8,128)S(1)} collective-permute-done((f32[54,8,128]{2,1,0:T(8,128)S(1)}, f32[54,8,128]{2,1,0:T(8,128)S(1)}, u32[]{:S(2)}, u32[]{:S(2)}) %collective-permute-start.1) | collective-permute-done | bytes 221216 | tf_op jit(solution)/shard_map/ppermute | solution.py:486
  12.7 0.0 collective-permute-done.2
  12.7 0.2 edges.1
  12.9 0.0 collective-permute-done.3.halo_ref
  12.9 4.1 %collective-permute-done.4 = f32[48,8,128]{2,1,0:T(8,128)S(1)} collective-permute-done((f32[48,8,128]{2,1,0:T(8,128)S(1)}, f32[48,8,128]{2,1,0:T(8,128)S(1)}, u32[]{:S(2)}, u32[]{:S(2)}) %collective-permute-start.4) | collective-permute-done | bytes 196640 | tf_op jit(solution)/shard_map/ppermute | solution.py:486
  17.0 1.0 %sums.1 = (bf16[240,3072]{1,0:T(8,128)(2,1)S(1)}, f32[32,128]{1,0:T(8,128)S(1)}) custom-call(s32[1]{0:T(128)} %bitcast.place_ref, s32[1]{0:T(128)} %bitcast.1.slab_ref, f32[8,72,128]{2,1,0:T(8,128)S(1)} %get-tuple-element.23.fields_ref, f32[24,16,128]{2,1,0:T(8,128)S(1)} %get-tuple-element.27.applied_ref, f32[384,128]{1,0:T(8,128)S(1)} %collective-permute-done.3.halo_ref, ...), custom_call_target="tpu_custom_call" | custom-call | tf_op jit(solution)/shard_map/sums/pallas_call | solution.py:368
  18.0 0.8 %collective-permute-start.7 = (f32[32,128]{1,0:T(8,128)S(1)}, f32[32,128]{1,0:T(8,128)S(1)}, u32[]{:S(2)}, u32[]{:S(2)}) collective-permute-start(f32[32,128]{1,0:T(8,128)S(1)} %get-tuple-element.32), channel_id=1, source_target_pairs={{0,3},{1,2},{2,1},{3,0},{4,7},{5,6},{6,5},{7,4},{8,11},{9,10},{10,... | collective-permute-start | bytes 49160 | tf_op jit(solution)/shard_map/ppermute | solution.py:384
  18.7 1.0 %collective-permute-start.6 = (f32[32,128]{1,0:T(8,128)S(1)}, f32[32,128]{1,0:T(8,128)S(1)}, u32[]{:S(2)}, u32[]{:S(2)}) collective-permute-start(f32[32,128]{1,0:T(8,128)S(1)} %get-tuple-element.32), channel_id=1, source_target_pairs={{0,2},{1,3},{2,0},{3,1},{4,6},{5,7},{6,4},{7,5},{8,10},{9,11},{10,... | collective-permute-start | bytes 49160 | tf_op jit(solution)/shard_map/ppermute | solution.py:384
  19.7 0.2 collective-permute-start.5
  19.9 1.3 %collective-permute-done.7 = f32[32,128]{1,0:T(8,128)S(1)} collective-permute-done((f32[32,128]{1,0:T(8,128)S(1)}, f32[32,128]{1,0:T(8,128)S(1)}, u32[]{:S(2)}, u32[]{:S(2)}) %collective-permute-start.7) | collective-permute-done | bytes 16416 | tf_op jit(solution)/shard_map/ppermute | solution.py:384
  21.2 1.3 %collective-permute-done.6 = f32[32,128]{1,0:T(8,128)S(1)} collective-permute-done((f32[32,128]{1,0:T(8,128)S(1)}, f32[32,128]{1,0:T(8,128)S(1)}, u32[]{:S(2)}, u32[]{:S(2)}) %collective-permute-start.6) | collective-permute-done | bytes 16416 | tf_op jit(solution)/shard_map/ppermute | solution.py:384
  22.5 0.0 collective-permute-done.5
  22.5 12.0 %all_to_all.5.parts_ref = f32[8,32,128]{2,1,0:T(8,128)S(1)} all-to-all(f32[8,32,128]{2,1,0:T(8,128)S(1)} %broadcast_in_dim.2), channel_id=1, replica_groups=mesh['space'=8,'basis'=4] {'space'}, dimensions={0} | all-to-all | bytes 262144 | tf_op jit(solution)/shard_map/all_to_all | solution.py:393
  34.5 3.1 %finish.1 = (f32[384,128]{1,0:T(8,128)}, f32[16,16]{1,0:T(8,128)}, f32[16,16]{1,0:T(8,128)}) custom-call(s32[1]{0:T(128)} %bitcast.place_ref, f32[8,32,128]{2,1,0:T(8,128)S(1)} %all_to_all.5.parts_ref, bf16[240,3072]{1,0:T(8,128)(2,1)S(1)} %get-tuple-element.33.stack_ref), custom_call_target="tpu_custom_call" | custom-call | tf_op jit(solution)/shard_map/finish/pallas_call | solution.py:453
  (2 shorter events, 0.0 us)
Async XLA Ops:
  0.6 9.6 %collective-permute-start = (f32[384,128]{1,0:T(8,128)}, f32[384,128]{1,0:T(8,128)S(1)}, u32[]{:S(2)}, u32[]{:S(2)}) collective-permute-start(f32[384,128]{1,0:T(8,128)} %bitcast.21), channel_id=1, source_target_pairs={{0,4},{8,12},{16,20},{24,28},{4,0},{12,8},{20,16},{28,24},{1,5},{9... | collective-permute-start | bytes 589832 | tf_op jit(solution)/shard_map/ppermute | solution.py:37
  5.0 7.7 %collective-permute-start.1 = (f32[54,8,128]{2,1,0:T(8,128)S(1)}, f32[54,8,128]{2,1,0:T(8,128)S(1)}, u32[]{:S(2)}, u32[]{:S(2)}) collective-permute-start(f32[54,8,128]{2,1,0:T(8,128)S(1)} %get-tuple-element.25), channel_id=1, source_target_pairs={{0,3},{1,2},{2,1},{3,0},{4,7},{5,6},{6,5},{7,4},{8,11},{9,10},{10,... | collective-permute-start | bytes 663560 | tf_op jit(solution)/shard_map/ppermute | solution.py:486
  5.7 7.0 %collective-permute-start.2 = (f32[54,8,128]{2,1,0:T(8,128)S(1)}, f32[54,8,128]{2,1,0:T(8,128)S(1)}, u32[]{:S(2)}, u32[]{:S(2)}) collective-permute-start(f32[54,8,128]{2,1,0:T(8,128)S(1)} %get-tuple-element.26), channel_id=1, source_target_pairs={{0,1},{1,0},{2,3},{3,2},{4,5},{5,4},{6,7},{7,6},{8,9},{9,8},{10,11... | collective-permute-start | bytes 663560 | tf_op jit(solution)/shard_map/ppermute | solution.py:486
  6.7 6.2 %collective-permute-start.3 = (f32[384,128]{1,0:T(8,128)}, f32[384,128]{1,0:T(8,128)S(1)}, u32[]{:S(2)}, u32[]{:S(2)}) collective-permute-start(f32[384,128]{1,0:T(8,128)} %bitcast.23), channel_id=1, source_target_pairs={{4,8},{12,16},{20,24},{8,4},{16,12},{24,20},{5,9},{13,17},{21,25},... | collective-permute-start | bytes 589832 | tf_op jit(solution)/shard_map/ppermute | solution.py:37
  7.4 9.6 %collective-permute-start.4 = (f32[48,8,128]{2,1,0:T(8,128)S(1)}, f32[48,8,128]{2,1,0:T(8,128)S(1)}, u32[]{:S(2)}, u32[]{:S(2)}) collective-permute-start(f32[48,8,128]{2,1,0:T(8,128)S(1)} %get-tuple-element.31), channel_id=1, source_target_pairs={{0,2},{1,3},{2,0},{3,1},{4,6},{5,7},{6,4},{7,5},{8,10},{9,11},{10,... | collective-permute-start | bytes 589832 | tf_op jit(solution)/shard_map/ppermute | solution.py:486
  18.0 3.2 %collective-permute-start.7 = (f32[32,128]{1,0:T(8,128)S(1)}, f32[32,128]{1,0:T(8,128)S(1)}, u32[]{:S(2)}, u32[]{:S(2)}) collective-permute-start(f32[32,128]{1,0:T(8,128)S(1)} %get-tuple-element.32), channel_id=1, source_target_pairs={{0,3},{1,2},{2,1},{3,0},{4,7},{5,6},{6,5},{7,4},{8,11},{9,10},{10,... | collective-permute-start | bytes 49160 | tf_op jit(solution)/shard_map/ppermute | solution.py:384
  18.7 3.8 %collective-permute-start.6 = (f32[32,128]{1,0:T(8,128)S(1)}, f32[32,128]{1,0:T(8,128)S(1)}, u32[]{:S(2)}, u32[]{:S(2)}) collective-permute-start(f32[32,128]{1,0:T(8,128)S(1)} %get-tuple-element.32), channel_id=1, source_target_pairs={{0,2},{1,3},{2,0},{3,1},{4,6},{5,7},{6,4},{7,5},{8,10},{9,11},{10,... | collective-permute-start | bytes 49160 | tf_op jit(solution)/shard_map/ppermute | solution.py:384
  19.7 2.8 %collective-permute-start.5 = (f32[32,128]{1,0:T(8,128)S(1)}, f32[32,128]{1,0:T(8,128)S(1)}, u32[]{:S(2)}, u32[]{:S(2)}) collective-permute-start(f32[32,128]{1,0:T(8,128)S(1)} %get-tuple-element.32), channel_id=1, source_target_pairs={{0,1},{1,0},{2,3},{3,2},{4,5},{5,4},{6,7},{7,6},{8,9},{9,8},{10,11... | collective-permute-start | bytes 49160 | tf_op jit(solution)/shard_map/ppermute | solution.py:384

commit v11 on v10

--- a/solution.py
+++ b/solution.py
@@ -394,14 +394,13 @@
 
 
 def finish_kernel(
-    row_count, place_ref, parts_ref, stack_ref, block_ref, coeffs_ref, upper_ref,
-    coeffs_scratch,
+    row_count, comps, place_ref, parts_ref, stack_ref, block_ref, coeffs_ref, upper_ref,
+    coeffs_scratch, block_scratch, sems,
 ):
     block_cols = upper_ref.shape[0]
     basis_cols = parts_ref.shape[2] // 2
     joined = basis_cols + block_cols
-    lines = block_ref.shape[0] // block_cols
-    lanes = block_ref.shape[1]
+    lines, lanes = block_ref.shape[1:]
     total = jnp.sum(parts_ref[...], axis=0) / row_count
     gram, first, block_gram = unfold(total, block_cols)
 
@@ -413,7 +412,9 @@
 
     coeffs = first + (first - times(first, gram))
     image = times(coeffs, gram)
-    matrix = block_gram - times(coeffs, first, 1) - times(first - image, coeffs, 1)
+    matrix = block_gram - times(
+        jnp.concatenate((coeffs, first - image), axis=1), jnp.concatenate((first, coeffs), axis=1), 1
+    )
     coeffs_scratch[...] = coeffs.T
     group_cols = coeffs_ref.shape[0]
     start = pl.multiple_of(place_ref[0] * group_cols, group_cols)
@@ -425,39 +426,69 @@
     pad = jnp.zeros((block_cols, 2 * basis_cols - joined - block_cols), jnp.float32)
     work = jnp.concatenate((-coeffs, unit, matrix, pad), axis=1)
     height = lax.broadcasted_iota(jnp.int32, work.shape, 0)
-    for step in range(block_cols):
-        pivots = jnp.broadcast_to(work[:, joined + step : joined + step + 1], work.shape)
-        pivot = pivots[step : step + 1, :]
-        pivot_row = work[step : step + 1, :]
-        scaled = pivot_row / pivot
-        new_row = pivot_row * lax.rsqrt(pivot)
-        work = jnp.where(
-            height > step, work - pivots * scaled, jnp.where(height == step, new_row, work)
-        )
-    upper_ref[...] = work[:, joined : joined + block_cols]
+    width = 4
+    for begin in range(0, block_cols, width):
+        done, new_rows = [], []
+        for step in range(begin, begin + width):
+            column_here = jnp.broadcast_to(work[:, joined + step : joined + step + 1], work.shape)
+            pivot_row = work[step : step + 1]
+            for other_column, other_row, inverse in done:
+                entry = other_column[step : step + 1]
+                pivot_row = pivot_row - entry * other_row
+                column_here = column_here - other_column * (entry * inverse)
+            pivot = column_here[step : step + 1]
+            inverse = 1.0 / pivot
+            done.append((column_here, pivot_row * inverse, inverse))
+            new_rows.append(pivot_row * lax.rsqrt(pivot))
+        rest = work
+        for column_here, scaled, _ in done:
+            rest = rest - column_here * scaled
+        work = jnp.where(height >= begin + width, rest, work)
+        for step, new_row in enumerate(new_rows, begin):
+            work = jnp.where(height == step, new_row, work)
+    upper_ref[...] = jnp.where(row <= column, work[:, joined : joined + block_cols], 0.0)
     weights = three_parts(work[:, :joined])
     wide = jnp.concatenate(
         [jnp.concatenate((part, part, part), axis=1) for part in weights], axis=0
     )
-    result = jnp.dot(wide, stack_ref[...], preferred_element_type=jnp.float32)
-    result = result[:block_cols] + result[block_cols : 2 * block_cols] + result[2 * block_cols :]
-    for line in range(lines):
-        block_ref[pl.ds(line, block_cols, stride=lines), :] = result[
-            :, line * lanes : (line + 1) * lanes
-        ]
-
-
-def finish(place, parts, stack, row_count, block_cols, group_cols, lines):
+    rows = lines // comps
+    copies = []
+    for comp in range(comps):
+        there = pl.ds(comp * rows * lanes, rows * lanes)
+        result = jnp.dot(wide, stack_ref[:, there], preferred_element_type=jnp.float32)
+        result = result[:block_cols] + result[block_cols : 2 * block_cols] + result[2 * block_cols :]
+        for index in range(rows):
+            block_scratch[pl.ds(comp * rows + index, block_cols, stride=lines), :] = result[
+                :, index * lanes : (index + 1) * lanes
+            ]
+        part = pl.ds(comp * rows, rows)
+        copies.append(
+            pltpu.make_async_copy(
+                block_scratch.reshape(block_cols, lines, lanes).at[:, part, :],
+                block_ref.at[:, part, :],
+                sems.at[comp],
+            )
+        )
+        copies[-1].start()
+    for copy in copies:
+        copy.wait()
+
+
+def finish(place, parts, stack, row_count, block_cols, group_cols, lines, comps):
     lanes = stack.shape[1] // lines
     basis_cols = parts.shape[2] // 2
     return pl.pallas_call(
-        functools.partial(finish_kernel, row_count),
+        functools.partial(finish_kernel, row_count, comps),
         out_shape=(
-            f32(block_cols * lines, lanes), f32(group_cols, block_cols), f32(block_cols, block_cols),
+            f32(block_cols, lines, lanes), f32(group_cols, block_cols), f32(block_cols, block_cols),
         ),
         in_specs=[SMEM] + [VMEM] * 2,
-        out_specs=(VMEM, VMEM, VMEM),
-        scratch_shapes=[pltpu.VMEM((basis_cols, block_cols), jnp.float32)],
+        out_specs=(HBM, VMEM, VMEM),
+        scratch_shapes=[
+            pltpu.VMEM((basis_cols, block_cols), jnp.float32),
+            pltpu.VMEM((block_cols * lines, lanes), jnp.float32),
+            pltpu.SemaphoreType.DMA((comps,)),
+        ],
         compiler_params=SCRATCH,
         name="finish",
     )(place, *kept(parts, stack))
@@ -495,7 +526,9 @@
     split = {0: own, **dict(zip(pieces, parts))}
     stack, part = sums(place, slab, fields, applied, got.pop("odd"), split, got, comps)
     parts = exchange(exchange_sum(part, "basis"), "space")
-    block, coeffs, upper = finish(place, parts, stack, row_count, block_cols, group_cols, lines)
+    block, coeffs, upper = finish(
+        place, parts, stack, row_count, block_cols, group_cols, lines, comps
+    )
     return (block.reshape(x_block.shape), coeffs, upper)
 
 

time: 37.9 us -> 37.8 us (level)
  no operation moved by 1% of the time
where the time goes in v11:
time: 37.8 us; the launch traced here: 37.6 us
  blocking collectives  12 us (32%)
  waiting for transfers between devices  9.11 us (24%)
  starting transfers between devices  7.86 us (21%)
  Pallas kernels  7.2 us (19%)
  between operations  1.35 us (4%)
    all_to_all x1, blocking collectives, exchange(): lax.all_to_all(jnp.broadcast_to(part[None], (count,) + part.shape), axis,...  12 us
    ppermute x3, waiting for transfers between devices, shards(): lax.ppermute(pieces[name - 1], 'basis', [(i, i ^ name) for i in range(cou...  6.49 us
    ppermute x2, starting transfers between devices, swap(): return lax.ppermute(values, axis, pairs + [(j, i) for i, j in pairs])  3.66 us
    pallas_call x1, Pallas kernels, finish(): pl.pallas_call(functools.partial(finish_kernel, row_count, comps), out_sh...  3.02 us
    ppermute x3, waiting for transfers between devices, exchange_sum(): lax.ppermute(part, axis, [(i, i ^ k) for i in range(count)])  2.62 us
    ppermute x3, starting transfers between devices, shards(): lax.ppermute(pieces[name - 1], 'basis', [(i, i ^ name) for i in range(cou...  2.27 us
    ppermute x3, starting transfers between devices, exchange_sum(): lax.ppermute(part, axis, [(i, i ^ k) for i in range(count)])  1.93 us
    pallas_call x1, Pallas kernels, ahead(): pl.pallas_call(ahead_kernel, out_shape=(near(rows, comps * comps * stride...  1.64 us
  transfers between devices with their start and end apart: 8, of which 4 were waited for; matrix products, arithmetic and copies ran while one was open for 0% of the time, Pallas kernels for 9%

profile of v11, /device:TPU:0, one launch (start us, length us, event | category | flops | bytes accessed | tf_op | source)
XLA Modules:
  0.0 37.6 jit_solution(5292747990927882410)
XLA Ops:
  0.6 3.0 %collective-permute-start = (f32[384,128]{1,0:T(8,128)}, f32[384,128]{1,0:T(8,128)S(1)}, u32[]{:S(2)}, u32[]{:S(2)}) collective-permute-start(f32[384,128]{1,0:T(8,128)} %bitcast.21), channel_id=1, source_target_pairs={{0,4},{8,12},{16,20},{24,28},{4,0},{12,8},{20,16},{28,24},{1,5},{9... | collective-permute-start | bytes 589832 | tf_op jit(solution)/shard_map/ppermute | solution.py:37
  3.6 1.3 %pack.1 = (f32[48,8,128]{2,1,0:T(8,128)S(1)}, f32[54,8,128]{2,1,0:T(8,128)S(1)}, f32[48,8,128]{2,1,0:T(8,128)S(1)}, f32[54,8,128]{2,1,0:T(8,128)S(1)}, f32[384,128]{1,0:T(8,128)S(1)}, /*index=5*/s32[8,128]{1,0:T(8,128)S(1)}) custom-call(s32[1]{0:T(128)} %bitcast.place_ref, f32[48,4,8,128]{3,2,1,0:T(8,128)} %bitcast.20, f32[384,128]{1,0:T(8,128)} %bitcast.22, ...), custom_call_target="tpu_custom_call" | custom-call | tf_op jit(solution)/shard_map/pack/pallas_call | solution.py:87
  5.0 0.7 %collective-permute-start.1 = (f32[54,8,128]{2,1,0:T(8,128)S(1)}, f32[54,8,128]{2,1,0:T(8,128)S(1)}, u32[]{:S(2)}, u32[]{:S(2)}) collective-permute-start(f32[54,8,128]{2,1,0:T(8,128)S(1)} %get-tuple-element.25), channel_id=1, source_target_pairs={{0,3},{1,2},{2,1},{3,0},{4,7},{5,6},{6,5},{7,4},{8,11},{9,10},{10,... | collective-permute-start | bytes 663560 | tf_op jit(solution)/shard_map/ppermute | solution.py:517
  5.7 1.0 %collective-permute-start.2 = (f32[54,8,128]{2,1,0:T(8,128)S(1)}, f32[54,8,128]{2,1,0:T(8,128)S(1)}, u32[]{:S(2)}, u32[]{:S(2)}) collective-permute-start(f32[54,8,128]{2,1,0:T(8,128)S(1)} %get-tuple-element.26), channel_id=1, source_target_pairs={{0,1},{1,0},{2,3},{3,2},{4,5},{5,4},{6,7},{7,6},{8,9},{9,8},{10,11... | collective-permute-start | bytes 663560 | tf_op jit(solution)/shard_map/ppermute | solution.py:517
  6.7 0.7 %collective-permute-start.3 = (f32[384,128]{1,0:T(8,128)}, f32[384,128]{1,0:T(8,128)S(1)}, u32[]{:S(2)}, u32[]{:S(2)}) collective-permute-start(f32[384,128]{1,0:T(8,128)} %bitcast.23), channel_id=1, source_target_pairs={{4,8},{12,16},{20,24},{8,4},{16,12},{24,20},{5,9},{13,17},{21,25},... | collective-permute-start | bytes 589832 | tf_op jit(solution)/shard_map/ppermute | solution.py:37
  7.4 0.6 %collective-permute-start.4 = (f32[48,8,128]{2,1,0:T(8,128)S(1)}, f32[48,8,128]{2,1,0:T(8,128)S(1)}, u32[]{:S(2)}, u32[]{:S(2)}) collective-permute-start(f32[48,8,128]{2,1,0:T(8,128)S(1)} %get-tuple-element.31), channel_id=1, source_target_pairs={{0,2},{1,3},{2,0},{3,1},{4,6},{5,7},{6,4},{7,5},{8,10},{9,11},{10,... | collective-permute-start | bytes 589832 | tf_op jit(solution)/shard_map/ppermute | solution.py:517
  8.6 1.6 %ahead.1 = (f32[8,72,128]{2,1,0:T(8,128)S(1)}, f32[24,16,128]{2,1,0:T(8,128)S(1)}, bf16[48,3072]{1,0:T(8,128)(2,1)S(1)}) custom-call(s32[1]{0:T(128)S(6)} %copy.14.sample_ref, f32[1024]{0:T(1024)} %refs_0_.1, f32[1024]{0:T(1024)} %refs_1_.1, f32[3,3,8,7]{3,2,1,0:T(8,128)} %bitcast.24, f32[3,3,8,7]{3,2,1,0:T(8,128)} %bitcast.25, f32[3,8]{1,0:T(4,128)} %bitcast.27, ...), custom_call_target="tpu_custom_call" | custom-call | tf_op jit(solution)/shard_map/ahead/pallas_call | solution.py:184
  10.2 0.0 collective-permute-done.halo_ref
  10.2 0.1 side.1.applied_ref
  10.3 2.4 %collective-permute-done.1 = f32[54,8,128]{2,1,0:T(8,128)S(1)} collective-permute-done((f32[54,8,128]{2,1,0:T(8,128)S(1)}, f32[54,8,128]{2,1,0:T(8,128)S(1)}, u32[]{:S(2)}, u32[]{:S(2)}) %collective-permute-start.1) | collective-permute-done | bytes 221216 | tf_op jit(solution)/shard_map/ppermute | solution.py:517
  12.7 0.0 collective-permute-done.2
  12.7 0.2 edges.1
  12.9 0.0 collective-permute-done.3.halo_ref
  12.9 4.1 %collective-permute-done.4 = f32[48,8,128]{2,1,0:T(8,128)S(1)} collective-permute-done((f32[48,8,128]{2,1,0:T(8,128)S(1)}, f32[48,8,128]{2,1,0:T(8,128)S(1)}, u32[]{:S(2)}, u32[]{:S(2)}) %collective-permute-start.4) | collective-permute-done | bytes 196640 | tf_op jit(solution)/shard_map/ppermute | solution.py:517
  17.0 1.0 %sums.1 = (bf16[240,3072]{1,0:T(8,128)(2,1)S(1)}, f32[32,128]{1,0:T(8,128)S(1)}) custom-call(s32[1]{0:T(128)} %bitcast.place_ref, s32[1]{0:T(128)} %bitcast.1.slab_ref, f32[8,72,128]{2,1,0:T(8,128)S(1)} %get-tuple-element.23.fields_ref, f32[24,16,128]{2,1,0:T(8,128)S(1)} %get-tuple-element.27.applied_ref, f32[384,128]{1,0:T(8,128)S(1)} %collective-permute-done.3.halo_ref, ...), custom_call_target="tpu_custom_call" | custom-call | tf_op jit(solution)/shard_map/sums/pallas_call | solution.py:368
  18.0 0.8 %collective-permute-start.7 = (f32[32,128]{1,0:T(8,128)S(1)}, f32[32,128]{1,0:T(8,128)S(1)}, u32[]{:S(2)}, u32[]{:S(2)}) collective-permute-start(f32[32,128]{1,0:T(8,128)S(1)} %get-tuple-element.32), channel_id=1, source_target_pairs={{0,3},{1,2},{2,1},{3,0},{4,7},{5,6},{6,5},{7,4},{8,11},{9,10},{10,... | collective-permute-start | bytes 49160 | tf_op jit(solution)/shard_map/ppermute | solution.py:384
  18.7 1.0 %collective-permute-start.6 = (f32[32,128]{1,0:T(8,128)S(1)}, f32[32,128]{1,0:T(8,128)S(1)}, u32[]{:S(2)}, u32[]{:S(2)}) collective-permute-start(f32[32,128]{1,0:T(8,128)S(1)} %get-tuple-element.32), channel_id=1, source_target_pairs={{0,2},{1,3},{2,0},{3,1},{4,6},{5,7},{6,4},{7,5},{8,10},{9,11},{10,... | collective-permute-start | bytes 49160 | tf_op jit(solution)/shard_map/ppermute | solution.py:384
  19.7 0.2 collective-permute-start.5
  19.9 1.3 %collective-permute-done.7 = f32[32,128]{1,0:T(8,128)S(1)} collective-permute-done((f32[32,128]{1,0:T(8,128)S(1)}, f32[32,128]{1,0:T(8,128)S(1)}, u32[]{:S(2)}, u32[]{:S(2)}) %collective-permute-start.7) | collective-permute-done | bytes 16416 | tf_op jit(solution)/shard_map/ppermute | solution.py:384
  21.2 1.3 %collective-permute-done.6 = f32[32,128]{1,0:T(8,128)S(1)} collective-permute-done((f32[32,128]{1,0:T(8,128)S(1)}, f32[32,128]{1,0:T(8,128)S(1)}, u32[]{:S(2)}, u32[]{:S(2)}) %collective-permute-start.6) | collective-permute-done | bytes 16416 | tf_op jit(solution)/shard_map/ppermute | solution.py:384
  22.5 0.0 collective-permute-done.5
  22.5 12.0 %all_to_all.5.parts_ref = f32[8,32,128]{2,1,0:T(8,128)S(1)} all-to-all(f32[8,32,128]{2,1,0:T(8,128)S(1)} %broadcast_in_dim.2), channel_id=1, replica_groups=mesh['space'=8,'basis'=4] {'space'}, dimensions={0} | all-to-all | bytes 262144 | tf_op jit(solution)/shard_map/all_to_all | solution.py:393
  34.5 3.0 %finish.1 = (f32[16,24,128]{2,1,0:T(8,128)}, f32[16,16]{1,0:T(8,128)}, f32[16,16]{1,0:T(8,128)}) custom-call(s32[1]{0:T(128)} %bitcast.place_ref, f32[8,32,128]{2,1,0:T(8,128)S(1)} %all_to_all.5.parts_ref, bf16[240,3072]{1,0:T(8,128)(2,1)S(1)} %get-tuple-element.33.stack_ref), custom_call_target="tpu_custom_call" | custom-call | tf_op jit(solution)/shard_map/finish/pallas_call | solution.py:480
  (2 shorter events, 0.0 us)
Async XLA Ops:
  0.6 9.6 %collective-permute-start = (f32[384,128]{1,0:T(8,128)}, f32[384,128]{1,0:T(8,128)S(1)}, u32[]{:S(2)}, u32[]{:S(2)}) collective-permute-start(f32[384,128]{1,0:T(8,128)} %bitcast.21), channel_id=1, source_target_pairs={{0,4},{8,12},{16,20},{24,28},{4,0},{12,8},{20,16},{28,24},{1,5},{9... | collective-permute-start | bytes 589832 | tf_op jit(solution)/shard_map/ppermute | solution.py:37
  5.0 7.7 %collective-permute-start.1 = (f32[54,8,128]{2,1,0:T(8,128)S(1)}, f32[54,8,128]{2,1,0:T(8,128)S(1)}, u32[]{:S(2)}, u32[]{:S(2)}) collective-permute-start(f32[54,8,128]{2,1,0:T(8,128)S(1)} %get-tuple-element.25), channel_id=1, source_target_pairs={{0,3},{1,2},{2,1},{3,0},{4,7},{5,6},{6,5},{7,4},{8,11},{9,10},{10,... | collective-permute-start | bytes 663560 | tf_op jit(solution)/shard_map/ppermute | solution.py:517
  5.7 7.0 %collective-permute-start.2 = (f32[54,8,128]{2,1,0:T(8,128)S(1)}, f32[54,8,128]{2,1,0:T(8,128)S(1)}, u32[]{:S(2)}, u32[]{:S(2)}) collective-permute-start(f32[54,8,128]{2,1,0:T(8,128)S(1)} %get-tuple-element.26), channel_id=1, source_target_pairs={{0,1},{1,0},{2,3},{3,2},{4,5},{5,4},{6,7},{7,6},{8,9},{9,8},{10,11... | collective-permute-start | bytes 663560 | tf_op jit(solution)/shard_map/ppermute | solution.py:517
  6.7 6.2 %collective-permute-start.3 = (f32[384,128]{1,0:T(8,128)}, f32[384,128]{1,0:T(8,128)S(1)}, u32[]{:S(2)}, u32[]{:S(2)}) collective-permute-start(f32[384,128]{1,0:T(8,128)} %bitcast.23), channel_id=1, source_target_pairs={{4,8},{12,16},{20,24},{8,4},{16,12},{24,20},{5,9},{13,17},{21,25},... | collective-permute-start | bytes 589832 | tf_op jit(solution)/shard_map/ppermute | solution.py:37
  7.4 9.6 %collective-permute-start.4 = (f32[48,8,128]{2,1,0:T(8,128)S(1)}, f32[48,8,128]{2,1,0:T(8,128)S(1)}, u32[]{:S(2)}, u32[]{:S(2)}) collective-permute-start(f32[48,8,128]{2,1,0:T(8,128)S(1)} %get-tuple-element.31), channel_id=1, source_target_pairs={{0,2},{1,3},{2,0},{3,1},{4,6},{5,7},{6,4},{7,5},{8,10},{9,11},{10,... | collective-permute-start | bytes 589832 | tf_op jit(solution)/shard_map/ppermute | solution.py:517
  18.0 3.2 %collective-permute-start.7 = (f32[32,128]{1,0:T(8,128)S(1)}, f32[32,128]{1,0:T(8,128)S(1)}, u32[]{:S(2)}, u32[]{:S(2)}) collective-permute-start(f32[32,128]{1,0:T(8,128)S(1)} %get-tuple-element.32), channel_id=1, source_target_pairs={{0,3},{1,2},{2,1},{3,0},{4,7},{5,6},{6,5},{7,4},{8,11},{9,10},{10,... | collective-permute-start | bytes 49160 | tf_op jit(solution)/shard_map/ppermute | solution.py:384
  18.7 3.8 %collective-permute-start.6 = (f32[32,128]{1,0:T(8,128)S(1)}, f32[32,128]{1,0:T(8,128)S(1)}, u32[]{:S(2)}, u32[]{:S(2)}) collective-permute-start(f32[32,128]{1,0:T(8,128)S(1)} %get-tuple-element.32), channel_id=1, source_target_pairs={{0,2},{1,3},{2,0},{3,1},{4,6},{5,7},{6,4},{7,5},{8,10},{9,11},{10,... | collective-permute-start | bytes 49160 | tf_op jit(solution)/shard_map/ppermute | solution.py:384
  19.7 2.8 %collective-permute-start.5 = (f32[32,128]{1,0:T(8,128)S(1)}, f32[32,128]{1,0:T(8,128)S(1)}, u32[]{:S(2)}, u32[]{:S(2)}) collective-permute-start(f32[32,128]{1,0:T(8,128)S(1)} %get-tuple-element.32), channel_id=1, source_target_pairs={{0,1},{1,0},{2,3},{3,2},{4,5},{5,4},{6,7},{7,6},{8,9},{9,8},{10,11... | collective-permute-start | bytes 49160 | tf_op jit(solution)/shard_map/ppermute | solution.py:384

commit v12 on v11

--- a/solution.py
+++ b/solution.py
@@ -380,12 +380,11 @@
 
 def exchange_sum(part, axis):
     count = lax.axis_size(axis)
-    terms = [part] + [
-        lax.ppermute(part, axis, [(i, i ^ k) for i in range(count)]) for k in range(1, count)
-    ]
-    while len(terms) > 1:
-        terms = [a + b for a, b in zip(terms[::2], terms[1::2])]
-    return terms[0]
+    mask = 1
+    while mask < count:
+        part = part + lax.ppermute(part, axis, [(i, i ^ mask) for i in range(count)])
+        mask *= 2
+    return part
 
 
 def exchange(part, axis):
@@ -395,7 +394,7 @@
 
 def finish_kernel(
     row_count, comps, place_ref, parts_ref, stack_ref, block_ref, coeffs_ref, upper_ref,
-    coeffs_scratch, block_scratch, sems,
+    coeffs_scratch, upper_scratch, block_scratch, sems,
 ):
     block_cols = upper_ref.shape[0]
     basis_cols = parts_ref.shape[2] // 2
@@ -418,7 +417,12 @@
     coeffs_scratch[...] = coeffs.T
     group_cols = coeffs_ref.shape[0]
     start = pl.multiple_of(place_ref[0] * group_cols, group_cols)
-    coeffs_ref[...] = coeffs_scratch[pl.ds(start, group_cols), :]
+    copies = [
+        pltpu.make_async_copy(
+            coeffs_scratch.at[pl.ds(start, group_cols)], coeffs_ref, sems.at[comps]
+        )
+    ]
+    copies[0].start()
 
     row = lax.broadcasted_iota(jnp.int32, (block_cols, block_cols), 0)
     column = lax.broadcasted_iota(jnp.int32, (block_cols, block_cols), 1)
@@ -446,13 +450,14 @@
         work = jnp.where(height >= begin + width, rest, work)
         for step, new_row in enumerate(new_rows, begin):
             work = jnp.where(height == step, new_row, work)
-    upper_ref[...] = jnp.where(row <= column, work[:, joined : joined + block_cols], 0.0)
+    upper_scratch[...] = jnp.where(row <= column, work[:, joined : joined + block_cols], 0.0)
+    copies.append(pltpu.make_async_copy(upper_scratch, upper_ref, sems.at[comps + 1]))
+    copies[1].start()
     weights = three_parts(work[:, :joined])
     wide = jnp.concatenate(
         [jnp.concatenate((part, part, part), axis=1) for part in weights], axis=0
     )
     rows = lines // comps
-    copies = []
     for comp in range(comps):
         there = pl.ds(comp * rows * lanes, rows * lanes)
         result = jnp.dot(wide, stack_ref[:, there], preferred_element_type=jnp.float32)
@@ -483,11 +488,12 @@
             f32(block_cols, lines, lanes), f32(group_cols, block_cols), f32(block_cols, block_cols),
         ),
         in_specs=[SMEM] + [VMEM] * 2,
-        out_specs=(HBM, VMEM, VMEM),
+        out_specs=(HBM,) * 3,
         scratch_shapes=[
             pltpu.VMEM((basis_cols, block_cols), jnp.float32),
+            pltpu.VMEM((block_cols, block_cols), jnp.float32),
             pltpu.VMEM((block_cols * lines, lanes), jnp.float32),
-            pltpu.SemaphoreType.DMA((comps,)),
+            pltpu.SemaphoreType.DMA((comps + 2,)),
         ],
         compiler_params=SCRATCH,
         name="finish",

time: 37.8 us -> 37.7 us (level)
  waiting for transfers between devices: 9.11 us -> 10.4 us
  starting transfers between devices: 7.86 us -> 7.02 us
  Pallas kernels: 7.2 us -> 6.63 us
    ppermute x3 -> x2, waiting for transfers between devices: 2.62 us -> 3.9 us  [exchange_sum(): lax.ppermute(part, axis, [(i, i ^ mask) for i in range(count)])]
    ppermute x3 -> x2, starting transfers between devices: 1.93 us -> 1.09 us  [exchange_sum(): lax.ppermute(part, axis, [(i, i ^ mask) for i in range(count)])]
    pallas_call x1, Pallas kernels: 3.02 us -> 2.44 us  [finish(): pl.pallas_call(functools.partial(finish_kernel, row_count, comps), out_sh...]
  transfers between devices with their start and end apart: 8 -> 7, of which waited for: 4 -> 4; matrix products, arithmetic and copies ran while one was open for 0% -> 0% of each run, Pallas kernels for 9% -> 9%
where the time goes in v12:
time: 37.7 us; the launch traced here: 37.4 us
  blocking collectives  12 us (32%)
  waiting for transfers between devices  10.4 us (28%)
  starting transfers between devices  7.02 us (19%)
  Pallas kernels  6.63 us (18%)
  between operations  1.34 us (4%)
    all_to_all x1, blocking collectives, exchange(): lax.all_to_all(jnp.broadcast_to(part[None], (count,) + part.shape), axis,...  12 us
    ppermute x3, waiting for transfers between devices, shards(): lax.ppermute(pieces[name - 1], 'basis', [(i, i ^ name) for i in range(cou...  6.49 us
    ppermute x2, waiting for transfers between devices, exchange_sum(): lax.ppermute(part, axis, [(i, i ^ mask) for i in range(count)])  3.9 us
    ppermute x2, starting transfers between devices, swap(): return lax.ppermute(values, axis, pairs + [(j, i) for i, j in pairs])  3.66 us
    pallas_call x1, Pallas kernels, finish(): pl.pallas_call(functools.partial(finish_kernel, row_count, comps), out_sh...  2.44 us
    ppermute x3, starting transfers between devices, shards(): lax.ppermute(pieces[name - 1], 'basis', [(i, i ^ name) for i in range(cou...  2.27 us
    pallas_call x1, Pallas kernels, ahead(): pl.pallas_call(ahead_kernel, out_shape=(near(rows, comps * comps * stride...  1.64 us
    pallas_call x1, Pallas kernels, pack(): pl.pallas_call(functools.partial(pack_kernel, comps), out_shape=(*pieces,...  1.34 us
  transfers between devices with their start and end apart: 7, of which 4 were waited for; matrix products, arithmetic and copies ran while one was open for 0% of the time, Pallas kernels for 9%

profile of v12, /device:TPU:0, one launch (start us, length us, event | category | flops | bytes accessed | tf_op | source)
XLA Modules:
  0.0 37.4 jit_solution(11931539878114398316)
XLA Ops:
  0.6 3.0 %collective-permute-start = (f32[384,128]{1,0:T(8,128)}, f32[384,128]{1,0:T(8,128)S(1)}, u32[]{:S(2)}, u32[]{:S(2)}) collective-permute-start(f32[384,128]{1,0:T(8,128)} %bitcast.21), channel_id=1, source_target_pairs={{0,4},{8,12},{16,20},{24,28},{4,0},{12,8},{20,16},{28,24},{1,5},{9... | collective-permute-start | bytes 589832 | tf_op jit(solution)/shard_map/ppermute | solution.py:37
  3.6 1.3 %pack.1 = (f32[48,8,128]{2,1,0:T(8,128)S(1)}, f32[54,8,128]{2,1,0:T(8,128)S(1)}, f32[48,8,128]{2,1,0:T(8,128)S(1)}, f32[54,8,128]{2,1,0:T(8,128)S(1)}, f32[384,128]{1,0:T(8,128)S(1)}, /*index=5*/s32[8,128]{1,0:T(8,128)S(1)}) custom-call(s32[1]{0:T(128)} %bitcast.place_ref, f32[48,4,8,128]{3,2,1,0:T(8,128)} %bitcast.20, f32[384,128]{1,0:T(8,128)} %bitcast.22, ...), custom_call_target="tpu_custom_call" | custom-call | tf_op jit(solution)/shard_map/pack/pallas_call | solution.py:87
  5.0 0.7 %collective-permute-start.1 = (f32[54,8,128]{2,1,0:T(8,128)S(1)}, f32[54,8,128]{2,1,0:T(8,128)S(1)}, u32[]{:S(2)}, u32[]{:S(2)}) collective-permute-start(f32[54,8,128]{2,1,0:T(8,128)S(1)} %get-tuple-element.25), channel_id=1, source_target_pairs={{0,3},{1,2},{2,1},{3,0},{4,7},{5,6},{6,5},{7,4},{8,11},{9,10},{10,... | collective-permute-start | bytes 663560 | tf_op jit(solution)/shard_map/ppermute | solution.py:523
  5.7 1.0 %collective-permute-start.2 = (f32[54,8,128]{2,1,0:T(8,128)S(1)}, f32[54,8,128]{2,1,0:T(8,128)S(1)}, u32[]{:S(2)}, u32[]{:S(2)}) collective-permute-start(f32[54,8,128]{2,1,0:T(8,128)S(1)} %get-tuple-element.26), channel_id=1, source_target_pairs={{0,1},{1,0},{2,3},{3,2},{4,5},{5,4},{6,7},{7,6},{8,9},{9,8},{10,11... | collective-permute-start | bytes 663560 | tf_op jit(solution)/shard_map/ppermute | solution.py:523
  6.7 0.7 %collective-permute-start.3 = (f32[384,128]{1,0:T(8,128)}, f32[384,128]{1,0:T(8,128)S(1)}, u32[]{:S(2)}, u32[]{:S(2)}) collective-permute-start(f32[384,128]{1,0:T(8,128)} %bitcast.23), channel_id=1, source_target_pairs={{4,8},{12,16},{20,24},{8,4},{16,12},{24,20},{5,9},{13,17},{21,25},... | collective-permute-start | bytes 589832 | tf_op jit(solution)/shard_map/ppermute | solution.py:37
  7.4 0.6 %collective-permute-start.4 = (f32[48,8,128]{2,1,0:T(8,128)S(1)}, f32[48,8,128]{2,1,0:T(8,128)S(1)}, u32[]{:S(2)}, u32[]{:S(2)}) collective-permute-start(f32[48,8,128]{2,1,0:T(8,128)S(1)} %get-tuple-element.31), channel_id=1, source_target_pairs={{0,2},{1,3},{2,0},{3,1},{4,6},{5,7},{6,4},{7,5},{8,10},{9,11},{10,... | collective-permute-start | bytes 589832 | tf_op jit(solution)/shard_map/ppermute | solution.py:523
  8.6 1.6 %ahead.1 = (f32[8,72,128]{2,1,0:T(8,128)S(1)}, f32[24,16,128]{2,1,0:T(8,128)S(1)}, bf16[48,3072]{1,0:T(8,128)(2,1)S(1)}) custom-call(s32[1]{0:T(128)S(6)} %copy.14.sample_ref, f32[1024]{0:T(1024)} %refs_0_.1, f32[1024]{0:T(1024)} %refs_1_.1, f32[3,3,8,7]{3,2,1,0:T(8,128)} %bitcast.24, f32[3,3,8,7]{3,2,1,0:T(8,128)} %bitcast.25, f32[3,8]{1,0:T(4,128)} %bitcast.27, ...), custom_call_target="tpu_custom_call" | custom-call | tf_op jit(solution)/shard_map/ahead/pallas_call | solution.py:184
  10.2 0.0 collective-permute-done.halo_ref
  10.2 0.1 side.1.applied_ref
  10.3 2.4 %collective-permute-done.1 = f32[54,8,128]{2,1,0:T(8,128)S(1)} collective-permute-done((f32[54,8,128]{2,1,0:T(8,128)S(1)}, f32[54,8,128]{2,1,0:T(8,128)S(1)}, u32[]{:S(2)}, u32[]{:S(2)}) %collective-permute-start.1) | collective-permute-done | bytes 221216 | tf_op jit(solution)/shard_map/ppermute | solution.py:523
  12.7 0.0 collective-permute-done.2
  12.7 0.2 edges.1
  12.9 0.0 collective-permute-done.3.halo_ref
  12.9 4.1 %collective-permute-done.4 = f32[48,8,128]{2,1,0:T(8,128)S(1)} collective-permute-done((f32[48,8,128]{2,1,0:T(8,128)S(1)}, f32[48,8,128]{2,1,0:T(8,128)S(1)}, u32[]{:S(2)}, u32[]{:S(2)}) %collective-permute-start.4) | collective-permute-done | bytes 196640 | tf_op jit(solution)/shard_map/ppermute | solution.py:523
  17.0 1.0 %sums.1 = (bf16[240,3072]{1,0:T(8,128)(2,1)S(1)}, f32[32,128]{1,0:T(8,128)S(1)}) custom-call(s32[1]{0:T(128)} %bitcast.place_ref, s32[1]{0:T(128)} %bitcast.1.slab_ref, f32[8,72,128]{2,1,0:T(8,128)S(1)} %get-tuple-element.23.fields_ref, f32[24,16,128]{2,1,0:T(8,128)S(1)} %get-tuple-element.27.applied_ref, f32[384,128]{1,0:T(8,128)S(1)} %collective-permute-done.3.halo_ref, ...), custom_call_target="tpu_custom_call" | custom-call | tf_op jit(solution)/shard_map/sums/pallas_call | solution.py:368
  18.0 0.1 collective-permute-start.5
  18.1 1.1 %collective-permute-done.5 = f32[32,128]{1,0:T(8,128)S(1)} collective-permute-done((f32[32,128]{1,0:T(8,128)S(1)}, f32[32,128]{1,0:T(8,128)S(1)}, u32[]{:S(2)}, u32[]{:S(2)}) %collective-permute-start.5) | collective-permute-done | bytes 16416 | tf_op jit(solution)/shard_map/ppermute | solution.py:385
  19.2 1.0 %collective-permute-start.6 = (f32[32,128]{1,0:T(8,128)S(1)}, f32[32,128]{1,0:T(8,128)S(1)}, u32[]{:S(2)}, u32[]{:S(2)}) collective-permute-start(f32[32,128]{1,0:T(8,128)S(1)} %add.6), channel_id=1, source_target_pairs={{0,2},{1,3},{2,0},{3,1},{4,6},{5,7},{6,4},{7,5},{8,10},{9,11},{10,... | collective-permute-start | bytes 49160 | tf_op jit(solution)/shard_map/ppermute | solution.py:385
  20.2 2.8 %collective-permute-done.6 = f32[32,128]{1,0:T(8,128)S(1)} collective-permute-done((f32[32,128]{1,0:T(8,128)S(1)}, f32[32,128]{1,0:T(8,128)S(1)}, u32[]{:S(2)}, u32[]{:S(2)}) %collective-permute-start.6) | collective-permute-done | bytes 16416 | tf_op jit(solution)/shard_map/ppermute | solution.py:385
  23.0 12.0 %all_to_all.5.parts_ref = f32[8,32,128]{2,1,0:T(8,128)S(1)} all-to-all(f32[8,32,128]{2,1,0:T(8,128)S(1)} %broadcast_in_dim.2), channel_id=1, replica_groups=mesh['space'=8,'basis'=4] {'space'}, dimensions={0} | all-to-all | bytes 262144 | tf_op jit(solution)/shard_map/all_to_all | solution.py:392
  35.0 2.4 %finish.1 = (f32[16,24,128]{2,1,0:T(8,128)}, f32[16,16]{1,0:T(8,128)}, f32[16,16]{1,0:T(8,128)}) custom-call(s32[1]{0:T(128)} %bitcast.place_ref, f32[8,32,128]{2,1,0:T(8,128)S(1)} %all_to_all.5.parts_ref, bf16[240,3072]{1,0:T(8,128)(2,1)S(1)} %get-tuple-element.33.stack_ref), custom_call_target="tpu_custom_call" | custom-call | tf_op jit(solution)/shard_map/finish/pallas_call | solution.py:485
  (3 shorter events, 0.0 us)
Async XLA Ops:
  0.6 9.6 %collective-permute-start = (f32[384,128]{1,0:T(8,128)}, f32[384,128]{1,0:T(8,128)S(1)}, u32[]{:S(2)}, u32[]{:S(2)}) collective-permute-start(f32[384,128]{1,0:T(8,128)} %bitcast.21), channel_id=1, source_target_pairs={{0,4},{8,12},{16,20},{24,28},{4,0},{12,8},{20,16},{28,24},{1,5},{9... | collective-permute-start | bytes 589832 | tf_op jit(solution)/shard_map/ppermute | solution.py:37
  5.0 7.7 %collective-permute-start.1 = (f32[54,8,128]{2,1,0:T(8,128)S(1)}, f32[54,8,128]{2,1,0:T(8,128)S(1)}, u32[]{:S(2)}, u32[]{:S(2)}) collective-permute-start(f32[54,8,128]{2,1,0:T(8,128)S(1)} %get-tuple-element.25), channel_id=1, source_target_pairs={{0,3},{1,2},{2,1},{3,0},{4,7},{5,6},{6,5},{7,4},{8,11},{9,10},{10,... | collective-permute-start | bytes 663560 | tf_op jit(solution)/shard_map/ppermute | solution.py:523
  5.7 7.0 %collective-permute-start.2 = (f32[54,8,128]{2,1,0:T(8,128)S(1)}, f32[54,8,128]{2,1,0:T(8,128)S(1)}, u32[]{:S(2)}, u32[]{:S(2)}) collective-permute-start(f32[54,8,128]{2,1,0:T(8,128)S(1)} %get-tuple-element.26), channel_id=1, source_target_pairs={{0,1},{1,0},{2,3},{3,2},{4,5},{5,4},{6,7},{7,6},{8,9},{9,8},{10,11... | collective-permute-start | bytes 663560 | tf_op jit(solution)/shard_map/ppermute | solution.py:523
  6.7 6.2 %collective-permute-start.3 = (f32[384,128]{1,0:T(8,128)}, f32[384,128]{1,0:T(8,128)S(1)}, u32[]{:S(2)}, u32[]{:S(2)}) collective-permute-start(f32[384,128]{1,0:T(8,128)} %bitcast.23), channel_id=1, source_target_pairs={{4,8},{12,16},{20,24},{8,4},{16,12},{24,20},{5,9},{13,17},{21,25},... | collective-permute-start | bytes 589832 | tf_op jit(solution)/shard_map/ppermute | solution.py:37
  7.4 9.6 %collective-permute-start.4 = (f32[48,8,128]{2,1,0:T(8,128)S(1)}, f32[48,8,128]{2,1,0:T(8,128)S(1)}, u32[]{:S(2)}, u32[]{:S(2)}) collective-permute-start(f32[48,8,128]{2,1,0:T(8,128)S(1)} %get-tuple-element.31), channel_id=1, source_target_pairs={{0,2},{1,3},{2,0},{3,1},{4,6},{5,7},{6,4},{7,5},{8,10},{9,11},{10,... | collective-permute-start | bytes 589832 | tf_op jit(solution)/shard_map/ppermute | solution.py:523
  18.0 1.2 %collective-permute-start.5 = (f32[32,128]{1,0:T(8,128)S(1)}, f32[32,128]{1,0:T(8,128)S(1)}, u32[]{:S(2)}, u32[]{:S(2)}) collective-permute-start(f32[32,128]{1,0:T(8,128)S(1)} %get-tuple-element.32), channel_id=1, source_target_pairs={{0,1},{1,0},{2,3},{3,2},{4,5},{5,4},{6,7},{7,6},{8,9},{9,8},{10,11... | collective-permute-start | bytes 49160 | tf_op jit(solution)/shard_map/ppermute | solution.py:385
  19.2 3.7 %collective-permute-start.6 = (f32[32,128]{1,0:T(8,128)S(1)}, f32[32,128]{1,0:T(8,128)S(1)}, u32[]{:S(2)}, u32[]{:S(2)}) collective-permute-start(f32[32,128]{1,0:T(8,128)S(1)} %add.6), channel_id=1, source_target_pairs={{0,2},{1,3},{2,0},{3,1},{4,6},{5,7},{6,4},{7,5},{8,10},{9,11},{10,... | collective-permute-start | bytes 49160 | tf_op jit(solution)/shard_map/ppermute | solution.py:385

commit v13 on v12

--- a/solution.py
+++ b/solution.py
@@ -378,18 +378,21 @@
     )(place, slab, *kept(fields, applied, halo, *split.values(), *raw.values()))
 
 
-def exchange_sum(part, axis):
+def pair_sum(part, axis, mask):
     count = lax.axis_size(axis)
+    return part + lax.ppermute(part, axis, [(i, i ^ mask) for i in range(count)])
+
+
+def exchange_all(part):
     mask = 1
-    while mask < count:
-        part = part + lax.ppermute(part, axis, [(i, i ^ mask) for i in range(count)])
+    while mask < lax.axis_size("basis"):
+        part = pair_sum(part, "basis", mask)
         mask *= 2
-    return part
-
-
-def exchange(part, axis):
-    count = lax.axis_size(axis)
-    return lax.all_to_all(jnp.broadcast_to(part[None], (count,) + part.shape), axis, 0, 0)
+    part = pair_sum(part, "space", 1)
+    count = lax.axis_size("space")
+    groups = [list(range(first, count, 2)) for first in range(2)]
+    copies = jnp.broadcast_to(part[None], (count // 2,) + part.shape)
+    return lax.all_to_all(copies, "space", 0, 0, axis_index_groups=groups)
 
 
 def finish_kernel(
@@ -531,7 +534,7 @@
     applied, *parts = add_edges(place, fields, applied, pieces, comps, group_cols)
     split = {0: own, **dict(zip(pieces, parts))}
     stack, part = sums(place, slab, fields, applied, got.pop("odd"), split, got, comps)
-    parts = exchange(exchange_sum(part, "basis"), "space")
+    parts = exchange_all(part)
     block, coeffs, upper = finish(
         place, parts, stack, row_count, block_cols, group_cols, lines, comps
     )

time: 37.7 us -> 39.8 us (1.056)
  waiting for transfers between devices: 10.4 us -> 12.9 us
  blocking collectives: 12 us -> 10.4 us
  starting transfers between devices: 7.02 us -> 8.26 us
    ppermute x2 -> x3, waiting for transfers between devices: 3.9 us -> 6.4 us  [pair_sum(): lax.ppermute(part, axis, [(i, i ^ mask) for i in range(count)])]
    all_to_all x1, blocking collectives: 12 us -> 10.4 us  [exchange_all(): return lax.all_to_all(copies, 'space', 0, 0, axis_index_groups=groups)]
    ppermute x2 -> x3, starting transfers between devices: 1.09 us -> 2.32 us  [pair_sum(): lax.ppermute(part, axis, [(i, i ^ mask) for i in range(count)])]
  transfers between devices with their start and end apart: 7 -> 8, of which waited for: 4 -> 5; matrix products, arithmetic and copies ran while one was open for 0% -> 0% of each run, Pallas kernels for 9% -> 8%
where the time goes in v13:
time: 39.8 us; the launch traced here: 39.6 us
  waiting for transfers between devices  12.9 us (32%)
  blocking collectives  10.4 us (26%)
  starting transfers between devices  8.26 us (21%)
  Pallas kernels  6.63 us (17%)
  between operations  1.35 us (3%)
    all_to_all x1, blocking collectives, exchange_all(): return lax.all_to_all(copies, 'space', 0, 0, axis_index_groups=groups)  10.4 us
    ppermute x3, waiting for transfers between devices, shards(): lax.ppermute(pieces[name - 1], 'basis', [(i, i ^ name) for i in range(cou...  6.49 us
    ppermute x3, waiting for transfers between devices, pair_sum(): lax.ppermute(part, axis, [(i, i ^ mask) for i in range(count)])  6.4 us
    ppermute x2, starting transfers between devices, swap(): return lax.ppermute(values, axis, pairs + [(j, i) for i, j in pairs])  3.66 us
    pallas_call x1, Pallas kernels, finish(): pl.pallas_call(functools.partial(finish_kernel, row_count, comps), out_sh...  2.44 us
    ppermute x3, starting transfers between devices, pair_sum(): lax.ppermute(part, axis, [(i, i ^ mask) for i in range(count)])  2.32 us
    ppermute x3, starting transfers between devices, shards(): lax.ppermute(pieces[name - 1], 'basis', [(i, i ^ name) for i in range(cou...  2.27 us
    pallas_call x1, Pallas kernels, ahead(): pl.pallas_call(ahead_kernel, out_shape=(near(rows, comps * comps * stride...  1.64 us
  transfers between devices with their start and end apart: 8, of which 5 were waited for; matrix products, arithmetic and copies ran while one was open for 0% of the time, Pallas kernels for 8%

profile of v13, /device:TPU:0, one launch (start us, length us, event | category | flops | bytes accessed | tf_op | source)
XLA Modules:
  0.0 39.6 jit_solution(17585824472439179695)
XLA Ops:
  0.6 3.0 %collective-permute-start = (f32[384,128]{1,0:T(8,128)}, f32[384,128]{1,0:T(8,128)S(1)}, u32[]{:S(2)}, u32[]{:S(2)}) collective-permute-start(f32[384,128]{1,0:T(8,128)} %bitcast.21), channel_id=1, source_target_pairs={{0,4},{8,12},{16,20},{24,28},{4,0},{12,8},{20,16},{28,24},{1,5},{9... | collective-permute-start | bytes 589832 | tf_op jit(solution)/shard_map/ppermute | solution.py:37
  3.6 1.3 %pack.1 = (f32[48,8,128]{2,1,0:T(8,128)S(1)}, f32[54,8,128]{2,1,0:T(8,128)S(1)}, f32[48,8,128]{2,1,0:T(8,128)S(1)}, f32[54,8,128]{2,1,0:T(8,128)S(1)}, f32[384,128]{1,0:T(8,128)S(1)}, /*index=5*/s32[8,128]{1,0:T(8,128)S(1)}) custom-call(s32[1]{0:T(128)} %bitcast.place_ref, f32[48,4,8,128]{3,2,1,0:T(8,128)} %bitcast.20, f32[384,128]{1,0:T(8,128)} %bitcast.22, ...), custom_call_target="tpu_custom_call" | custom-call | tf_op jit(solution)/shard_map/pack/pallas_call | solution.py:87
  5.0 0.7 %collective-permute-start.1 = (f32[54,8,128]{2,1,0:T(8,128)S(1)}, f32[54,8,128]{2,1,0:T(8,128)S(1)}, u32[]{:S(2)}, u32[]{:S(2)}) collective-permute-start(f32[54,8,128]{2,1,0:T(8,128)S(1)} %get-tuple-element.25), channel_id=1, source_target_pairs={{0,3},{1,2},{2,1},{3,0},{4,7},{5,6},{6,5},{7,4},{8,11},{9,10},{10,... | collective-permute-start | bytes 663560 | tf_op jit(solution)/shard_map/ppermute | solution.py:526
  5.7 1.0 %collective-permute-start.2 = (f32[54,8,128]{2,1,0:T(8,128)S(1)}, f32[54,8,128]{2,1,0:T(8,128)S(1)}, u32[]{:S(2)}, u32[]{:S(2)}) collective-permute-start(f32[54,8,128]{2,1,0:T(8,128)S(1)} %get-tuple-element.26), channel_id=1, source_target_pairs={{0,1},{1,0},{2,3},{3,2},{4,5},{5,4},{6,7},{7,6},{8,9},{9,8},{10,11... | collective-permute-start | bytes 663560 | tf_op jit(solution)/shard_map/ppermute | solution.py:526
  6.7 0.7 %collective-permute-start.3 = (f32[384,128]{1,0:T(8,128)}, f32[384,128]{1,0:T(8,128)S(1)}, u32[]{:S(2)}, u32[]{:S(2)}) collective-permute-start(f32[384,128]{1,0:T(8,128)} %bitcast.23), channel_id=1, source_target_pairs={{4,8},{12,16},{20,24},{8,4},{16,12},{24,20},{5,9},{13,17},{21,25},... | collective-permute-start | bytes 589832 | tf_op jit(solution)/shard_map/ppermute | solution.py:37
  7.4 0.6 %collective-permute-start.4 = (f32[48,8,128]{2,1,0:T(8,128)S(1)}, f32[48,8,128]{2,1,0:T(8,128)S(1)}, u32[]{:S(2)}, u32[]{:S(2)}) collective-permute-start(f32[48,8,128]{2,1,0:T(8,128)S(1)} %get-tuple-element.31), channel_id=1, source_target_pairs={{0,2},{1,3},{2,0},{3,1},{4,6},{5,7},{6,4},{7,5},{8,10},{9,11},{10,... | collective-permute-start | bytes 589832 | tf_op jit(solution)/shard_map/ppermute | solution.py:526
  8.6 1.6 %ahead.1 = (f32[8,72,128]{2,1,0:T(8,128)S(1)}, f32[24,16,128]{2,1,0:T(8,128)S(1)}, bf16[48,3072]{1,0:T(8,128)(2,1)S(1)}) custom-call(s32[1]{0:T(128)S(6)} %copy.14.sample_ref, f32[1024]{0:T(1024)} %refs_0_.1, f32[1024]{0:T(1024)} %refs_1_.1, f32[3,3,8,7]{3,2,1,0:T(8,128)} %bitcast.24, f32[3,3,8,7]{3,2,1,0:T(8,128)} %bitcast.25, f32[3,8]{1,0:T(4,128)} %bitcast.27, ...), custom_call_target="tpu_custom_call" | custom-call | tf_op jit(solution)/shard_map/ahead/pallas_call | solution.py:184
  10.2 0.0 collective-permute-done.halo_ref
  10.2 0.1 side.1.applied_ref
  10.3 2.4 %collective-permute-done.1 = f32[54,8,128]{2,1,0:T(8,128)S(1)} collective-permute-done((f32[54,8,128]{2,1,0:T(8,128)S(1)}, f32[54,8,128]{2,1,0:T(8,128)S(1)}, u32[]{:S(2)}, u32[]{:S(2)}) %collective-permute-start.1) | collective-permute-done | bytes 221216 | tf_op jit(solution)/shard_map/ppermute | solution.py:526
  12.7 0.0 collective-permute-done.2
  12.7 0.2 edges.1
  12.9 0.0 collective-permute-done.3.halo_ref
  12.9 4.1 %collective-permute-done.4 = f32[48,8,128]{2,1,0:T(8,128)S(1)} collective-permute-done((f32[48,8,128]{2,1,0:T(8,128)S(1)}, f32[48,8,128]{2,1,0:T(8,128)S(1)}, u32[]{:S(2)}, u32[]{:S(2)}) %collective-permute-start.4) | collective-permute-done | bytes 196640 | tf_op jit(solution)/shard_map/ppermute | solution.py:526
  17.0 1.0 %sums.1 = (bf16[240,3072]{1,0:T(8,128)(2,1)S(1)}, f32[32,128]{1,0:T(8,128)S(1)}) custom-call(s32[1]{0:T(128)} %bitcast.place_ref, s32[1]{0:T(128)} %bitcast.1.slab_ref, f32[8,72,128]{2,1,0:T(8,128)S(1)} %get-tuple-element.23.fields_ref, f32[24,16,128]{2,1,0:T(8,128)S(1)} %get-tuple-element.27.applied_ref, f32[384,128]{1,0:T(8,128)S(1)} %collective-permute-done.3.halo_ref, ...), custom_call_target="tpu_custom_call" | custom-call | tf_op jit(solution)/shard_map/sums/pallas_call | solution.py:368
  18.0 0.1 collective-permute-start.5
  18.1 1.1 %collective-permute-done.5 = f32[32,128]{1,0:T(8,128)S(1)} collective-permute-done((f32[32,128]{1,0:T(8,128)S(1)}, f32[32,128]{1,0:T(8,128)S(1)}, u32[]{:S(2)}, u32[]{:S(2)}) %collective-permute-start.5) | collective-permute-done | bytes 16416 | tf_op jit(solution)/shard_map/ppermute | solution.py:383
  19.2 1.0 %collective-permute-start.6 = (f32[32,128]{1,0:T(8,128)S(1)}, f32[32,128]{1,0:T(8,128)S(1)}, u32[]{:S(2)}, u32[]{:S(2)}) collective-permute-start(f32[32,128]{1,0:T(8,128)S(1)} %add.9), channel_id=1, source_target_pairs={{0,2},{1,3},{2,0},{3,1},{4,6},{5,7},{6,4},{7,5},{8,10},{9,11},{10,... | collective-permute-start | bytes 49160 | tf_op jit(solution)/shard_map/ppermute | solution.py:383
  20.2 2.8 %collective-permute-done.6 = f32[32,128]{1,0:T(8,128)S(1)} collective-permute-done((f32[32,128]{1,0:T(8,128)S(1)}, f32[32,128]{1,0:T(8,128)S(1)}, u32[]{:S(2)}, u32[]{:S(2)}) %collective-permute-start.6) | collective-permute-done | bytes 16416 | tf_op jit(solution)/shard_map/ppermute | solution.py:383
  23.0 1.2 %collective-permute-start.7 = (f32[32,128]{1,0:T(8,128)S(1)}, f32[32,128]{1,0:T(8,128)S(1)}, u32[]{:S(2)}, u32[]{:S(2)}) collective-permute-start(f32[32,128]{1,0:T(8,128)S(1)} %add.10), channel_id=1, source_target_pairs={{0,4},{4,0},{8,12},{12,8},{16,20},{20,16},{24,28},{28,24},{1,5},{5... | collective-permute-start | bytes 49160 | tf_op jit(solution)/shard_map/ppermute | solution.py:383
  24.2 2.5 %collective-permute-done.7 = f32[32,128]{1,0:T(8,128)S(1)} collective-permute-done((f32[32,128]{1,0:T(8,128)S(1)}, f32[32,128]{1,0:T(8,128)S(1)}, u32[]{:S(2)}, u32[]{:S(2)}) %collective-permute-start.7) | collective-permute-done | bytes 16416 | tf_op jit(solution)/shard_map/ppermute | solution.py:383
  26.7 10.4 %all_to_all.5.parts_ref = f32[4,32,128]{2,1,0:T(8,128)S(1)} all-to-all(f32[4,32,128]{2,1,0:T(8,128)S(1)} %broadcast_in_dim.2), channel_id=1, replica_groups={{0,8,16,24},{4,12,20,28},{1,9,17,25},{5,13,21,29},{2,10,18,26},{6,14,22..., dimensions={0} | all-to-all | bytes 131072 | tf_op jit(solution)/shard_map/all_to_all | solution.py:395
  37.1 2.4 %finish.1 = (f32[16,24,128]{2,1,0:T(8,128)}, f32[16,16]{1,0:T(8,128)}, f32[16,16]{1,0:T(8,128)}) custom-call(s32[1]{0:T(128)} %bitcast.place_ref, f32[4,32,128]{2,1,0:T(8,128)S(1)} %all_to_all.5.parts_ref, bf16[240,3072]{1,0:T(8,128)(2,1)S(1)} %get-tuple-element.33.stack_ref), custom_call_target="tpu_custom_call" | custom-call | tf_op jit(solution)/shard_map/finish/pallas_call | solution.py:488
  (4 shorter events, 0.0 us)
Async XLA Ops:
  0.6 9.6 %collective-permute-start = (f32[384,128]{1,0:T(8,128)}, f32[384,128]{1,0:T(8,128)S(1)}, u32[]{:S(2)}, u32[]{:S(2)}) collective-permute-start(f32[384,128]{1,0:T(8,128)} %bitcast.21), channel_id=1, source_target_pairs={{0,4},{8,12},{16,20},{24,28},{4,0},{12,8},{20,16},{28,24},{1,5},{9... | collective-permute-start | bytes 589832 | tf_op jit(solution)/shard_map/ppermute | solution.py:37
  5.0 7.7 %collective-permute-start.1 = (f32[54,8,128]{2,1,0:T(8,128)S(1)}, f32[54,8,128]{2,1,0:T(8,128)S(1)}, u32[]{:S(2)}, u32[]{:S(2)}) collective-permute-start(f32[54,8,128]{2,1,0:T(8,128)S(1)} %get-tuple-element.25), channel_id=1, source_target_pairs={{0,3},{1,2},{2,1},{3,0},{4,7},{5,6},{6,5},{7,4},{8,11},{9,10},{10,... | collective-permute-start | bytes 663560 | tf_op jit(solution)/shard_map/ppermute | solution.py:526
  5.7 7.0 %collective-permute-start.2 = (f32[54,8,128]{2,1,0:T(8,128)S(1)}, f32[54,8,128]{2,1,0:T(8,128)S(1)}, u32[]{:S(2)}, u32[]{:S(2)}) collective-permute-start(f32[54,8,128]{2,1,0:T(8,128)S(1)} %get-tuple-element.26), channel_id=1, source_target_pairs={{0,1},{1,0},{2,3},{3,2},{4,5},{5,4},{6,7},{7,6},{8,9},{9,8},{10,11... | collective-permute-start | bytes 663560 | tf_op jit(solution)/shard_map/ppermute | solution.py:526
  6.7 6.2 %collective-permute-start.3 = (f32[384,128]{1,0:T(8,128)}, f32[384,128]{1,0:T(8,128)S(1)}, u32[]{:S(2)}, u32[]{:S(2)}) collective-permute-start(f32[384,128]{1,0:T(8,128)} %bitcast.23), channel_id=1, source_target_pairs={{4,8},{12,16},{20,24},{8,4},{16,12},{24,20},{5,9},{13,17},{21,25},... | collective-permute-start | bytes 589832 | tf_op jit(solution)/shard_map/ppermute | solution.py:37
  7.4 9.6 %collective-permute-start.4 = (f32[48,8,128]{2,1,0:T(8,128)S(1)}, f32[48,8,128]{2,1,0:T(8,128)S(1)}, u32[]{:S(2)}, u32[]{:S(2)}) collective-permute-start(f32[48,8,128]{2,1,0:T(8,128)S(1)} %get-tuple-element.31), channel_id=1, source_target_pairs={{0,2},{1,3},{2,0},{3,1},{4,6},{5,7},{6,4},{7,5},{8,10},{9,11},{10,... | collective-permute-start | bytes 589832 | tf_op jit(solution)/shard_map/ppermute | solution.py:526
  18.0 1.2 %collective-permute-start.5 = (f32[32,128]{1,0:T(8,128)S(1)}, f32[32,128]{1,0:T(8,128)S(1)}, u32[]{:S(2)}, u32[]{:S(2)}) collective-permute-start(f32[32,128]{1,0:T(8,128)S(1)} %get-tuple-element.32), channel_id=1, source_target_pairs={{0,1},{1,0},{2,3},{3,2},{4,5},{5,4},{6,7},{7,6},{8,9},{9,8},{10,11... | collective-permute-start | bytes 49160 | tf_op jit(solution)/shard_map/ppermute | solution.py:383
  19.2 3.7 %collective-permute-start.6 = (f32[32,128]{1,0:T(8,128)S(1)}, f32[32,128]{1,0:T(8,128)S(1)}, u32[]{:S(2)}, u32[]{:S(2)}) collective-permute-start(f32[32,128]{1,0:T(8,128)S(1)} %add.9), channel_id=1, source_target_pairs={{0,2},{1,3},{2,0},{3,1},{4,6},{5,7},{6,4},{7,5},{8,10},{9,11},{10,... | collective-permute-start | bytes 49160 | tf_op jit(solution)/shard_map/ppermute | solution.py:383
  23.0 3.7 %collective-permute-start.7 = (f32[32,128]{1,0:T(8,128)S(1)}, f32[32,128]{1,0:T(8,128)S(1)}, u32[]{:S(2)}, u32[]{:S(2)}) collective-permute-start(f32[32,128]{1,0:T(8,128)S(1)} %add.10), channel_id=1, source_target_pairs={{0,4},{4,0},{8,12},{12,8},{16,20},{20,16},{24,28},{28,24},{1,5},{5... | collective-permute-start | bytes 49160 | tf_op jit(solution)/shard_map/ppermute | solution.py:383

commit v14 on v12

--- a/solution.py
+++ b/solution.py
@@ -11,6 +11,7 @@
 VMEM = pl.BlockSpec(memory_space=pltpu.VMEM)
 SMEM = pl.BlockSpec(memory_space=pltpu.SMEM)
 HBM = pl.BlockSpec(memory_space=pltpu.HBM)
+LOSS = 64.0
 EARLY = pl.CostEstimate(flops=10**9, bytes_accessed=10**6, transcendentals=0)
 NEXT = pl.CostEstimate(flops=10**6, bytes_accessed=10**6, transcendentals=0)
 SCRATCH = pltpu.CompilerParams(vmem_limit_bytes=8 * 2**20)
@@ -393,7 +394,7 @@
 
 
 def finish_kernel(
-    row_count, comps, place_ref, parts_ref, stack_ref, block_ref, coeffs_ref, upper_ref,
+    row_count, comps, place_ref, parts_ref, stack_ref, block_ref, coeffs_ref, upper_ref, bad_ref,
     coeffs_scratch, upper_scratch, block_scratch, sems,
 ):
     block_cols = upper_ref.shape[0]
@@ -450,7 +451,10 @@
         work = jnp.where(height >= begin + width, rest, work)
         for step, new_row in enumerate(new_rows, begin):
             work = jnp.where(height == step, new_row, work)
-    upper_scratch[...] = jnp.where(row <= column, work[:, joined : joined + block_cols], 0.0)
+    upper = jnp.where(row <= column, work[:, joined : joined + block_cols], 0.0)
+    upper_scratch[...] = upper
+    kept_enough = jnp.where(row == column, upper * upper * LOSS, block_gram) >= block_gram
+    bad_ref[0] = 1 - jnp.min(jnp.where(kept_enough, 1, 0))
     copies.append(pltpu.make_async_copy(upper_scratch, upper_ref, sems.at[comps + 1]))
     copies[1].start()
     weights = three_parts(work[:, :joined])
@@ -486,9 +490,10 @@
         functools.partial(finish_kernel, row_count, comps),
         out_shape=(
             f32(block_cols, lines, lanes), f32(group_cols, block_cols), f32(block_cols, block_cols),
+            jax.ShapeDtypeStruct((1,), jnp.int32),
         ),
         in_specs=[SMEM] + [VMEM] * 2,
-        out_specs=(HBM,) * 3,
+        out_specs=(HBM,) * 3 + (SMEM,),
         scratch_shapes=[
             pltpu.VMEM((basis_cols, block_cols), jnp.float32),
             pltpu.VMEM((block_cols, block_cols), jnp.float32),
@@ -500,9 +505,121 @@
     )(place, *kept(parts, stack))
 
 
+def stencil_tables(k0_blocks, k0_diag, ke_blocks, mass, velocities, shifts, sample):
+    velocity = jnp.take(velocities, sample, axis=0)[0]
+    sigma_value = jnp.take(shifts, sample, axis=0)[0]
+    center = (k0_diag - sigma_value * mass)[:, :, None] * jnp.eye(3, dtype=jnp.float32)
+    tables = k0_blocks - velocity * velocity * ke_blocks
+    return tables.at[:, 0].add(center)
+
+
+def shifted(cells, dim, axis, up):
+    extent = cells.shape[dim]
+    edge = lax.slice_in_dim(cells, 0, 1, axis=dim) if up else (
+        lax.slice_in_dim(cells, extent - 1, extent, axis=dim)
+    )
+    if axis is None:
+        edge = jnp.zeros_like(edge)
+    else:
+        ends = [(i, i + 1) for i in range(lax.axis_size(axis) - 1)]
+        edge = lax.ppermute(edge, axis, [(j, i) for i, j in ends] if up else ends)
+    if up:
+        return jnp.concatenate((lax.slice_in_dim(cells, 1, extent, axis=dim), edge), axis=dim)
+    return jnp.concatenate((edge, lax.slice_in_dim(cells, 0, extent - 1, axis=dim)), axis=dim)
+
+
+def hold_kernel(*refs):
+    *refs, sems = refs
+    half = len(refs) // 2
+    copies = [
+        pltpu.make_async_copy(source, target, sems.at[index])
+        for index, (source, target) in enumerate(zip(refs[:half], refs[half:]))
+    ]
+    for copy in copies:
+        copy.start()
+    for copy in copies:
+        copy.wait()
+
+
+def hold(*arrays):
+    return pl.pallas_call(
+        hold_kernel,
+        out_shape=[jax.ShapeDtypeStruct(array.shape, array.dtype) for array in arrays],
+        in_specs=[HBM] * len(arrays),
+        out_specs=[HBM] * len(arrays),
+        scratch_shapes=[pltpu.SemaphoreType.DMA((len(arrays),))],
+        compiler_params=SCRATCH,
+        name="hold",
+    )(*far(*arrays))
+
+
+def careful(arguments):
+    x_block, basis, material, k0_blocks, k0_diag, ke_blocks, mass, velocities, shifts, sample = arguments
+    x_block, basis, material, k0_blocks, k0_diag, ke_blocks, mass, velocities, shifts = hold(
+        x_block, basis, material, jnp.transpose(k0_blocks, (2, 3, 0, 1)), k0_diag.T,
+        jnp.transpose(ke_blocks, (2, 3, 0, 1)), mass.T, velocities, shifts,
+    )
+    k0_blocks, ke_blocks = (jnp.transpose(blocks, (2, 3, 0, 1)) for blocks in (k0_blocks, ke_blocks))
+    k0_diag, mass = k0_diag.T, mass.T
+    tables = stencil_tables(k0_blocks, k0_diag, ke_blocks, mass, velocities, shifts, sample)
+    block_cols, comps, extent_x, _, lanes = x_block.shape
+    group_cols = basis.shape[0]
+    row_count = float(comps * extent_x * lax.axis_size("space") * basis.shape[3] * lanes)
+    fields = jnp.zeros((7, comps, comps) + material.shape, jnp.float32)
+    for level in range(tables.shape[0]):
+        chosen = (material == level).astype(jnp.float32)
+        fields = fields + tables[level][:, :, :, None, None, None] * chosen
+    views = [x_block]
+    for dim, axis in ((2, "space"), (3, "basis"), (4, None)):
+        views += [shifted(x_block, dim, axis, False), shifted(x_block, dim, axis, True)]
+    applied = jnp.zeros_like(x_block)
+    for offset, view in enumerate(views):
+        for comp in range(comps):
+            applied = applied + fields[offset, :, comp][None] * view[:, comp : comp + 1]
+
+    count = lax.axis_size("basis")
+    place = lax.axis_index("basis")
+    pieces = jnp.moveaxis(basis.reshape(basis.shape[:3] + (count, -1, lanes)), 3, 0)
+    rows = jnp.zeros((count,) + pieces.shape[1:], jnp.float32)
+    for k in range(count):
+        piece = lax.dynamic_index_in_dim(pieces, place ^ k, 0, keepdims=False)
+        if k:
+            piece = lax.ppermute(piece, "basis", [(i, i ^ k) for i in range(count)])
+        rows = lax.dynamic_update_index_in_dim(rows, piece, place ^ k, 0)
+    rows = rows.reshape((count * group_cols,) + pieces.shape[2:])
+
+    def total(part):
+        for axis in ("basis", "space"):
+            mask = 1
+            while mask < lax.axis_size(axis):
+                pairs = [(i, i ^ mask) for i in range(lax.axis_size(axis))]
+                part = part + lax.ppermute(part, axis, pairs)
+                mask *= 2
+        return part / row_count
+
+    running = jnp.zeros((count * group_cols, block_cols), jnp.float32)
+    for repeat in range(2):
+        coeffs = total(
+            jnp.einsum("kcxyz,ncxyz->kn", rows, applied, precision=exact_precision)
+        )
+        applied = applied - jnp.einsum("kcxyz,kn->ncxyz", rows, coeffs, precision=exact_precision)
+        running = running + coeffs
+    gram = total(jnp.einsum("ncxyz,mcxyz->nm", applied, applied, precision=exact_precision))
+    lower = jnp.linalg.cholesky(gram)
+    inverse = lax.linalg.triangular_solve(
+        lower, jnp.eye(block_cols, dtype=jnp.float32), left_side=True, lower=True
+    )
+    block = jnp.einsum("mcxyz,nm->ncxyz", applied, inverse, precision=exact_precision)
+    own = lax.dynamic_slice_in_dim(running, place * group_cols, group_cols, axis=0)
+    return tuple(hold(block.reshape(block_cols, -1, lanes), own, lower.T))
+
+
 def shards(
     x_block, basis, material, k0_blocks, k0_diag, ke_blocks, mass, velocities, shifts, sample
 ):
+    arguments = (
+        x_block, basis, material, k0_blocks, k0_diag, ke_blocks, mass, velocities, shifts, sample
+    )
     block_cols, comps, extent_x, rows, lanes = x_block.shape
     group_cols = basis.shape[0]
     lines = comps * rows
@@ -532,10 +649,15 @@
     split = {0: own, **dict(zip(pieces, parts))}
     stack, part = sums(place, slab, fields, applied, got.pop("odd"), split, got, comps)
     parts = exchange(exchange_sum(part, "basis"), "space")
-    block, coeffs, upper = finish(
+    block, coeffs, upper, bad = finish(
         place, parts, stack, row_count, block_cols, group_cols, lines, comps
     )
-    return (block.reshape(x_block.shape), coeffs, upper)
+    block, coeffs, upper = lax.while_loop(
+        lambda state: state[0] > 0,
+        lambda state: (jnp.zeros_like(state[0]), careful(arguments)),
+        (bad[0], (block, coeffs, upper)),
+    )[1]
+    return block.reshape(x_block.shape), coeffs, upper
 
 
 def solution(mesh):

time: 37.7 us -> 38.9 us (1.032)
  loops' own time: 0 us -> 0.7 us
  Pallas kernels: 6.63 us -> 7.19 us
    another operation x0 -> x1, loops' own time: none -> 0.7 us  [shards(): lax.while_loop(lambda state: state[0] > 0, lambda state: (jnp.zeros_like(...]
    pallas_call x1, Pallas kernels: 2.44 us -> 2.97 us  [finish(): pl.pallas_call(functools.partial(finish_kernel, row_count, comps), out_sh...]
  transfers between devices with their start and end apart: 7 -> 7, of which waited for: 4 -> 4; matrix products, arithmetic and copies ran while one was open for 0% -> 0% of each run, Pallas kernels for 9% -> 8%
where the time goes in v14:
time: 38.9 us; the launch traced here: 38.7 us
  blocking collectives  12 us (31%)
  waiting for transfers between devices  10.5 us (27%)
  Pallas kernels  7.19 us (18%)
  starting transfers between devices  6.94 us (18%)
  between operations  1.34 us (3%)
  loops' own time  0.7 us (2%)
    all_to_all x1, blocking collectives, exchange(): lax.all_to_all(jnp.broadcast_to(part[None], (count,) + part.shape), axis,...  12 us
    ppermute x3, waiting for transfers between devices, shards(): lax.ppermute(pieces[name - 1], 'basis', [(i, i ^ name) for i in range(cou...  6.55 us
    ppermute x2, waiting for transfers between devices, exchange_sum(): lax.ppermute(part, axis, [(i, i ^ mask) for i in range(count)])  3.92 us
    ppermute x2, starting transfers between devices, swap(): return lax.ppermute(values, axis, pairs + [(j, i) for i, j in pairs])  3.66 us
    pallas_call x1, Pallas kernels, finish(): pl.pallas_call(functools.partial(finish_kernel, row_count, comps), out_sh...  2.97 us
    ppermute x3, starting transfers between devices, shards(): lax.ppermute(pieces[name - 1], 'basis', [(i, i ^ name) for i in range(cou...  2.21 us
    pallas_call x1, Pallas kernels, ahead(): pl.pallas_call(ahead_kernel, out_shape=(near(rows, comps * comps * stride...  1.65 us
    pallas_call x1, Pallas kernels, pack(): pl.pallas_call(functools.partial(pack_kernel, comps), out_shape=(*pieces,...  1.34 us
  transfers between devices with their start and end apart: 7, of which 4 were waited for; matrix products, arithmetic and copies ran while one was open for 0% of the time, Pallas kernels for 8%

profile of v14, /device:TPU:0, one launch (start us, length us, event | category | flops | bytes accessed | tf_op | source)
XLA Modules:
  0.0 38.7 jit_solution(10485882678771254230)
XLA Ops:
  0.6 3.0 %collective-permute-start.22 = (f32[384,128]{1,0:T(8,128)}, f32[384,128]{1,0:T(8,128)S(1)}, u32[]{:S(2)}, u32[]{:S(2)}) collective-permute-start(f32[384,128]{1,0:T(8,128)} %bitcast.279), channel_id=1, source_target_pairs={{0,4},{8,12},{16,20},{24,28},{4,0},{12,8},{20,16},{28,24},{1,5},{9... | collective-permute-start | bytes 589832 | tf_op jit(solution)/shard_map/ppermute | solution.py:38
  3.6 1.3 %pack.1 = (f32[48,8,128]{2,1,0:T(8,128)S(1)}, f32[54,8,128]{2,1,0:T(8,128)S(1)}, f32[48,8,128]{2,1,0:T(8,128)S(1)}, f32[54,8,128]{2,1,0:T(8,128)S(1)}, f32[384,128]{1,0:T(8,128)S(1)}, /*index=5*/s32[8,128]{1,0:T(8,128)S(1)}) custom-call(s32[1]{0:T(128)} %bitcast.116.place_ref, f32[48,4,8,128]{3,2,1,0:T(8,128)} %bitcast.273, f32[384,128]{1,0:T(8,128)} %bitcast.280, ...), custom_call_target="tpu_custom_call" | custom-call | tf_op jit(solution)/shard_map/pack/pallas_call | solution.py:88
  5.0 0.7 %collective-permute-start.23 = (f32[54,8,128]{2,1,0:T(8,128)S(1)}, f32[54,8,128]{2,1,0:T(8,128)S(1)}, u32[]{:S(2)}, u32[]{:S(2)}) collective-permute-start(f32[54,8,128]{2,1,0:T(8,128)S(1)} %get-tuple-element.120), channel_id=1, source_target_pairs={{0,3},{1,2},{2,1},{3,0},{4,7},{5,6},{6,5},{7,4},{8,11},{9,10},{10,... | collective-permute-start | bytes 663560 | tf_op jit(solution)/shard_map/ppermute | solution.py:640
  5.7 1.0 %collective-permute-start.24 = (f32[54,8,128]{2,1,0:T(8,128)S(1)}, f32[54,8,128]{2,1,0:T(8,128)S(1)}, u32[]{:S(2)}, u32[]{:S(2)}) collective-permute-start(f32[54,8,128]{2,1,0:T(8,128)S(1)} %get-tuple-element.121), channel_id=1, source_target_pairs={{0,1},{1,0},{2,3},{3,2},{4,5},{5,4},{6,7},{7,6},{8,9},{9,8},{10,11... | collective-permute-start | bytes 663560 | tf_op jit(solution)/shard_map/ppermute | solution.py:640
  6.7 0.5 %collective-permute-start.26 = (f32[48,8,128]{2,1,0:T(8,128)S(1)}, f32[48,8,128]{2,1,0:T(8,128)S(1)}, u32[]{:S(2)}, u32[]{:S(2)}) collective-permute-start(f32[48,8,128]{2,1,0:T(8,128)S(1)} %get-tuple-element.126), channel_id=1, source_target_pairs={{0,2},{1,3},{2,0},{3,1},{4,6},{5,7},{6,4},{7,5},{8,10},{9,11},{10,... | collective-permute-start | bytes 589832 | tf_op jit(solution)/shard_map/ppermute | solution.py:640
  7.2 0.7 %collective-permute-start.25 = (f32[384,128]{1,0:T(8,128)}, f32[384,128]{1,0:T(8,128)S(1)}, u32[]{:S(2)}, u32[]{:S(2)}) collective-permute-start(f32[384,128]{1,0:T(8,128)} %bitcast.281), channel_id=1, source_target_pairs={{4,8},{12,16},{20,24},{8,4},{16,12},{24,20},{5,9},{13,17},{21,25},... | collective-permute-start | bytes 589832 | tf_op jit(solution)/shard_map/ppermute | solution.py:38
  8.5 1.7 %ahead.1 = (f32[8,72,128]{2,1,0:T(8,128)S(1)}, f32[24,16,128]{2,1,0:T(8,128)S(1)}, bf16[48,3072]{1,0:T(8,128)(2,1)S(1)}) custom-call(s32[1]{0:T(128)S(6)} %copy.194.sample_ref, f32[1024]{0:T(1024)} %refs_0_.1, f32[1024]{0:T(1024)} %refs_1_.1, f32[3,3,8,7]{3,2,1,0:T(8,128)} %bitcast.293, f32[3,3,8,7]{3,2,1,0:T(8,128)} %bitcast.295, f32[3,8]{1,0:T(4,128)} %bitcast.298, ...), custom_call_target="tpu_custom_call" | custom-call | tf_op jit(solution)/shard_map/ahead/pallas_call | solution.py:185
  10.2 0.0 collective-permute-done.22.halo_ref
  10.2 0.1 side.1.applied_ref
  10.3 2.4 %collective-permute-done.23 = f32[54,8,128]{2,1,0:T(8,128)S(1)} collective-permute-done((f32[54,8,128]{2,1,0:T(8,128)S(1)}, f32[54,8,128]{2,1,0:T(8,128)S(1)}, u32[]{:S(2)}, u32[]{:S(2)}) %collective-permute-start.23) | collective-permute-done | bytes 221216 | tf_op jit(solution)/shard_map/ppermute | solution.py:640
  12.7 0.0 collective-permute-done.24
  12.7 0.2 edges.1
  12.9 4.1 %collective-permute-done.26 = f32[48,8,128]{2,1,0:T(8,128)S(1)} collective-permute-done((f32[48,8,128]{2,1,0:T(8,128)S(1)}, f32[48,8,128]{2,1,0:T(8,128)S(1)}, u32[]{:S(2)}, u32[]{:S(2)}) %collective-permute-start.26) | collective-permute-done | bytes 196640 | tf_op jit(solution)/shard_map/ppermute | solution.py:640
  17.0 0.0 collective-permute-done.25.halo_ref
  17.0 1.0 %sums.1 = (bf16[240,3072]{1,0:T(8,128)(2,1)S(1)}, f32[32,128]{1,0:T(8,128)S(1)}) custom-call(s32[1]{0:T(128)} %bitcast.116.place_ref, s32[1]{0:T(128)} %bitcast.117.slab_ref, f32[8,72,128]{2,1,0:T(8,128)S(1)} %get-tuple-element.118.fields_ref, f32[24,16,128]{2,1,0:T(8,128)S(1)} %get-tuple-element.122.applied_ref, ...), custom_call_target="tpu_custom_call" | custom-call | tf_op jit(solution)/shard_map/sums/pallas_call | solution.py:369
  18.0 0.1 collective-permute-start.27
  18.1 1.1 %collective-permute-done.27 = f32[32,128]{1,0:T(8,128)S(1)} collective-permute-done((f32[32,128]{1,0:T(8,128)S(1)}, f32[32,128]{1,0:T(8,128)S(1)}, u32[]{:S(2)}, u32[]{:S(2)}) %collective-permute-start.27) | collective-permute-done | bytes 16416 | tf_op jit(solution)/shard_map/ppermute | solution.py:386
  19.2 1.0 %collective-permute-start.28 = (f32[32,128]{1,0:T(8,128)S(1)}, f32[32,128]{1,0:T(8,128)S(1)}, u32[]{:S(2)}, u32[]{:S(2)}) collective-permute-start(f32[32,128]{1,0:T(8,128)S(1)} %add.359), channel_id=1, source_target_pairs={{0,2},{1,3},{2,0},{3,1},{4,6},{5,7},{6,4},{7,5},{8,10},{9,11},{10,... | collective-permute-start | bytes 49160 | tf_op jit(solution)/shard_map/ppermute | solution.py:386
  20.2 2.8 %collective-permute-done.28 = f32[32,128]{1,0:T(8,128)S(1)} collective-permute-done((f32[32,128]{1,0:T(8,128)S(1)}, f32[32,128]{1,0:T(8,128)S(1)}, u32[]{:S(2)}, u32[]{:S(2)}) %collective-permute-start.28) | collective-permute-done | bytes 16416 | tf_op jit(solution)/shard_map/ppermute | solution.py:386
  23.0 12.0 %all_to_all.5.parts_ref = f32[8,32,128]{2,1,0:T(8,128)S(1)} all-to-all(f32[8,32,128]{2,1,0:T(8,128)S(1)} %broadcast_in_dim.34), channel_id=1, replica_groups=mesh['space'=8,'basis'=4] {'space'}, dimensions={0} | all-to-all | bytes 262144 | tf_op jit(solution)/shard_map/all_to_all | solution.py:393
  35.0 3.0 %finish.1 = (f32[16,24,128]{2,1,0:T(8,128)}, f32[16,16]{1,0:T(8,128)}, f32[16,16]{1,0:T(8,128)}, s32[1]{0:T(128)}) custom-call(s32[1]{0:T(128)} %bitcast.116.place_ref, f32[8,32,128]{2,1,0:T(8,128)S(1)} %all_to_all.5.parts_ref, bf16[240,3072]{1,0:T(8,128)(2,1)S(1)} %get-tuple-element.128.stack_ref), custom_call_target="tpu_custom_call" | custom-call | tf_op jit(solution)/shard_map/finish/pallas_call | solution.py:489
  38.0 0.7 %while.14 = (s32[]{:T(128)}, f32[16,24,128]{2,1,0:T(8,128)}, f32[16,16]{1,0:T(8,128)}, f32[16,16]{1,0:T(8,128)}, f32[8,7,3,3]{1,0,3,2:T(8,128)}, /*index=5*/f32[...) while((s32[]{:T(128)}, f32[16,24,128]{2,1,0:T(8,128)}, ...), condition=%region_3.4_spmd, body=%region_0.3_spmd | while | flops 175311344 | bytes 29713228 | solution.py:655
  (3 shorter events, 0.0 us)
Async XLA Ops:
  0.6 9.5 %collective-permute-start.22 = (f32[384,128]{1,0:T(8,128)}, f32[384,128]{1,0:T(8,128)S(1)}, u32[]{:S(2)}, u32[]{:S(2)}) collective-permute-start(f32[384,128]{1,0:T(8,128)} %bitcast.279), channel_id=1, source_target_pairs={{0,4},{8,12},{16,20},{24,28},{4,0},{12,8},{20,16},{28,24},{1,5},{9... | collective-permute-start | bytes 589832 | tf_op jit(solution)/shard_map/ppermute | solution.py:38
  5.0 7.7 %collective-permute-start.23 = (f32[54,8,128]{2,1,0:T(8,128)S(1)}, f32[54,8,128]{2,1,0:T(8,128)S(1)}, u32[]{:S(2)}, u32[]{:S(2)}) collective-permute-start(f32[54,8,128]{2,1,0:T(8,128)S(1)} %get-tuple-element.120), channel_id=1, source_target_pairs={{0,3},{1,2},{2,1},{3,0},{4,7},{5,6},{6,5},{7,4},{8,11},{9,10},{10,... | collective-permute-start | bytes 663560 | tf_op jit(solution)/shard_map/ppermute | solution.py:640
  5.7 7.0 %collective-permute-start.24 = (f32[54,8,128]{2,1,0:T(8,128)S(1)}, f32[54,8,128]{2,1,0:T(8,128)S(1)}, u32[]{:S(2)}, u32[]{:S(2)}) collective-permute-start(f32[54,8,128]{2,1,0:T(8,128)S(1)} %get-tuple-element.121), channel_id=1, source_target_pairs={{0,1},{1,0},{2,3},{3,2},{4,5},{5,4},{6,7},{7,6},{8,9},{9,8},{10,11... | collective-permute-start | bytes 663560 | tf_op jit(solution)/shard_map/ppermute | solution.py:640
  6.7 10.3 %collective-permute-start.26 = (f32[48,8,128]{2,1,0:T(8,128)S(1)}, f32[48,8,128]{2,1,0:T(8,128)S(1)}, u32[]{:S(2)}, u32[]{:S(2)}) collective-permute-start(f32[48,8,128]{2,1,0:T(8,128)S(1)} %get-tuple-element.126), channel_id=1, source_target_pairs={{0,2},{1,3},{2,0},{3,1},{4,6},{5,7},{6,4},{7,5},{8,10},{9,11},{10,... | collective-permute-start | bytes 589832 | tf_op jit(solution)/shard_map/ppermute | solution.py:640
  7.2 9.8 %collective-permute-start.25 = (f32[384,128]{1,0:T(8,128)}, f32[384,128]{1,0:T(8,128)S(1)}, u32[]{:S(2)}, u32[]{:S(2)}) collective-permute-start(f32[384,128]{1,0:T(8,128)} %bitcast.281), channel_id=1, source_target_pairs={{4,8},{12,16},{20,24},{8,4},{16,12},{24,20},{5,9},{13,17},{21,25},... | collective-permute-start | bytes 589832 | tf_op jit(solution)/shard_map/ppermute | solution.py:38
  18.0 1.2 %collective-permute-start.27 = (f32[32,128]{1,0:T(8,128)S(1)}, f32[32,128]{1,0:T(8,128)S(1)}, u32[]{:S(2)}, u32[]{:S(2)}) collective-permute-start(f32[32,128]{1,0:T(8,128)S(1)} %get-tuple-element.127), channel_id=1, source_target_pairs={{0,1},{1,0},{2,3},{3,2},{4,5},{5,4},{6,7},{7,6},{8,9},{9,8},{10,11... | collective-permute-start | bytes 49160 | tf_op jit(solution)/shard_map/ppermute | solution.py:386
  19.2 3.7 %collective-permute-start.28 = (f32[32,128]{1,0:T(8,128)S(1)}, f32[32,128]{1,0:T(8,128)S(1)}, u32[]{:S(2)}, u32[]{:S(2)}) collective-permute-start(f32[32,128]{1,0:T(8,128)S(1)} %add.359), channel_id=1, source_target_pairs={{0,2},{1,3},{2,0},{3,1},{4,6},{5,7},{6,4},{7,5},{8,10},{9,11},{10,... | collective-permute-start | bytes 49160 | tf_op jit(solution)/shard_map/ppermute | solution.py:386

commit v15 on v14

--- a/solution.py
+++ b/solution.py
@@ -11,7 +11,7 @@
 VMEM = pl.BlockSpec(memory_space=pltpu.VMEM)
 SMEM = pl.BlockSpec(memory_space=pltpu.SMEM)
 HBM = pl.BlockSpec(memory_space=pltpu.HBM)
-LOSS = 64.0
+LOSS = 256.0
 EARLY = pl.CostEstimate(flops=10**9, bytes_accessed=10**6, transcendentals=0)
 NEXT = pl.CostEstimate(flops=10**6, bytes_accessed=10**6, transcendentals=0)
 SCRATCH = pltpu.CompilerParams(vmem_limit_bytes=8 * 2**20)
@@ -321,9 +321,9 @@
 
 
 def sums_kernel(
-    comps, split, raw, place_ref, slab_ref, fields_ref, applied_ref, halo_ref, *refs
+    comps, split, raw, place_ref, slab_ref, fields_ref, applied_ref, *refs
 ):
-    *refs, stack_ref, sums_ref = refs
+    *refs, halo_ref, stack_ref, sums_ref = refs
     lines, block_cols, lanes = applied_ref.shape
     rows = lines // comps
     group_cols = refs[0].shape[0] // 3
@@ -376,7 +376,7 @@
         out_specs=(VMEM, VMEM),
         compiler_params=SCRATCH,
         name="sums",
-    )(place, slab, *kept(fields, applied, halo, *split.values(), *raw.values()))
+    )(place, slab, *kept(fields, applied, *split.values(), *raw.values(), halo))
 
 
 def exchange_sum(part, axis):
@@ -395,7 +395,7 @@
 
 def finish_kernel(
     row_count, comps, place_ref, parts_ref, stack_ref, block_ref, coeffs_ref, upper_ref, bad_ref,
-    coeffs_scratch, upper_scratch, block_scratch, sems,
+    coeffs_scratch, upper_scratch, bad_scratch, block_scratch, sems,
 ):
     block_cols = upper_ref.shape[0]
     basis_cols = parts_ref.shape[2] // 2
@@ -454,9 +454,13 @@
     upper = jnp.where(row <= column, work[:, joined : joined + block_cols], 0.0)
     upper_scratch[...] = upper
     kept_enough = jnp.where(row == column, upper * upper * LOSS, block_gram) >= block_gram
-    bad_ref[0] = 1 - jnp.min(jnp.where(kept_enough, 1, 0))
+    kept_enough = jnp.min(jnp.where(kept_enough, 1.0, 0.0), axis=0, keepdims=True)
+    kept_enough = jnp.min(kept_enough, axis=1, keepdims=True)
+    bad_scratch[...] = jnp.where(kept_enough > 0.0, 0, 1)
+    copies.append(pltpu.make_async_copy(bad_scratch, bad_ref, sems.at[comps + 2]))
+    copies[-1].start()
     copies.append(pltpu.make_async_copy(upper_scratch, upper_ref, sems.at[comps + 1]))
-    copies[1].start()
+    copies[-1].start()
     weights = three_parts(work[:, :joined])
     wide = jnp.concatenate(
         [jnp.concatenate((part, part, part), axis=1) for part in weights], axis=0
@@ -490,15 +494,16 @@
         functools.partial(finish_kernel, row_count, comps),
         out_shape=(
             f32(block_cols, lines, lanes), f32(group_cols, block_cols), f32(block_cols, block_cols),
-            jax.ShapeDtypeStruct((1,), jnp.int32),
+            jax.ShapeDtypeStruct((1, 1), jnp.int32),
         ),
         in_specs=[SMEM] + [VMEM] * 2,
-        out_specs=(HBM,) * 3 + (SMEM,),
+        out_specs=(HBM,) * 4,
         scratch_shapes=[
             pltpu.VMEM((basis_cols, block_cols), jnp.float32),
             pltpu.VMEM((block_cols, block_cols), jnp.float32),
+            pltpu.VMEM((1, 1), jnp.int32),
             pltpu.VMEM((block_cols * lines, lanes), jnp.float32),
-            pltpu.SemaphoreType.DMA((comps + 2,)),
+            pltpu.SemaphoreType.DMA((comps + 3,)),
         ],
         compiler_params=SCRATCH,
         name="finish",
@@ -655,7 +660,7 @@
     block, coeffs, upper = lax.while_loop(
         lambda state: state[0] > 0,
         lambda state: (jnp.zeros_like(state[0]), careful(arguments)),
-        (bad[0], (block, coeffs, upper)),
+        (bad[0, 0], (block, coeffs, upper)),
     )[1]
     return block.reshape(x_block.shape), coeffs, upper
 

time: 38.9 us -> 38.4 us (0.987)
  Pallas kernels: 7.19 us -> 6.67 us
    pallas_call x1, Pallas kernels: 2.97 us -> 2.45 us  [finish(): pl.pallas_call(functools.partial(finish_kernel, row_count, comps), out_sh...]
  transfers between devices with their start and end apart: 7 -> 7, of which waited for: 4 -> 4; matrix products, arithmetic and copies ran while one was open for 0% -> 0% of each run, Pallas kernels for 8% -> 9%
where the time goes in v15:
time: 38.4 us; the launch traced here: 38.1 us
  blocking collectives  12 us (31%)
  waiting for transfers between devices  10.5 us (27%)
  starting transfers between devices  6.94 us (18%)
  Pallas kernels  6.67 us (17%)
  between operations  1.34 us (3%)
  loops' own time  0.7 us (2%)
    all_to_all x1, blocking collectives, exchange(): lax.all_to_all(jnp.broadcast_to(part[None], (count,) + part.shape), axis,...  12 us
    ppermute x3, waiting for transfers between devices, shards(): lax.ppermute(pieces[name - 1], 'basis', [(i, i ^ name) for i in range(cou...  6.55 us
    ppermute x2, waiting for transfers between devices, exchange_sum(): lax.ppermute(part, axis, [(i, i ^ mask) for i in range(count)])  3.92 us
    ppermute x2, starting transfers between devices, swap(): return lax.ppermute(values, axis, pairs + [(j, i) for i, j in pairs])  3.66 us
    pallas_call x1, Pallas kernels, finish(): pl.pallas_call(functools.partial(finish_kernel, row_count, comps), out_sh...  2.45 us
    ppermute x3, starting transfers between devices, shards(): lax.ppermute(pieces[name - 1], 'basis', [(i, i ^ name) for i in range(cou...  2.21 us
    pallas_call x1, Pallas kernels, ahead(): pl.pallas_call(ahead_kernel, out_shape=(near(rows, comps * comps * stride...  1.65 us
    pallas_call x1, Pallas kernels, pack(): pl.pallas_call(functools.partial(pack_kernel, comps), out_shape=(*pieces,...  1.34 us
  transfers between devices with their start and end apart: 7, of which 4 were waited for; matrix products, arithmetic and copies ran while one was open for 0% of the time, Pallas kernels for 9%

profile of v15, /device:TPU:0, one launch (start us, length us, event | category | flops | bytes accessed | tf_op | source)
XLA Modules:
  0.0 38.1 jit_solution(17882151585294340277)
XLA Ops:
  0.6 3.0 %collective-permute-start.22 = (f32[384,128]{1,0:T(8,128)}, f32[384,128]{1,0:T(8,128)S(1)}, u32[]{:S(2)}, u32[]{:S(2)}) collective-permute-start(f32[384,128]{1,0:T(8,128)} %bitcast.279), channel_id=1, source_target_pairs={{0,4},{8,12},{16,20},{24,28},{4,0},{12,8},{20,16},{28,24},{1,5},{9... | collective-permute-start | bytes 589832 | tf_op jit(solution)/shard_map/ppermute | solution.py:38
  3.6 1.3 %pack.1 = (f32[48,8,128]{2,1,0:T(8,128)S(1)}, f32[54,8,128]{2,1,0:T(8,128)S(1)}, f32[48,8,128]{2,1,0:T(8,128)S(1)}, f32[54,8,128]{2,1,0:T(8,128)S(1)}, f32[384,128]{1,0:T(8,128)S(1)}, /*index=5*/s32[8,128]{1,0:T(8,128)S(1)}) custom-call(s32[1]{0:T(128)} %bitcast.116.place_ref, f32[48,4,8,128]{3,2,1,0:T(8,128)} %bitcast.273, f32[384,128]{1,0:T(8,128)} %bitcast.280, ...), custom_call_target="tpu_custom_call" | custom-call | tf_op jit(solution)/shard_map/pack/pallas_call | solution.py:88
  5.0 0.7 %collective-permute-start.23 = (f32[54,8,128]{2,1,0:T(8,128)S(1)}, f32[54,8,128]{2,1,0:T(8,128)S(1)}, u32[]{:S(2)}, u32[]{:S(2)}) collective-permute-start(f32[54,8,128]{2,1,0:T(8,128)S(1)} %get-tuple-element.120), channel_id=1, source_target_pairs={{0,3},{1,2},{2,1},{3,0},{4,7},{5,6},{6,5},{7,4},{8,11},{9,10},{10,... | collective-permute-start | bytes 663560 | tf_op jit(solution)/shard_map/ppermute | solution.py:645
  5.7 1.0 %collective-permute-start.24 = (f32[54,8,128]{2,1,0:T(8,128)S(1)}, f32[54,8,128]{2,1,0:T(8,128)S(1)}, u32[]{:S(2)}, u32[]{:S(2)}) collective-permute-start(f32[54,8,128]{2,1,0:T(8,128)S(1)} %get-tuple-element.121), channel_id=1, source_target_pairs={{0,1},{1,0},{2,3},{3,2},{4,5},{5,4},{6,7},{7,6},{8,9},{9,8},{10,11... | collective-permute-start | bytes 663560 | tf_op jit(solution)/shard_map/ppermute | solution.py:645
  6.7 0.5 %collective-permute-start.25 = (f32[48,8,128]{2,1,0:T(8,128)S(1)}, f32[48,8,128]{2,1,0:T(8,128)S(1)}, u32[]{:S(2)}, u32[]{:S(2)}) collective-permute-start(f32[48,8,128]{2,1,0:T(8,128)S(1)} %get-tuple-element.126), channel_id=1, source_target_pairs={{0,2},{1,3},{2,0},{3,1},{4,6},{5,7},{6,4},{7,5},{8,10},{9,11},{10,... | collective-permute-start | bytes 589832 | tf_op jit(solution)/shard_map/ppermute | solution.py:645
  7.2 0.7 %collective-permute-start.26 = (f32[384,128]{1,0:T(8,128)}, f32[384,128]{1,0:T(8,128)S(1)}, u32[]{:S(2)}, u32[]{:S(2)}) collective-permute-start(f32[384,128]{1,0:T(8,128)} %bitcast.281), channel_id=1, source_target_pairs={{4,8},{12,16},{20,24},{8,4},{16,12},{24,20},{5,9},{13,17},{21,25},... | collective-permute-start | bytes 589832 | tf_op jit(solution)/shard_map/ppermute | solution.py:38
  8.5 1.7 %ahead.1 = (f32[8,72,128]{2,1,0:T(8,128)S(1)}, f32[24,16,128]{2,1,0:T(8,128)S(1)}, bf16[48,3072]{1,0:T(8,128)(2,1)S(1)}) custom-call(s32[1]{0:T(128)S(6)} %copy.194.sample_ref, f32[1024]{0:T(1024)} %refs_0_.1, f32[1024]{0:T(1024)} %refs_1_.1, f32[3,3,8,7]{3,2,1,0:T(8,128)} %bitcast.293, f32[3,3,8,7]{3,2,1,0:T(8,128)} %bitcast.295, f32[3,8]{1,0:T(4,128)} %bitcast.298, ...), custom_call_target="tpu_custom_call" | custom-call | tf_op jit(solution)/shard_map/ahead/pallas_call | solution.py:185
  10.2 0.0 collective-permute-done.22.halo_ref
  10.2 0.1 side.1.applied_ref
  10.3 2.4 %collective-permute-done.23 = f32[54,8,128]{2,1,0:T(8,128)S(1)} collective-permute-done((f32[54,8,128]{2,1,0:T(8,128)S(1)}, f32[54,8,128]{2,1,0:T(8,128)S(1)}, u32[]{:S(2)}, u32[]{:S(2)}) %collective-permute-start.23) | collective-permute-done | bytes 221216 | tf_op jit(solution)/shard_map/ppermute | solution.py:645
  12.7 0.0 collective-permute-done.24
  12.7 0.2 edges.1
  12.9 4.1 %collective-permute-done.25 = f32[48,8,128]{2,1,0:T(8,128)S(1)} collective-permute-done((f32[48,8,128]{2,1,0:T(8,128)S(1)}, f32[48,8,128]{2,1,0:T(8,128)S(1)}, u32[]{:S(2)}, u32[]{:S(2)}) %collective-permute-start.25) | collective-permute-done | bytes 196640 | tf_op jit(solution)/shard_map/ppermute | solution.py:645
  17.0 0.0 collective-permute-done.26.refs_4_
  17.0 1.0 %sums.1 = (bf16[240,3072]{1,0:T(8,128)(2,1)S(1)}, f32[32,128]{1,0:T(8,128)S(1)}) custom-call(s32[1]{0:T(128)} %bitcast.116.place_ref, s32[1]{0:T(128)} %bitcast.117.slab_ref, f32[8,72,128]{2,1,0:T(8,128)S(1)} %get-tuple-element.118.fields_ref, f32[24,16,128]{2,1,0:T(8,128)S(1)} %get-tuple-element.122.applied_ref, ...), custom_call_target="tpu_custom_call" | custom-call | tf_op jit(solution)/shard_map/sums/pallas_call | solution.py:369
  18.0 0.1 collective-permute-start.27
  18.1 1.1 %collective-permute-done.27 = f32[32,128]{1,0:T(8,128)S(1)} collective-permute-done((f32[32,128]{1,0:T(8,128)S(1)}, f32[32,128]{1,0:T(8,128)S(1)}, u32[]{:S(2)}, u32[]{:S(2)}) %collective-permute-start.27) | collective-permute-done | bytes 16416 | tf_op jit(solution)/shard_map/ppermute | solution.py:386
  19.2 1.0 %collective-permute-start.28 = (f32[32,128]{1,0:T(8,128)S(1)}, f32[32,128]{1,0:T(8,128)S(1)}, u32[]{:S(2)}, u32[]{:S(2)}) collective-permute-start(f32[32,128]{1,0:T(8,128)S(1)} %add.359), channel_id=1, source_target_pairs={{0,2},{1,3},{2,0},{3,1},{4,6},{5,7},{6,4},{7,5},{8,10},{9,11},{10,... | collective-permute-start | bytes 49160 | tf_op jit(solution)/shard_map/ppermute | solution.py:386
  20.2 2.8 %collective-permute-done.28 = f32[32,128]{1,0:T(8,128)S(1)} collective-permute-done((f32[32,128]{1,0:T(8,128)S(1)}, f32[32,128]{1,0:T(8,128)S(1)}, u32[]{:S(2)}, u32[]{:S(2)}) %collective-permute-start.28) | collective-permute-done | bytes 16416 | tf_op jit(solution)/shard_map/ppermute | solution.py:386
  23.0 12.0 %all_to_all.5.parts_ref = f32[8,32,128]{2,1,0:T(8,128)S(1)} all-to-all(f32[8,32,128]{2,1,0:T(8,128)S(1)} %broadcast_in_dim.34), channel_id=1, replica_groups=mesh['space'=8,'basis'=4] {'space'}, dimensions={0} | all-to-all | bytes 262144 | tf_op jit(solution)/shard_map/all_to_all | solution.py:393
  35.0 2.5 %finish.1 = (f32[16,24,128]{2,1,0:T(8,128)}, f32[16,16]{1,0:T(8,128)}, f32[16,16]{1,0:T(8,128)}, s32[1,1]{1,0:T(1,128)}) custom-call(s32[1]{0:T(128)} %bitcast.116.place_ref, f32[8,32,128]{2,1,0:T(8,128)S(1)} %all_to_all.5.parts_ref, bf16[240,3072]{1,0:T(8,128)(2,1)S(1)} %get-tuple-element.128.stack_ref), custom_call_target="tpu_custom_call" | custom-call | tf_op jit(solution)/shard_map/finish/pallas_call | solution.py:493
  37.4 0.7 %while.14 = (s32[]{:T(128)}, f32[16,24,128]{2,1,0:T(8,128)}, f32[16,16]{1,0:T(8,128)}, f32[16,16]{1,0:T(8,128)}, f32[8,7,3,3]{1,0,3,2:T(8,128)}, /*index=5*/f32[...) while((s32[]{:T(128)}, f32[16,24,128]{2,1,0:T(8,128)}, ...), condition=%region_3.4_spmd, body=%region_0.3_spmd | while | flops 175311344 | bytes 29713228 | solution.py:660
  (3 shorter events, 0.0 us)
Async XLA Ops:
  0.6 9.5 %collective-permute-start.22 = (f32[384,128]{1,0:T(8,128)}, f32[384,128]{1,0:T(8,128)S(1)}, u32[]{:S(2)}, u32[]{:S(2)}) collective-permute-start(f32[384,128]{1,0:T(8,128)} %bitcast.279), channel_id=1, source_target_pairs={{0,4},{8,12},{16,20},{24,28},{4,0},{12,8},{20,16},{28,24},{1,5},{9... | collective-permute-start | bytes 589832 | tf_op jit(solution)/shard_map/ppermute | solution.py:38
  5.0 7.7 %collective-permute-start.23 = (f32[54,8,128]{2,1,0:T(8,128)S(1)}, f32[54,8,128]{2,1,0:T(8,128)S(1)}, u32[]{:S(2)}, u32[]{:S(2)}) collective-permute-start(f32[54,8,128]{2,1,0:T(8,128)S(1)} %get-tuple-element.120), channel_id=1, source_target_pairs={{0,3},{1,2},{2,1},{3,0},{4,7},{5,6},{6,5},{7,4},{8,11},{9,10},{10,... | collective-permute-start | bytes 663560 | tf_op jit(solution)/shard_map/ppermute | solution.py:645
  5.7 7.0 %collective-permute-start.24 = (f32[54,8,128]{2,1,0:T(8,128)S(1)}, f32[54,8,128]{2,1,0:T(8,128)S(1)}, u32[]{:S(2)}, u32[]{:S(2)}) collective-permute-start(f32[54,8,128]{2,1,0:T(8,128)S(1)} %get-tuple-element.121), channel_id=1, source_target_pairs={{0,1},{1,0},{2,3},{3,2},{4,5},{5,4},{6,7},{7,6},{8,9},{9,8},{10,11... | collective-permute-start | bytes 663560 | tf_op jit(solution)/shard_map/ppermute | solution.py:645
  6.7 10.3 %collective-permute-start.25 = (f32[48,8,128]{2,1,0:T(8,128)S(1)}, f32[48,8,128]{2,1,0:T(8,128)S(1)}, u32[]{:S(2)}, u32[]{:S(2)}) collective-permute-start(f32[48,8,128]{2,1,0:T(8,128)S(1)} %get-tuple-element.126), channel_id=1, source_target_pairs={{0,2},{1,3},{2,0},{3,1},{4,6},{5,7},{6,4},{7,5},{8,10},{9,11},{10,... | collective-permute-start | bytes 589832 | tf_op jit(solution)/shard_map/ppermute | solution.py:645
  7.2 9.8 %collective-permute-start.26 = (f32[384,128]{1,0:T(8,128)}, f32[384,128]{1,0:T(8,128)S(1)}, u32[]{:S(2)}, u32[]{:S(2)}) collective-permute-start(f32[384,128]{1,0:T(8,128)} %bitcast.281), channel_id=1, source_target_pairs={{4,8},{12,16},{20,24},{8,4},{16,12},{24,20},{5,9},{13,17},{21,25},... | collective-permute-start | bytes 589832 | tf_op jit(solution)/shard_map/ppermute | solution.py:38
  18.0 1.2 %collective-permute-start.27 = (f32[32,128]{1,0:T(8,128)S(1)}, f32[32,128]{1,0:T(8,128)S(1)}, u32[]{:S(2)}, u32[]{:S(2)}) collective-permute-start(f32[32,128]{1,0:T(8,128)S(1)} %get-tuple-element.127), channel_id=1, source_target_pairs={{0,1},{1,0},{2,3},{3,2},{4,5},{5,4},{6,7},{7,6},{8,9},{9,8},{10,11... | collective-permute-start | bytes 49160 | tf_op jit(solution)/shard_map/ppermute | solution.py:386
  19.2 3.7 %collective-permute-start.28 = (f32[32,128]{1,0:T(8,128)S(1)}, f32[32,128]{1,0:T(8,128)S(1)}, u32[]{:S(2)}, u32[]{:S(2)}) collective-permute-start(f32[32,128]{1,0:T(8,128)S(1)} %add.359), channel_id=1, source_target_pairs={{0,2},{1,3},{2,0},{3,1},{4,6},{5,7},{6,4},{7,5},{8,10},{9,11},{10,... | collective-permute-start | bytes 49160 | tf_op jit(solution)/shard_map/ppermute | solution.py:386

commit v16 on v15

--- a/solution.py
+++ b/solution.py
@@ -379,29 +379,32 @@
     )(place, slab, *kept(fields, applied, *split.values(), *raw.values(), halo))
 
 
-def exchange_sum(part, axis):
-    count = lax.axis_size(axis)
-    mask = 1
-    while mask < count:
-        part = part + lax.ppermute(part, axis, [(i, i ^ mask) for i in range(count)])
+def exchange_all(part):
+    sizes = [lax.axis_size(axis) for axis in ("space", "basis")]
+    part = part + lax.ppermute(part, "basis", [(i, i ^ 1) for i in range(sizes[1])])
+    mask = 2
+    while mask < sizes[1]:
+        part = part + lax.ppermute(part, "basis", [(i, i ^ mask) for i in range(1, sizes[1], 2)])
         mask *= 2
-    return part
-
-
-def exchange(part, axis):
-    count = lax.axis_size(axis)
-    return lax.all_to_all(jnp.broadcast_to(part[None], (count,) + part.shape), axis, 0, 0)
+    index = [[i * sizes[1] + j for j in range(sizes[1])] for i in range(sizes[0])]
+    groups = [[row[j] for row in index] for j in range(1, sizes[1], 2)]
+    others = [row[j] for row in index for j in range(0, sizes[1], 2)]
+    groups += [others[i : i + sizes[0]] for i in range(0, len(others), sizes[0])]
+    copies = jnp.broadcast_to(part[None], (sizes[0],) + part.shape)
+    parts = lax.all_to_all(copies, ("space", "basis"), 0, 0, axis_index_groups=groups)
+    own = jnp.sum(parts, axis=0)
+    return own, lax.ppermute(own, "basis", [(i, i - 1) for i in range(1, sizes[1], 2)])
 
 
 def finish_kernel(
-    row_count, comps, place_ref, parts_ref, stack_ref, block_ref, coeffs_ref, upper_ref, bad_ref,
+    row_count, comps, place_ref, own_ref, given_ref, stack_ref, block_ref, coeffs_ref, upper_ref, bad_ref,
     coeffs_scratch, upper_scratch, bad_scratch, block_scratch, sems,
 ):
     block_cols = upper_ref.shape[0]
-    basis_cols = parts_ref.shape[2] // 2
+    basis_cols = own_ref.shape[1] // 2
     joined = basis_cols + block_cols
     lines, lanes = block_ref.shape[1:]
-    total = jnp.sum(parts_ref[...], axis=0) / row_count
+    total = jnp.where(place_ref[0] % 2 == 0, given_ref[...], own_ref[...]) / row_count
     gram, first, block_gram = unfold(total, block_cols)
 
     def times(left, right, right_dim=0):
@@ -487,16 +490,16 @@
         copy.wait()
 
 
-def finish(place, parts, stack, row_count, block_cols, group_cols, lines, comps):
+def finish(place, totals, stack, row_count, block_cols, group_cols, lines, comps):
     lanes = stack.shape[1] // lines
-    basis_cols = parts.shape[2] // 2
+    basis_cols = totals[0].shape[1] // 2
     return pl.pallas_call(
         functools.partial(finish_kernel, row_count, comps),
         out_shape=(
             f32(block_cols, lines, lanes), f32(group_cols, block_cols), f32(block_cols, block_cols),
             jax.ShapeDtypeStruct((1, 1), jnp.int32),
         ),
-        in_specs=[SMEM] + [VMEM] * 2,
+        in_specs=[SMEM] + [VMEM] * 3,
         out_specs=(HBM,) * 4,
         scratch_shapes=[
             pltpu.VMEM((basis_cols, block_cols), jnp.float32),
@@ -507,7 +510,7 @@
         ],
         compiler_params=SCRATCH,
         name="finish",
-    )(place, *kept(parts, stack))
+    )(place, *kept(*totals, stack))
 
 
 def stencil_tables(k0_blocks, k0_diag, ke_blocks, mass, velocities, shifts, sample):
@@ -653,9 +656,9 @@
     applied, *parts = add_edges(place, fields, applied, pieces, comps, group_cols)
     split = {0: own, **dict(zip(pieces, parts))}
     stack, part = sums(place, slab, fields, applied, got.pop("odd"), split, got, comps)
-    parts = exchange(exchange_sum(part, "basis"), "space")
+    totals = exchange_all(part)
     block, coeffs, upper, bad = finish(
-        place, parts, stack, row_count, block_cols, group_cols, lines, comps
+        place, totals, stack, row_count, block_cols, group_cols, lines, comps
     )
     block, coeffs, upper = lax.while_loop(
         lambda state: state[0] > 0,

time: 38.4 us -> 39.7 us (1.034)
  waiting for transfers between devices: 10.5 us -> 13.5 us
  blocking collectives: 12 us -> 9.41 us
  starting transfers between devices: 6.94 us -> 7.92 us
    ppermute x2 -> x3, waiting for transfers between devices: 3.92 us -> 6.93 us  [the longest x1 5.78 us: exchange_all(): lax.ppermute(own, 'basis', [(i, i - 1) for i in range(1, sizes[1], 2)])]
    all_to_all x1, blocking collectives: 12 us -> 9.41 us  [exchange_all(): lax.all_to_all(copies, ('space', 'basis'), 0, 0, axis_index_groups=groups)]
    ppermute x2 -> x3, starting transfers between devices: 1.07 us -> 2.05 us  [the longest x1 1.29 us: exchange_all(): lax.ppermute(own, 'basis', [(i, i - 1) for i in range(1, sizes[1], 2)])]
  transfers between devices with their start and end apart: 7 -> 8, of which waited for: 4 -> 4; matrix products, arithmetic and copies ran while one was open for 0% -> 0% of each run, Pallas kernels for 9% -> 8%
where the time goes in v16:
time: 39.7 us; the launch traced here: 39.4 us
  waiting for transfers between devices  13.5 us (34%)
  blocking collectives  9.41 us (24%)
  starting transfers between devices  7.92 us (20%)
  Pallas kernels  6.63 us (17%)
  between operations  1.38 us (3%)
  loops' own time  0.56 us (1%)
    all_to_all x1, blocking collectives, exchange_all(): lax.all_to_all(copies, ('space', 'basis'), 0, 0, axis_index_groups=groups)  9.41 us
    ppermute x3, waiting for transfers between devices, shards(): lax.ppermute(pieces[name - 1], 'basis', [(i, i ^ name) for i in range(cou...  6.55 us
    ppermute x1, waiting for transfers between devices, exchange_all(): lax.ppermute(own, 'basis', [(i, i - 1) for i in range(1, sizes[1], 2)])  5.78 us
    ppermute x2, starting transfers between devices, swap(): return lax.ppermute(values, axis, pairs + [(j, i) for i, j in pairs])  3.66 us
    pallas_call x1, Pallas kernels, finish(): pl.pallas_call(functools.partial(finish_kernel, row_count, comps), out_sh...  2.43 us
    ppermute x3, starting transfers between devices, shards(): lax.ppermute(pieces[name - 1], 'basis', [(i, i ^ name) for i in range(cou...  2.21 us
    pallas_call x1, Pallas kernels, ahead(): pl.pallas_call(ahead_kernel, out_shape=(near(rows, comps * comps * stride...  1.65 us
    pallas_call x1, Pallas kernels, pack(): pl.pallas_call(functools.partial(pack_kernel, comps), out_shape=(*pieces,...  1.34 us
  transfers between devices with their start and end apart: 8, of which 4 were waited for; matrix products, arithmetic and copies ran while one was open for 0% of the time, Pallas kernels for 8%

profile of v16, /device:TPU:0, one launch (start us, length us, event | category | flops | bytes accessed | tf_op | source)
XLA Modules:
  0.0 39.4 jit_solution(12856926243258027967)
XLA Ops:
  0.6 3.0 %collective-permute-start.22 = (f32[384,128]{1,0:T(8,128)}, f32[384,128]{1,0:T(8,128)S(1)}, u32[]{:S(2)}, u32[]{:S(2)}) collective-permute-start(f32[384,128]{1,0:T(8,128)} %bitcast.279), channel_id=1, source_target_pairs={{0,4},{8,12},{16,20},{24,28},{4,0},{12,8},{20,16},{28,24},{1,5},{9... | collective-permute-start | bytes 589832 | tf_op jit(solution)/shard_map/ppermute | solution.py:38
  3.6 1.3 %pack.1 = (f32[48,8,128]{2,1,0:T(8,128)S(1)}, f32[54,8,128]{2,1,0:T(8,128)S(1)}, f32[48,8,128]{2,1,0:T(8,128)S(1)}, f32[54,8,128]{2,1,0:T(8,128)S(1)}, f32[384,128]{1,0:T(8,128)S(1)}, /*index=5*/s32[8,128]{1,0:T(8,128)S(1)}) custom-call(s32[1]{0:T(128)} %bitcast.116.place_ref, f32[48,4,8,128]{3,2,1,0:T(8,128)} %bitcast.273, f32[384,128]{1,0:T(8,128)} %bitcast.280, ...), custom_call_target="tpu_custom_call" | custom-call | tf_op jit(solution)/shard_map/pack/pallas_call | solution.py:88
  5.0 0.7 %collective-permute-start.23 = (f32[54,8,128]{2,1,0:T(8,128)S(1)}, f32[54,8,128]{2,1,0:T(8,128)S(1)}, u32[]{:S(2)}, u32[]{:S(2)}) collective-permute-start(f32[54,8,128]{2,1,0:T(8,128)S(1)} %get-tuple-element.120), channel_id=1, source_target_pairs={{0,3},{1,2},{2,1},{3,0},{4,7},{5,6},{6,5},{7,4},{8,11},{9,10},{10,... | collective-permute-start | bytes 663560 | tf_op jit(solution)/shard_map/ppermute | solution.py:648
  5.7 1.0 %collective-permute-start.24 = (f32[54,8,128]{2,1,0:T(8,128)S(1)}, f32[54,8,128]{2,1,0:T(8,128)S(1)}, u32[]{:S(2)}, u32[]{:S(2)}) collective-permute-start(f32[54,8,128]{2,1,0:T(8,128)S(1)} %get-tuple-element.121), channel_id=1, source_target_pairs={{0,1},{1,0},{2,3},{3,2},{4,5},{5,4},{6,7},{7,6},{8,9},{9,8},{10,11... | collective-permute-start | bytes 663560 | tf_op jit(solution)/shard_map/ppermute | solution.py:648
  6.7 0.5 %collective-permute-start.25 = (f32[48,8,128]{2,1,0:T(8,128)S(1)}, f32[48,8,128]{2,1,0:T(8,128)S(1)}, u32[]{:S(2)}, u32[]{:S(2)}) collective-permute-start(f32[48,8,128]{2,1,0:T(8,128)S(1)} %get-tuple-element.126), channel_id=1, source_target_pairs={{0,2},{1,3},{2,0},{3,1},{4,6},{5,7},{6,4},{7,5},{8,10},{9,11},{10,... | collective-permute-start | bytes 589832 | tf_op jit(solution)/shard_map/ppermute | solution.py:648
  7.2 0.7 %collective-permute-start.26 = (f32[384,128]{1,0:T(8,128)}, f32[384,128]{1,0:T(8,128)S(1)}, u32[]{:S(2)}, u32[]{:S(2)}) collective-permute-start(f32[384,128]{1,0:T(8,128)} %bitcast.281), channel_id=1, source_target_pairs={{4,8},{12,16},{20,24},{8,4},{16,12},{24,20},{5,9},{13,17},{21,25},... | collective-permute-start | bytes 589832 | tf_op jit(solution)/shard_map/ppermute | solution.py:38
  8.5 1.7 %ahead.1 = (f32[8,72,128]{2,1,0:T(8,128)S(1)}, f32[24,16,128]{2,1,0:T(8,128)S(1)}, bf16[48,3072]{1,0:T(8,128)(2,1)S(1)}) custom-call(s32[1]{0:T(128)S(6)} %copy.265.sample_ref, f32[1024]{0:T(1024)} %refs_0_.1, f32[1024]{0:T(1024)} %refs_1_.1, f32[3,3,8,7]{3,2,1,0:T(8,128)} %bitcast.293, f32[3,3,8,7]{3,2,1,0:T(8,128)} %bitcast.295, f32[3,8]{1,0:T(4,128)} %bitcast.298, ...), custom_call_target="tpu_custom_call" | custom-call | tf_op jit(solution)/shard_map/ahead/pallas_call | solution.py:185
  10.2 0.0 collective-permute-done.22.halo_ref
  10.2 0.1 side.1.applied_ref
  10.3 2.4 %collective-permute-done.23 = f32[54,8,128]{2,1,0:T(8,128)S(1)} collective-permute-done((f32[54,8,128]{2,1,0:T(8,128)S(1)}, f32[54,8,128]{2,1,0:T(8,128)S(1)}, u32[]{:S(2)}, u32[]{:S(2)}) %collective-permute-start.23) | collective-permute-done | bytes 221216 | tf_op jit(solution)/shard_map/ppermute | solution.py:648
  12.7 0.0 collective-permute-done.24
  12.7 0.2 edges.1
  12.9 4.1 %collective-permute-done.25 = f32[48,8,128]{2,1,0:T(8,128)S(1)} collective-permute-done((f32[48,8,128]{2,1,0:T(8,128)S(1)}, f32[48,8,128]{2,1,0:T(8,128)S(1)}, u32[]{:S(2)}, u32[]{:S(2)}) %collective-permute-start.25) | collective-permute-done | bytes 196640 | tf_op jit(solution)/shard_map/ppermute | solution.py:648
  17.0 0.0 collective-permute-done.26.refs_4_
  17.0 1.0 %sums.1 = (bf16[240,3072]{1,0:T(8,128)(2,1)S(1)}, f32[32,128]{1,0:T(8,128)S(1)}) custom-call(s32[1]{0:T(128)} %bitcast.116.place_ref, s32[1]{0:T(128)} %bitcast.117.slab_ref, f32[8,72,128]{2,1,0:T(8,128)S(1)} %get-tuple-element.118.fields_ref, f32[24,16,128]{2,1,0:T(8,128)S(1)} %get-tuple-element.122.applied_ref, ...), custom_call_target="tpu_custom_call" | custom-call | tf_op jit(solution)/shard_map/sums/pallas_call | solution.py:369
  18.0 0.1 collective-permute-start.27
  18.1 1.1 %collective-permute-done.27 = f32[32,128]{1,0:T(8,128)S(1)} collective-permute-done((f32[32,128]{1,0:T(8,128)S(1)}, f32[32,128]{1,0:T(8,128)S(1)}, u32[]{:S(2)}, u32[]{:S(2)}) %collective-permute-start.27) | collective-permute-done | bytes 16416 | tf_op jit(solution)/shard_map/ppermute | solution.py:384
  19.2 0.7 %collective-permute-start.28 = (f32[32,128]{1,0:T(8,128)S(1)}, f32[32,128]{1,0:T(8,128)S(1)}, u32[]{:S(2)}, u32[]{:S(2)}) collective-permute-start(f32[32,128]{1,0:T(8,128)S(1)} %add.359), channel_id=1, source_target_pairs={{1,3},{3,1},{5,7},{7,5},{9,11},{11,9},{13,15},{15,13},{17,19},{19,... | collective-permute-start | bytes 49160 | tf_op jit(solution)/shard_map/ppermute | solution.py:387
  19.9 0.0 collective-permute-done.28
  19.9 9.4 %all_to_all.5 = f32[8,32,128]{2,1,0:T(8,128)S(1)} all-to-all(f32[8,32,128]{2,1,0:T(8,128)S(1)} %broadcast_in_dim.34), channel_id=1, replica_groups={{1,5,9,13,17,21,25,29},{3,7,11,15,19,23,27,31},{0,2,4,6,8,10,12,14},{16..., dimensions={0} | all-to-all | bytes 262144 | tf_op jit(solution)/shard_map/all_to_all | solution.py:394
  29.3 1.3 %collective-permute-start.29 = (f32[32,128]{1,0:T(8,128)S(1)}, f32[32,128]{1,0:T(8,128)S(1)}, u32[]{:S(2)}, u32[]{:S(2)}) collective-permute-start(f32[32,128]{1,0:T(8,128)S(1)} %reduce_sum.9.own_ref), channel_id=1, source_target_pairs={{1,0},{3,2},{5,4},{7,6},{9,8},{11,10},{13,12},{15,14},{17,16},{19,... | collective-permute-start | bytes 49160 | tf_op jit(solution)/shard_map/ppermute | solution.py:396
  30.6 5.8 %collective-permute-done.29.given_ref = f32[32,128]{1,0:T(8,128)S(1)} collective-permute-done((f32[32,128]{1,0:T(8,128)S(1)}, f32[32,128]{1,0:T(8,128)S(1)}, u32[]{:S(2)}, u32[]{:S(2)}) %collective-permute-start.29) | collective-permute-done | bytes 16416 | tf_op jit(solution)/shard_map/ppermute | solution.py:396
  36.4 2.4 %finish.1 = (f32[16,24,128]{2,1,0:T(8,128)}, f32[16,16]{1,0:T(8,128)}, f32[16,16]{1,0:T(8,128)}, s32[1,1]{1,0:T(1,128)}) custom-call(s32[1]{0:T(128)} %bitcast.116.place_ref, f32[32,128]{1,0:T(8,128)S(1)} %reduce_sum.9.own_ref, f32[32,128]{1,0:T(8,128)S(1)} %collective-permute-done.29.given_ref, bf16[240,3072]{1,0:T(8,128)(2,1)S(1)} %get-tuple-element.128.stack_ref), custom_call_target="tpu_custom_call" | custom-call | tf_op jit(solution)/shard_map/finish/pallas_call | solution.py:496
  38.9 0.6 %while.14 = (s32[]{:T(128)}, f32[16,24,128]{2,1,0:T(8,128)}, f32[16,16]{1,0:T(8,128)}, f32[16,16]{1,0:T(8,128)}, f32[8,7,3,3]{1,0,3,2:T(8,128)}, /*index=5*/f32[...) while((s32[]{:T(128)}, f32[16,24,128]{2,1,0:T(8,128)}, ...), condition=%region_4.5_spmd, body=%region_1.4_spmd | while | flops 175311344 | bytes 29713228 | solution.py:663
  (4 shorter events, 0.0 us)
Async XLA Ops:
  0.6 9.5 %collective-permute-start.22 = (f32[384,128]{1,0:T(8,128)}, f32[384,128]{1,0:T(8,128)S(1)}, u32[]{:S(2)}, u32[]{:S(2)}) collective-permute-start(f32[384,128]{1,0:T(8,128)} %bitcast.279), channel_id=1, source_target_pairs={{0,4},{8,12},{16,20},{24,28},{4,0},{12,8},{20,16},{28,24},{1,5},{9... | collective-permute-start | bytes 589832 | tf_op jit(solution)/shard_map/ppermute | solution.py:38
  5.0 7.7 %collective-permute-start.23 = (f32[54,8,128]{2,1,0:T(8,128)S(1)}, f32[54,8,128]{2,1,0:T(8,128)S(1)}, u32[]{:S(2)}, u32[]{:S(2)}) collective-permute-start(f32[54,8,128]{2,1,0:T(8,128)S(1)} %get-tuple-element.120), channel_id=1, source_target_pairs={{0,3},{1,2},{2,1},{3,0},{4,7},{5,6},{6,5},{7,4},{8,11},{9,10},{10,... | collective-permute-start | bytes 663560 | tf_op jit(solution)/shard_map/ppermute | solution.py:648
  5.7 7.0 %collective-permute-start.24 = (f32[54,8,128]{2,1,0:T(8,128)S(1)}, f32[54,8,128]{2,1,0:T(8,128)S(1)}, u32[]{:S(2)}, u32[]{:S(2)}) collective-permute-start(f32[54,8,128]{2,1,0:T(8,128)S(1)} %get-tuple-element.121), channel_id=1, source_target_pairs={{0,1},{1,0},{2,3},{3,2},{4,5},{5,4},{6,7},{7,6},{8,9},{9,8},{10,11... | collective-permute-start | bytes 663560 | tf_op jit(solution)/shard_map/ppermute | solution.py:648
  6.7 10.3 %collective-permute-start.25 = (f32[48,8,128]{2,1,0:T(8,128)S(1)}, f32[48,8,128]{2,1,0:T(8,128)S(1)}, u32[]{:S(2)}, u32[]{:S(2)}) collective-permute-start(f32[48,8,128]{2,1,0:T(8,128)S(1)} %get-tuple-element.126), channel_id=1, source_target_pairs={{0,2},{1,3},{2,0},{3,1},{4,6},{5,7},{6,4},{7,5},{8,10},{9,11},{10,... | collective-permute-start | bytes 589832 | tf_op jit(solution)/shard_map/ppermute | solution.py:648
  7.2 9.8 %collective-permute-start.26 = (f32[384,128]{1,0:T(8,128)}, f32[384,128]{1,0:T(8,128)S(1)}, u32[]{:S(2)}, u32[]{:S(2)}) collective-permute-start(f32[384,128]{1,0:T(8,128)} %bitcast.281), channel_id=1, source_target_pairs={{4,8},{12,16},{20,24},{8,4},{16,12},{24,20},{5,9},{13,17},{21,25},... | collective-permute-start | bytes 589832 | tf_op jit(solution)/shard_map/ppermute | solution.py:38
  18.0 1.2 %collective-permute-start.27 = (f32[32,128]{1,0:T(8,128)S(1)}, f32[32,128]{1,0:T(8,128)S(1)}, u32[]{:S(2)}, u32[]{:S(2)}) collective-permute-start(f32[32,128]{1,0:T(8,128)S(1)} %get-tuple-element.127), channel_id=1, source_target_pairs={{0,1},{1,0},{2,3},{3,2},{4,5},{5,4},{6,7},{7,6},{8,9},{9,8},{10,11... | collective-permute-start | bytes 49160 | tf_op jit(solution)/shard_map/ppermute | solution.py:384
  19.2 0.7 %collective-permute-start.28 = (f32[32,128]{1,0:T(8,128)S(1)}, f32[32,128]{1,0:T(8,128)S(1)}, u32[]{:S(2)}, u32[]{:S(2)}) collective-permute-start(f32[32,128]{1,0:T(8,128)S(1)} %add.359), channel_id=1, source_target_pairs={{1,3},{3,1},{5,7},{7,5},{9,11},{11,9},{13,15},{15,13},{17,19},{19,... | collective-permute-start | bytes 49160 | tf_op jit(solution)/shard_map/ppermute | solution.py:387
  29.3 7.1 %collective-permute-start.29 = (f32[32,128]{1,0:T(8,128)S(1)}, f32[32,128]{1,0:T(8,128)S(1)}, u32[]{:S(2)}, u32[]{:S(2)}) collective-permute-start(f32[32,128]{1,0:T(8,128)S(1)} %reduce_sum.9.own_ref), channel_id=1, source_target_pairs={{1,0},{3,2},{5,4},{7,6},{9,8},{11,10},{13,12},{15,14},{17,16},{19,... | collective-permute-start | bytes 49160 | tf_op jit(solution)/shard_map/ppermute | solution.py:396

commit v17 on v16

--- a/solution.py
+++ b/solution.py
@@ -323,7 +323,7 @@
 def sums_kernel(
     comps, split, raw, place_ref, slab_ref, fields_ref, applied_ref, *refs
 ):
-    *refs, halo_ref, stack_ref, sums_ref = refs
+    *refs, halo_ref, stack_ref, keep_ref, give_ref = refs
     lines, block_cols, lanes = applied_ref.shape
     rows = lines // comps
     group_cols = refs[0].shape[0] // 3
@@ -359,7 +359,11 @@
     )
     wide = products[:joined] + products[joined : 2 * joined] + products[2 * joined :]
     total = wide[:, :joined] + wide[:, joined : 2 * joined] + wide[:, 2 * joined :]
-    sums_ref[...] = fold(total, basis_cols, block_cols, sums_ref.shape[1])
+    folded = fold(total, basis_cols, block_cols, keep_ref.shape[1])
+    half = keep_ref.shape[0]
+    odd = place % 2 == 1
+    keep_ref[...] = jnp.where(odd, folded[half:], folded[:half])
+    give_ref[...] = jnp.where(odd, folded[:half], folded[half:])
 
 
 def sums(place, slab, fields, applied, halo, split, raw, comps):
@@ -370,30 +374,28 @@
         functools.partial(sums_kernel, comps, tuple(split), tuple(raw)),
         out_shape=(
             near(3 * joined, lines * lanes, dtype=jnp.bfloat16),
-            near(basis_cols // 2, 2 * basis_cols),
+            near(basis_cols // 4, 2 * basis_cols),
+            near(basis_cols // 4, 2 * basis_cols),
         ),
         in_specs=[SMEM] * 2 + [VMEM] * (3 + len(split) + len(raw)),
-        out_specs=(VMEM, VMEM),
+        out_specs=(VMEM,) * 3,
         compiler_params=SCRATCH,
         name="sums",
     )(place, slab, *kept(fields, applied, *split.values(), *raw.values(), halo))
 
 
-def exchange_all(part):
+def exchange_all(keep, give):
     sizes = [lax.axis_size(axis) for axis in ("space", "basis")]
-    part = part + lax.ppermute(part, "basis", [(i, i ^ 1) for i in range(sizes[1])])
-    mask = 2
-    while mask < sizes[1]:
-        part = part + lax.ppermute(part, "basis", [(i, i ^ mask) for i in range(1, sizes[1], 2)])
-        mask *= 2
-    index = [[i * sizes[1] + j for j in range(sizes[1])] for i in range(sizes[0])]
-    groups = [[row[j] for row in index] for j in range(1, sizes[1], 2)]
-    others = [row[j] for row in index for j in range(0, sizes[1], 2)]
-    groups += [others[i : i + sizes[0]] for i in range(0, len(others), sizes[0])]
-    copies = jnp.broadcast_to(part[None], (sizes[0],) + part.shape)
+    pairs = [(i, i ^ 1) for i in range(sizes[1])]
+    part = keep + lax.ppermute(give, "basis", pairs)
+    groups = [
+        [i * sizes[1] + j for i in range(sizes[0]) for j in range(first, sizes[1], 2)]
+        for first in range(2)
+    ]
+    copies = jnp.broadcast_to(part[None], (len(groups[0]),) + part.shape)
     parts = lax.all_to_all(copies, ("space", "basis"), 0, 0, axis_index_groups=groups)
     own = jnp.sum(parts, axis=0)
-    return own, lax.ppermute(own, "basis", [(i, i - 1) for i in range(1, sizes[1], 2)])
+    return own, lax.ppermute(own, "basis", pairs)
 
 
 def finish_kernel(
@@ -404,7 +406,10 @@
     basis_cols = own_ref.shape[1] // 2
     joined = basis_cols + block_cols
     lines, lanes = block_ref.shape[1:]
-    total = jnp.where(place_ref[0] % 2 == 0, given_ref[...], own_ref[...]) / row_count
+    odd = place_ref[0] % 2 == 1
+    own, given = own_ref[...], given_ref[...]
+    total = jnp.concatenate((jnp.where(odd, given, own), jnp.where(odd, own, given)), axis=0)
+    total = total / row_count
     gram, first, block_gram = unfold(total, block_cols)
 
     def times(left, right, right_dim=0):
@@ -490,9 +495,9 @@
         copy.wait()
 
 
-def finish(place, totals, stack, row_count, block_cols, group_cols, lines, comps):
+def finish(place, halves, stack, row_count, block_cols, group_cols, lines, comps):
     lanes = stack.shape[1] // lines
-    basis_cols = totals[0].shape[1] // 2
+    basis_cols = halves[0].shape[1] // 2
     return pl.pallas_call(
         functools.partial(finish_kernel, row_count, comps),
         out_shape=(
@@ -510,7 +515,7 @@
         ],
         compiler_params=SCRATCH,
         name="finish",
-    )(place, *kept(*totals, stack))
+    )(place, *kept(*halves, stack))
 
 
 def stencil_tables(k0_blocks, k0_diag, ke_blocks, mass, velocities, shifts, sample):
@@ -655,10 +660,10 @@
     pieces = {k: got.pop(k) for k in reversed(partners(count)[1])}
     applied, *parts = add_edges(place, fields, applied, pieces, comps, group_cols)
     split = {0: own, **dict(zip(pieces, parts))}
-    stack, part = sums(place, slab, fields, applied, got.pop("odd"), split, got, comps)
-    totals = exchange_all(part)
+    stack, keep, give = sums(place, slab, fields, applied, got.pop("odd"), split, got, comps)
+    halves = exchange_all(keep, give)
     block, coeffs, upper, bad = finish(
-        place, totals, stack, row_count, block_cols, group_cols, lines, comps
+        place, halves, stack, row_count, block_cols, group_cols, lines, comps
     )
     block, coeffs, upper = lax.while_loop(
         lambda state: state[0] > 0,

time: 39.7 us -> 37.1 us (0.935)
  waiting for transfers between devices: 13.5 us -> 8.85 us
  blocking collectives: 9.41 us -> 13.2 us
  starting transfers between devices: 7.92 us -> 6.05 us
    ppermute x3 -> x2, waiting for transfers between devices: 6.93 us -> 2.29 us  [the longest x1 1.16 us: exchange_all(): return (own, lax.ppermute(own, 'basis', pairs))]
    all_to_all x1, blocking collectives: 9.41 us -> 13.2 us  [exchange_all(): lax.all_to_all(copies, ('space', 'basis'), 0, 0, axis_index_groups=groups)]
    ppermute x3 -> x2, starting transfers between devices: 2.05 us -> 0.17 us  [the longest x1 0.1 us: exchange_all(): part = keep + lax.ppermute(give, 'basis', pairs)]
  transfers between devices with their start and end apart: 8 -> 7, of which waited for: 4 -> 4; matrix products, arithmetic and copies ran while one was open for 0% -> 0% of each run, Pallas kernels for 8% -> 9%
where the time goes in v17:
time: 37.1 us; the launch traced here: 36.9 us
  blocking collectives  13.2 us (36%)
  waiting for transfers between devices  8.85 us (24%)
  Pallas kernels  6.65 us (18%)
  starting transfers between devices  6.05 us (16%)
  between operations  1.35 us (4%)
  loops' own time  0.68 us (2%)
    all_to_all x1, blocking collectives, exchange_all(): lax.all_to_all(copies, ('space', 'basis'), 0, 0, axis_index_groups=groups)  13.2 us
    ppermute x3, waiting for transfers between devices, shards(): lax.ppermute(pieces[name - 1], 'basis', [(i, i ^ name) for i in range(cou...  6.55 us
    ppermute x2, starting transfers between devices, swap(): return lax.ppermute(values, axis, pairs + [(j, i) for i, j in pairs])  3.66 us
    pallas_call x1, Pallas kernels, finish(): pl.pallas_call(functools.partial(finish_kernel, row_count, comps), out_sh...  2.45 us
    ppermute x3, starting transfers between devices, shards(): lax.ppermute(pieces[name - 1], 'basis', [(i, i ^ name) for i in range(cou...  2.21 us
    pallas_call x1, Pallas kernels, ahead(): pl.pallas_call(ahead_kernel, out_shape=(near(rows, comps * comps * stride...  1.65 us
    pallas_call x1, Pallas kernels, pack(): pl.pallas_call(functools.partial(pack_kernel, comps), out_shape=(*pieces,...  1.34 us
    ppermute x1, waiting for transfers between devices, exchange_all(): return (own, lax.ppermute(own, 'basis', pairs))  1.16 us
  transfers between devices with their start and end apart: 7, of which 4 were waited for; matrix products, arithmetic and copies ran while one was open for 0% of the time, Pallas kernels for 9%

profile of v17, /device:TPU:0, one launch (start us, length us, event | category | flops | bytes accessed | tf_op | source)
XLA Modules:
  0.0 36.9 jit_solution(969576182236540102)
XLA Ops:
  0.6 3.0 %collective-permute-start.22 = (f32[384,128]{1,0:T(8,128)}, f32[384,128]{1,0:T(8,128)S(1)}, u32[]{:S(2)}, u32[]{:S(2)}) collective-permute-start(f32[384,128]{1,0:T(8,128)} %bitcast.279), channel_id=1, source_target_pairs={{0,4},{8,12},{16,20},{24,28},{4,0},{12,8},{20,16},{28,24},{1,5},{9... | collective-permute-start | bytes 589832 | tf_op jit(solution)/shard_map/ppermute | solution.py:38
  3.6 1.3 %pack.1 = (f32[48,8,128]{2,1,0:T(8,128)S(1)}, f32[54,8,128]{2,1,0:T(8,128)S(1)}, f32[48,8,128]{2,1,0:T(8,128)S(1)}, f32[54,8,128]{2,1,0:T(8,128)S(1)}, f32[384,128]{1,0:T(8,128)S(1)}, /*index=5*/s32[8,128]{1,0:T(8,128)S(1)}) custom-call(s32[1]{0:T(128)} %bitcast.116.place_ref, f32[48,4,8,128]{3,2,1,0:T(8,128)} %bitcast.273, f32[384,128]{1,0:T(8,128)} %bitcast.280, ...), custom_call_target="tpu_custom_call" | custom-call | tf_op jit(solution)/shard_map/pack/pallas_call | solution.py:88
  5.0 0.7 %collective-permute-start.23 = (f32[54,8,128]{2,1,0:T(8,128)S(1)}, f32[54,8,128]{2,1,0:T(8,128)S(1)}, u32[]{:S(2)}, u32[]{:S(2)}) collective-permute-start(f32[54,8,128]{2,1,0:T(8,128)S(1)} %get-tuple-element.121), channel_id=1, source_target_pairs={{0,3},{1,2},{2,1},{3,0},{4,7},{5,6},{6,5},{7,4},{8,11},{9,10},{10,... | collective-permute-start | bytes 663560 | tf_op jit(solution)/shard_map/ppermute | solution.py:653
  5.7 1.0 %collective-permute-start.24 = (f32[54,8,128]{2,1,0:T(8,128)S(1)}, f32[54,8,128]{2,1,0:T(8,128)S(1)}, u32[]{:S(2)}, u32[]{:S(2)}) collective-permute-start(f32[54,8,128]{2,1,0:T(8,128)S(1)} %get-tuple-element.122), channel_id=1, source_target_pairs={{0,1},{1,0},{2,3},{3,2},{4,5},{5,4},{6,7},{7,6},{8,9},{9,8},{10,11... | collective-permute-start | bytes 663560 | tf_op jit(solution)/shard_map/ppermute | solution.py:653
  6.7 0.5 %collective-permute-start.25 = (f32[48,8,128]{2,1,0:T(8,128)S(1)}, f32[48,8,128]{2,1,0:T(8,128)S(1)}, u32[]{:S(2)}, u32[]{:S(2)}) collective-permute-start(f32[48,8,128]{2,1,0:T(8,128)S(1)} %get-tuple-element.127), channel_id=1, source_target_pairs={{0,2},{1,3},{2,0},{3,1},{4,6},{5,7},{6,4},{7,5},{8,10},{9,11},{10,... | collective-permute-start | bytes 589832 | tf_op jit(solution)/shard_map/ppermute | solution.py:653
  7.2 0.7 %collective-permute-start.26 = (f32[384,128]{1,0:T(8,128)}, f32[384,128]{1,0:T(8,128)S(1)}, u32[]{:S(2)}, u32[]{:S(2)}) collective-permute-start(f32[384,128]{1,0:T(8,128)} %bitcast.281), channel_id=1, source_target_pairs={{4,8},{12,16},{20,24},{8,4},{16,12},{24,20},{5,9},{13,17},{21,25},... | collective-permute-start | bytes 589832 | tf_op jit(solution)/shard_map/ppermute | solution.py:38
  8.5 1.7 %ahead.1 = (f32[8,72,128]{2,1,0:T(8,128)S(1)}, f32[24,16,128]{2,1,0:T(8,128)S(1)}, bf16[48,3072]{1,0:T(8,128)(2,1)S(1)}) custom-call(s32[1]{0:T(128)S(6)} %copy.265.sample_ref, f32[1024]{0:T(1024)} %refs_0_.1, f32[1024]{0:T(1024)} %refs_1_.1, f32[3,3,8,7]{3,2,1,0:T(8,128)} %bitcast.293, f32[3,3,8,7]{3,2,1,0:T(8,128)} %bitcast.295, f32[3,8]{1,0:T(4,128)} %bitcast.298, ...), custom_call_target="tpu_custom_call" | custom-call | tf_op jit(solution)/shard_map/ahead/pallas_call | solution.py:185
  10.2 0.0 collective-permute-done.22.halo_ref
  10.2 0.1 side.1.applied_ref
  10.3 2.4 %collective-permute-done.23 = f32[54,8,128]{2,1,0:T(8,128)S(1)} collective-permute-done((f32[54,8,128]{2,1,0:T(8,128)S(1)}, f32[54,8,128]{2,1,0:T(8,128)S(1)}, u32[]{:S(2)}, u32[]{:S(2)}) %collective-permute-start.23) | collective-permute-done | bytes 221216 | tf_op jit(solution)/shard_map/ppermute | solution.py:653
  12.7 0.0 collective-permute-done.24
  12.7 0.2 edges.1
  12.9 4.1 %collective-permute-done.25 = f32[48,8,128]{2,1,0:T(8,128)S(1)} collective-permute-done((f32[48,8,128]{2,1,0:T(8,128)S(1)}, f32[48,8,128]{2,1,0:T(8,128)S(1)}, u32[]{:S(2)}, u32[]{:S(2)}) %collective-permute-start.25) | collective-permute-done | bytes 196640 | tf_op jit(solution)/shard_map/ppermute | solution.py:653
  17.0 0.0 collective-permute-done.26.refs_4_
  17.0 1.0 %sums.1 = (bf16[240,3072]{1,0:T(8,128)(2,1)S(1)}, f32[16,128]{1,0:T(8,128)S(1)}, f32[16,128]{1,0:T(8,128)S(1)}) custom-call(s32[1]{0:T(128)} %bitcast.116.place_ref, s32[1]{0:T(128)} %bitcast.117.slab_ref, f32[8,72,128]{2,1,0:T(8,128)S(1)} %get-tuple-element.119.fields_ref, f32[24,16,128]{2,1,0:T(8,128)S(1)} %get-tuple-element.123.applied_ref, ...), custom_call_target="tpu_custom_call" | custom-call | tf_op jit(solution)/shard_map/sums/pallas_call | solution.py:373
  18.0 0.1 collective-permute-start.27
  18.1 1.1 %collective-permute-done.27 = f32[16,128]{1,0:T(8,128)S(1)} collective-permute-done((f32[16,128]{1,0:T(8,128)S(1)}, f32[16,128]{1,0:T(8,128)S(1)}, u32[]{:S(2)}, u32[]{:S(2)}) %collective-permute-start.27) | collective-permute-done | bytes 8224 | tf_op jit(solution)/shard_map/ppermute | solution.py:390
  19.2 13.2 %all_to_all.5 = f32[16,16,128]{2,1,0:T(8,128)S(1)} all-to-all(f32[16,16,128]{2,1,0:T(8,128)S(1)} %broadcast_in_dim.34), channel_id=1, replica_groups={{0,2,4,6,8,10,12,14,16,18,20,22,24,26,28,30},{1,3,5,7,9,11,13,15,17,19,..., dimensions={0} | all-to-all | bytes 262144 | tf_op jit(solution)/shard_map/all_to_all | solution.py:396
  32.5 0.1 collective-permute-start.28
  32.6 1.2 %collective-permute-done.28.given_ref = f32[16,128]{1,0:T(8,128)S(1)} collective-permute-done((f32[16,128]{1,0:T(8,128)S(1)}, f32[16,128]{1,0:T(8,128)S(1)}, u32[]{:S(2)}, u32[]{:S(2)}) %collective-permute-start.28) | collective-permute-done | bytes 8224 | tf_op jit(solution)/shard_map/ppermute | solution.py:398
  33.7 2.4 %finish.1 = (f32[16,24,128]{2,1,0:T(8,128)}, f32[16,16]{1,0:T(8,128)}, f32[16,16]{1,0:T(8,128)}, s32[1,1]{1,0:T(1,128)}) custom-call(s32[1]{0:T(128)} %bitcast.116.place_ref, f32[16,128]{1,0:T(8,128)S(1)} %reduce_sum.9.own_ref, f32[16,128]{1,0:T(8,128)S(1)} %collective-permute-done.28.given_ref, bf16[240,3072]{1,0:T(8,128)(2,1)S(1)} %get-tuple-element.130.stack_ref), custom_call_target="tpu_custom_call" | custom-call | tf_op jit(solution)/shard_map/finish/pallas_call | solution.py:501
  36.2 0.7 %while.14 = (s32[]{:T(128)}, f32[16,24,128]{2,1,0:T(8,128)}, f32[16,16]{1,0:T(8,128)}, f32[16,16]{1,0:T(8,128)}, f32[8,7,3,3]{1,0,3,2:T(8,128)}, /*index=5*/f32[...) while((s32[]{:T(128)}, f32[16,24,128]{2,1,0:T(8,128)}, ...), condition=%region_4.5_spmd, body=%region_1.4_spmd | while | flops 175311344 | bytes 29713228 | solution.py:668
  (3 shorter events, 0.0 us)
Async XLA Ops:
  0.6 9.5 %collective-permute-start.22 = (f32[384,128]{1,0:T(8,128)}, f32[384,128]{1,0:T(8,128)S(1)}, u32[]{:S(2)}, u32[]{:S(2)}) collective-permute-start(f32[384,128]{1,0:T(8,128)} %bitcast.279), channel_id=1, source_target_pairs={{0,4},{8,12},{16,20},{24,28},{4,0},{12,8},{20,16},{28,24},{1,5},{9... | collective-permute-start | bytes 589832 | tf_op jit(solution)/shard_map/ppermute | solution.py:38
  5.0 7.7 %collective-permute-start.23 = (f32[54,8,128]{2,1,0:T(8,128)S(1)}, f32[54,8,128]{2,1,0:T(8,128)S(1)}, u32[]{:S(2)}, u32[]{:S(2)}) collective-permute-start(f32[54,8,128]{2,1,0:T(8,128)S(1)} %get-tuple-element.121), channel_id=1, source_target_pairs={{0,3},{1,2},{2,1},{3,0},{4,7},{5,6},{6,5},{7,4},{8,11},{9,10},{10,... | collective-permute-start | bytes 663560 | tf_op jit(solution)/shard_map/ppermute | solution.py:653
  5.7 7.0 %collective-permute-start.24 = (f32[54,8,128]{2,1,0:T(8,128)S(1)}, f32[54,8,128]{2,1,0:T(8,128)S(1)}, u32[]{:S(2)}, u32[]{:S(2)}) collective-permute-start(f32[54,8,128]{2,1,0:T(8,128)S(1)} %get-tuple-element.122), channel_id=1, source_target_pairs={{0,1},{1,0},{2,3},{3,2},{4,5},{5,4},{6,7},{7,6},{8,9},{9,8},{10,11... | collective-permute-start | bytes 663560 | tf_op jit(solution)/shard_map/ppermute | solution.py:653
  6.7 10.3 %collective-permute-start.25 = (f32[48,8,128]{2,1,0:T(8,128)S(1)}, f32[48,8,128]{2,1,0:T(8,128)S(1)}, u32[]{:S(2)}, u32[]{:S(2)}) collective-permute-start(f32[48,8,128]{2,1,0:T(8,128)S(1)} %get-tuple-element.127), channel_id=1, source_target_pairs={{0,2},{1,3},{2,0},{3,1},{4,6},{5,7},{6,4},{7,5},{8,10},{9,11},{10,... | collective-permute-start | bytes 589832 | tf_op jit(solution)/shard_map/ppermute | solution.py:653
  7.2 9.8 %collective-permute-start.26 = (f32[384,128]{1,0:T(8,128)}, f32[384,128]{1,0:T(8,128)S(1)}, u32[]{:S(2)}, u32[]{:S(2)}) collective-permute-start(f32[384,128]{1,0:T(8,128)} %bitcast.281), channel_id=1, source_target_pairs={{4,8},{12,16},{20,24},{8,4},{16,12},{24,20},{5,9},{13,17},{21,25},... | collective-permute-start | bytes 589832 | tf_op jit(solution)/shard_map/ppermute | solution.py:38
  18.0 1.2 %collective-permute-start.27 = (f32[16,128]{1,0:T(8,128)S(1)}, f32[16,128]{1,0:T(8,128)S(1)}, u32[]{:S(2)}, u32[]{:S(2)}) collective-permute-start(f32[16,128]{1,0:T(8,128)S(1)} %get-tuple-element.129), channel_id=1, source_target_pairs={{0,1},{1,0},{2,3},{3,2},{4,5},{5,4},{6,7},{7,6},{8,9},{9,8},{10,11... | collective-permute-start | bytes 24584 | tf_op jit(solution)/shard_map/ppermute | solution.py:390
  32.5 1.2 %collective-permute-start.28 = (f32[16,128]{1,0:T(8,128)S(1)}, f32[16,128]{1,0:T(8,128)S(1)}, u32[]{:S(2)}, u32[]{:S(2)}) collective-permute-start(f32[16,128]{1,0:T(8,128)S(1)} %reduce_sum.9.own_ref), channel_id=1, source_target_pairs={{0,1},{1,0},{2,3},{3,2},{4,5},{5,4},{6,7},{7,6},{8,9},{9,8},{10,11... | collective-permute-start | bytes 24584 | tf_op jit(solution)/shard_map/ppermute | solution.py:398

commit v18 on v17

--- a/solution.py
+++ b/solution.py
@@ -13,7 +13,7 @@
 HBM = pl.BlockSpec(memory_space=pltpu.HBM)
 LOSS = 256.0
 EARLY = pl.CostEstimate(flops=10**9, bytes_accessed=10**6, transcendentals=0)
-NEXT = pl.CostEstimate(flops=10**6, bytes_accessed=10**6, transcendentals=0)
+NEXT = pl.CostEstimate(flops=3 * 10**8, bytes_accessed=10**6, transcendentals=0)
 SCRATCH = pltpu.CompilerParams(vmem_limit_bytes=8 * 2**20)
 
 
@@ -229,7 +229,7 @@
         in_specs=[SMEM] + [VMEM] * 3,
         out_specs=VMEM,
         compiler_params=SCRATCH,
-        cost_estimate=EARLY,
+        cost_estimate=NEXT,
         name="side",
     )(slab, *kept(fields, applied, halo))
 
@@ -271,7 +271,7 @@
         split_lines(piece_ref, parts_ref, lines, group_cols, [i * group_cols for i in range(3)])
 
 
-def add_edges(place, fields, applied, pieces, comps, group_cols):
+def add_edges(place, fields, applied, pieces, comps, group_cols, weight):
     lines, _, lanes = applied.shape
     parts = near(3 * group_cols, lines * lanes, dtype=jnp.bfloat16)
     return pl.pallas_call(
@@ -280,7 +280,7 @@
         in_specs=[SMEM] + [VMEM] * (2 + len(pieces)),
         out_specs=(VMEM,) * (1 + len(pieces)),
         compiler_params=SCRATCH,
-        cost_estimate=NEXT,
+        cost_estimate=weight,
         name="edges",
     )(place, *kept(fields, applied, *pieces.values()))
 
@@ -656,10 +656,16 @@
         sample, velocities, shifts, k0_blocks, ke_blocks, k0_diag, mass, material, x_rows,
         own.reshape(-1, lanes), comps,
     )
+    split = {0: own}
+    first, *rest = reversed(partners(count)[1])
+    applied, split[first] = add_edges(
+        place, fields, applied, {first: got.pop(first)}, comps, group_cols, EARLY
+    )
     applied = add_side(slab, fields, applied, got.pop("even"), comps, "even")
-    pieces = {k: got.pop(k) for k in reversed(partners(count)[1])}
-    applied, *parts = add_edges(place, fields, applied, pieces, comps, group_cols)
-    split = {0: own, **dict(zip(pieces, parts))}
+    for k in rest:
+        applied, split[k] = add_edges(
+            place, fields, applied, {k: got.pop(k)}, comps, group_cols, None
+        )
     stack, keep, give = sums(place, slab, fields, applied, got.pop("odd"), split, got, comps)
     halves = exchange_all(keep, give)
     block, coeffs, upper, bad = finish(

time: 37.1 us -> 36.8 us (level)
  blocking collectives: 13.2 us -> 14.3 us
  waiting for transfers between devices: 8.85 us -> 7.92 us
  starting transfers between devices: 6.05 us -> 5.67 us
    ppermute x3, waiting for transfers between devices: 6.55 us -> 0.45 us  [shards(): lax.ppermute(pieces[name - 1], 'basis', [(i, i ^ name) for i in range(cou...]
    ppermute x2, waiting for transfers between devices: 0.01 us -> 5.15 us  [swap(): return lax.ppermute(values, axis, pairs + [(j, i) for i, j in pairs])]
    ppermute x2, starting transfers between devices: 3.66 us -> 2.15 us  [swap(): return lax.ppermute(values, axis, pairs + [(j, i) for i, j in pairs])]
    ppermute x3, starting transfers between devices: 2.21 us -> 3.37 us  [shards(): lax.ppermute(pieces[name - 1], 'basis', [(i, i ^ name) for i in range(cou...]
    all_to_all x1, blocking collectives: 13.2 us -> 14.3 us  [exchange_all(): lax.all_to_all(copies, ('space', 'basis'), 0, 0, axis_index_groups=groups)]
  transfers between devices with their start and end apart: 7 -> 7, of which waited for: 4 -> 4; matrix products, arithmetic and copies ran while one was open for 0% -> 0% of each run, Pallas kernels for 9% -> 5%
where the time goes in v18:
time: 36.8 us; the launch traced here: 36.5 us
  blocking collectives  14.3 us (39%)
  waiting for transfers between devices  7.92 us (22%)
  Pallas kernels  6.66 us (18%)
  starting transfers between devices  5.67 us (15%)
  between operations  1.38 us (4%)
  loops' own time  0.56 us (2%)
    all_to_all x1, blocking collectives, exchange_all(): lax.all_to_all(copies, ('space', 'basis'), 0, 0, axis_index_groups=groups)  14.3 us
    ppermute x2, waiting for transfers between devices, swap(): return lax.ppermute(values, axis, pairs + [(j, i) for i, j in pairs])  5.15 us
    ppermute x3, starting transfers between devices, shards(): lax.ppermute(pieces[name - 1], 'basis', [(i, i ^ name) for i in range(cou...  3.37 us
    pallas_call x1, Pallas kernels, finish(): pl.pallas_call(functools.partial(finish_kernel, row_count, comps), out_sh...  2.44 us
    ppermute x2, starting transfers between devices, swap(): return lax.ppermute(values, axis, pairs + [(j, i) for i, j in pairs])  2.15 us
    pallas_call x1, Pallas kernels, ahead(): pl.pallas_call(ahead_kernel, out_shape=(near(rows, comps * comps * stride...  1.65 us
    pallas_call x1, Pallas kernels, pack(): pl.pallas_call(functools.partial(pack_kernel, comps), out_shape=(*pieces,...  1.36 us
    ppermute x1, waiting for transfers between devices, exchange_all(): part = keep + lax.ppermute(give, 'basis', pairs)  1.16 us
  transfers between devices with their start and end apart: 7, of which 4 were waited for; matrix products, arithmetic and copies ran while one was open for 0% of the time, Pallas kernels for 5%

profile of v18, /device:TPU:0, one launch (start us, length us, event | category | flops | bytes accessed | tf_op | source)
XLA Modules:
  0.0 36.5 jit_solution(9745272747173558464)
XLA Ops:
  0.6 1.4 %pack.1 = (f32[48,8,128]{2,1,0:T(8,128)S(1)}, f32[54,8,128]{2,1,0:T(8,128)S(1)}, f32[48,8,128]{2,1,0:T(8,128)S(1)}, f32[54,8,128]{2,1,0:T(8,128)S(1)}, f32[384,128]{1,0:T(8,128)S(1)}, /*index=5*/s32[8,128]{1,0:T(8,128)S(1)}) custom-call(s32[1]{0:T(128)} %bitcast.116.place_ref, f32[48,4,8,128]{3,2,1,0:T(8,128)} %bitcast.273, f32[384,128]{1,0:T(8,128)} %bitcast.279, ...), custom_call_target="tpu_custom_call" | custom-call | tf_op jit(solution)/shard_map/pack/pallas_call | solution.py:88
  2.0 2.5 %collective-permute-start.22 = (f32[54,8,128]{2,1,0:T(8,128)S(1)}, f32[54,8,128]{2,1,0:T(8,128)S(1)}, u32[]{:S(2)}, u32[]{:S(2)}) collective-permute-start(f32[54,8,128]{2,1,0:T(8,128)S(1)} %get-tuple-element.122), channel_id=1, source_target_pairs={{0,3},{1,2},{2,1},{3,0},{4,7},{5,6},{6,5},{7,4},{8,11},{9,10},{10,... | collective-permute-start | bytes 663560 | tf_op jit(solution)/shard_map/ppermute | solution.py:653
  4.5 1.5 %collective-permute-start.23 = (f32[384,128]{1,0:T(8,128)}, f32[384,128]{1,0:T(8,128)S(1)}, u32[]{:S(2)}, u32[]{:S(2)}) collective-permute-start(f32[384,128]{1,0:T(8,128)} %bitcast.280), channel_id=1, source_target_pairs={{0,4},{8,12},{16,20},{24,28},{4,0},{12,8},{20,16},{28,24},{1,5},{9... | collective-permute-start | bytes 589832 | tf_op jit(solution)/shard_map/ppermute | solution.py:38
  6.0 0.4 %collective-permute-start.24 = (f32[54,8,128]{2,1,0:T(8,128)S(1)}, f32[54,8,128]{2,1,0:T(8,128)S(1)}, u32[]{:S(2)}, u32[]{:S(2)}) collective-permute-start(f32[54,8,128]{2,1,0:T(8,128)S(1)} %get-tuple-element.124), channel_id=1, source_target_pairs={{0,1},{1,0},{2,3},{3,2},{4,5},{5,4},{6,7},{7,6},{8,9},{9,8},{10,11... | collective-permute-start | bytes 663560 | tf_op jit(solution)/shard_map/ppermute | solution.py:653
  6.4 0.5 %collective-permute-start.25 = (f32[48,8,128]{2,1,0:T(8,128)S(1)}, f32[48,8,128]{2,1,0:T(8,128)S(1)}, u32[]{:S(2)}, u32[]{:S(2)}) collective-permute-start(f32[48,8,128]{2,1,0:T(8,128)S(1)} %get-tuple-element.129), channel_id=1, source_target_pairs={{0,2},{1,3},{2,0},{3,1},{4,6},{5,7},{6,4},{7,5},{8,10},{9,11},{10,... | collective-permute-start | bytes 589832 | tf_op jit(solution)/shard_map/ppermute | solution.py:653
  6.9 0.7 %collective-permute-start.26 = (f32[384,128]{1,0:T(8,128)}, f32[384,128]{1,0:T(8,128)S(1)}, u32[]{:S(2)}, u32[]{:S(2)}) collective-permute-start(f32[384,128]{1,0:T(8,128)} %bitcast.281), channel_id=1, source_target_pairs={{4,8},{12,16},{20,24},{8,4},{16,12},{24,20},{5,9},{13,17},{21,25},... | collective-permute-start | bytes 589832 | tf_op jit(solution)/shard_map/ppermute | solution.py:38
  8.2 1.6 %ahead.1 = (f32[8,72,128]{2,1,0:T(8,128)S(1)}, f32[24,16,128]{2,1,0:T(8,128)S(1)}, bf16[48,3072]{1,0:T(8,128)(2,1)S(1)}) custom-call(s32[1]{0:T(128)S(6)} %copy.265.sample_ref, f32[1024]{0:T(1024)} %refs_0_.1, f32[1024]{0:T(1024)} %refs_1_.1, f32[3,3,8,7]{3,2,1,0:T(8,128)} %bitcast.293, f32[3,3,8,7]{3,2,1,0:T(8,128)} %bitcast.295, f32[3,8]{1,0:T(4,128)} %bitcast.298, ...), custom_call_target="tpu_custom_call" | custom-call | tf_op jit(solution)/shard_map/ahead/pallas_call | solution.py:185
  9.8 0.4 %collective-permute-done.22 = f32[54,8,128]{2,1,0:T(8,128)S(1)} collective-permute-done((f32[54,8,128]{2,1,0:T(8,128)S(1)}, f32[54,8,128]{2,1,0:T(8,128)S(1)}, u32[]{:S(2)}, u32[]{:S(2)}) %collective-permute-start.22) | collective-permute-done | bytes 221216 | tf_op jit(solution)/shard_map/ppermute | solution.py:653
  10.3 0.1 edges.2
  10.4 5.1 %collective-permute-done.23.halo_ref = f32[384,128]{1,0:T(8,128)S(1)} collective-permute-done((f32[384,128]{1,0:T(8,128)}, f32[384,128]{1,0:T(8,128)S(1)}, u32[]{:S(2)}, u32[]{:S(2)}) %collective-permute-start.23) | collective-permute-done | bytes 196640 | tf_op jit(solution)/shard_map/ppermute | solution.py:38
  15.5 0.1 side.1.applied_ref
  15.6 0.0 collective-permute-done.24
  15.6 0.1 edges.3
  15.7 0.0 collective-permute-done.25
  15.7 0.0 collective-permute-done.26.refs_4_
  15.8 0.9 %sums.1 = (bf16[240,3072]{1,0:T(8,128)(2,1)S(1)}, f32[16,128]{1,0:T(8,128)S(1)}, f32[16,128]{1,0:T(8,128)S(1)}) custom-call(s32[1]{0:T(128)} %bitcast.116.place_ref, s32[1]{0:T(128)} %bitcast.117.slab_ref, f32[8,72,128]{2,1,0:T(8,128)S(1)} %get-tuple-element.120.fields_ref, f32[24,16,128]{2,1,0:T(8,128)S(1)} %get-tuple-element.125.applied_ref, ...), custom_call_target="tpu_custom_call" | custom-call | tf_op jit(solution)/shard_map/sums/pallas_call | solution.py:373
  16.7 0.1 collective-permute-start.27
  16.8 1.2 %collective-permute-done.27 = f32[16,128]{1,0:T(8,128)S(1)} collective-permute-done((f32[16,128]{1,0:T(8,128)S(1)}, f32[16,128]{1,0:T(8,128)S(1)}, u32[]{:S(2)}, u32[]{:S(2)}) %collective-permute-start.27) | collective-permute-done | bytes 8224 | tf_op jit(solution)/shard_map/ppermute | solution.py:390
  18.0 14.3 %all_to_all.5 = f32[16,16,128]{2,1,0:T(8,128)S(1)} all-to-all(f32[16,16,128]{2,1,0:T(8,128)S(1)} %broadcast_in_dim.34), channel_id=1, replica_groups={{0,2,4,6,8,10,12,14,16,18,20,22,24,26,28,30},{1,3,5,7,9,11,13,15,17,19,..., dimensions={0} | all-to-all | bytes 262144 | tf_op jit(solution)/shard_map/all_to_all | solution.py:396
  32.3 0.1 collective-permute-start.28
  32.4 1.2 %collective-permute-done.28.given_ref = f32[16,128]{1,0:T(8,128)S(1)} collective-permute-done((f32[16,128]{1,0:T(8,128)S(1)}, f32[16,128]{1,0:T(8,128)S(1)}, u32[]{:S(2)}, u32[]{:S(2)}) %collective-permute-start.28) | collective-permute-done | bytes 8224 | tf_op jit(solution)/shard_map/ppermute | solution.py:398
  33.5 2.4 %finish.1 = (f32[16,24,128]{2,1,0:T(8,128)}, f32[16,16]{1,0:T(8,128)}, f32[16,16]{1,0:T(8,128)}, s32[1,1]{1,0:T(1,128)}) custom-call(s32[1]{0:T(128)} %bitcast.116.place_ref, f32[16,128]{1,0:T(8,128)S(1)} %reduce_sum.9.own_ref, f32[16,128]{1,0:T(8,128)S(1)} %collective-permute-done.28.given_ref, bf16[240,3072]{1,0:T(8,128)(2,1)S(1)} %get-tuple-element.132.stack_ref), custom_call_target="tpu_custom_call" | custom-call | tf_op jit(solution)/shard_map/finish/pallas_call | solution.py:501
  36.0 0.6 %while.14 = (s32[]{:T(128)}, f32[16,24,128]{2,1,0:T(8,128)}, f32[16,16]{1,0:T(8,128)}, f32[16,16]{1,0:T(8,128)}, f32[8,7,3,3]{1,0,3,2:T(8,128)}, /*index=5*/f32[...) while((s32[]{:T(128)}, f32[16,24,128]{2,1,0:T(8,128)}, ...), condition=%region_4.5_spmd, body=%region_1.4_spmd | while | flops 175311344 | bytes 29713228 | solution.py:674
  (3 shorter events, 0.0 us)
Async XLA Ops:
  2.0 8.3 %collective-permute-start.22 = (f32[54,8,128]{2,1,0:T(8,128)S(1)}, f32[54,8,128]{2,1,0:T(8,128)S(1)}, u32[]{:S(2)}, u32[]{:S(2)}) collective-permute-start(f32[54,8,128]{2,1,0:T(8,128)S(1)} %get-tuple-element.122), channel_id=1, source_target_pairs={{0,3},{1,2},{2,1},{3,0},{4,7},{5,6},{6,5},{7,4},{8,11},{9,10},{10,... | collective-permute-start | bytes 663560 | tf_op jit(solution)/shard_map/ppermute | solution.py:653
  4.5 11.1 %collective-permute-start.23 = (f32[384,128]{1,0:T(8,128)}, f32[384,128]{1,0:T(8,128)S(1)}, u32[]{:S(2)}, u32[]{:S(2)}) collective-permute-start(f32[384,128]{1,0:T(8,128)} %bitcast.280), channel_id=1, source_target_pairs={{0,4},{8,12},{16,20},{24,28},{4,0},{12,8},{20,16},{28,24},{1,5},{9... | collective-permute-start | bytes 589832 | tf_op jit(solution)/shard_map/ppermute | solution.py:38
  6.0 9.7 %collective-permute-start.24 = (f32[54,8,128]{2,1,0:T(8,128)S(1)}, f32[54,8,128]{2,1,0:T(8,128)S(1)}, u32[]{:S(2)}, u32[]{:S(2)}) collective-permute-start(f32[54,8,128]{2,1,0:T(8,128)S(1)} %get-tuple-element.124), channel_id=1, source_target_pairs={{0,1},{1,0},{2,3},{3,2},{4,5},{5,4},{6,7},{7,6},{8,9},{9,8},{10,11... | collective-permute-start | bytes 663560 | tf_op jit(solution)/shard_map/ppermute | solution.py:653
  6.4 9.4 %collective-permute-start.25 = (f32[48,8,128]{2,1,0:T(8,128)S(1)}, f32[48,8,128]{2,1,0:T(8,128)S(1)}, u32[]{:S(2)}, u32[]{:S(2)}) collective-permute-start(f32[48,8,128]{2,1,0:T(8,128)S(1)} %get-tuple-element.129), channel_id=1, source_target_pairs={{0,2},{1,3},{2,0},{3,1},{4,6},{5,7},{6,4},{7,5},{8,10},{9,11},{10,... | collective-permute-start | bytes 589832 | tf_op jit(solution)/shard_map/ppermute | solution.py:653
  6.9 8.9 %collective-permute-start.26 = (f32[384,128]{1,0:T(8,128)}, f32[384,128]{1,0:T(8,128)S(1)}, u32[]{:S(2)}, u32[]{:S(2)}) collective-permute-start(f32[384,128]{1,0:T(8,128)} %bitcast.281), channel_id=1, source_target_pairs={{4,8},{12,16},{20,24},{8,4},{16,12},{24,20},{5,9},{13,17},{21,25},... | collective-permute-start | bytes 589832 | tf_op jit(solution)/shard_map/ppermute | solution.py:38
  16.7 1.2 %collective-permute-start.27 = (f32[16,128]{1,0:T(8,128)S(1)}, f32[16,128]{1,0:T(8,128)S(1)}, u32[]{:S(2)}, u32[]{:S(2)}) collective-permute-start(f32[16,128]{1,0:T(8,128)S(1)} %get-tuple-element.131), channel_id=1, source_target_pairs={{0,1},{1,0},{2,3},{3,2},{4,5},{5,4},{6,7},{7,6},{8,9},{9,8},{10,11... | collective-permute-start | bytes 24584 | tf_op jit(solution)/shard_map/ppermute | solution.py:390
  32.3 1.2 %collective-permute-start.28 = (f32[16,128]{1,0:T(8,128)S(1)}, f32[16,128]{1,0:T(8,128)S(1)}, u32[]{:S(2)}, u32[]{:S(2)}) collective-permute-start(f32[16,128]{1,0:T(8,128)S(1)} %reduce_sum.9.own_ref), channel_id=1, source_target_pairs={{0,1},{1,0},{2,3},{3,2},{4,5},{5,4},{6,7},{7,6},{8,9},{9,8},{10,11... | collective-permute-start | bytes 24584 | tf_op jit(solution)/shard_map/ppermute | solution.py:398

commit v19 on v18

--- a/solution.py
+++ b/solution.py
@@ -42,58 +42,57 @@
     return range(1, count), [k for k in range(1, count) if k & (k + 1) == 0]
 
 
-def pack_kernel(comps, place_ref, basis_ref, x_ref, material_ref, *refs):
-    *piece_refs, x_out_ref, material_out_ref, sems = refs
-    count = len(piece_refs)
+def pack_kernel(comps, ks, edge_ks, place_ref, basis_ref, rider_ref, *refs):
+    x_refs, refs = refs[: len(refs) - len(ks) - 2], refs[len(refs) - len(ks) - 2 :]
+    *piece_refs, rider_out_ref, sems = refs
+    x_ref = x_refs[0] if x_refs else rider_out_ref
     tiles, _, rows, lanes = basis_ref.shape
     block_cols = x_ref.shape[0] // (comps * rows)
     place = place_ref[0]
-    x_copy = pltpu.make_async_copy(x_ref, x_out_ref, sems.at[count])
-    x_copy.start()
-    copies = [pltpu.make_async_copy(material_ref, material_out_ref, sems.at[count + 1])]
-    for k in reversed(range(count)):
-        copies.append(
-            pltpu.make_async_copy(
-                basis_ref.at[:, place ^ k], piece_refs[k].at[pl.ds(0, tiles)], sems.at[k]
-            )
+    rider = pltpu.make_async_copy(rider_ref, rider_out_ref, sems.at[len(ks)])
+    rider.start()
+    copies = [
+        pltpu.make_async_copy(
+            basis_ref.at[:, place ^ k], piece_ref.at[pl.ds(0, tiles)], sems.at[index]
         )
+        for index, (k, piece_ref) in enumerate(zip(ks, piece_refs))
+    ]
     for copy in copies:
         copy.start()
-    x_copy.wait()
+    rider.wait()
     for comp in range(comps):
         first, last = (
-            x_out_ref[pl.ds(comp * rows + row, block_cols, stride=comps * rows), :]
+            x_ref[pl.ds(comp * rows + row, block_cols, stride=comps * rows), :]
             for row in (0, rows - 1)
         )
-        for k in partners(count)[1]:
-            edge = jnp.where((place ^ k) > place, last, first)
-            for part in range(block_cols // rows):
-                piece_refs[k][tiles + comp * (block_cols // rows) + part] = edge[
-                    part * rows : (part + 1) * rows
-                ]
+        for k, piece_ref in zip(ks, piece_refs):
+            if k in edge_ks:
+                edge = jnp.where((place ^ k) > place, last, first)
+                for part in range(block_cols // rows):
+                    piece_ref[tiles + comp * (block_cols // rows) + part] = edge[
+                        part * rows : (part + 1) * rows
+                    ]
     for copy in copies:
         copy.wait()
 
 
-def pack(place, basis, x_rows, material, block_cols):
+def pack(place, basis, rider, block_cols, ks, *x_rows):
     group_cols, comps, _, full_y, lanes = basis.shape
     count = lax.axis_size("basis")
     rows = full_y // count
     tiles = group_cols * comps
     edge_tiles = block_cols * comps // rows
-    pieces = [
-        near(tiles + (edge_tiles if k in partners(count)[1] else 0), rows, lanes)
-        for k in range(count)
-    ]
+    edge_ks = partners(count)[1]
+    pieces = [near(tiles + (edge_tiles if k in edge_ks else 0), rows, lanes) for k in ks]
     return pl.pallas_call(
-        functools.partial(pack_kernel, comps),
-        out_shape=(*pieces, near(*x_rows.shape), near(*material.shape, dtype=jnp.int32)),
-        in_specs=[SMEM, HBM, HBM, HBM],
-        out_specs=(VMEM,) * (count + 2),
-        scratch_shapes=[pltpu.SemaphoreType.DMA((count + 2,))],
+        functools.partial(pack_kernel, comps, tuple(ks), tuple(edge_ks)),
+        out_shape=(*pieces, near(*rider.shape, dtype=rider.dtype)),
+        in_specs=[SMEM, HBM, HBM] + [VMEM] * len(x_rows),
+        out_specs=(VMEM,) * (len(ks) + 1),
+        scratch_shapes=[pltpu.SemaphoreType.DMA((len(ks) + 1,))],
         compiler_params=SCRATCH,
         name="pack",
-    )(place, *far(basis.reshape(tiles, count, rows, lanes), x_rows, material))
+    )(place, *far(basis.reshape(tiles, count, rows, lanes), rider), *kept(*x_rows))
 
 
 def three_parts(values):
@@ -642,15 +641,23 @@
     slab = lax.axis_index("space").astype(jnp.int32).reshape(1)
     count = lax.axis_size("basis")
     x_far = x_block.reshape(block_cols * lines, lanes)
-    own, *pieces, x_rows, material = pack(place, basis, x_far, material.reshape(rows, lanes), block_cols)
+    first = partners(count)[1][-1]
+    rest = [k for k in range(count) if k != first]
+    piece, x_rows = pack(place, basis, x_far, block_cols, [first])
+    pieces = {first: piece}
+    *packed, material = pack(
+        place, basis, material.reshape(rows, lanes), block_cols, rest, x_rows
+    )
+    pieces.update(zip(rest, packed))
+    own = pieces.pop(0)
     got = {}
-    for name in ("even", 3, "odd", 2, 1):
+    for name in ("even", *reversed(partners(count)[0]), "odd"):
         if name == "even":
             got[name] = swap(x_far, "space", 0)
         elif name == "odd":
             got[name] = swap(x_far, "space", 1)
         else:
-            piece = lax.ppermute(pieces[name - 1], "basis", [(i, i ^ name) for i in range(count)])
+            piece = lax.ppermute(pieces[name], "basis", [(i, i ^ name) for i in range(count)])
             got[name] = piece.reshape(-1, lanes)
     fields, applied, own = ahead(
         sample, velocities, shifts, k0_blocks, ke_blocks, k0_diag, mass, material, x_rows,

time: 36.8 us -> 37.7 us (1.024)
  waiting for transfers between devices: 7.92 us -> 5.6 us
  blocking collectives: 14.3 us -> 16.4 us
  Pallas kernels: 6.66 us -> 7.55 us
    ppermute x2, waiting for transfers between devices: 5.15 us -> 0.97 us  [swap(): return lax.ppermute(values, axis, pairs + [(j, i) for i, j in pairs])]
    all_to_all x1, blocking collectives: 14.3 us -> 16.4 us  [exchange_all(): lax.all_to_all(copies, ('space', 'basis'), 0, 0, axis_index_groups=groups)]
    ppermute x3, waiting for transfers between devices: 0.45 us -> 2.31 us  [shards(): lax.ppermute(pieces[name], 'basis', [(i, i ^ name) for i in range(count)])]
    pallas_call x1 -> x2, Pallas kernels: 1.36 us -> 2.25 us  [pack(): pl.pallas_call(functools.partial(pack_kernel, comps, tuple(ks), tuple(edg...]
  transfers between devices with their start and end apart: 7 -> 7, of which waited for: 4 -> 4; matrix products, arithmetic and copies ran while one was open for 0% -> 0% of each run, Pallas kernels for 5% -> 8%
where the time goes in v19:
time: 37.7 us; the launch traced here: 37.4 us
  blocking collectives  16.4 us (44%)
  Pallas kernels  7.55 us (20%)
  starting transfers between devices  5.73 us (15%)
  waiting for transfers between devices  5.6 us (15%)
  between operations  1.4 us (4%)
  loops' own time  0.7 us (2%)
    all_to_all x1, blocking collectives, exchange_all(): lax.all_to_all(copies, ('space', 'basis'), 0, 0, axis_index_groups=groups)  16.4 us
    ppermute x3, starting transfers between devices, shards(): lax.ppermute(pieces[name], 'basis', [(i, i ^ name) for i in range(count)])  3.44 us
    pallas_call x1, Pallas kernels, finish(): pl.pallas_call(functools.partial(finish_kernel, row_count, comps), out_sh...  2.43 us
    ppermute x3, waiting for transfers between devices, shards(): lax.ppermute(pieces[name], 'basis', [(i, i ^ name) for i in range(count)])  2.31 us
    pallas_call x2, Pallas kernels, pack(): pl.pallas_call(functools.partial(pack_kernel, comps, tuple(ks), tuple(edg...  2.25 us
    ppermute x2, starting transfers between devices, swap(): return lax.ppermute(values, axis, pairs + [(j, i) for i, j in pairs])  2.15 us
    pallas_call x1, Pallas kernels, ahead(): pl.pallas_call(ahead_kernel, out_shape=(near(rows, comps * comps * stride...  1.65 us
    ppermute x1, waiting for transfers between devices, exchange_all(): part = keep + lax.ppermute(give, 'basis', pairs)  1.16 us
  transfers between devices with their start and end apart: 7, of which 4 were waited for; matrix products, arithmetic and copies ran while one was open for 0% of the time, Pallas kernels for 8%

profile of v19, /device:TPU:0, one launch (start us, length us, event | category | flops | bytes accessed | tf_op | source)
XLA Modules:
  0.0 37.4 jit_solution(9795453183105282189)
XLA Ops:
  0.6 0.0 copy-start
  0.6 1.1 %pack.2 = (f32[54,8,128]{2,1,0:T(8,128)S(1)}, f32[384,128]{1,0:T(8,128)S(1)}) custom-call(s32[1]{0:T(128)} %bitcast.116.place_ref, f32[48,4,8,128]{3,2,1,0:T(8,128)} %bitcast.273, f32[384,128]{1,0:T(8,128)} %bitcast.280), custom_call_target="tpu_custom_call" | custom-call | tf_op jit(solution)/shard_map/pack/pallas_call | solution.py:87
  1.7 2.5 %collective-permute-start.22 = (f32[54,8,128]{2,1,0:T(8,128)S(1)}, f32[54,8,128]{2,1,0:T(8,128)S(1)}, u32[]{:S(2)}, u32[]{:S(2)}) collective-permute-start(f32[54,8,128]{2,1,0:T(8,128)S(1)} %get-tuple-element.122), channel_id=1, source_target_pairs={{0,3},{1,2},{2,1},{3,0},{4,7},{5,6},{6,5},{7,4},{8,11},{9,10},{10,... | collective-permute-start | bytes 663560 | tf_op jit(solution)/shard_map/ppermute | solution.py:660
  4.2 1.5 %collective-permute-start.23 = (f32[384,128]{1,0:T(8,128)}, f32[384,128]{1,0:T(8,128)S(1)}, u32[]{:S(2)}, u32[]{:S(2)}) collective-permute-start(f32[384,128]{1,0:T(8,128)} %bitcast.281), channel_id=1, source_target_pairs={{0,4},{8,12},{16,20},{24,28},{4,0},{12,8},{20,16},{28,24},{1,5},{9... | collective-permute-start | bytes 589832 | tf_op jit(solution)/shard_map/ppermute | solution.py:38
  5.7 1.2 %pack.3 = (f32[48,8,128]{2,1,0:T(8,128)S(1)}, f32[54,8,128]{2,1,0:T(8,128)S(1)}, f32[48,8,128]{2,1,0:T(8,128)S(1)}, s32[8,128]{1,0:T(8,128)S(1)}) custom-call(s32[1]{0:T(128)} %bitcast.116.place_ref, f32[48,4,8,128]{3,2,1,0:T(8,128)} %bitcast.274, s32[8,128]{1,0:T(8,128)} %bitcast.298, f32[384,128]{1,0:T(8,128)S(1)} %get-tuple-element.117.refs_0_.refs_7_), custom_call_target="tpu_custom_call" | custom-call | tf_op jit(solution)/shard_map/pack/pallas_call | solution.py:87
  6.9 0.5 %collective-permute-start.24 = (f32[54,8,128]{2,1,0:T(8,128)S(1)}, f32[54,8,128]{2,1,0:T(8,128)S(1)}, u32[]{:S(2)}, u32[]{:S(2)}) collective-permute-start(f32[54,8,128]{2,1,0:T(8,128)S(1)} %get-tuple-element.124), channel_id=1, source_target_pairs={{0,1},{1,0},{2,3},{3,2},{4,5},{5,4},{6,7},{7,6},{8,9},{9,8},{10,11... | collective-permute-start | bytes 663560 | tf_op jit(solution)/shard_map/ppermute | solution.py:660
  7.3 0.5 %collective-permute-start.25 = (f32[48,8,128]{2,1,0:T(8,128)S(1)}, f32[48,8,128]{2,1,0:T(8,128)S(1)}, u32[]{:S(2)}, u32[]{:S(2)}) collective-permute-start(f32[48,8,128]{2,1,0:T(8,128)S(1)} %get-tuple-element.129), channel_id=1, source_target_pairs={{0,2},{1,3},{2,0},{3,1},{4,6},{5,7},{6,4},{7,5},{8,10},{9,11},{10,... | collective-permute-start | bytes 589832 | tf_op jit(solution)/shard_map/ppermute | solution.py:660
  7.8 0.0 copy-done
  7.8 0.7 %collective-permute-start.26 = (f32[384,128]{1,0:T(8,128)S(1)}, f32[384,128]{1,0:T(8,128)S(1)}, u32[]{:S(2)}, u32[]{:S(2)}) collective-permute-start(f32[384,128]{1,0:T(8,128)S(1)} %bitcast.282), channel_id=1, source_target_pairs={{4,8},{12,16},{20,24},{8,4},{16,12},{24,20},{5,9},{13,17},{21,25},... | collective-permute-start | bytes 589832 | tf_op jit(solution)/shard_map/ppermute | solution.py:38
  9.2 1.6 %ahead.1 = (f32[8,72,128]{2,1,0:T(8,128)S(1)}, f32[24,16,128]{2,1,0:T(8,128)S(1)}, bf16[48,3072]{1,0:T(8,128)(2,1)S(1)}) custom-call(s32[1]{0:T(128)S(6)} %copy.265.sample_ref, f32[1024]{0:T(1024)} %refs_0_.1, f32[1024]{0:T(1024)} %refs_1_.1, f32[3,3,8,7]{3,2,1,0:T(8,128)} %bitcast.294, f32[3,3,8,7]{3,2,1,0:T(8,128)} %bitcast.296, f32[3,8]{1,0:T(4,128)} %bitcast.299, ...), custom_call_target="tpu_custom_call" | custom-call | tf_op jit(solution)/shard_map/ahead/pallas_call | solution.py:184
  10.8 0.0 collective-permute-done.22
  10.8 0.1 edges.2
  10.9 1.0 %collective-permute-done.23.halo_ref = f32[384,128]{1,0:T(8,128)S(1)} collective-permute-done((f32[384,128]{1,0:T(8,128)}, f32[384,128]{1,0:T(8,128)S(1)}, u32[]{:S(2)}, u32[]{:S(2)}) %collective-permute-start.23) | collective-permute-done | bytes 196640 | tf_op jit(solution)/shard_map/ppermute | solution.py:38
  11.9 0.1 side.1.applied_ref
  12.0 0.0 collective-permute-done.24
  12.0 0.1 edges.3
  12.1 2.3 %collective-permute-done.25 = f32[48,8,128]{2,1,0:T(8,128)S(1)} collective-permute-done((f32[48,8,128]{2,1,0:T(8,128)S(1)}, f32[48,8,128]{2,1,0:T(8,128)S(1)}, u32[]{:S(2)}, u32[]{:S(2)}) %collective-permute-start.25) | collective-permute-done | bytes 196640 | tf_op jit(solution)/shard_map/ppermute | solution.py:660
  14.4 0.0 collective-permute-done.26.refs_4_
  14.4 1.0 %sums.1 = (bf16[240,3072]{1,0:T(8,128)(2,1)S(1)}, f32[16,128]{1,0:T(8,128)S(1)}, f32[16,128]{1,0:T(8,128)S(1)}) custom-call(s32[1]{0:T(128)} %bitcast.116.place_ref, s32[1]{0:T(128)} %bitcast.117.slab_ref, f32[8,72,128]{2,1,0:T(8,128)S(1)} %get-tuple-element.120.fields_ref, f32[24,16,128]{2,1,0:T(8,128)S(1)} %get-tuple-element.125.applied_ref, ...), custom_call_target="tpu_custom_call" | custom-call | tf_op jit(solution)/shard_map/sums/pallas_call | solution.py:372
  15.4 0.1 collective-permute-start.27
  15.5 1.2 %collective-permute-done.27 = f32[16,128]{1,0:T(8,128)S(1)} collective-permute-done((f32[16,128]{1,0:T(8,128)S(1)}, f32[16,128]{1,0:T(8,128)S(1)}, u32[]{:S(2)}, u32[]{:S(2)}) %collective-permute-start.27) | collective-permute-done | bytes 8224 | tf_op jit(solution)/shard_map/ppermute | solution.py:389
  16.6 16.4 %all_to_all.5 = f32[16,16,128]{2,1,0:T(8,128)S(1)} all-to-all(f32[16,16,128]{2,1,0:T(8,128)S(1)} %broadcast_in_dim.34), channel_id=1, replica_groups={{0,2,4,6,8,10,12,14,16,18,20,22,24,26,28,30},{1,3,5,7,9,11,13,15,17,19,..., dimensions={0} | all-to-all | bytes 262144 | tf_op jit(solution)/shard_map/all_to_all | solution.py:395
  33.0 0.1 collective-permute-start.28
  33.1 1.2 %collective-permute-done.28.given_ref = f32[16,128]{1,0:T(8,128)S(1)} collective-permute-done((f32[16,128]{1,0:T(8,128)S(1)}, f32[16,128]{1,0:T(8,128)S(1)}, u32[]{:S(2)}, u32[]{:S(2)}) %collective-permute-start.28) | collective-permute-done | bytes 8224 | tf_op jit(solution)/shard_map/ppermute | solution.py:397
  34.3 2.4 %finish.1 = (f32[16,24,128]{2,1,0:T(8,128)}, f32[16,16]{1,0:T(8,128)}, f32[16,16]{1,0:T(8,128)}, s32[1,1]{1,0:T(1,128)}) custom-call(s32[1]{0:T(128)} %bitcast.116.place_ref, f32[16,128]{1,0:T(8,128)S(1)} %reduce_sum.9.own_ref, f32[16,128]{1,0:T(8,128)S(1)} %collective-permute-done.28.given_ref, bf16[240,3072]{1,0:T(8,128)(2,1)S(1)} %get-tuple-element.132.stack_ref), custom_call_target="tpu_custom_call" | custom-call | tf_op jit(solution)/shard_map/finish/pallas_call | solution.py:500
  36.7 0.7 %while.14 = (s32[]{:T(128)}, f32[16,24,128]{2,1,0:T(8,128)}, f32[16,16]{1,0:T(8,128)}, f32[16,16]{1,0:T(8,128)}, f32[8,7,3,3]{1,0,3,2:T(8,128)}, /*index=5*/f32[...) while((s32[]{:T(128)}, f32[16,24,128]{2,1,0:T(8,128)}, ...), condition=%region_4.5_spmd, body=%region_1.4_spmd | while | flops 175311344 | bytes 30499696 | solution.py:681
  (3 shorter events, 0.0 us)
Async XLA Ops:
  0.6 7.2 %copy-start = (f32[16,3,1,8,128]{4,3,2,1,0:T(8,128)S(1)}, f32[16,3,1,8,128]{4,3,2,1,0:T(8,128)}, u32[]{:S(2)}) copy-start(f32[16,3,1,8,128]{4,3,2,1,0:T(8,128)} %param.14) | copy-start | bytes 589828
  1.7 9.1 %collective-permute-start.22 = (f32[54,8,128]{2,1,0:T(8,128)S(1)}, f32[54,8,128]{2,1,0:T(8,128)S(1)}, u32[]{:S(2)}, u32[]{:S(2)}) collective-permute-start(f32[54,8,128]{2,1,0:T(8,128)S(1)} %get-tuple-element.122), channel_id=1, source_target_pairs={{0,3},{1,2},{2,1},{3,0},{4,7},{5,6},{6,5},{7,4},{8,11},{9,10},{10,... | collective-permute-start | bytes 663560 | tf_op jit(solution)/shard_map/ppermute | solution.py:660
  4.2 7.7 %collective-permute-start.23 = (f32[384,128]{1,0:T(8,128)}, f32[384,128]{1,0:T(8,128)S(1)}, u32[]{:S(2)}, u32[]{:S(2)}) collective-permute-start(f32[384,128]{1,0:T(8,128)} %bitcast.281), channel_id=1, source_target_pairs={{0,4},{8,12},{16,20},{24,28},{4,0},{12,8},{20,16},{28,24},{1,5},{9... | collective-permute-start | bytes 589832 | tf_op jit(solution)/shard_map/ppermute | solution.py:38
  6.9 5.1 %collective-permute-start.24 = (f32[54,8,128]{2,1,0:T(8,128)S(1)}, f32[54,8,128]{2,1,0:T(8,128)S(1)}, u32[]{:S(2)}, u32[]{:S(2)}) collective-permute-start(f32[54,8,128]{2,1,0:T(8,128)S(1)} %get-tuple-element.124), channel_id=1, source_target_pairs={{0,1},{1,0},{2,3},{3,2},{4,5},{5,4},{6,7},{7,6},{8,9},{9,8},{10,11... | collective-permute-start | bytes 663560 | tf_op jit(solution)/shard_map/ppermute | solution.py:660
  7.3 7.1 %collective-permute-start.25 = (f32[48,8,128]{2,1,0:T(8,128)S(1)}, f32[48,8,128]{2,1,0:T(8,128)S(1)}, u32[]{:S(2)}, u32[]{:S(2)}) collective-permute-start(f32[48,8,128]{2,1,0:T(8,128)S(1)} %get-tuple-element.129), channel_id=1, source_target_pairs={{0,2},{1,3},{2,0},{3,1},{4,6},{5,7},{6,4},{7,5},{8,10},{9,11},{10,... | collective-permute-start | bytes 589832 | tf_op jit(solution)/shard_map/ppermute | solution.py:660
  7.8 6.6 %collective-permute-start.26 = (f32[384,128]{1,0:T(8,128)S(1)}, f32[384,128]{1,0:T(8,128)S(1)}, u32[]{:S(2)}, u32[]{:S(2)}) collective-permute-start(f32[384,128]{1,0:T(8,128)S(1)} %bitcast.282), channel_id=1, source_target_pairs={{4,8},{12,16},{20,24},{8,4},{16,12},{24,20},{5,9},{13,17},{21,25},... | collective-permute-start | bytes 589832 | tf_op jit(solution)/shard_map/ppermute | solution.py:38
  15.4 1.2 %collective-permute-start.27 = (f32[16,128]{1,0:T(8,128)S(1)}, f32[16,128]{1,0:T(8,128)S(1)}, u32[]{:S(2)}, u32[]{:S(2)}) collective-permute-start(f32[16,128]{1,0:T(8,128)S(1)} %get-tuple-element.131), channel_id=1, source_target_pairs={{0,1},{1,0},{2,3},{3,2},{4,5},{5,4},{6,7},{7,6},{8,9},{9,8},{10,11... | collective-permute-start | bytes 24584 | tf_op jit(solution)/shard_map/ppermute | solution.py:389
  33.0 1.2 %collective-permute-start.28 = (f32[16,128]{1,0:T(8,128)S(1)}, f32[16,128]{1,0:T(8,128)S(1)}, u32[]{:S(2)}, u32[]{:S(2)}) collective-permute-start(f32[16,128]{1,0:T(8,128)S(1)} %reduce_sum.9.own_ref), channel_id=1, source_target_pairs={{0,1},{1,0},{2,3},{3,2},{4,5},{5,4},{6,7},{7,6},{8,9},{9,8},{10,11... | collective-permute-start | bytes 24584 | tf_op jit(solution)/shard_map/ppermute | solution.py:397

commit v20 on v18

--- a/solution.py
+++ b/solution.py
@@ -14,6 +14,7 @@
 LOSS = 256.0
 EARLY = pl.CostEstimate(flops=10**9, bytes_accessed=10**6, transcendentals=0)
 NEXT = pl.CostEstimate(flops=3 * 10**8, bytes_accessed=10**6, transcendentals=0)
+LATE = pl.CostEstimate(flops=10**6, bytes_accessed=10**6, transcendentals=0)
 SCRATCH = pltpu.CompilerParams(vmem_limit_bytes=8 * 2**20)
 
 
@@ -222,14 +223,14 @@
             out_ref[out * rows + row] = total
 
 
-def add_side(slab, fields, applied, halo, comps, side):
+def add_side(slab, fields, applied, halo, comps, side, weight):
     return pl.pallas_call(
         functools.partial(side_kernel, comps, side),
         out_shape=near(*applied.shape),
         in_specs=[SMEM] + [VMEM] * 3,
         out_specs=VMEM,
         compiler_params=SCRATCH,
-        cost_estimate=NEXT,
+        cost_estimate=weight,
         name="side",
     )(slab, *kept(fields, applied, halo))
 
@@ -321,16 +322,14 @@
 
 
 def sums_kernel(
-    comps, split, raw, place_ref, slab_ref, fields_ref, applied_ref, *refs
+    split, raw, place_ref, applied_ref, *refs
 ):
-    *refs, halo_ref, stack_ref, keep_ref, give_ref = refs
+    *refs, stack_ref, keep_ref, give_ref = refs
     lines, block_cols, lanes = applied_ref.shape
-    rows = lines // comps
     group_cols = refs[0].shape[0] // 3
     basis_cols = (len(split) + len(raw)) * group_cols
     joined = basis_cols + block_cols
     place = place_ref[0]
-    swapped = slab_ref[0] % 2 == 1
     for k, ref in zip(split + raw, refs):
         begin = pl.multiple_of((place ^ k) * group_cols, group_cols)
         begins = [index * joined + begin for index in range(3)]
@@ -341,17 +340,10 @@
                 ]
         else:
             split_lines(ref, stack_ref, lines, group_cols, begins)
-    for row in range(rows):
-        field_row = fields_ref[row]
-        views = [line_of(halo_ref, comp, row, comps, rows, block_cols) for comp in range(comps)]
-        for out in range(comps):
-            line = out * rows + row
-            total = applied_ref[line]
-            for comp, view in enumerate(views):
-                total = total + side_terms(field_row, swapped, "odd", out, comp, comps) * view
-            for index, part in enumerate(three_parts(total)):
-                there = pl.ds(index * joined + basis_cols, block_cols)
-                stack_ref[there, pl.ds(line * lanes, lanes)] = part
+    for line in range(lines):
+        for index, part in enumerate(three_parts(applied_ref[line])):
+            there = pl.ds(index * joined + basis_cols, block_cols)
+            stack_ref[there, pl.ds(line * lanes, lanes)] = part
 
     stack = stack_ref[...]
     products = lax.dot_general(
@@ -366,22 +358,22 @@
     give_ref[...] = jnp.where(odd, folded[:half], folded[half:])
 
 
-def sums(place, slab, fields, applied, halo, split, raw, comps):
+def sums(place, applied, split, raw):
     lines, block_cols, lanes = applied.shape
     basis_cols = (len(split) + len(raw)) * (split[0].shape[0] // 3)
     joined = basis_cols + block_cols
     return pl.pallas_call(
-        functools.partial(sums_kernel, comps, tuple(split), tuple(raw)),
+        functools.partial(sums_kernel, tuple(split), tuple(raw)),
         out_shape=(
             near(3 * joined, lines * lanes, dtype=jnp.bfloat16),
             near(basis_cols // 4, 2 * basis_cols),
             near(basis_cols // 4, 2 * basis_cols),
         ),
-        in_specs=[SMEM] * 2 + [VMEM] * (3 + len(split) + len(raw)),
+        in_specs=[SMEM] + [VMEM] * (1 + len(split) + len(raw)),
         out_specs=(VMEM,) * 3,
         compiler_params=SCRATCH,
         name="sums",
-    )(place, slab, *kept(fields, applied, *split.values(), *raw.values(), halo))
+    )(place, *kept(applied, *split.values(), *raw.values()))
 
 
 def exchange_all(keep, give):
@@ -644,7 +636,7 @@
     x_far = x_block.reshape(block_cols * lines, lanes)
     own, *pieces, x_rows, material = pack(place, basis, x_far, material.reshape(rows, lanes), block_cols)
     got = {}
-    for name in ("even", 3, "odd", 2, 1):
+    for name in ("even", *reversed(partners(count)[0]), "odd"):
         if name == "even":
             got[name] = swap(x_far, "space", 0)
         elif name == "odd":
@@ -661,12 +653,13 @@
     applied, split[first] = add_edges(
         place, fields, applied, {first: got.pop(first)}, comps, group_cols, EARLY
     )
-    applied = add_side(slab, fields, applied, got.pop("even"), comps, "even")
+    applied = add_side(slab, fields, applied, got.pop("even"), comps, "even", NEXT)
     for k in rest:
         applied, split[k] = add_edges(
             place, fields, applied, {k: got.pop(k)}, comps, group_cols, None
         )
-    stack, keep, give = sums(place, slab, fields, applied, got.pop("odd"), split, got, comps)
+    applied = add_side(slab, fields, applied, got.pop("odd"), comps, "odd", LATE)
+    stack, keep, give = sums(place, applied, split, got)
     halves = exchange_all(keep, give)
     block, coeffs, upper, bad = finish(
         place, halves, stack, row_count, block_cols, group_cols, lines, comps

time: 36.8 us -> 36.6 us (level)
  transfers between devices with their start and end apart: 7 -> 7, of which waited for: 4 -> 4; matrix products, arithmetic and copies ran while one was open for 0% -> 0% of each run, Pallas kernels for 5% -> 6%
where the time goes in v20:
time: 36.6 us; the launch traced here: 36.4 us
  blocking collectives  14.1 us (39%)
  waiting for transfers between devices  7.82 us (21%)
  Pallas kernels  6.72 us (18%)
  starting transfers between devices  5.73 us (16%)
  between operations  1.39 us (4%)
  loops' own time  0.56 us (2%)
    all_to_all x1, blocking collectives, exchange_all(): lax.all_to_all(copies, ('space', 'basis'), 0, 0, axis_index_groups=groups)  14.1 us
    ppermute x2, waiting for transfers between devices, swap(): return lax.ppermute(values, axis, pairs + [(j, i) for i, j in pairs])  5.12 us
    ppermute x3, starting transfers between devices, shards(): lax.ppermute(pieces[name - 1], 'basis', [(i, i ^ name) for i in range(cou...  3.44 us
    pallas_call x1, Pallas kernels, finish(): pl.pallas_call(functools.partial(finish_kernel, row_count, comps), out_sh...  2.43 us
    ppermute x2, starting transfers between devices, swap(): return lax.ppermute(values, axis, pairs + [(j, i) for i, j in pairs])  2.15 us
    pallas_call x1, Pallas kernels, ahead(): pl.pallas_call(ahead_kernel, out_shape=(near(rows, comps * comps * stride...  1.65 us
    pallas_call x1, Pallas kernels, pack(): pl.pallas_call(functools.partial(pack_kernel, comps), out_shape=(*pieces,...  1.36 us
    ppermute x1, waiting for transfers between devices, exchange_all(): return (own, lax.ppermute(own, 'basis', pairs))  1.16 us
  transfers between devices with their start and end apart: 7, of which 4 were waited for; matrix products, arithmetic and copies ran while one was open for 0% of the time, Pallas kernels for 6%

profile of v20, /device:TPU:0, one launch (start us, length us, event | category | flops | bytes accessed | tf_op | source)
XLA Modules:
  0.0 36.4 jit_solution(10668044097694185630)
XLA Ops:
  0.6 1.4 %pack.1 = (f32[48,8,128]{2,1,0:T(8,128)S(1)}, f32[54,8,128]{2,1,0:T(8,128)S(1)}, f32[48,8,128]{2,1,0:T(8,128)S(1)}, f32[54,8,128]{2,1,0:T(8,128)S(1)}, f32[384,128]{1,0:T(8,128)S(1)}, /*index=5*/s32[8,128]{1,0:T(8,128)S(1)}) custom-call(s32[1]{0:T(128)} %bitcast.116.place_ref, f32[48,4,8,128]{3,2,1,0:T(8,128)} %bitcast.273, f32[384,128]{1,0:T(8,128)} %bitcast.279, ...), custom_call_target="tpu_custom_call" | custom-call | tf_op jit(solution)/shard_map/pack/pallas_call | solution.py:89
  2.0 2.5 %collective-permute-start.22 = (f32[54,8,128]{2,1,0:T(8,128)S(1)}, f32[54,8,128]{2,1,0:T(8,128)S(1)}, u32[]{:S(2)}, u32[]{:S(2)}) collective-permute-start(f32[54,8,128]{2,1,0:T(8,128)S(1)} %get-tuple-element.122), channel_id=1, source_target_pairs={{0,3},{1,2},{2,1},{3,0},{4,7},{5,6},{6,5},{7,4},{8,11},{9,10},{10,... | collective-permute-start | bytes 663560 | tf_op jit(solution)/shard_map/ppermute | solution.py:645
  4.5 1.5 %collective-permute-start.23 = (f32[384,128]{1,0:T(8,128)}, f32[384,128]{1,0:T(8,128)S(1)}, u32[]{:S(2)}, u32[]{:S(2)}) collective-permute-start(f32[384,128]{1,0:T(8,128)} %bitcast.280), channel_id=1, source_target_pairs={{0,4},{8,12},{16,20},{24,28},{4,0},{12,8},{20,16},{28,24},{1,5},{9... | collective-permute-start | bytes 589832 | tf_op jit(solution)/shard_map/ppermute | solution.py:39
  6.0 0.4 %collective-permute-start.24 = (f32[54,8,128]{2,1,0:T(8,128)S(1)}, f32[54,8,128]{2,1,0:T(8,128)S(1)}, u32[]{:S(2)}, u32[]{:S(2)}) collective-permute-start(f32[54,8,128]{2,1,0:T(8,128)S(1)} %get-tuple-element.124), channel_id=1, source_target_pairs={{0,1},{1,0},{2,3},{3,2},{4,5},{5,4},{6,7},{7,6},{8,9},{9,8},{10,11... | collective-permute-start | bytes 663560 | tf_op jit(solution)/shard_map/ppermute | solution.py:645
  6.4 0.7 %collective-permute-start.25 = (f32[384,128]{1,0:T(8,128)}, f32[384,128]{1,0:T(8,128)S(1)}, u32[]{:S(2)}, u32[]{:S(2)}) collective-permute-start(f32[384,128]{1,0:T(8,128)} %bitcast.281), channel_id=1, source_target_pairs={{4,8},{12,16},{20,24},{8,4},{16,12},{24,20},{5,9},{13,17},{21,25},... | collective-permute-start | bytes 589832 | tf_op jit(solution)/shard_map/ppermute | solution.py:39
  7.0 0.6 %collective-permute-start.26 = (f32[48,8,128]{2,1,0:T(8,128)S(1)}, f32[48,8,128]{2,1,0:T(8,128)S(1)}, u32[]{:S(2)}, u32[]{:S(2)}) collective-permute-start(f32[48,8,128]{2,1,0:T(8,128)S(1)} %get-tuple-element.129), channel_id=1, source_target_pairs={{0,2},{1,3},{2,0},{3,1},{4,6},{5,7},{6,4},{7,5},{8,10},{9,11},{10,... | collective-permute-start | bytes 589832 | tf_op jit(solution)/shard_map/ppermute | solution.py:645
  8.3 1.6 %ahead.1 = (f32[8,72,128]{2,1,0:T(8,128)S(1)}, f32[24,16,128]{2,1,0:T(8,128)S(1)}, bf16[48,3072]{1,0:T(8,128)(2,1)S(1)}) custom-call(s32[1]{0:T(128)S(6)} %copy.265.sample_ref, f32[1024]{0:T(1024)} %refs_0_.1, f32[1024]{0:T(1024)} %refs_1_.1, f32[3,3,8,7]{3,2,1,0:T(8,128)} %bitcast.293, f32[3,3,8,7]{3,2,1,0:T(8,128)} %bitcast.295, f32[3,8]{1,0:T(4,128)} %bitcast.298, ...), custom_call_target="tpu_custom_call" | custom-call | tf_op jit(solution)/shard_map/ahead/pallas_call | solution.py:186
  9.9 0.4 %collective-permute-done.22 = f32[54,8,128]{2,1,0:T(8,128)S(1)} collective-permute-done((f32[54,8,128]{2,1,0:T(8,128)S(1)}, f32[54,8,128]{2,1,0:T(8,128)S(1)}, u32[]{:S(2)}, u32[]{:S(2)}) %collective-permute-start.22) | collective-permute-done | bytes 221216 | tf_op jit(solution)/shard_map/ppermute | solution.py:645
  10.3 0.1 edges.2
  10.4 5.1 %collective-permute-done.23.halo_ref = f32[384,128]{1,0:T(8,128)S(1)} collective-permute-done((f32[384,128]{1,0:T(8,128)}, f32[384,128]{1,0:T(8,128)S(1)}, u32[]{:S(2)}, u32[]{:S(2)}) %collective-permute-start.23) | collective-permute-done | bytes 196640 | tf_op jit(solution)/shard_map/ppermute | solution.py:39
  15.5 0.1 side.2.applied_ref
  15.6 0.0 collective-permute-done.24
  15.6 0.1 edges.3
  15.7 0.0 collective-permute-done.25.halo_ref
  15.7 0.1 side.3.applied_ref
  15.8 0.0 collective-permute-done.26
  15.8 0.9 %sums.1 = (bf16[240,3072]{1,0:T(8,128)(2,1)S(1)}, f32[16,128]{1,0:T(8,128)S(1)}, f32[16,128]{1,0:T(8,128)S(1)}) custom-call(s32[1]{0:T(128)} %bitcast.116.place_ref, f32[24,16,128]{2,1,0:T(8,128)S(1)} %side.3.applied_ref, bf16[48,3072]{1,0:T(8,128)(2,1)S(1)} %get-tuple-element.126.refs_0_, bf16[48,3072]{1,0:T(8,128)(2,1)S(1)} %get-tuple-element.127.refs_1_, ...), custom_call_target="tpu_custom_call" | custom-call | tf_op jit(solution)/shard_map/sums/pallas_call | solution.py:365
  16.7 0.1 collective-permute-start.27
  16.8 1.2 %collective-permute-done.27 = f32[16,128]{1,0:T(8,128)S(1)} collective-permute-done((f32[16,128]{1,0:T(8,128)S(1)}, f32[16,128]{1,0:T(8,128)S(1)}, u32[]{:S(2)}, u32[]{:S(2)}) %collective-permute-start.27) | collective-permute-done | bytes 8224 | tf_op jit(solution)/shard_map/ppermute | solution.py:382
  18.0 14.1 %all_to_all.5 = f32[16,16,128]{2,1,0:T(8,128)S(1)} all-to-all(f32[16,16,128]{2,1,0:T(8,128)S(1)} %broadcast_in_dim.34), channel_id=1, replica_groups={{0,2,4,6,8,10,12,14,16,18,20,22,24,26,28,30},{1,3,5,7,9,11,13,15,17,19,..., dimensions={0} | all-to-all | bytes 262144 | tf_op jit(solution)/shard_map/all_to_all | solution.py:388
  32.1 0.1 collective-permute-start.28
  32.2 1.2 %collective-permute-done.28.given_ref = f32[16,128]{1,0:T(8,128)S(1)} collective-permute-done((f32[16,128]{1,0:T(8,128)S(1)}, f32[16,128]{1,0:T(8,128)S(1)}, u32[]{:S(2)}, u32[]{:S(2)}) %collective-permute-start.28) | collective-permute-done | bytes 8224 | tf_op jit(solution)/shard_map/ppermute | solution.py:390
  33.4 2.4 %finish.1 = (f32[16,24,128]{2,1,0:T(8,128)}, f32[16,16]{1,0:T(8,128)}, f32[16,16]{1,0:T(8,128)}, s32[1,1]{1,0:T(1,128)}) custom-call(s32[1]{0:T(128)} %bitcast.116.place_ref, f32[16,128]{1,0:T(8,128)S(1)} %reduce_sum.9.own_ref, f32[16,128]{1,0:T(8,128)S(1)} %collective-permute-done.28.given_ref, bf16[240,3072]{1,0:T(8,128)(2,1)S(1)} %get-tuple-element.132.stack_ref), custom_call_target="tpu_custom_call" | custom-call | tf_op jit(solution)/shard_map/finish/pallas_call | solution.py:493
  35.8 0.6 %while.14 = (s32[]{:T(128)}, f32[16,24,128]{2,1,0:T(8,128)}, f32[16,16]{1,0:T(8,128)}, f32[16,16]{1,0:T(8,128)}, f32[8,7,3,3]{1,0,3,2:T(8,128)}, /*index=5*/f32[...) while((s32[]{:T(128)}, f32[16,24,128]{2,1,0:T(8,128)}, ...), condition=%region_4.5_spmd, body=%region_1.4_spmd | while | flops 175311344 | bytes 29713228 | solution.py:667
  (3 shorter events, 0.0 us)
Async XLA Ops:
  2.0 8.3 %collective-permute-start.22 = (f32[54,8,128]{2,1,0:T(8,128)S(1)}, f32[54,8,128]{2,1,0:T(8,128)S(1)}, u32[]{:S(2)}, u32[]{:S(2)}) collective-permute-start(f32[54,8,128]{2,1,0:T(8,128)S(1)} %get-tuple-element.122), channel_id=1, source_target_pairs={{0,3},{1,2},{2,1},{3,0},{4,7},{5,6},{6,5},{7,4},{8,11},{9,10},{10,... | collective-permute-start | bytes 663560 | tf_op jit(solution)/shard_map/ppermute | solution.py:645
  4.5 11.0 %collective-permute-start.23 = (f32[384,128]{1,0:T(8,128)}, f32[384,128]{1,0:T(8,128)S(1)}, u32[]{:S(2)}, u32[]{:S(2)}) collective-permute-start(f32[384,128]{1,0:T(8,128)} %bitcast.280), channel_id=1, source_target_pairs={{0,4},{8,12},{16,20},{24,28},{4,0},{12,8},{20,16},{28,24},{1,5},{9... | collective-permute-start | bytes 589832 | tf_op jit(solution)/shard_map/ppermute | solution.py:39
  6.0 9.6 %collective-permute-start.24 = (f32[54,8,128]{2,1,0:T(8,128)S(1)}, f32[54,8,128]{2,1,0:T(8,128)S(1)}, u32[]{:S(2)}, u32[]{:S(2)}) collective-permute-start(f32[54,8,128]{2,1,0:T(8,128)S(1)} %get-tuple-element.124), channel_id=1, source_target_pairs={{0,1},{1,0},{2,3},{3,2},{4,5},{5,4},{6,7},{7,6},{8,9},{9,8},{10,11... | collective-permute-start | bytes 663560 | tf_op jit(solution)/shard_map/ppermute | solution.py:645
  6.4 9.3 %collective-permute-start.25 = (f32[384,128]{1,0:T(8,128)}, f32[384,128]{1,0:T(8,128)S(1)}, u32[]{:S(2)}, u32[]{:S(2)}) collective-permute-start(f32[384,128]{1,0:T(8,128)} %bitcast.281), channel_id=1, source_target_pairs={{4,8},{12,16},{20,24},{8,4},{16,12},{24,20},{5,9},{13,17},{21,25},... | collective-permute-start | bytes 589832 | tf_op jit(solution)/shard_map/ppermute | solution.py:39
  7.0 8.8 %collective-permute-start.26 = (f32[48,8,128]{2,1,0:T(8,128)S(1)}, f32[48,8,128]{2,1,0:T(8,128)S(1)}, u32[]{:S(2)}, u32[]{:S(2)}) collective-permute-start(f32[48,8,128]{2,1,0:T(8,128)S(1)} %get-tuple-element.129), channel_id=1, source_target_pairs={{0,2},{1,3},{2,0},{3,1},{4,6},{5,7},{6,4},{7,5},{8,10},{9,11},{10,... | collective-permute-start | bytes 589832 | tf_op jit(solution)/shard_map/ppermute | solution.py:645
  16.7 1.2 %collective-permute-start.27 = (f32[16,128]{1,0:T(8,128)S(1)}, f32[16,128]{1,0:T(8,128)S(1)}, u32[]{:S(2)}, u32[]{:S(2)}) collective-permute-start(f32[16,128]{1,0:T(8,128)S(1)} %get-tuple-element.131), channel_id=1, source_target_pairs={{0,1},{1,0},{2,3},{3,2},{4,5},{5,4},{6,7},{7,6},{8,9},{9,8},{10,11... | collective-permute-start | bytes 24584 | tf_op jit(solution)/shard_map/ppermute | solution.py:382
  32.1 1.2 %collective-permute-start.28 = (f32[16,128]{1,0:T(8,128)S(1)}, f32[16,128]{1,0:T(8,128)S(1)}, u32[]{:S(2)}, u32[]{:S(2)}) collective-permute-start(f32[16,128]{1,0:T(8,128)S(1)} %reduce_sum.9.own_ref), channel_id=1, source_target_pairs={{0,1},{1,0},{2,3},{3,2},{4,5},{5,4},{6,7},{7,6},{8,9},{9,8},{10,11... | collective-permute-start | bytes 24584 | tf_op jit(solution)/shard_map/ppermute | solution.py:390

commit v21 on v20

--- a/solution.py
+++ b/solution.py
@@ -381,7 +381,12 @@
     pairs = [(i, i ^ 1) for i in range(sizes[1])]
     part = keep + lax.ppermute(give, "basis", pairs)
     groups = [
-        [i * sizes[1] + j for i in range(sizes[0]) for j in range(first, sizes[1], 2)]
+        [
+            i * sizes[1] + j
+            for side in range(2)
+            for j in range(first, sizes[1], 2)
+            for i in range(side, sizes[0], 2)
+        ]
         for first in range(2)
     ]
     copies = jnp.broadcast_to(part[None], (len(groups[0]),) + part.shape)

time: 36.6 us -> 37 us (1.011)
  blocking collectives: 14.1 us -> 14.5 us
    all_to_all x1, blocking collectives: 14.1 us -> 14.5 us  [exchange_all(): lax.all_to_all(copies, ('space', 'basis'), 0, 0, axis_index_groups=groups)]
  transfers between devices with their start and end apart: 7 -> 7, of which waited for: 4 -> 4; matrix products, arithmetic and copies ran while one was open for 0% -> 0% of each run, Pallas kernels for 6% -> 5%
where the time goes in v21:
time: 37 us; the launch traced here: 36.8 us
  blocking collectives  14.5 us (39%)
  waiting for transfers between devices  7.82 us (21%)
  Pallas kernels  6.73 us (18%)
  starting transfers between devices  5.73 us (15%)
  between operations  1.39 us (4%)
  loops' own time  0.56 us (2%)
    all_to_all x1, blocking collectives, exchange_all(): lax.all_to_all(copies, ('space', 'basis'), 0, 0, axis_index_groups=groups)  14.5 us
    ppermute x2, waiting for transfers between devices, swap(): return lax.ppermute(values, axis, pairs + [(j, i) for i, j in pairs])  5.12 us
    ppermute x3, starting transfers between devices, shards(): lax.ppermute(pieces[name - 1], 'basis', [(i, i ^ name) for i in range(cou...  3.44 us
    pallas_call x1, Pallas kernels, finish(): pl.pallas_call(functools.partial(finish_kernel, row_count, comps), out_sh...  2.44 us
    ppermute x2, starting transfers between devices, swap(): return lax.ppermute(values, axis, pairs + [(j, i) for i, j in pairs])  2.15 us
    pallas_call x1, Pallas kernels, ahead(): pl.pallas_call(ahead_kernel, out_shape=(near(rows, comps * comps * stride...  1.65 us
    pallas_call x1, Pallas kernels, pack(): pl.pallas_call(functools.partial(pack_kernel, comps), out_shape=(*pieces,...  1.36 us
    ppermute x1, waiting for transfers between devices, exchange_all(): part = keep + lax.ppermute(give, 'basis', pairs)  1.16 us
  transfers between devices with their start and end apart: 7, of which 4 were waited for; matrix products, arithmetic and copies ran while one was open for 0% of the time, Pallas kernels for 5%

profile of v21, /device:TPU:0, one launch (start us, length us, event | category | flops | bytes accessed | tf_op | source)
XLA Modules:
  0.0 36.8 jit_solution(5398153855935886909)
XLA Ops:
  0.6 1.4 %pack.1 = (f32[48,8,128]{2,1,0:T(8,128)S(1)}, f32[54,8,128]{2,1,0:T(8,128)S(1)}, f32[48,8,128]{2,1,0:T(8,128)S(1)}, f32[54,8,128]{2,1,0:T(8,128)S(1)}, f32[384,128]{1,0:T(8,128)S(1)}, /*index=5*/s32[8,128]{1,0:T(8,128)S(1)}) custom-call(s32[1]{0:T(128)} %bitcast.116.place_ref, f32[48,4,8,128]{3,2,1,0:T(8,128)} %bitcast.273, f32[384,128]{1,0:T(8,128)} %bitcast.279, ...), custom_call_target="tpu_custom_call" | custom-call | tf_op jit(solution)/shard_map/pack/pallas_call | solution.py:89
  2.0 2.5 %collective-permute-start.22 = (f32[54,8,128]{2,1,0:T(8,128)S(1)}, f32[54,8,128]{2,1,0:T(8,128)S(1)}, u32[]{:S(2)}, u32[]{:S(2)}) collective-permute-start(f32[54,8,128]{2,1,0:T(8,128)S(1)} %get-tuple-element.122), channel_id=1, source_target_pairs={{0,3},{1,2},{2,1},{3,0},{4,7},{5,6},{6,5},{7,4},{8,11},{9,10},{10,... | collective-permute-start | bytes 663560 | tf_op jit(solution)/shard_map/ppermute | solution.py:650
  4.5 1.5 %collective-permute-start.23 = (f32[384,128]{1,0:T(8,128)}, f32[384,128]{1,0:T(8,128)S(1)}, u32[]{:S(2)}, u32[]{:S(2)}) collective-permute-start(f32[384,128]{1,0:T(8,128)} %bitcast.280), channel_id=1, source_target_pairs={{0,4},{8,12},{16,20},{24,28},{4,0},{12,8},{20,16},{28,24},{1,5},{9... | collective-permute-start | bytes 589832 | tf_op jit(solution)/shard_map/ppermute | solution.py:39
  6.0 0.4 %collective-permute-start.24 = (f32[54,8,128]{2,1,0:T(8,128)S(1)}, f32[54,8,128]{2,1,0:T(8,128)S(1)}, u32[]{:S(2)}, u32[]{:S(2)}) collective-permute-start(f32[54,8,128]{2,1,0:T(8,128)S(1)} %get-tuple-element.124), channel_id=1, source_target_pairs={{0,1},{1,0},{2,3},{3,2},{4,5},{5,4},{6,7},{7,6},{8,9},{9,8},{10,11... | collective-permute-start | bytes 663560 | tf_op jit(solution)/shard_map/ppermute | solution.py:650
  6.4 0.7 %collective-permute-start.25 = (f32[384,128]{1,0:T(8,128)}, f32[384,128]{1,0:T(8,128)S(1)}, u32[]{:S(2)}, u32[]{:S(2)}) collective-permute-start(f32[384,128]{1,0:T(8,128)} %bitcast.281), channel_id=1, source_target_pairs={{4,8},{12,16},{20,24},{8,4},{16,12},{24,20},{5,9},{13,17},{21,25},... | collective-permute-start | bytes 589832 | tf_op jit(solution)/shard_map/ppermute | solution.py:39
  7.0 0.6 %collective-permute-start.26 = (f32[48,8,128]{2,1,0:T(8,128)S(1)}, f32[48,8,128]{2,1,0:T(8,128)S(1)}, u32[]{:S(2)}, u32[]{:S(2)}) collective-permute-start(f32[48,8,128]{2,1,0:T(8,128)S(1)} %get-tuple-element.129), channel_id=1, source_target_pairs={{0,2},{1,3},{2,0},{3,1},{4,6},{5,7},{6,4},{7,5},{8,10},{9,11},{10,... | collective-permute-start | bytes 589832 | tf_op jit(solution)/shard_map/ppermute | solution.py:650
  8.3 1.6 %ahead.1 = (f32[8,72,128]{2,1,0:T(8,128)S(1)}, f32[24,16,128]{2,1,0:T(8,128)S(1)}, bf16[48,3072]{1,0:T(8,128)(2,1)S(1)}) custom-call(s32[1]{0:T(128)S(6)} %copy.265.sample_ref, f32[1024]{0:T(1024)} %refs_0_.1, f32[1024]{0:T(1024)} %refs_1_.1, f32[3,3,8,7]{3,2,1,0:T(8,128)} %bitcast.293, f32[3,3,8,7]{3,2,1,0:T(8,128)} %bitcast.295, f32[3,8]{1,0:T(4,128)} %bitcast.298, ...), custom_call_target="tpu_custom_call" | custom-call | tf_op jit(solution)/shard_map/ahead/pallas_call | solution.py:186
  9.9 0.4 %collective-permute-done.22 = f32[54,8,128]{2,1,0:T(8,128)S(1)} collective-permute-done((f32[54,8,128]{2,1,0:T(8,128)S(1)}, f32[54,8,128]{2,1,0:T(8,128)S(1)}, u32[]{:S(2)}, u32[]{:S(2)}) %collective-permute-start.22) | collective-permute-done | bytes 221216 | tf_op jit(solution)/shard_map/ppermute | solution.py:650
  10.3 0.1 edges.2
  10.4 5.1 %collective-permute-done.23.halo_ref = f32[384,128]{1,0:T(8,128)S(1)} collective-permute-done((f32[384,128]{1,0:T(8,128)}, f32[384,128]{1,0:T(8,128)S(1)}, u32[]{:S(2)}, u32[]{:S(2)}) %collective-permute-start.23) | collective-permute-done | bytes 196640 | tf_op jit(solution)/shard_map/ppermute | solution.py:39
  15.5 0.1 side.2.applied_ref
  15.6 0.0 collective-permute-done.24
  15.6 0.1 edges.3
  15.7 0.0 collective-permute-done.25.halo_ref
  15.7 0.1 side.3.applied_ref
  15.8 0.0 collective-permute-done.26
  15.8 0.9 %sums.1 = (bf16[240,3072]{1,0:T(8,128)(2,1)S(1)}, f32[16,128]{1,0:T(8,128)S(1)}, f32[16,128]{1,0:T(8,128)S(1)}) custom-call(s32[1]{0:T(128)} %bitcast.116.place_ref, f32[24,16,128]{2,1,0:T(8,128)S(1)} %side.3.applied_ref, bf16[48,3072]{1,0:T(8,128)(2,1)S(1)} %get-tuple-element.126.refs_0_, bf16[48,3072]{1,0:T(8,128)(2,1)S(1)} %get-tuple-element.127.refs_1_, ...), custom_call_target="tpu_custom_call" | custom-call | tf_op jit(solution)/shard_map/sums/pallas_call | solution.py:365
  16.7 0.1 collective-permute-start.27
  16.8 1.2 %collective-permute-done.27 = f32[16,128]{1,0:T(8,128)S(1)} collective-permute-done((f32[16,128]{1,0:T(8,128)S(1)}, f32[16,128]{1,0:T(8,128)S(1)}, u32[]{:S(2)}, u32[]{:S(2)}) %collective-permute-start.27) | collective-permute-done | bytes 8224 | tf_op jit(solution)/shard_map/ppermute | solution.py:382
  18.0 14.5 %all_to_all.5 = f32[16,16,128]{2,1,0:T(8,128)S(1)} all-to-all(f32[16,16,128]{2,1,0:T(8,128)S(1)} %broadcast_in_dim.34), channel_id=1, replica_groups={{0,8,16,24,2,10,18,26,4,12,20,28,6,14,22,30},{1,9,17,25,3,11,19,27,5,13..., dimensions={0} | all-to-all | bytes 262144 | tf_op jit(solution)/shard_map/all_to_all | solution.py:393
  32.5 0.1 collective-permute-start.28
  32.6 1.2 %collective-permute-done.28.given_ref = f32[16,128]{1,0:T(8,128)S(1)} collective-permute-done((f32[16,128]{1,0:T(8,128)S(1)}, f32[16,128]{1,0:T(8,128)S(1)}, u32[]{:S(2)}, u32[]{:S(2)}) %collective-permute-start.28) | collective-permute-done | bytes 8224 | tf_op jit(solution)/shard_map/ppermute | solution.py:395
  33.8 2.4 %finish.1 = (f32[16,24,128]{2,1,0:T(8,128)}, f32[16,16]{1,0:T(8,128)}, f32[16,16]{1,0:T(8,128)}, s32[1,1]{1,0:T(1,128)}) custom-call(s32[1]{0:T(128)} %bitcast.116.place_ref, f32[16,128]{1,0:T(8,128)S(1)} %reduce_sum.9.own_ref, f32[16,128]{1,0:T(8,128)S(1)} %collective-permute-done.28.given_ref, bf16[240,3072]{1,0:T(8,128)(2,1)S(1)} %get-tuple-element.132.stack_ref), custom_call_target="tpu_custom_call" | custom-call | tf_op jit(solution)/shard_map/finish/pallas_call | solution.py:498
  36.2 0.6 %while.14 = (s32[]{:T(128)}, f32[16,24,128]{2,1,0:T(8,128)}, f32[16,16]{1,0:T(8,128)}, f32[16,16]{1,0:T(8,128)}, f32[8,7,3,3]{1,0,3,2:T(8,128)}, /*index=5*/f32[...) while((s32[]{:T(128)}, f32[16,24,128]{2,1,0:T(8,128)}, ...), condition=%region_4.5_spmd, body=%region_1.4_spmd | while | flops 175311344 | bytes 29713228 | solution.py:672
  (3 shorter events, 0.0 us)
Async XLA Ops:
  2.0 8.3 %collective-permute-start.22 = (f32[54,8,128]{2,1,0:T(8,128)S(1)}, f32[54,8,128]{2,1,0:T(8,128)S(1)}, u32[]{:S(2)}, u32[]{:S(2)}) collective-permute-start(f32[54,8,128]{2,1,0:T(8,128)S(1)} %get-tuple-element.122), channel_id=1, source_target_pairs={{0,3},{1,2},{2,1},{3,0},{4,7},{5,6},{6,5},{7,4},{8,11},{9,10},{10,... | collective-permute-start | bytes 663560 | tf_op jit(solution)/shard_map/ppermute | solution.py:650
  4.5 11.0 %collective-permute-start.23 = (f32[384,128]{1,0:T(8,128)}, f32[384,128]{1,0:T(8,128)S(1)}, u32[]{:S(2)}, u32[]{:S(2)}) collective-permute-start(f32[384,128]{1,0:T(8,128)} %bitcast.280), channel_id=1, source_target_pairs={{0,4},{8,12},{16,20},{24,28},{4,0},{12,8},{20,16},{28,24},{1,5},{9... | collective-permute-start | bytes 589832 | tf_op jit(solution)/shard_map/ppermute | solution.py:39
  6.0 9.6 %collective-permute-start.24 = (f32[54,8,128]{2,1,0:T(8,128)S(1)}, f32[54,8,128]{2,1,0:T(8,128)S(1)}, u32[]{:S(2)}, u32[]{:S(2)}) collective-permute-start(f32[54,8,128]{2,1,0:T(8,128)S(1)} %get-tuple-element.124), channel_id=1, source_target_pairs={{0,1},{1,0},{2,3},{3,2},{4,5},{5,4},{6,7},{7,6},{8,9},{9,8},{10,11... | collective-permute-start | bytes 663560 | tf_op jit(solution)/shard_map/ppermute | solution.py:650
  6.4 9.3 %collective-permute-start.25 = (f32[384,128]{1,0:T(8,128)}, f32[384,128]{1,0:T(8,128)S(1)}, u32[]{:S(2)}, u32[]{:S(2)}) collective-permute-start(f32[384,128]{1,0:T(8,128)} %bitcast.281), channel_id=1, source_target_pairs={{4,8},{12,16},{20,24},{8,4},{16,12},{24,20},{5,9},{13,17},{21,25},... | collective-permute-start | bytes 589832 | tf_op jit(solution)/shard_map/ppermute | solution.py:39
  7.0 8.8 %collective-permute-start.26 = (f32[48,8,128]{2,1,0:T(8,128)S(1)}, f32[48,8,128]{2,1,0:T(8,128)S(1)}, u32[]{:S(2)}, u32[]{:S(2)}) collective-permute-start(f32[48,8,128]{2,1,0:T(8,128)S(1)} %get-tuple-element.129), channel_id=1, source_target_pairs={{0,2},{1,3},{2,0},{3,1},{4,6},{5,7},{6,4},{7,5},{8,10},{9,11},{10,... | collective-permute-start | bytes 589832 | tf_op jit(solution)/shard_map/ppermute | solution.py:650
  16.7 1.2 %collective-permute-start.27 = (f32[16,128]{1,0:T(8,128)S(1)}, f32[16,128]{1,0:T(8,128)S(1)}, u32[]{:S(2)}, u32[]{:S(2)}) collective-permute-start(f32[16,128]{1,0:T(8,128)S(1)} %get-tuple-element.131), channel_id=1, source_target_pairs={{0,1},{1,0},{2,3},{3,2},{4,5},{5,4},{6,7},{7,6},{8,9},{9,8},{10,11... | collective-permute-start | bytes 24584 | tf_op jit(solution)/shard_map/ppermute | solution.py:382
  32.5 1.2 %collective-permute-start.28 = (f32[16,128]{1,0:T(8,128)S(1)}, f32[16,128]{1,0:T(8,128)S(1)}, u32[]{:S(2)}, u32[]{:S(2)}) collective-permute-start(f32[16,128]{1,0:T(8,128)S(1)} %reduce_sum.9.own_ref), channel_id=1, source_target_pairs={{0,1},{1,0},{2,3},{3,2},{4,5},{5,4},{6,7},{7,6},{8,9},{9,8},{10,11... | collective-permute-start | bytes 24584 | tf_op jit(solution)/shard_map/ppermute | solution.py:395

commit v22 on v20

--- a/solution.py
+++ b/solution.py
@@ -43,16 +43,17 @@
     return range(1, count), [k for k in range(1, count) if k & (k + 1) == 0]
 
 
-def pack_kernel(comps, place_ref, basis_ref, x_ref, material_ref, *refs):
-    *piece_refs, x_out_ref, material_out_ref, sems = refs
-    count = len(piece_refs)
+def pack_kernel(comps, place_ref, basis_ref, x_ref, *refs):
+    *piece_refs, x_out_ref, sems = refs
+    piece_refs = dict(enumerate(piece_refs, 1))
+    count = 1 + len(piece_refs)
     tiles, _, rows, lanes = basis_ref.shape
     block_cols = x_ref.shape[0] // (comps * rows)
     place = place_ref[0]
-    x_copy = pltpu.make_async_copy(x_ref, x_out_ref, sems.at[count])
+    x_copy = pltpu.make_async_copy(x_ref, x_out_ref, sems.at[0])
     x_copy.start()
-    copies = [pltpu.make_async_copy(material_ref, material_out_ref, sems.at[count + 1])]
-    for k in reversed(range(count)):
+    copies = []
+    for k in reversed(range(1, count)):
         copies.append(
             pltpu.make_async_copy(
                 basis_ref.at[:, place ^ k], piece_refs[k].at[pl.ds(0, tiles)], sems.at[k]
@@ -76,7 +77,7 @@
         copy.wait()
 
 
-def pack(place, basis, x_rows, material, block_cols):
+def pack(place, basis, x_rows, block_cols):
     group_cols, comps, _, full_y, lanes = basis.shape
     count = lax.axis_size("basis")
     rows = full_y // count
@@ -84,17 +85,17 @@
     edge_tiles = block_cols * comps // rows
     pieces = [
         near(tiles + (edge_tiles if k in partners(count)[1] else 0), rows, lanes)
-        for k in range(count)
+        for k in range(1, count)
     ]
     return pl.pallas_call(
         functools.partial(pack_kernel, comps),
-        out_shape=(*pieces, near(*x_rows.shape), near(*material.shape, dtype=jnp.int32)),
-        in_specs=[SMEM, HBM, HBM, HBM],
-        out_specs=(VMEM,) * (count + 2),
-        scratch_shapes=[pltpu.SemaphoreType.DMA((count + 2,))],
+        out_shape=(*pieces, near(*x_rows.shape)),
+        in_specs=[SMEM, HBM, HBM],
+        out_specs=(VMEM,) * count,
+        scratch_shapes=[pltpu.SemaphoreType.DMA((count,))],
         compiler_params=SCRATCH,
         name="pack",
-    )(place, *far(basis.reshape(tiles, count, rows, lanes), x_rows, material))
+    )(place, *far(basis.reshape(tiles, count, rows, lanes), x_rows))
 
 
 def three_parts(values):
@@ -110,11 +111,13 @@
 
 
 def ahead_kernel(
-    sample_ref, *refs
+    sample_ref, place_ref, basis_ref, *refs
 ):
-    far_refs, refs = refs[:6], refs[6:]
-    material_ref, x_ref, own_ref, fields_ref, applied_ref, stack_ref, *near_refs, sems = refs
-    velocities_ref, shifts_ref, k0_ref, ke_ref, diag_ref, mass_ref = near_refs
+    far_refs, refs = refs[:7], refs[7:]
+    x_ref, fields_ref, applied_ref, stack_ref, *near_refs, piece_ref, sems = refs
+    velocities_ref, shifts_ref, k0_ref, ke_ref, diag_ref, mass_ref, material_ref = near_refs
+    own = pltpu.make_async_copy(basis_ref.at[:, place_ref[0]], piece_ref, sems.at[len(near_refs)])
+    own.start()
     copies = [
         pltpu.make_async_copy(source, target, sems.at[index])
         for index, (source, target) in enumerate(zip(far_refs, near_refs))
@@ -122,6 +125,8 @@
     for copy in copies:
         copy.start()
     group_cols = stack_ref.shape[0] // 3
+    own.wait()
+    own_ref = piece_ref.reshape(piece_ref.shape[0] * piece_ref.shape[1], piece_ref.shape[2])
     split_lines(
         own_ref, stack_ref, applied_ref.shape[0], group_cols, [i * group_cols for i in range(3)]
     )
@@ -177,28 +182,34 @@
             applied_ref[out * rows + row] = sums[out]
 
 
-def ahead(sample, velocities, shifts, k0, ke, diag, mass, material, x_rows, own, comps):
+def ahead(sample, place, basis, velocities, shifts, k0, ke, diag, mass, material, x_rows, comps):
     rows, lanes = material.shape
     lines = comps * rows
     stride = -(-k0.shape[1] // 8) * 8
     k0, ke = (jnp.transpose(blocks, (2, 3, 0, 1)) for blocks in (k0, ke))
-    tables = far(velocities, shifts, k0, ke, diag.T, mass.T)
+    tables = far(velocities, shifts, k0, ke, diag.T, mass.T, material)
+    group_cols, _, _, full_y, _ = basis.shape
+    tiles = group_cols * comps
+    basis = basis.reshape(tiles, full_y // rows, rows, lanes)
     return pl.pallas_call(
         ahead_kernel,
         out_shape=(
             near(rows, comps * comps * stride, lanes),
             near(lines, x_rows.shape[0] // lines, lanes),
-            near(3 * own.shape[0] // lines, lines * lanes, dtype=jnp.bfloat16),
+            near(3 * group_cols, lines * lanes, dtype=jnp.bfloat16),
         ),
-        in_specs=[SMEM] + [HBM] * 6 + [VMEM] * 3,
+        in_specs=[SMEM] * 2 + [HBM] * (1 + len(tables)) + [VMEM],
         out_specs=(VMEM,) * 3,
         scratch_shapes=[
-            (pltpu.SMEM if array.ndim == 1 else pltpu.VMEM)(array.shape, jnp.float32)
+            (pltpu.SMEM if array.ndim == 1 else pltpu.VMEM)(array.shape, array.dtype)
             for array in tables
-        ] + [pltpu.SemaphoreType.DMA((len(tables),))],
+        ] + [
+            pltpu.VMEM((tiles, rows, lanes), jnp.float32),
+            pltpu.SemaphoreType.DMA((len(tables) + 1,)),
+        ],
         compiler_params=SCRATCH,
         name="ahead",
-    )(sample, *tables, *kept(material, x_rows, own))
+    )(sample, place, *far(basis), *tables, *kept(x_rows))
 
 
 def side_terms(field_row, swapped, side, out, comp, comps):
@@ -634,7 +645,7 @@
     slab = lax.axis_index("space").astype(jnp.int32).reshape(1)
     count = lax.axis_size("basis")
     x_far = x_block.reshape(block_cols * lines, lanes)
-    own, *pieces, x_rows, material = pack(place, basis, x_far, material.reshape(rows, lanes), block_cols)
+    *pieces, x_rows = pack(place, basis, x_far, block_cols)
     got = {}
     for name in ("even", *reversed(partners(count)[0]), "odd"):
         if name == "even":
@@ -645,8 +656,8 @@
             piece = lax.ppermute(pieces[name - 1], "basis", [(i, i ^ name) for i in range(count)])
             got[name] = piece.reshape(-1, lanes)
     fields, applied, own = ahead(
-        sample, velocities, shifts, k0_blocks, ke_blocks, k0_diag, mass, material, x_rows,
-        own.reshape(-1, lanes), comps,
+        sample, place, basis, velocities, shifts, k0_blocks, ke_blocks, k0_diag, mass,
+        material.reshape(rows, lanes), x_rows, comps,
     )
     split = {0: own}
     first, *rest = reversed(partners(count)[1])

time: 36.6 us -> 36.5 us (level)
  no operation moved by 1% of the time
where the time goes in v22:
time: 36.5 us; the launch traced here: 36.3 us
  blocking collectives  14.1 us (39%)
  waiting for transfers between devices  7.57 us (21%)
  Pallas kernels  6.89 us (19%)
  starting transfers between devices  5.73 us (16%)
  between operations  1.39 us (4%)
  loops' own time  0.56 us (2%)
    all_to_all x1, blocking collectives, exchange_all(): lax.all_to_all(copies, ('space', 'basis'), 0, 0, axis_index_groups=groups)  14.1 us
    ppermute x2, waiting for transfers between devices, swap(): return lax.ppermute(values, axis, pairs + [(j, i) for i, j in pairs])  5.12 us
    ppermute x3, starting transfers between devices, shards(): lax.ppermute(pieces[name - 1], 'basis', [(i, i ^ name) for i in range(cou...  3.44 us
    pallas_call x1, Pallas kernels, finish(): pl.pallas_call(functools.partial(finish_kernel, row_count, comps), out_sh...  2.45 us
    ppermute x2, starting transfers between devices, swap(): return lax.ppermute(values, axis, pairs + [(j, i) for i, j in pairs])  2.15 us
    pallas_call x1, Pallas kernels, ahead(): pl.pallas_call(ahead_kernel, out_shape=(near(rows, comps * comps * stride...  1.9 us
    pallas_call x1, Pallas kernels, pack(): pl.pallas_call(functools.partial(pack_kernel, comps), out_shape=(*pieces,...  1.26 us
    ppermute x1, waiting for transfers between devices, exchange_all(): return (own, lax.ppermute(own, 'basis', pairs))  1.16 us
  transfers between devices with their start and end apart: 7, of which 4 were waited for; matrix products, arithmetic and copies ran while one was open for 0% of the time, Pallas kernels for 6%

profile of v22, /device:TPU:0, one launch (start us, length us, event | category | flops | bytes accessed | tf_op | source)
XLA Modules:
  0.0 36.3 jit_solution(10701714637827104047)
XLA Ops:
  0.6 1.3 %pack.1 = (f32[54,8,128]{2,1,0:T(8,128)S(1)}, f32[48,8,128]{2,1,0:T(8,128)S(1)}, f32[54,8,128]{2,1,0:T(8,128)S(1)}, f32[384,128]{1,0:T(8,128)S(1)}) custom-call(s32[1]{0:T(128)} %bitcast.116.place_ref, f32[48,4,8,128]{3,2,1,0:T(8,128)} %bitcast.271, f32[384,128]{1,0:T(8,128)} %bitcast.278), custom_call_target="tpu_custom_call" | custom-call | tf_op jit(solution)/shard_map/pack/pallas_call | solution.py:90
  1.9 2.5 %collective-permute-start.22 = (f32[54,8,128]{2,1,0:T(8,128)S(1)}, f32[54,8,128]{2,1,0:T(8,128)S(1)}, u32[]{:S(2)}, u32[]{:S(2)}) collective-permute-start(f32[54,8,128]{2,1,0:T(8,128)S(1)} %get-tuple-element.118), channel_id=1, source_target_pairs={{0,3},{1,2},{2,1},{3,0},{4,7},{5,6},{6,5},{7,4},{8,11},{9,10},{10,... | collective-permute-start | bytes 663560 | tf_op jit(solution)/shard_map/ppermute | solution.py:656
  4.4 1.5 %collective-permute-start.23 = (f32[384,128]{1,0:T(8,128)}, f32[384,128]{1,0:T(8,128)S(1)}, u32[]{:S(2)}, u32[]{:S(2)}) collective-permute-start(f32[384,128]{1,0:T(8,128)} %bitcast.279), channel_id=1, source_target_pairs={{0,4},{8,12},{16,20},{24,28},{4,0},{12,8},{20,16},{28,24},{1,5},{9... | collective-permute-start | bytes 589832 | tf_op jit(solution)/shard_map/ppermute | solution.py:39
  5.9 0.4 %collective-permute-start.24 = (f32[54,8,128]{2,1,0:T(8,128)S(1)}, f32[54,8,128]{2,1,0:T(8,128)S(1)}, u32[]{:S(2)}, u32[]{:S(2)}) collective-permute-start(f32[54,8,128]{2,1,0:T(8,128)S(1)} %get-tuple-element.120), channel_id=1, source_target_pairs={{0,1},{1,0},{2,3},{3,2},{4,5},{5,4},{6,7},{7,6},{8,9},{9,8},{10,11... | collective-permute-start | bytes 663560 | tf_op jit(solution)/shard_map/ppermute | solution.py:656
  6.3 0.7 %collective-permute-start.25 = (f32[384,128]{1,0:T(8,128)}, f32[384,128]{1,0:T(8,128)S(1)}, u32[]{:S(2)}, u32[]{:S(2)}) collective-permute-start(f32[384,128]{1,0:T(8,128)} %bitcast.280), channel_id=1, source_target_pairs={{4,8},{12,16},{20,24},{8,4},{16,12},{24,20},{5,9},{13,17},{21,25},... | collective-permute-start | bytes 589832 | tf_op jit(solution)/shard_map/ppermute | solution.py:39
  6.9 0.6 %collective-permute-start.26 = (f32[48,8,128]{2,1,0:T(8,128)S(1)}, f32[48,8,128]{2,1,0:T(8,128)S(1)}, u32[]{:S(2)}, u32[]{:S(2)}) collective-permute-start(f32[48,8,128]{2,1,0:T(8,128)S(1)} %get-tuple-element.125), channel_id=1, source_target_pairs={{0,2},{1,3},{2,0},{3,1},{4,6},{5,7},{6,4},{7,5},{8,10},{9,11},{10,... | collective-permute-start | bytes 589832 | tf_op jit(solution)/shard_map/ppermute | solution.py:656
  8.2 1.9 %ahead.1 = (f32[8,72,128]{2,1,0:T(8,128)S(1)}, f32[24,16,128]{2,1,0:T(8,128)S(1)}, bf16[48,3072]{1,0:T(8,128)(2,1)S(1)}) custom-call(s32[1]{0:T(128)S(6)} %copy.265.sample_ref, s32[1]{0:T(128)} %bitcast.116.place_ref, f32[48,4,8,128]{3,2,1,0:T(8,128)} %bitcast.272, f32[1024]{0:T(1024)} %refs_0_.1, f32[1024]{0:T(1024)} %refs_1_.1, f32[3,3,8,7]{3,2,1,0:T(8,128)} %bitcast.292, ...), custom_call_target="tpu_custom_call" | custom-call | tf_op jit(solution)/shard_map/ahead/pallas_call | solution.py:194
  10.1 0.1 collective-permute-done.22
  10.2 0.1 edges.2
  10.3 5.1 %collective-permute-done.23.halo_ref = f32[384,128]{1,0:T(8,128)S(1)} collective-permute-done((f32[384,128]{1,0:T(8,128)}, f32[384,128]{1,0:T(8,128)S(1)}, u32[]{:S(2)}, u32[]{:S(2)}) %collective-permute-start.23) | collective-permute-done | bytes 196640 | tf_op jit(solution)/shard_map/ppermute | solution.py:39
  15.4 0.1 side.2.applied_ref
  15.5 0.0 collective-permute-done.24
  15.5 0.1 edges.3
  15.6 0.0 collective-permute-done.25.halo_ref
  15.6 0.1 side.3.applied_ref
  15.7 0.0 collective-permute-done.26
  15.7 0.9 %sums.1 = (bf16[240,3072]{1,0:T(8,128)(2,1)S(1)}, f32[16,128]{1,0:T(8,128)S(1)}, f32[16,128]{1,0:T(8,128)S(1)}) custom-call(s32[1]{0:T(128)} %bitcast.116.place_ref, f32[24,16,128]{2,1,0:T(8,128)S(1)} %side.3.applied_ref, bf16[48,3072]{1,0:T(8,128)(2,1)S(1)} %get-tuple-element.122.refs_0_, bf16[48,3072]{1,0:T(8,128)(2,1)S(1)} %get-tuple-element.123.refs_1_, ...), custom_call_target="tpu_custom_call" | custom-call | tf_op jit(solution)/shard_map/sums/pallas_call | solution.py:376
  16.6 0.1 collective-permute-start.27
  16.7 1.2 %collective-permute-done.27 = f32[16,128]{1,0:T(8,128)S(1)} collective-permute-done((f32[16,128]{1,0:T(8,128)S(1)}, f32[16,128]{1,0:T(8,128)S(1)}, u32[]{:S(2)}, u32[]{:S(2)}) %collective-permute-start.27) | collective-permute-done | bytes 8224 | tf_op jit(solution)/shard_map/ppermute | solution.py:393
  17.9 14.1 %all_to_all.5 = f32[16,16,128]{2,1,0:T(8,128)S(1)} all-to-all(f32[16,16,128]{2,1,0:T(8,128)S(1)} %broadcast_in_dim.34), channel_id=1, replica_groups={{0,2,4,6,8,10,12,14,16,18,20,22,24,26,28,30},{1,3,5,7,9,11,13,15,17,19,..., dimensions={0} | all-to-all | bytes 262144 | tf_op jit(solution)/shard_map/all_to_all | solution.py:399
  32.0 0.1 collective-permute-start.28
  32.1 1.2 %collective-permute-done.28.given_ref = f32[16,128]{1,0:T(8,128)S(1)} collective-permute-done((f32[16,128]{1,0:T(8,128)S(1)}, f32[16,128]{1,0:T(8,128)S(1)}, u32[]{:S(2)}, u32[]{:S(2)}) %collective-permute-start.28) | collective-permute-done | bytes 8224 | tf_op jit(solution)/shard_map/ppermute | solution.py:401
  33.3 2.4 %finish.1 = (f32[16,24,128]{2,1,0:T(8,128)}, f32[16,16]{1,0:T(8,128)}, f32[16,16]{1,0:T(8,128)}, s32[1,1]{1,0:T(1,128)}) custom-call(s32[1]{0:T(128)} %bitcast.116.place_ref, f32[16,128]{1,0:T(8,128)S(1)} %reduce_sum.9.own_ref, f32[16,128]{1,0:T(8,128)S(1)} %collective-permute-done.28.given_ref, bf16[240,3072]{1,0:T(8,128)(2,1)S(1)} %get-tuple-element.128.stack_ref), custom_call_target="tpu_custom_call" | custom-call | tf_op jit(solution)/shard_map/finish/pallas_call | solution.py:504
  35.7 0.6 %while.14 = (s32[]{:T(128)}, f32[16,24,128]{2,1,0:T(8,128)}, f32[16,16]{1,0:T(8,128)}, f32[16,16]{1,0:T(8,128)}, f32[8,7,3,3]{1,0,3,2:T(8,128)}, /*index=5*/f32[...) while((s32[]{:T(128)}, f32[16,24,128]{2,1,0:T(8,128)}, ...), condition=%region_4.5_spmd, body=%region_1.4_spmd | while | flops 175311344 | bytes 29713228 | solution.py:678
  (3 shorter events, 0.0 us)
Async XLA Ops:
  1.9 8.3 %collective-permute-start.22 = (f32[54,8,128]{2,1,0:T(8,128)S(1)}, f32[54,8,128]{2,1,0:T(8,128)S(1)}, u32[]{:S(2)}, u32[]{:S(2)}) collective-permute-start(f32[54,8,128]{2,1,0:T(8,128)S(1)} %get-tuple-element.118), channel_id=1, source_target_pairs={{0,3},{1,2},{2,1},{3,0},{4,7},{5,6},{6,5},{7,4},{8,11},{9,10},{10,... | collective-permute-start | bytes 663560 | tf_op jit(solution)/shard_map/ppermute | solution.py:656
  4.4 11.0 %collective-permute-start.23 = (f32[384,128]{1,0:T(8,128)}, f32[384,128]{1,0:T(8,128)S(1)}, u32[]{:S(2)}, u32[]{:S(2)}) collective-permute-start(f32[384,128]{1,0:T(8,128)} %bitcast.279), channel_id=1, source_target_pairs={{0,4},{8,12},{16,20},{24,28},{4,0},{12,8},{20,16},{28,24},{1,5},{9... | collective-permute-start | bytes 589832 | tf_op jit(solution)/shard_map/ppermute | solution.py:39
  5.9 9.6 %collective-permute-start.24 = (f32[54,8,128]{2,1,0:T(8,128)S(1)}, f32[54,8,128]{2,1,0:T(8,128)S(1)}, u32[]{:S(2)}, u32[]{:S(2)}) collective-permute-start(f32[54,8,128]{2,1,0:T(8,128)S(1)} %get-tuple-element.120), channel_id=1, source_target_pairs={{0,1},{1,0},{2,3},{3,2},{4,5},{5,4},{6,7},{7,6},{8,9},{9,8},{10,11... | collective-permute-start | bytes 663560 | tf_op jit(solution)/shard_map/ppermute | solution.py:656
  6.3 9.3 %collective-permute-start.25 = (f32[384,128]{1,0:T(8,128)}, f32[384,128]{1,0:T(8,128)S(1)}, u32[]{:S(2)}, u32[]{:S(2)}) collective-permute-start(f32[384,128]{1,0:T(8,128)} %bitcast.280), channel_id=1, source_target_pairs={{4,8},{12,16},{20,24},{8,4},{16,12},{24,20},{5,9},{13,17},{21,25},... | collective-permute-start | bytes 589832 | tf_op jit(solution)/shard_map/ppermute | solution.py:39
  6.9 8.8 %collective-permute-start.26 = (f32[48,8,128]{2,1,0:T(8,128)S(1)}, f32[48,8,128]{2,1,0:T(8,128)S(1)}, u32[]{:S(2)}, u32[]{:S(2)}) collective-permute-start(f32[48,8,128]{2,1,0:T(8,128)S(1)} %get-tuple-element.125), channel_id=1, source_target_pairs={{0,2},{1,3},{2,0},{3,1},{4,6},{5,7},{6,4},{7,5},{8,10},{9,11},{10,... | collective-permute-start | bytes 589832 | tf_op jit(solution)/shard_map/ppermute | solution.py:656
  16.6 1.2 %collective-permute-start.27 = (f32[16,128]{1,0:T(8,128)S(1)}, f32[16,128]{1,0:T(8,128)S(1)}, u32[]{:S(2)}, u32[]{:S(2)}) collective-permute-start(f32[16,128]{1,0:T(8,128)S(1)} %get-tuple-element.127), channel_id=1, source_target_pairs={{0,1},{1,0},{2,3},{3,2},{4,5},{5,4},{6,7},{7,6},{8,9},{9,8},{10,11... | collective-permute-start | bytes 24584 | tf_op jit(solution)/shard_map/ppermute | solution.py:393
  32.0 1.2 %collective-permute-start.28 = (f32[16,128]{1,0:T(8,128)S(1)}, f32[16,128]{1,0:T(8,128)S(1)}, u32[]{:S(2)}, u32[]{:S(2)}) collective-permute-start(f32[16,128]{1,0:T(8,128)S(1)} %reduce_sum.9.own_ref), channel_id=1, source_target_pairs={{0,1},{1,0},{2,3},{3,2},{4,5},{5,4},{6,7},{7,6},{8,9},{9,8},{10,11... | collective-permute-start | bytes 24584 | tf_op jit(solution)/shard_map/ppermute | solution.py:401

commit v23 on v22

--- a/solution.py
+++ b/solution.py
@@ -392,7 +392,7 @@
     pairs = [(i, i ^ 1) for i in range(sizes[1])]
     part = keep + lax.ppermute(give, "basis", pairs)
     groups = [
-        [i * sizes[1] + j for i in range(sizes[0]) for j in range(first, sizes[1], 2)]
+        [i * sizes[1] + j for i in range(sizes[0]) for j in range(first, sizes[1], 2)][::-1]
         for first in range(2)
     ]
     copies = jnp.broadcast_to(part[None], (len(groups[0]),) + part.shape)

time: 36.5 us -> 34.3 us (0.940)
  blocking collectives: 14.1 us -> 11.9 us
    all_to_all x1, blocking collectives: 14.1 us -> 11.9 us  [exchange_all(): lax.all_to_all(copies, ('space', 'basis'), 0, 0, axis_index_groups=groups)]
  transfers between devices with their start and end apart: 7 -> 7, of which waited for: 4 -> 4; matrix products, arithmetic and copies ran while one was open for 0% -> 0% of each run, Pallas kernels for 6% -> 7%
where the time goes in v23:
time: 34.3 us; the launch traced here: 34.1 us
  blocking collectives  11.9 us (35%)
  waiting for transfers between devices  7.57 us (22%)
  Pallas kernels  6.89 us (20%)
  starting transfers between devices  5.73 us (17%)
  between operations  1.39 us (4%)
  loops' own time  0.56 us (2%)
    all_to_all x1, blocking collectives, exchange_all(): lax.all_to_all(copies, ('space', 'basis'), 0, 0, axis_index_groups=groups)  11.9 us
    ppermute x2, waiting for transfers between devices, swap(): return lax.ppermute(values, axis, pairs + [(j, i) for i, j in pairs])  5.12 us
    ppermute x3, starting transfers between devices, shards(): lax.ppermute(pieces[name - 1], 'basis', [(i, i ^ name) for i in range(cou...  3.44 us
    pallas_call x1, Pallas kernels, finish(): pl.pallas_call(functools.partial(finish_kernel, row_count, comps), out_sh...  2.45 us
    ppermute x2, starting transfers between devices, swap(): return lax.ppermute(values, axis, pairs + [(j, i) for i, j in pairs])  2.15 us
    pallas_call x1, Pallas kernels, ahead(): pl.pallas_call(ahead_kernel, out_shape=(near(rows, comps * comps * stride...  1.9 us
    pallas_call x1, Pallas kernels, pack(): pl.pallas_call(functools.partial(pack_kernel, comps), out_shape=(*pieces,...  1.26 us
    ppermute x1, waiting for transfers between devices, exchange_all(): part = keep + lax.ppermute(give, 'basis', pairs)  1.16 us
  transfers between devices with their start and end apart: 7, of which 4 were waited for; matrix products, arithmetic and copies ran while one was open for 0% of the time, Pallas kernels for 7%

profile of v23, /device:TPU:0, one launch (start us, length us, event | category | flops | bytes accessed | tf_op | source)
XLA Modules:
  0.0 34.1 jit_solution(4763607803315595881)
XLA Ops:
  0.6 1.3 %pack.1 = (f32[54,8,128]{2,1,0:T(8,128)S(1)}, f32[48,8,128]{2,1,0:T(8,128)S(1)}, f32[54,8,128]{2,1,0:T(8,128)S(1)}, f32[384,128]{1,0:T(8,128)S(1)}) custom-call(s32[1]{0:T(128)} %bitcast.116.place_ref, f32[48,4,8,128]{3,2,1,0:T(8,128)} %bitcast.271, f32[384,128]{1,0:T(8,128)} %bitcast.278), custom_call_target="tpu_custom_call" | custom-call | tf_op jit(solution)/shard_map/pack/pallas_call | solution.py:90
  1.9 2.5 %collective-permute-start.22 = (f32[54,8,128]{2,1,0:T(8,128)S(1)}, f32[54,8,128]{2,1,0:T(8,128)S(1)}, u32[]{:S(2)}, u32[]{:S(2)}) collective-permute-start(f32[54,8,128]{2,1,0:T(8,128)S(1)} %get-tuple-element.118), channel_id=1, source_target_pairs={{0,3},{1,2},{2,1},{3,0},{4,7},{5,6},{6,5},{7,4},{8,11},{9,10},{10,... | collective-permute-start | bytes 663560 | tf_op jit(solution)/shard_map/ppermute | solution.py:656
  4.4 1.5 %collective-permute-start.23 = (f32[384,128]{1,0:T(8,128)}, f32[384,128]{1,0:T(8,128)S(1)}, u32[]{:S(2)}, u32[]{:S(2)}) collective-permute-start(f32[384,128]{1,0:T(8,128)} %bitcast.279), channel_id=1, source_target_pairs={{0,4},{8,12},{16,20},{24,28},{4,0},{12,8},{20,16},{28,24},{1,5},{9... | collective-permute-start | bytes 589832 | tf_op jit(solution)/shard_map/ppermute | solution.py:39
  5.9 0.4 %collective-permute-start.24 = (f32[54,8,128]{2,1,0:T(8,128)S(1)}, f32[54,8,128]{2,1,0:T(8,128)S(1)}, u32[]{:S(2)}, u32[]{:S(2)}) collective-permute-start(f32[54,8,128]{2,1,0:T(8,128)S(1)} %get-tuple-element.120), channel_id=1, source_target_pairs={{0,1},{1,0},{2,3},{3,2},{4,5},{5,4},{6,7},{7,6},{8,9},{9,8},{10,11... | collective-permute-start | bytes 663560 | tf_op jit(solution)/shard_map/ppermute | solution.py:656
  6.3 0.7 %collective-permute-start.25 = (f32[384,128]{1,0:T(8,128)}, f32[384,128]{1,0:T(8,128)S(1)}, u32[]{:S(2)}, u32[]{:S(2)}) collective-permute-start(f32[384,128]{1,0:T(8,128)} %bitcast.280), channel_id=1, source_target_pairs={{4,8},{12,16},{20,24},{8,4},{16,12},{24,20},{5,9},{13,17},{21,25},... | collective-permute-start | bytes 589832 | tf_op jit(solution)/shard_map/ppermute | solution.py:39
  6.9 0.6 %collective-permute-start.26 = (f32[48,8,128]{2,1,0:T(8,128)S(1)}, f32[48,8,128]{2,1,0:T(8,128)S(1)}, u32[]{:S(2)}, u32[]{:S(2)}) collective-permute-start(f32[48,8,128]{2,1,0:T(8,128)S(1)} %get-tuple-element.125), channel_id=1, source_target_pairs={{0,2},{1,3},{2,0},{3,1},{4,6},{5,7},{6,4},{7,5},{8,10},{9,11},{10,... | collective-permute-start | bytes 589832 | tf_op jit(solution)/shard_map/ppermute | solution.py:656
  8.2 1.9 %ahead.1 = (f32[8,72,128]{2,1,0:T(8,128)S(1)}, f32[24,16,128]{2,1,0:T(8,128)S(1)}, bf16[48,3072]{1,0:T(8,128)(2,1)S(1)}) custom-call(s32[1]{0:T(128)S(6)} %copy.265.sample_ref, s32[1]{0:T(128)} %bitcast.116.place_ref, f32[48,4,8,128]{3,2,1,0:T(8,128)} %bitcast.272, f32[1024]{0:T(1024)} %refs_0_.1, f32[1024]{0:T(1024)} %refs_1_.1, f32[3,3,8,7]{3,2,1,0:T(8,128)} %bitcast.292, ...), custom_call_target="tpu_custom_call" | custom-call | tf_op jit(solution)/shard_map/ahead/pallas_call | solution.py:194
  10.1 0.1 collective-permute-done.22
  10.2 0.1 edges.2
  10.3 5.1 %collective-permute-done.23.halo_ref = f32[384,128]{1,0:T(8,128)S(1)} collective-permute-done((f32[384,128]{1,0:T(8,128)}, f32[384,128]{1,0:T(8,128)S(1)}, u32[]{:S(2)}, u32[]{:S(2)}) %collective-permute-start.23) | collective-permute-done | bytes 196640 | tf_op jit(solution)/shard_map/ppermute | solution.py:39
  15.4 0.1 side.2.applied_ref
  15.5 0.0 collective-permute-done.24
  15.5 0.1 edges.3
  15.6 0.0 collective-permute-done.25.halo_ref
  15.6 0.1 side.3.applied_ref
  15.7 0.0 collective-permute-done.26
  15.7 0.9 %sums.1 = (bf16[240,3072]{1,0:T(8,128)(2,1)S(1)}, f32[16,128]{1,0:T(8,128)S(1)}, f32[16,128]{1,0:T(8,128)S(1)}) custom-call(s32[1]{0:T(128)} %bitcast.116.place_ref, f32[24,16,128]{2,1,0:T(8,128)S(1)} %side.3.applied_ref, bf16[48,3072]{1,0:T(8,128)(2,1)S(1)} %get-tuple-element.122.refs_0_, bf16[48,3072]{1,0:T(8,128)(2,1)S(1)} %get-tuple-element.123.refs_1_, ...), custom_call_target="tpu_custom_call" | custom-call | tf_op jit(solution)/shard_map/sums/pallas_call | solution.py:376
  16.6 0.1 collective-permute-start.27
  16.7 1.2 %collective-permute-done.27 = f32[16,128]{1,0:T(8,128)S(1)} collective-permute-done((f32[16,128]{1,0:T(8,128)S(1)}, f32[16,128]{1,0:T(8,128)S(1)}, u32[]{:S(2)}, u32[]{:S(2)}) %collective-permute-start.27) | collective-permute-done | bytes 8224 | tf_op jit(solution)/shard_map/ppermute | solution.py:393
  17.9 11.9 %all_to_all.5 = f32[16,16,128]{2,1,0:T(8,128)S(1)} all-to-all(f32[16,16,128]{2,1,0:T(8,128)S(1)} %broadcast_in_dim.34), channel_id=1, replica_groups={{30,28,26,24,22,20,18,16,14,12,10,8,6,4,2,0},{31,29,27,25,23,21,19,17,1..., dimensions={0} | all-to-all | bytes 262144 | tf_op jit(solution)/shard_map/all_to_all | solution.py:399
  29.8 0.1 collective-permute-start.28
  29.9 1.2 %collective-permute-done.28.given_ref = f32[16,128]{1,0:T(8,128)S(1)} collective-permute-done((f32[16,128]{1,0:T(8,128)S(1)}, f32[16,128]{1,0:T(8,128)S(1)}, u32[]{:S(2)}, u32[]{:S(2)}) %collective-permute-start.28) | collective-permute-done | bytes 8224 | tf_op jit(solution)/shard_map/ppermute | solution.py:401
  31.1 2.4 %finish.1 = (f32[16,24,128]{2,1,0:T(8,128)}, f32[16,16]{1,0:T(8,128)}, f32[16,16]{1,0:T(8,128)}, s32[1,1]{1,0:T(1,128)}) custom-call(s32[1]{0:T(128)} %bitcast.116.place_ref, f32[16,128]{1,0:T(8,128)S(1)} %reduce_sum.9.own_ref, f32[16,128]{1,0:T(8,128)S(1)} %collective-permute-done.28.given_ref, bf16[240,3072]{1,0:T(8,128)(2,1)S(1)} %get-tuple-element.128.stack_ref), custom_call_target="tpu_custom_call" | custom-call | tf_op jit(solution)/shard_map/finish/pallas_call | solution.py:504
  33.5 0.6 %while.14 = (s32[]{:T(128)}, f32[16,24,128]{2,1,0:T(8,128)}, f32[16,16]{1,0:T(8,128)}, f32[16,16]{1,0:T(8,128)}, f32[8,7,3,3]{1,0,3,2:T(8,128)}, /*index=5*/f32[...) while((s32[]{:T(128)}, f32[16,24,128]{2,1,0:T(8,128)}, ...), condition=%region_4.5_spmd, body=%region_1.4_spmd | while | flops 175311344 | bytes 29713228 | solution.py:678
  (3 shorter events, 0.0 us)
Async XLA Ops:
  1.9 8.3 %collective-permute-start.22 = (f32[54,8,128]{2,1,0:T(8,128)S(1)}, f32[54,8,128]{2,1,0:T(8,128)S(1)}, u32[]{:S(2)}, u32[]{:S(2)}) collective-permute-start(f32[54,8,128]{2,1,0:T(8,128)S(1)} %get-tuple-element.118), channel_id=1, source_target_pairs={{0,3},{1,2},{2,1},{3,0},{4,7},{5,6},{6,5},{7,4},{8,11},{9,10},{10,... | collective-permute-start | bytes 663560 | tf_op jit(solution)/shard_map/ppermute | solution.py:656
  4.4 11.0 %collective-permute-start.23 = (f32[384,128]{1,0:T(8,128)}, f32[384,128]{1,0:T(8,128)S(1)}, u32[]{:S(2)}, u32[]{:S(2)}) collective-permute-start(f32[384,128]{1,0:T(8,128)} %bitcast.279), channel_id=1, source_target_pairs={{0,4},{8,12},{16,20},{24,28},{4,0},{12,8},{20,16},{28,24},{1,5},{9... | collective-permute-start | bytes 589832 | tf_op jit(solution)/shard_map/ppermute | solution.py:39
  5.9 9.6 %collective-permute-start.24 = (f32[54,8,128]{2,1,0:T(8,128)S(1)}, f32[54,8,128]{2,1,0:T(8,128)S(1)}, u32[]{:S(2)}, u32[]{:S(2)}) collective-permute-start(f32[54,8,128]{2,1,0:T(8,128)S(1)} %get-tuple-element.120), channel_id=1, source_target_pairs={{0,1},{1,0},{2,3},{3,2},{4,5},{5,4},{6,7},{7,6},{8,9},{9,8},{10,11... | collective-permute-start | bytes 663560 | tf_op jit(solution)/shard_map/ppermute | solution.py:656
  6.3 9.3 %collective-permute-start.25 = (f32[384,128]{1,0:T(8,128)}, f32[384,128]{1,0:T(8,128)S(1)}, u32[]{:S(2)}, u32[]{:S(2)}) collective-permute-start(f32[384,128]{1,0:T(8,128)} %bitcast.280), channel_id=1, source_target_pairs={{4,8},{12,16},{20,24},{8,4},{16,12},{24,20},{5,9},{13,17},{21,25},... | collective-permute-start | bytes 589832 | tf_op jit(solution)/shard_map/ppermute | solution.py:39
  6.9 8.8 %collective-permute-start.26 = (f32[48,8,128]{2,1,0:T(8,128)S(1)}, f32[48,8,128]{2,1,0:T(8,128)S(1)}, u32[]{:S(2)}, u32[]{:S(2)}) collective-permute-start(f32[48,8,128]{2,1,0:T(8,128)S(1)} %get-tuple-element.125), channel_id=1, source_target_pairs={{0,2},{1,3},{2,0},{3,1},{4,6},{5,7},{6,4},{7,5},{8,10},{9,11},{10,... | collective-permute-start | bytes 589832 | tf_op jit(solution)/shard_map/ppermute | solution.py:656
  16.6 1.2 %collective-permute-start.27 = (f32[16,128]{1,0:T(8,128)S(1)}, f32[16,128]{1,0:T(8,128)S(1)}, u32[]{:S(2)}, u32[]{:S(2)}) collective-permute-start(f32[16,128]{1,0:T(8,128)S(1)} %get-tuple-element.127), channel_id=1, source_target_pairs={{0,1},{1,0},{2,3},{3,2},{4,5},{5,4},{6,7},{7,6},{8,9},{9,8},{10,11... | collective-permute-start | bytes 24584 | tf_op jit(solution)/shard_map/ppermute | solution.py:393
  29.8 1.2 %collective-permute-start.28 = (f32[16,128]{1,0:T(8,128)S(1)}, f32[16,128]{1,0:T(8,128)S(1)}, u32[]{:S(2)}, u32[]{:S(2)}) collective-permute-start(f32[16,128]{1,0:T(8,128)S(1)} %reduce_sum.9.own_ref), channel_id=1, source_target_pairs={{0,1},{1,0},{2,3},{3,2},{4,5},{5,4},{6,7},{7,6},{8,9},{9,8},{10,11... | collective-permute-start | bytes 24584 | tf_op jit(solution)/shard_map/ppermute | solution.py:401
